TPU v7x, 32 devices: a whole 2x2x4 slice. The times are simulated.
32 devices in a mesh: shard: 2 (over x), rep: 16 (over z, y, core).
Axes of the slice: x: 2, y: 2, z: 4, core: 2. Of those that a mesh axis runs over, the one named last changes fastest.
Arguments:
- hidden: bfloat16 [4, 2048, 768], P('shard', 'rep'), may hold values from -6 to 6
- encoded: bfloat16 [4, 512, 768], P('shard', 'rep'), may hold values from -6 to 6
- out_grad: bfloat16 [4, 2048, 768], P('shard', 'rep'), may hold values from -6 to 6
- self_query: float32 [768, 768], P('shard'), may hold values from -0.078125 to 0.078125
- self_key: float32 [768, 768], P('shard'), may hold values from -0.078125 to 0.078125
- self_value: float32 [768, 768], P('shard'), may hold values from -0.21875 to 0.21875
- self_out: float32 [768, 768], P('shard'), may hold values from -1.25 to 1.25
- cross_query: float32 [768, 768], P('shard'), may hold values from -0.078125 to 0.078125
- cross_key: float32 [768, 768], P('shard'), may hold values from -0.078125 to 0.078125
- cross_value: float32 [768, 768], P('shard'), may hold values from -0.21875 to 0.21875
- cross_out: float32 [768, 768], P('shard'), may hold values from -0.625 to 0.625
- ffn_gate: float32 [768, 2048], P('shard'), may hold values from -0.21875 to 0.21875
- ffn_up: float32 [768, 2048], P('shard'), may hold values from -0.21875 to 0.21875
- ffn_down: float32 [2048, 768], P('shard'), may hold values from -0.125 to 0.125
- gain_self: float32 [768], P('shard'), may hold values from 0.5 to 1.5
- gain_cross: float32 [768], P('shard'), may hold values from 0.5 to 1.5
- gain_ffn: float32 [768], P('shard'), may hold values from 0.5 to 1.5
- bias_table: float32 [32, 12], P('shard'), may hold values from -4 to 4
- buckets: int32 [2048], replicated, may hold values from 0 to 31, as said below
Outputs:
- output: bfloat16 [4, 2048, 768], P('shard', 'rep')
- hidden_grad: bfloat16 [4, 2048, 768], P('shard', 'rep')
- encoded_grad: bfloat16 [4, 512, 768], P('shard', 'rep')
- self_query_grad: float32 [768, 768], P('shard')
- self_key_grad: float32 [768, 768], P('shard')
- self_value_grad: float32 [768, 768], P('shard')
- self_out_grad: float32 [768, 768], P('shard')
- cross_query_grad: float32 [768, 768], P('shard')
- cross_key_grad: float32 [768, 768], P('shard')
- cross_value_grad: float32 [768, 768], P('shard')
- cross_out_grad: float32 [768, 768], P('shard')
- ffn_gate_grad: float32 [768, 2048], P('shard')
- ffn_up_grad: float32 [768, 2048], P('shard')
- ffn_down_grad: float32 [2048, 768], P('shard')
- gain_self_grad: float32 [768], P('shard')
- gain_cross_grad: float32 [768], P('shard')
- gain_ffn_grad: float32 [768], P('shard')
- bias_table_grad: float32 [32, 12], P('shard')
Inputs may be any that keep to these rules, and one draw needn't show every extreme that they name: buckets[d] is a relabelling, by a permutation of the 32 buckets, of T5's causal relative position bucket of distance d with 32 buckets and max distance 128: distances below 16 have buckets of their own, distances up to 127 are spaced logarithmically over the other buckets, and every distance of 128 or more falls in the same bucket as 127.
All inputs are finite; a program needn't handle non-finite values.
Results may differ from a plain program's by a relative error of at most 0.03.
Values may be sent and summed in bfloat16 or wider, within the bound.
A program may use at most 256 MiB of HBM per device.

v0:
```python
import math

import jax
import jax.numpy as jnp
from jax import lax
from jax.sharding import PartitionSpec as P

D = 768
H = 12
DH = 64
NB = 32


EPS = 1e-06
F32 = jnp.float32
B16 = jnp.bfloat16


def normalize(rows, gain):
    return rows * lax.rsqrt(jnp.mean(rows * rows, axis=-1, keepdims=True) + EPS) * gain


def norm_back(rows, gain, grad):
    value, pull = jax.vjp(normalize, rows, gain)
    return pull(grad)


def gated(gate_in, up_in):
    return jax.nn.gelu(gate_in, approximate=True) * up_in


def matmul(left, right):
    return jnp.einsum("std,de->ste", left, right, preferred_element_type=F32)


def matmul_back(grad, weight):
    return jnp.einsum("ste,de->std", grad, weight, preferred_element_type=F32)


def outer_sum(left, grad):
    return jnp.einsum("std,ste->de", left, grad, preferred_element_type=F32)


def split_heads(rows):
    return rows.reshape(rows.shape[0], rows.shape[1], H, DH)


def join_heads(rows):
    return rows.reshape(rows.shape[0], rows.shape[1], H * DH)


def offset_table(buckets, table):
    onehot = (buckets[:, None] == jnp.arange(NB, dtype=jnp.int32)[None, :]).astype(B16)
    return jnp.einsum("lb,bh->hl", onehot, table, preferred_element_type=F32)


def diagonal_offsets(query_start, key_start, query_count, key_count):
    width = query_count + key_count
    column = jnp.arange(width, dtype=jnp.int32)
    signed = jnp.where(column < key_count, column, column - width)
    return query_start - key_start - signed


def self_scores(queries, keys, query_start, key_start, offset_bias):
    query_count = queries.shape[1]
    key_count = keys.shape[1]
    width = query_count + key_count
    offsets = diagonal_offsets(query_start, key_start, query_count, key_count)
    line = jnp.take(offset_bias, jnp.clip(offsets, 0, offset_bias.shape[1] - 1), axis=1)
    tiled = jnp.broadcast_to(line[:, None, :], (H, query_count + 1, width)).reshape(
        H, (query_count + 1) * width
    )
    bias = tiled[:, : query_count * (width - 1)].reshape(H, query_count, width - 1)[
        :, :, :key_count
    ]
    query_pos = query_start + jnp.arange(query_count, dtype=jnp.int32)
    key_pos = key_start + jnp.arange(key_count, dtype=jnp.int32)
    valid = query_pos[:, None] - key_pos[None, :] >= 0
    scores = jnp.einsum("sqhd,skhd->shqk", queries, keys, preferred_element_type=F32) + bias[None]
    return (scores, valid[None, None], offsets)


def table_terms(dscore, offsets, buckets):
    summed = jnp.sum(dscore.astype(F32), axis=0)
    query_count = summed.shape[1]
    key_count = summed.shape[2]
    width = query_count + key_count
    padded = jnp.pad(summed, ((0, 0), (0, 0), (0, width - 1 - key_count)))
    flat = padded.reshape(H, query_count * (width - 1))
    flat = jnp.pad(flat, ((0, 0), (0, (query_count + 1) * width - query_count * (width - 1))))
    diagonal = jnp.sum(flat.reshape(H, query_count + 1, width), axis=1)
    labels = jnp.take(buckets, jnp.clip(offsets, 0, buckets.shape[0] - 1))
    onehot = (
        (labels[:, None] == jnp.arange(NB, dtype=jnp.int32)[None, :]) & (offsets >= 0)[:, None]
    ).astype(F32)
    return jnp.einsum("hn,nb->bh", diagonal, onehot, precision=lax.Precision.HIGHEST)


def make_forward_fold(query_heads, own_start, offset_bias):

    def fold(carry, piece, start):
        keys_in, values_in = piece
        count = keys_in.shape[1]
        block = math.gcd(count, 512)

        def step(index, state):
            run_max, run_sum, accum = state
            offset = index * block
            key_heads = split_heads(lax.dynamic_slice_in_dim(keys_in, offset, block, 1))
            value_heads = split_heads(lax.dynamic_slice_in_dim(values_in, offset, block, 1))
            scores, valid, ignored = self_scores(
                query_heads, key_heads, own_start, offset, offset_bias
            )
            new_max = jnp.maximum(run_max, jnp.max(jnp.where(valid, scores, -1e30), axis=-1))
            expo = jnp.where(valid, jnp.exp(scores - new_max[..., None]), 0.0)
            shrink = jnp.exp(run_max - new_max)
            run_sum = run_sum * shrink + jnp.sum(expo, axis=-1)
            accum = accum * jnp.transpose(shrink, (0, 2, 1))[..., None] + jnp.einsum(
                "shqk,skhd->sqhd", expo.astype(B16), value_heads, preferred_element_type=F32
            )
            return (new_max, run_sum, accum)

        return lax.fori_loop(0, count // block, step, carry)

    return fold


def make_key_fold(query_heads, grad_heads, log_sum, delta_rows, own_start, offset_bias, buckets):

    def fold(carry, piece, start):
        keys_in, values_in = piece
        count = keys_in.shape[1]
        block = math.gcd(count, 512)

        def step(index, state):
            offset = index * block
            key_heads = split_heads(lax.dynamic_slice_in_dim(keys_in, offset, block, 1))
            value_heads = split_heads(lax.dynamic_slice_in_dim(values_in, offset, block, 1))
            scores, valid, offsets = self_scores(
                query_heads, key_heads, own_start, offset, offset_bias
            )
            prob = jnp.where(valid, jnp.exp(scores - log_sum[..., None]), 0.0)
            dprob = jnp.einsum(
                "sqhd,skhd->shqk", grad_heads, value_heads, preferred_element_type=F32
            )
            dscore = jnp.where(valid, prob * (dprob - delta_rows[..., None]), 0.0).astype(B16)
            query_acc = state[0] + jnp.einsum(
                "shqk,skhd->sqhd", dscore, key_heads, preferred_element_type=F32
            )
            table_acc = state[1] + table_terms(dscore, offsets, buckets)
            key_part = join_heads(
                jnp.einsum("shqk,sqhd->skhd", dscore, query_heads, preferred_element_type=F32)
            )
            value_part = join_heads(
                jnp.einsum(
                    "shqk,sqhd->skhd", prob.astype(B16), grad_heads, preferred_element_type=F32
                )
            )
            key_all = lax.dynamic_update_slice_in_dim(state[2], key_part, offset, 1)
            value_all = lax.dynamic_update_slice_in_dim(state[3], value_part, offset, 1)
            return (query_acc, table_acc, key_all, value_all)

        return lax.fori_loop(0, count // block, step, carry)

    return fold


def fetch_forward(parts):
    return (
        lax.all_gather(parts[0], "shard", axis=0, tiled=True),
        lax.all_gather(parts[1], "shard", axis=0, tiled=True),
        lax.all_gather(parts[2], "shard", axis=0, tiled=True),
        lax.all_gather(parts[3], "shard", axis=0, tiled=True),
        lax.all_gather(parts[4], "shard", axis=0, tiled=True),
        lax.all_gather(parts[5], "shard", axis=0, tiled=True),
        lax.all_gather(parts[6], "shard", axis=0, tiled=True),
        lax.all_gather(parts[7], "shard", axis=0, tiled=True),
        lax.all_gather(parts[8], "shard", axis=0, tiled=True),
        lax.all_gather(parts[9], "shard", axis=0, tiled=True),
        lax.all_gather(parts[10], "shard", axis=0, tiled=True),
        lax.all_gather(parts[11], "shard", axis=0, tiled=True),
        lax.all_gather(parts[12], "shard", axis=0, tiled=True),
        lax.all_gather(parts[13], "shard", axis=0, tiled=True),
        lax.all_gather(parts[14], "shard", axis=0, tiled=True),
    )


def fetch_backward(parts):
    return (
        lax.all_gather(parts[0], "shard", axis=0, tiled=True),
        lax.all_gather(parts[1], "shard", axis=0, tiled=True),
        lax.all_gather(parts[2], "shard", axis=0, tiled=True),
        lax.all_gather(parts[3], "shard", axis=0, tiled=True),
        lax.all_gather(parts[4], "shard", axis=0, tiled=True),
        lax.all_gather(parts[5], "shard", axis=0, tiled=True),
        lax.all_gather(parts[6], "shard", axis=0, tiled=True),
        lax.all_gather(parts[7], "shard", axis=0, tiled=True),
        lax.all_gather(parts[8], "shard", axis=0, tiled=True),
        lax.all_gather(parts[9], "shard", axis=0, tiled=True),
        lax.all_gather(parts[10], "shard", axis=0, tiled=True),
        lax.all_gather(parts[11], "shard", axis=0, tiled=True),
        lax.all_gather(parts[12], "shard", axis=0, tiled=True),
        lax.all_gather(parts[13], "shard", axis=0, tiled=True),
        lax.all_gather(parts[14], "shard", axis=0, tiled=True),
    )


def reduce_owner(parts):
    return (
        lax.psum_scatter(
            parts[0].astype(jnp.bfloat16), "shard", scatter_dimension=0, tiled=True
        ).astype(jnp.float32),
        lax.psum_scatter(
            parts[1].astype(jnp.bfloat16), "shard", scatter_dimension=0, tiled=True
        ).astype(jnp.float32),
        lax.psum_scatter(
            parts[2].astype(jnp.bfloat16), "shard", scatter_dimension=0, tiled=True
        ).astype(jnp.float32),
        lax.psum_scatter(
            parts[3].astype(jnp.bfloat16), "shard", scatter_dimension=0, tiled=True
        ).astype(jnp.float32),
        lax.psum_scatter(
            parts[4].astype(jnp.bfloat16), "shard", scatter_dimension=0, tiled=True
        ).astype(jnp.float32),
        lax.psum_scatter(
            parts[5].astype(jnp.bfloat16), "shard", scatter_dimension=0, tiled=True
        ).astype(jnp.float32),
        lax.psum_scatter(
            parts[6].astype(jnp.bfloat16), "shard", scatter_dimension=0, tiled=True
        ).astype(jnp.float32),
        lax.psum_scatter(
            parts[7].astype(jnp.bfloat16), "shard", scatter_dimension=0, tiled=True
        ).astype(jnp.float32),
        lax.psum_scatter(
            parts[8].astype(jnp.bfloat16), "shard", scatter_dimension=0, tiled=True
        ).astype(jnp.float32),
        lax.psum_scatter(
            parts[9].astype(jnp.bfloat16), "shard", scatter_dimension=0, tiled=True
        ).astype(jnp.float32),
        lax.psum_scatter(
            parts[10].astype(jnp.bfloat16), "shard", scatter_dimension=0, tiled=True
        ).astype(jnp.float32),
        lax.psum_scatter(
            parts[11].astype(jnp.bfloat16), "shard", scatter_dimension=0, tiled=True
        ).astype(jnp.float32),
        lax.psum_scatter(
            parts[12].astype(jnp.bfloat16), "shard", scatter_dimension=0, tiled=True
        ).astype(jnp.float32),
        lax.psum_scatter(
            parts[13].astype(jnp.bfloat16), "shard", scatter_dimension=0, tiled=True
        ).astype(jnp.float32),
        lax.psum_scatter(
            parts[14].astype(jnp.bfloat16), "shard", scatter_dimension=0, tiled=True
        ).astype(jnp.float32),
    )


def reduce_replicas(parts):
    return (
        lax.psum(parts[0].astype(jnp.bfloat16), "rep").astype(jnp.float32),
        lax.psum(parts[1].astype(jnp.bfloat16), "rep").astype(jnp.float32),
        lax.psum(parts[2].astype(jnp.bfloat16), "rep").astype(jnp.float32),
        lax.psum(parts[3].astype(jnp.bfloat16), "rep").astype(jnp.float32),
        lax.psum(parts[4].astype(jnp.bfloat16), "rep").astype(jnp.float32),
        lax.psum(parts[5].astype(jnp.bfloat16), "rep").astype(jnp.float32),
        lax.psum(parts[6].astype(jnp.bfloat16), "rep").astype(jnp.float32),
        lax.psum(parts[7].astype(jnp.bfloat16), "rep").astype(jnp.float32),
        lax.psum(parts[8].astype(jnp.bfloat16), "rep").astype(jnp.float32),
        lax.psum(parts[9].astype(jnp.bfloat16), "rep").astype(jnp.float32),
        lax.psum(parts[10].astype(jnp.bfloat16), "rep").astype(jnp.float32),
        lax.psum(parts[11].astype(jnp.bfloat16), "rep").astype(jnp.float32),
        lax.psum(parts[12].astype(jnp.bfloat16), "rep").astype(jnp.float32),
        lax.psum(parts[13].astype(jnp.bfloat16), "rep").astype(jnp.float32),
        lax.psum(parts[14].astype(jnp.bfloat16), "rep").astype(jnp.float32),
    )


def local(
    hidden,
    encoded,
    out_grad,
    self_query,
    self_key,
    self_value,
    self_out,
    cross_query,
    cross_key,
    cross_value,
    cross_out,
    ffn_gate,
    ffn_up,
    ffn_down,
    gain_self,
    gain_cross,
    gain_ffn,
    bias_table,
    buckets,
):
    masters = (
        self_query,
        self_key,
        self_value,
        self_out,
        cross_query,
        cross_key,
        cross_value,
        cross_out,
        ffn_gate,
        ffn_up,
        ffn_down,
        gain_self,
        gain_cross,
        gain_ffn,
        bias_table,
    )
    lowered = tuple((part.astype(B16) for part in masters))
    weights = fetch_forward(lowered)
    (
        w_query,
        w_key,
        w_value,
        w_out,
        c_query,
        c_key,
        c_value,
        c_out,
        w_gate,
        w_up,
        w_down,
        g_self,
        g_cross,
        g_ffn,
        w_table,
    ) = weights
    seq_count = hidden.shape[0]
    tok_count = hidden.shape[1]
    length = tok_count * lax.axis_size("rep")
    own_start = lax.axis_index("rep") * tok_count
    offset_bias = offset_table(buckets, w_table)
    inputs = hidden.astype(F32)
    normed1 = normalize(inputs, g_self.astype(F32)).astype(B16)
    queries = matmul(normed1, w_query).astype(B16)
    keys = matmul(normed1, w_key).astype(B16)
    values = matmul(normed1, w_value).astype(B16)
    query_heads = split_heads(queries)
    start_state = (
        jnp.full((seq_count, H, tok_count), -1e30, F32),
        jnp.zeros((seq_count, H, tok_count), F32),
        jnp.zeros((seq_count, tok_count, H, DH), F32),
    )
    forward_fold = make_forward_fold(query_heads, own_start, offset_bias)
    run_max, run_sum, accum = forward_fold(
        start_state,
        (
            lax.all_gather(keys, "rep", axis=1, tiled=True),
            lax.all_gather(values, "rep", axis=1, tiled=True),
        ),
        jnp.int32(0),
    )
    attn_f = join_heads(accum / jnp.transpose(run_sum, (0, 2, 1))[..., None])
    attn = attn_f.astype(B16)
    log_sum = run_max + jnp.log(run_sum)
    resid1 = inputs + matmul(attn, w_out)
    normed2 = normalize(resid1, g_cross.astype(F32)).astype(B16)
    cross_q = matmul(normed2, c_query).astype(B16)
    enc_keys = matmul(encoded, c_key).astype(B16)
    enc_values = matmul(encoded, c_value).astype(B16)
    all_keys, all_values = (
        lax.all_gather(enc_keys, "rep", axis=1, tiled=True),
        lax.all_gather(enc_values, "rep", axis=1, tiled=True),
    )
    cross_heads = split_heads(cross_q)
    key_heads_c = split_heads(all_keys)
    value_heads_c = split_heads(all_values)
    cross_scores = jnp.einsum(
        "sqhd,skhd->shqk", cross_heads, key_heads_c, preferred_element_type=F32
    )
    cross_max = jnp.max(cross_scores, axis=-1)
    cross_exp = jnp.exp(cross_scores - cross_max[..., None])
    cross_sum = jnp.sum(cross_exp, axis=-1)
    cross_f = join_heads(
        jnp.einsum(
            "shqk,skhd->sqhd", cross_exp.astype(B16), value_heads_c, preferred_element_type=F32
        )
        / jnp.transpose(cross_sum, (0, 2, 1))[..., None]
    )
    cross_attn = cross_f.astype(B16)
    cross_lse = cross_max + jnp.log(cross_sum)
    resid2 = resid1 + matmul(cross_attn, c_out)
    normed3 = normalize(resid2, g_ffn.astype(F32)).astype(B16)
    gate = matmul(normed3, w_gate)
    upper = matmul(normed3, w_up)
    inner = gated(gate, upper).astype(B16)
    output = (resid2 + matmul(inner, w_down)).astype(B16)
    weights_back = fetch_backward(lowered)
    (
        b_query,
        b_key,
        b_value,
        b_out,
        b_cquery,
        b_ckey,
        b_cvalue,
        b_cout,
        b_gate,
        b_up,
        b_down,
        b_gself,
        b_gcross,
        b_gffn,
        b_table,
    ) = weights_back
    grad_out = out_grad.astype(F32)
    ffn_down_grad = outer_sum(inner, out_grad)
    inner_grad = matmul_back(out_grad, b_down).astype(B16)
    ignored, pull = jax.vjp(gated, gate, upper)
    gate_grad, up_grad = pull(inner_grad.astype(F32))
    gate_grad = gate_grad.astype(B16)
    up_grad = up_grad.astype(B16)
    ffn_gate_grad = outer_sum(normed3, gate_grad)
    ffn_up_grad = outer_sum(normed3, up_grad)
    normed3_grad = matmul_back(gate_grad, b_gate) + matmul_back(up_grad, b_up)
    resid_term, gain_ffn_grad = norm_back(resid2, b_gffn.astype(F32), normed3_grad)
    resid2_grad = grad_out + resid_term
    cross_branch = resid2_grad.astype(B16)
    cross_out_grad = outer_sum(cross_attn, cross_branch)
    cross_attn_grad = matmul_back(cross_branch, b_cout).astype(B16)
    cross_grad_heads = split_heads(cross_attn_grad)
    cross_delta = jnp.sum(cross_grad_heads.astype(F32) * split_heads(cross_f), axis=-1)
    cross_prob = jnp.exp(cross_scores - cross_lse[..., None])
    cross_dprob = jnp.einsum(
        "sqhd,skhd->shqk", cross_grad_heads, value_heads_c, preferred_element_type=F32
    )
    cross_dscore = (
        cross_prob * (cross_dprob - jnp.transpose(cross_delta, (0, 2, 1))[..., None])
    ).astype(B16)
    cross_q_grad = join_heads(
        jnp.einsum("shqk,skhd->sqhd", cross_dscore, key_heads_c, preferred_element_type=F32)
    ).astype(B16)
    key_terms = join_heads(
        jnp.einsum("shqk,sqhd->skhd", cross_dscore, cross_heads, preferred_element_type=F32)
    )
    value_terms = join_heads(
        jnp.einsum(
            "shqk,sqhd->skhd", cross_prob.astype(B16), cross_grad_heads, preferred_element_type=F32
        )
    )
    enc_key_grad, enc_value_grad = (
        lax.psum_scatter(
            key_terms.astype(jnp.bfloat16), "rep", scatter_dimension=1, tiled=True
        ).astype(jnp.float32),
        lax.psum_scatter(
            value_terms.astype(jnp.bfloat16), "rep", scatter_dimension=1, tiled=True
        ).astype(jnp.float32),
    )
    enc_key_grad = enc_key_grad.astype(B16)
    enc_value_grad = enc_value_grad.astype(B16)
    cross_key_grad = outer_sum(encoded, enc_key_grad)
    cross_value_grad = outer_sum(encoded, enc_value_grad)
    encoded_grad = (
        matmul_back(enc_key_grad, b_ckey) + matmul_back(enc_value_grad, b_cvalue)
    ).astype(B16)
    cross_query_grad = outer_sum(normed2, cross_q_grad)
    resid_term, gain_cross_grad = norm_back(
        resid1, b_gcross.astype(F32), matmul_back(cross_q_grad, b_cquery)
    )
    resid1_grad = resid2_grad + resid_term
    self_branch = resid1_grad.astype(B16)
    self_out_grad = outer_sum(attn, self_branch)
    attn_grad = matmul_back(self_branch, b_out).astype(B16)
    grad_heads = split_heads(attn_grad)
    self_delta = jnp.sum(grad_heads.astype(F32) * split_heads(attn_f), axis=-1)
    delta_rows = jnp.transpose(self_delta, (0, 2, 1))
    query_zero = jnp.zeros((seq_count, tok_count, H, DH), F32)
    table_zero = jnp.zeros((NB, H), F32)
    key_fold = make_key_fold(
        query_heads, grad_heads, log_sum, delta_rows, own_start, offset_bias, buckets
    )
    key_start = (
        query_zero,
        table_zero,
        jnp.zeros((seq_count, length, D), F32),
        jnp.zeros((seq_count, length, D), F32),
    )
    key_state = key_fold(
        key_start,
        (
            lax.all_gather(keys, "rep", axis=1, tiled=True),
            lax.all_gather(values, "rep", axis=1, tiled=True),
        ),
        jnp.int32(0),
    )
    query_grad = join_heads(key_state[0]).astype(B16)
    bias_table_grad = key_state[1]
    key_grad, value_grad = (
        lax.psum_scatter(
            key_state[2].astype(jnp.bfloat16), "rep", scatter_dimension=1, tiled=True
        ).astype(jnp.float32),
        lax.psum_scatter(
            key_state[3].astype(jnp.bfloat16), "rep", scatter_dimension=1, tiled=True
        ).astype(jnp.float32),
    )
    key_grad = key_grad.astype(B16)
    value_grad = value_grad.astype(B16)
    self_query_grad = outer_sum(normed1, query_grad)
    self_key_grad = outer_sum(normed1, key_grad)
    self_value_grad = outer_sum(normed1, value_grad)
    normed1_grad = (
        matmul_back(query_grad, b_query)
        + matmul_back(key_grad, b_key)
        + matmul_back(value_grad, b_value)
    )
    resid_term, gain_self_grad = norm_back(inputs, b_gself.astype(F32), normed1_grad)
    hidden_grad = (resid1_grad + resid_term).astype(B16)
    local_grads = (
        self_query_grad,
        self_key_grad,
        self_value_grad,
        self_out_grad,
        cross_query_grad,
        cross_key_grad,
        cross_value_grad,
        cross_out_grad,
        ffn_gate_grad,
        ffn_up_grad,
        ffn_down_grad,
        gain_self_grad,
        gain_cross_grad,
        gain_ffn_grad,
        bias_table_grad,
    )
    owned = reduce_owner(local_grads)
    summed = reduce_replicas(owned)
    return (
        output,
        hidden_grad,
        encoded_grad,
        summed[0],
        summed[1],
        summed[2],
        summed[3],
        summed[4],
        summed[5],
        summed[6],
        summed[7],
        summed[8],
        summed[9],
        summed[10],
        summed[11],
        summed[12],
        summed[13],
        summed[14],
    )


def solution(mesh):
    in_specs = (
        P("shard", "rep", None),
        P("shard", "rep", None),
        P("shard", "rep", None),
        P("shard", None),
        P("shard", None),
        P("shard", None),
        P("shard", None),
        P("shard", None),
        P("shard", None),
        P("shard", None),
        P("shard", None),
        P("shard", None),
        P("shard", None),
        P("shard", None),
        P("shard"),
        P("shard"),
        P("shard"),
        P("shard", None),
        P(),
    )
    out_specs = (
        P("shard", "rep", None),
        P("shard", "rep", None),
        P("shard", "rep", None),
        P("shard", None),
        P("shard", None),
        P("shard", None),
        P("shard", None),
        P("shard", None),
        P("shard", None),
        P("shard", None),
        P("shard", None),
        P("shard", None),
        P("shard", None),
        P("shard", None),
        P("shard"),
        P("shard"),
        P("shard"),
        P("shard", None),
    )
    return jax.shard_map(local, mesh=mesh, in_specs=in_specs, out_specs=out_specs, check_vma=False)
```

profile of v0, /device:TPU:0, one launch (start us, length us, event | category | flops | bytes accessed | tf_op | source)
XLA Modules:
  0.0 1667.7 jit_solution(10523953040784607223)
XLA Ops:
  17.5 18.1 %all-gather.37.cloned.1.call-done = bf16[768,768]{1,0:T(8,128)(2,1)} async-done(((bf16[384,768]{1,0:T(8,128)(2,1)}), bf16[768,768]{1,0:T(8,128)(2,1)}) %all-gather.37.cloned.1.call-update) | async-done | bytes 1179664 | tf_op jit(solution)/shard_map/all_gather | solution.py:175
  38.0 22.6 %all-gather.31.cloned.1.call-done = bf16[768,768]{1,0:T(8,128)(2,1)} async-done(((bf16[384,768]{1,0:T(8,128)(2,1)}), bf16[768,768]{1,0:T(8,128)(2,1)}) %all-gather.31.cloned.1.call-update) | async-done | bytes 1179664 | tf_op jit(solution)/shard_map/all_gather | solution.py:176
  63.0 4.3 all-gather
  68.0 17.6 %all-gather.19.cloned.1.call-done = bf16[768,768]{1,0:T(8,128)(2,1)} async-done(((bf16[384,768]{1,0:T(8,128)(2,1)}), bf16[768,768]{1,0:T(8,128)(2,1)}) %all-gather.19.cloned.1.call-update) | async-done | bytes 1179664 | tf_op jit(solution)/shard_map/all_gather | solution.py:171
  88.2 22.2 %all-gather.25.cloned.1.call-done = bf16[768,768]{1,0:T(8,128)(2,1)} async-done(((bf16[384,768]{1,0:T(8,128)(2,1)}), bf16[768,768]{1,0:T(8,128)(2,1)}) %all-gather.25.cloned.1.call-update) | async-done | bytes 1179664 | tf_op jit(solution)/shard_map/all_gather | solution.py:172
  123.4 4.3 all-gather.2
  128.3 4.3 all-gather.1
  133.3 4.3 all_gather.77
  142.4 39.8 %all-gather.47.cloned.1.call-done = bf16[2048,768]{1,0:T(8,128)(2,1)} async-done(((bf16[1024,768]{1,0:T(8,128)(2,1)}), bf16[2048,768]{1,0:T(8,128)(2,1)}) %all-gather.47.cloned.1.call-update) | async-done | bytes 3145744 | tf_op jit(solution)/shard_map/all_gather | solution.py:180
  186.1 38.7 %all-gather.39.cloned.1.call-done = bf16[2,512,768]{2,1,0:T(8,128)(2,1)} async-done(((bf16[2,32,768]{2,1,0:T(8,128)(2,1)}), bf16[2,512,768]{2,1,0:T(8,128)(2,1)}) %all-gather.39.cloned.1.call-update) | async-done | bytes 1572880 | tf_op jit(solution)/shard_map/all_gather | solution.py:369
  227.4 38.9 %all-gather.33.cloned.1.call-done = bf16[2,512,768]{2,1,0:T(8,128)(2,1)} async-done(((bf16[2,32,768]{2,1,0:T(8,128)(2,1)}), bf16[2,512,768]{2,1,0:T(8,128)(2,1)}) %all-gather.33.cloned.1.call-update) | async-done | bytes 1572880 | tf_op jit(solution)/shard_map/all_gather | solution.py:370
  268.9 61.1 %all-gather.21.cloned.1.call-done = bf16[2,2048,768]{2,1,0:T(8,128)(2,1)} async-done(((bf16[2,128,768]{2,1,0:T(8,128)(2,1)}), bf16[2,2048,768]{2,1,0:T(8,128)(2,1)}) %all-gather.21.cloned.1.call-update) | async-done | bytes 6291472 | tf_op jit(solution)/shard_map/all_gather | solution.py:355
  330.0 8.7 copy.262
  338.7 54.6 %all-gather.27.cloned.1.call-done = bf16[2,2048,768]{2,1,0:T(8,128)(2,1)} async-done(((bf16[2,128,768]{2,1,0:T(8,128)(2,1)}), bf16[2,2048,768]{2,1,0:T(8,128)(2,1)}) %all-gather.27.cloned.1.call-update) | async-done | bytes 6291472 | tf_op jit(solution)/shard_map/all_gather | solution.py:356
  393.3 8.8 copy.264
  402.0 124.8 %while.42 = (s32[]{:T(128)}, f32[2,12,128]{2,1,0:T(8,128)S(1)}, f32[2,12,128]{2,1,0:T(8,128)S(1)}, f32[2,128,12,64]{1,3,2,0:T(8,128)}, s32[]{:T(128)}, /*index=5...) while((s32[]{:T(128)}, f32[2,12,128]{2,1,0:T(8,128)S(1)}, ...), condition=%wide.region_4.6_spmd.clone, body=%wide.region_1.5_spmd.clone.sunk | while | flops 420715520 | bytes 105054272 | solution.py:123
  413.8 6.9 reshape.518
  444.9 6.9 reshape.518
  475.9 7.0 reshape.518
  506.9 6.9 reshape.518
  542.5 4.3 fusion.55
  546.8 12.4 all-gather.43.cloned.1.call-done
  559.3 6.5 fusion.73
  573.9 5.2 fusion.74
  581.8 4.3 multiply_convert_fusion
  603.3 300.6 %while.43 = (s32[]{:T(128)}, f32[2,128,12,64]{1,3,2,0:T(8,128)}, f32[32,12]{0,1:T(8,128)S(1)}, bf16[2,2048,768]{1,2,0:T(8,128)(2,1)}, bf16[2,2048,768]{1,2,0:T(8...) while((s32[]{:T(128)}, f32[2,128,12,64]{1,3,2,0:T(8,128)}, ...), condition=%wide.region_16.18_spmd.clone, body=%wide.region_13.17_spmd.clone.sunk | while | flops 1030830464 | bytes 194277872 | solution.py:163
  620.5 6.9 reshape.523
  640.0 6.5 convert_reduce_fusion.5
  651.9 4.2 pad.22.clone.2
  656.1 6.1 reshape.524
  662.2 5.2 pad.43
  695.9 6.9 reshape.523
  715.4 6.5 convert_reduce_fusion.5
  731.4 6.0 reshape.524
  737.4 5.1 pad.43
  770.8 6.8 reshape.523
  790.3 6.5 convert_reduce_fusion.5
  806.3 6.0 reshape.524
  812.4 5.1 pad.43
  845.8 6.8 reshape.523
  865.2 6.5 convert_reduce_fusion.5
  881.3 6.0 reshape.524
  887.3 5.1 pad.43
  904.0 16.3 copy.318
  920.2 6.8 copy.330
  927.1 16.6 copy.316
  943.7 7.3 copy.329
  967.8 4.5 bitcast_convert_fusion.1
  976.3 36.0 %reduce-scatter.51.cloned.1.call-done = bf16[128,1536]{1,0:T(8,128)(2,1)} async-done(((bf16[2048,1536]{1,0:T(8,128)(2,1)}), bf16[128,1536]{1,0:T(8,128)(2,1)}) %reduce-scatter.51.cloned.1.call-update) | async-done | bytes 393232
  1015.6 85.8 %reduce-scatter.49.cloned.1.call-done = bf16[128,1536]{1,0:T(8,128)(2,1)} async-done(((bf16[2048,1536]{1,0:T(8,128)(2,1)}), bf16[128,1536]{1,0:T(8,128)(2,1)}) %reduce-scatter.49.cloned.1.call-update) | async-done | bytes 393232
  1105.8 19.2 %reduce-scatter.55.cloned.1.call-done = bf16[384,768]{1,0:T(8,128)(2,1)} async-done(((bf16[768,768]{1,0:T(8,128)(2,1)}), bf16[384,768]{1,0:T(8,128)(2,1)}) %reduce-scatter.55.cloned.1.call-update) | async-done | bytes 589840
  1127.1 22.6 %reduce-scatter.53.cloned.1.call-done = bf16[384,768]{1,0:T(8,128)(2,1)} async-done(((bf16[768,768]{1,0:T(8,128)(2,1)}), bf16[384,768]{1,0:T(8,128)(2,1)}) %reduce-scatter.53.cloned.1.call-update) | async-done | bytes 589840
  1151.8 22.5 %reduce-scatter.41.cloned.1.call-done = bf16[384,768]{1,0:T(8,128)(2,1)} async-done(((bf16[768,768]{1,0:T(8,128)(2,1)}), bf16[384,768]{1,0:T(8,128)(2,1)}) %reduce-scatter.41.cloned.1.call-update) | async-done | bytes 589840 | tf_op jit(solution)/shard_map/reduce_scatter | solution.py:231
  1174.3 24.7 %reduce-scatter.39.cloned.1.call-done = bf16[384,768]{1,0:T(8,128)(2,1)} async-done(((bf16[768,768]{1,0:T(8,128)(2,1)}), bf16[384,768]{1,0:T(8,128)(2,1)}) %reduce-scatter.39.cloned.1.call-update) | async-done | bytes 589840 | tf_op jit(solution)/shard_map/reduce_scatter | solution.py:222
  1199.0 24.4 %reduce-scatter.31.cloned.1.call-done = bf16[384,768]{1,0:T(8,128)(2,1)} async-done(((bf16[768,768]{1,0:T(8,128)(2,1)}), bf16[384,768]{1,0:T(8,128)(2,1)}) %reduce-scatter.31.cloned.1.call-update) | async-done | bytes 589840 | tf_op jit(solution)/shard_map/reduce_scatter | solution.py:210
  1223.4 24.7 %reduce-scatter.37.cloned.1.call-done = bf16[384,768]{1,0:T(8,128)(2,1)} async-done(((bf16[768,768]{1,0:T(8,128)(2,1)}), bf16[384,768]{1,0:T(8,128)(2,1)}) %reduce-scatter.37.cloned.1.call-update) | async-done | bytes 589840 | tf_op jit(solution)/shard_map/reduce_scatter | solution.py:219
  1248.2 46.0 %reduce-scatter.47.cloned.1.call-done = bf16[1024,768]{1,0:T(8,128)(2,1)} async-done(((bf16[2048,768]{1,0:T(8,128)(2,1)}), bf16[1024,768]{1,0:T(8,128)(2,1)}) %reduce-scatter.47.cloned.1.call-update) | async-done | bytes 1572880 | tf_op jit(solution)/shard_map/reduce_scatter | solution.py:240
  1294.2 46.2 %reduce-scatter.45.cloned.1.call-done = bf16[384,2048]{1,0:T(8,128)(2,1)} async-done(((bf16[768,2048]{1,0:T(8,128)(2,1)}), bf16[384,2048]{1,0:T(8,128)(2,1)}) %reduce-scatter.45.cloned.1.call-update) | async-done | bytes 1572880 | tf_op jit(solution)/shard_map/reduce_scatter | solution.py:237
  1340.4 46.2 %reduce-scatter.43.cloned.1.call-done = bf16[384,2048]{1,0:T(8,128)(2,1)} async-done(((bf16[768,2048]{1,0:T(8,128)(2,1)}), bf16[384,2048]{1,0:T(8,128)(2,1)}) %reduce-scatter.43.cloned.1.call-update) | async-done | bytes 1572880 | tf_op jit(solution)/shard_map/reduce_scatter | solution.py:234
  1386.5 24.7 %reduce-scatter.35.cloned.1.call-done = bf16[384,768]{1,0:T(8,128)(2,1)} async-done(((bf16[768,768]{1,0:T(8,128)(2,1)}), bf16[384,768]{1,0:T(8,128)(2,1)}) %reduce-scatter.35.cloned.1.call-update) | async-done | bytes 589840 | tf_op jit(solution)/shard_map/reduce_scatter | solution.py:216
  1411.2 24.5 %reduce-scatter.33.cloned.1.call-done = bf16[384,768]{1,0:T(8,128)(2,1)} async-done(((bf16[768,768]{1,0:T(8,128)(2,1)}), bf16[384,768]{1,0:T(8,128)(2,1)}) %reduce-scatter.33.cloned.1.call-update) | async-done | bytes 589840 | tf_op jit(solution)/shard_map/reduce_scatter | solution.py:213
  1453.5 5.0 all-reduce.7
  1458.7 34.4 %all-reduce.5 = (bf16[16,12]{0,1:T(8,128)(2,1)S(1)}, bf16[384]{0:T(512)(128)(2,1)S(1)}, bf16[384]{0:T(512)(128)(2,1)S(1)}, bf16[384]{0:T(512)(128)(2,1)S(1)}) all-reduce(bf16[16,12]{0,1:T(8,128)(2,1)S(1)} %copy.325, bf16[384]{0:T(512)(128)(2,1)S(1)} %dynamic-slice.1, ...), channel_id=1, replica_groups=mesh['shard'=2,'rep'=16] {'rep'}, use_global_device_ids=true, to_apply=%region_54.56 | all-reduce | flops 1344 | bytes 5376 | tf_op jit(solution)/shard_map/psum | solution.py:274
  1496.6 147.9 %all-reduce.10.cloned.1.call-done = (bf16[384,768]{0,1:T(8,128)(2,1)}, bf16[384,768]{0,1:T(8,128)(2,1)}, bf16[384,768]{1,0:T(8,128)(2,1)}, bf16[384,768]{1,0:T(8...) async-done(((bf16[384,768]{0,1:T(8,128)(2,1)}, ...) | async-done | bytes 9437200 | tf_op jit(solution)/shard_map/psum | solution.py:265
  (670 shorter events, 451.3 us)
Async XLA Ops:
  7.2 28.5 %copy-start = (bf16[2,32,768]{2,1,0:T(8,128)(2,1)S(1)}, bf16[2,32,768]{2,1,0:T(8,128)(2,1)}, u32[]{:S(2)}) copy-start(bf16[2,32,768]{2,1,0:T(8,128)(2,1)} %param.26) | copy-start | bytes 294916
  7.2 28.5 %all-gather.37.cloned.1.call-start = ((), (), s32[]{:S(2)}) async-start(), calls=%async_computation.25 | async-start | bytes 1769472 | tf_op jit(solution)/shard_map/all_gather | solution.py:175
  9.6 51.0 %all-gather.31.cloned.1.call-start = ((), (), s32[]{:S(2)}) async-start(), calls=%async_computation.22 | async-start | bytes 1769472 | tf_op jit(solution)/shard_map/all_gather | solution.py:176
  10.5 75.0 %all-gather.19.cloned.1.call-start = ((), (), s32[]{:S(2)}) async-start(), calls=%async_computation.16 | async-start | bytes 1769472 | tf_op jit(solution)/shard_map/all_gather | solution.py:171
  11.5 4.7 copy-start.52
  11.5 98.9 %all-gather.25.cloned.1.call-start = ((), (), s32[]{:S(2)}) async-start(), calls=%async_computation.19 | async-start | bytes 1769472 | tf_op jit(solution)/shard_map/all_gather | solution.py:172
  13.9 125.8 %all-gather.23.cloned.1.call-start = ((), (), s32[]{:S(2)}) async-start(), calls=%async_computation.18 | async-start | bytes 1769472 | tf_op jit(solution)/shard_map/all_gather | solution.py:170
  16.1 166.1 %all-gather.47.cloned.1.call-start = ((), (), s32[]{:S(2)}) async-start(), calls=%async_computation.30 | async-start | bytes 4718592 | tf_op jit(solution)/shard_map/all_gather | solution.py:180
  17.5 45.5 %copy-start.93 = (f32[384]{0:T(512)S(1)}, f32[384]{0:T(512)}, u32[]{:S(2)}) copy-start(f32[384]{0:T(512)} %param.39) | copy-start | bytes 4612
  17.5 49.9 %copy-start.20 = (bf16[2,128,768]{2,1,0:T(8,128)(2,1)S(1)}, bf16[2,128,768]{2,1,0:T(8,128)(2,1)}, u32[]{:S(2)}) copy-start(bf16[2,128,768]{2,1,0:T(8,128)(2,1)} %param.25) | copy-start | bytes 1179652
  17.5 207.3 %all-gather.39.cloned.1.call-start = ((), (), s32[]{:S(2)}) async-start(), calls=%async_computation.26 | async-start | bytes 1671168 | tf_op jit(solution)/shard_map/all_gather | solution.py:369
  38.0 228.3 %all-gather.33.cloned.1.call-start = ((), (), s32[]{:S(2)}) async-start(), calls=%async_computation.23 | async-start | bytes 1671168 | tf_op jit(solution)/shard_map/all_gather | solution.py:370
  62.9 267.1 %all-gather.21.cloned.1.call-start = ((), (), s32[]{:S(2)}) async-start(), calls=%async_computation.17 | async-start | bytes 6684672 | tf_op jit(solution)/shard_map/all_gather | solution.py:355
  67.3 72.3 %copy-start.78 = (f32[768]{0:T(1024)}, f32[768]{0:T(1024)S(1)}, u32[]{:S(2)}) copy-start(f32[768]{0:T(1024)S(1)} %reshape.445) | copy-start | bytes 9220
  68.0 71.6 %copy-start.83 = (f32[2,128]{1,0:T(2,128)}, f32[2,128]{1,0:T(2,128)S(1)}, u32[]{:S(2)}) copy-start(f32[2,128]{1,0:T(2,128)S(1)} %fusion.144) | copy-start | bytes 3076
  68.0 45.0 %copy-start.66 = (f32[384,768]{1,0:T(8,128)S(1)}, f32[384,768]{1,0:T(8,128)}, u32[]{:S(2)}) copy-start(f32[384,768]{1,0:T(8,128)} %param.31) | copy-start | bytes 3538948
  88.2 25.8 %copy-start.67 = (f32[384,768]{1,0:T(8,128)S(1)}, f32[384,768]{1,0:T(8,128)}, u32[]{:S(2)}) copy-start(f32[384,768]{1,0:T(8,128)} %param.32) | copy-start | bytes 3538948
  88.2 305.1 %all-gather.27.cloned.1.call-start = ((), (), s32[]{:S(2)}) async-start(), calls=%async_computation.20 | async-start | bytes 6684672 | tf_op jit(solution)/shard_map/all_gather | solution.py:356
  112.9 415.2 %all-gather.29.cloned.1.call-start = ((), (), s32[]{:S(2)}) async-start(), calls=%async_computation.21 | async-start | bytes 1769472 | tf_op jit(solution)/shard_map/all_gather | solution.py:173
  113.9 417.0 %all-gather.35.cloned.1.call-start = ((), (), s32[]{:S(2)}) async-start(), calls=%async_computation.24 | async-start | bytes 1769472 | tf_op jit(solution)/shard_map/all_gather | solution.py:174
  114.9 424.6 %all-gather.41.cloned.1.call-start = ((), (), s32[]{:S(2)}) async-start(), calls=%async_computation.27 | async-start | bytes 1769472 | tf_op jit(solution)/shard_map/all_gather | solution.py:177
  116.3 426.2 %all-gather.45.cloned.1.call-start = ((), (), s32[]{:S(2)}) async-start(), calls=%async_computation.29 | async-start | bytes 4718592 | tf_op jit(solution)/shard_map/all_gather | solution.py:179
  119.7 13.6 copy-start.91
  119.7 18.0 %copy-start.1 = (s32[2048]{0:T(1024)S(1)}, s32[2048]{0:T(1024)}, u32[]{:S(2)}) copy-start(s32[2048]{0:T(1024)} %param.43) | copy-start | bytes 24580
  119.7 439.6 %all-gather.43.cloned.1.call-start = ((), (), s32[]{:S(2)}) async-start(), calls=%async_computation.28 | async-start | bytes 4718592 | tf_op jit(solution)/shard_map/all_gather | solution.py:178
  123.2 827.8 %reduce-scatter.29.cloned.1.call-start = ((), (), s32[]{:S(2)}) async-start(), calls=%async_computation.32 | async-start | bytes 1671168 | tf_op jit(solution)/shard_map/reduce_scatter | solution.py:452
  138.3 43.9 %copy-start.56 = (bf16[2,128,768]{2,1,0:T(8,128)(2,1)S(1)}, bf16[2,128,768]{2,1,0:T(8,128)(2,1)}, u32[]{:S(2)}) copy-start(bf16[2,128,768]{2,1,0:T(8,128)(2,1)} %param.27) | copy-start | bytes 1179652
  530.8 58.6 %copy-start.18 = (f32[2,128,768]{2,1,0:T(8,128)}, f32[2,128,768]{2,1,0:T(8,128)S(1)}, u32[]{:S(2)}) copy-start(f32[2,128,768]{2,1,0:T(8,128)S(1)} %get-tuple-element.986) | copy-start | bytes 2359300
  530.9 58.5 %copy-start.85 = (f32[2,128]{1,0:T(2,128)}, f32[2,128]{1,0:T(2,128)S(1)}, u32[]{:S(2)}) copy-start(f32[2,128]{1,0:T(2,128)S(1)} %fusion.145) | copy-start | bytes 3076
  541.5 29.1 %copy-start.24 = (f32[2,128,768]{2,1,0:T(8,128)}, f32[2,128,768]{2,1,0:T(8,128)S(1)}, u32[]{:S(2)}) copy-start(f32[2,128,768]{2,1,0:T(8,128)S(1)} %get-tuple-element.992) | copy-start | bytes 2359300
  559.2 6.5 copy-start.54
  559.3 6.5 copy-start.97
  581.7 372.3 %reduce-scatter.27.cloned.1.call-start = ((), (), s32[]{:S(2)}) async-start(), calls=%async_computation.31 | async-start | bytes 1671168 | tf_op jit(solution)/shard_map/reduce_scatter | solution.py:449
  596.3 416.0 %reduce-scatter.51.cloned.1.call-start = ((), (), s32[]{:S(2)}) async-start(), calls=%async_computation.43 | async-start | bytes 6684672
  640.0 6.5 copy-start.4
  640.0 6.5 copy-start.14
  715.4 6.5 copy-start.4
  715.4 6.5 copy-start.14
  790.3 6.5 copy-start.4
  790.3 6.5 copy-start.14
  865.2 6.5 copy-start.4
  865.2 6.5 copy-start.14
  927.1 174.4 %reduce-scatter.49.cloned.1.call-start = ((), (), s32[]{:S(2)}) async-start(), calls=%async_computation.42 | async-start | bytes 6684672
  951.0 174.0 %reduce-scatter.55.cloned.1.call-start = ((), (), s32[]{:S(2)}) async-start(), calls=%async_computation.45 | async-start | bytes 1769472
  953.9 195.8 %reduce-scatter.53.cloned.1.call-start = ((), (), s32[]{:S(2)}) async-start(), calls=%async_computation.44 | async-start | bytes 1769472
  956.9 217.4 %reduce-scatter.41.cloned.1.call-start = ((), (), s32[]{:S(2)}) async-start(), calls=%async_computation.38 | async-start | bytes 1769472 | tf_op jit(solution)/shard_map/reduce_scatter | solution.py:231
  958.5 240.5 %reduce-scatter.39.cloned.1.call-start = ((), (), s32[]{:S(2)}) async-start(), calls=%async_computation.37 | async-start | bytes 1769472 | tf_op jit(solution)/shard_map/reduce_scatter | solution.py:222
  960.3 263.2 %reduce-scatter.31.cloned.1.call-start = ((), (), s32[]{:S(2)}) async-start(), calls=%async_computation.33 | async-start | bytes 1769472 | tf_op jit(solution)/shard_map/reduce_scatter | solution.py:210
  962.1 286.0 %reduce-scatter.37.cloned.1.call-start = ((), (), s32[]{:S(2)}) async-start(), calls=%async_computation.36 | async-start | bytes 1769472 | tf_op jit(solution)/shard_map/reduce_scatter | solution.py:219
  963.7 330.5 %reduce-scatter.47.cloned.1.call-start = ((), (), s32[]{:S(2)}) async-start(), calls=%async_computation.41 | async-start | bytes 4718592 | tf_op jit(solution)/shard_map/reduce_scatter | solution.py:240
  966.5 373.8 %reduce-scatter.45.cloned.1.call-start = ((), (), s32[]{:S(2)}) async-start(), calls=%async_computation.40 | async-start | bytes 4718592 | tf_op jit(solution)/shard_map/reduce_scatter | solution.py:237
  972.4 414.2 %reduce-scatter.43.cloned.1.call-start = ((), (), s32[]{:S(2)}) async-start(), calls=%async_computation.39 | async-start | bytes 4718592 | tf_op jit(solution)/shard_map/reduce_scatter | solution.py:234
  976.3 435.0 %reduce-scatter.35.cloned.1.call-start = ((), (), s32[]{:S(2)}) async-start(), calls=%async_computation.35 | async-start | bytes 1769472 | tf_op jit(solution)/shard_map/reduce_scatter | solution.py:216
  1013.9 89.1 %copy-start.42 = (bf16[2,128,768]{1,2,0:T(8,128)(2,1)}, bf16[2,128,768]{1,2,0:T(8,128)(2,1)S(1)}, u32[]{:S(2)}) copy-start(bf16[2,128,768]{1,2,0:T(8,128)(2,1)S(1)} %copy.319) | copy-start | bytes 1179652
  1015.6 420.1 %reduce-scatter.33.cloned.1.call-start = ((), (), s32[]{:S(2)}) async-start(), calls=%async_computation.34 | async-start | bytes 1769472 | tf_op jit(solution)/shard_map/reduce_scatter | solution.py:213
  1103.0 24.1 %copy-start.44 = (bf16[2,128,768]{1,2,0:T(8,128)(2,1)}, bf16[2,128,768]{1,2,0:T(8,128)(2,1)S(1)}, u32[]{:S(2)}) copy-start(bf16[2,128,768]{1,2,0:T(8,128)(2,1)S(1)} %copy.317) | copy-start | bytes 1179652
  1104.7 343.6 %reduce-scatter.57.cloned.1.call-start = ((), (), s32[]{:S(2)}) async-start(), calls=%async_computation.46 | async-start | bytes 12288
  1105.7 538.8 %all-reduce.10.cloned.1.call-start = ((), (), s32[]{:S(2)}) async-start(), calls=%async_computation.47 | async-start | bytes 18874368 | tf_op jit(solution)/shard_map/psum | solution.py:265
  1435.7 4.5 copy-start.25
  1440.3 8.8 copy-start.34
  1440.3 8.8 copy-start.77
  1440.3 9.3 copy-start.76
  1444.3 7.9 copy-start.45
  1452.8 42.8 %copy-start.88 = (f32[2,128]{1,0:T(2,128)S(1)}, f32[2,128]{1,0:T(2,128)}, u32[]{:S(2)}) copy-start(f32[2,128]{1,0:T(2,128)} %copy-done.87) | copy-start | bytes 3076
  (98 other events, 218.7 us)
Sparse Core Ops, SparseCore 0:
  10.2 25.4 all-gather.36
  37.8 22.7 all-gather.30
  62.7 22.8 all-gather.18
  87.6 22.7 all-gather.24
  112.3 22.8 all-gather.22
  137.2 44.9 all-gather.46
  185.1 39.6 all-gather.38
  227.7 38.5 all-gather.32
  269.2 60.8 all-gather.20
  332.7 60.5 all-gather.26
  395.4 21.3 all-gather.28
  418.8 22.7 all-gather.34
  443.7 22.7 all-gather.40
  467.9 44.9 all-gather.44
  514.3 44.9 all-gather.42
  581.9 59.4 reduce-scatter.28
  645.9 58.4 reduce-scatter.26
  927.2 85.0 reduce-scatter.50
  1016.8 84.6 reduce-scatter.48
  1104.1 20.8 reduce-scatter.54
  1127.9 21.7 reduce-scatter.52
  1152.5 21.7 reduce-scatter.40
  1177.2 21.7 reduce-scatter.38
  1201.7 21.7 reduce-scatter.30
  1226.4 21.7 reduce-scatter.36
  1250.8 43.3 reduce-scatter.46
  1296.9 43.3 reduce-scatter.44
  1343.2 43.3 reduce-scatter.42
  1389.4 21.7 reduce-scatter.34
  1413.9 21.7 reduce-scatter.32
  1438.5 9.7 reduce-scatter.56
  1454.8 189.5 all-reduce.9
where the time goes:
time: 1680 us; the launch traced here: 1670 us
  waiting for transfers between devices  926 us (55%)
  local copies, waits for them, and re-layouts  433 us (26%)
  matrix products  173 us (10%)
  other arithmetic  58.2 us (3%)
  blocking collectives  56.7 us (3%)
    unnamed x37, waiting for transfers between devices  168 us
    psum x1, waiting for transfers between devices, reduce_replicas(): lax.psum(parts[5].astype(jnp.bfloat16), 'rep').astype(jnp.float32)  148 us
    unnamed x207, local copies, waits for them, and re-layouts  93.8 us
    slice x24, local copies, waits for them, and re-layouts, self_scores(): tiled[:, :query_count * (width - 1)].reshape(H, query_count, width - 1)  71.4 us
    all_gather x1, waiting for transfers between devices, local(): lax.all_gather(keys, 'rep', axis=1, tiled=True)  61.1 us
    reshape x8, local copies, waits for them, and re-layouts, self_scores(): tiled[:, :query_count * (width - 1)].reshape(H, query_count, width - 1)  55 us
    all_gather x1, waiting for transfers between devices, local(): lax.all_gather(values, 'rep', axis=1, tiled=True)  54.6 us
    reduce_scatter x1, waiting for transfers between devices, reduce_owner(): lax.psum_scatter(parts[8].astype(jnp.bfloat16), 'shard', scatter_dimensio...  46.2 us
  transfers between devices with their start and end apart: 32, of which 25 were waited for; matrix products, arithmetic and copies ran while one was open for 37% of the time, Pallas kernels for 0%

commit v1 on v0

v1 whole, which is shorter than its diff:
```python
import functools

import jax
import jax.numpy as jnp
from jax import lax
from jax.experimental import pallas as pl
from jax.experimental.pallas import tpu as pltpu
from jax.sharding import PartitionSpec as P

D = 768
H = 12
DH = 64
NB = 32
EPS = 1e-06
F32 = jnp.float32
B16 = jnp.bfloat16
ONES = 16
HIDE = -1e30
MESH = pl.DeviceIdType.MESH
GELU_A = 0.7978845608028654
GELU_B = 0.044715


def dot(a, b):
    return lax.dot_general(a, b, (((1,), (0,)), ((), ())), preferred_element_type=F32)


def dot_t(a, b):
    return lax.dot_general(a, b, (((1,), (1,)), ((), ())), preferred_element_type=F32)


def t_dot(a, b):
    return lax.dot_general(a, b, (((0,), (0,)), ((), ())), preferred_element_type=F32)


def scale_of(v):
    return lax.rsqrt(jnp.mean(v * v, axis=-1, keepdims=True) + EPS)


def norm_back(v, gain, grad):
    r = scale_of(v)
    n = v * r
    c = grad * gain
    dv = r * (c - n * jnp.mean(c * n, axis=-1, keepdims=True))
    return dv, jnp.sum(grad * n, axis=0, keepdims=True)


def whole(shape):
    return pl.BlockSpec(shape, lambda *_: (0,) * len(shape))


def plain_call(kernel, outs, args, name, scratch=(), vmem=60):
    return pl.pallas_call(
        kernel,
        out_shape=[jax.ShapeDtypeStruct(s, t) for s, t in outs],
        in_specs=[pl.BlockSpec(memory_space=pltpu.VMEM)] * len(args),
        out_specs=[pl.BlockSpec(memory_space=pltpu.VMEM)] * len(outs),
        scratch_shapes=list(scratch),
        compiler_params=pltpu.CompilerParams(vmem_limit_bytes=vmem * 2**20),
        name=name,
    )(*args)


class Plan:
    def __init__(self, seqs, toks, rows):
        self.S, self.T, self.R = seqs, toks, rows
        groups = 1
        for g in range(1, H + 1):
            if H % g == 0 and seqs * g <= rows and rows % (2 * seqs * g) == 0:
                groups = g
        self.G = groups
        self.HG = H // groups
        self.F = self.HG * DH
        self.U = seqs * groups
        self.W = rows // self.U
        self.J = rows // self.W
        self.NP = self.J // 2
        self.CK = 2 * self.W * toks
        self.L = rows * toks

    def worker_of(self, r):
        m = r % (2 * self.W)
        late = m // self.W
        return m * (1 - late) + (2 * self.W - 1 - m) * late

    def slot_of(self, r):
        return 2 * (r // (2 * self.W)) + (r % (2 * self.W)) // self.W

    def source(self, j, w):
        if j % 2 == 0:
            return 2 * self.W * (j // 2) + w
        return 2 * self.W * (j // 2) + 2 * self.W - 1 - w


def enter(rows):
    me = lax.axis_index("rep")
    barrier = pltpu.get_barrier_semaphore()
    for k in range(1, rows):
        pl.semaphore_signal(
            barrier, inc=1, device_id={"rep": (me + k) % rows}, device_id_type=MESH
        )
    pl.semaphore_wait(barrier, rows - 1)
    return me


def remote(src, dst, send, recv, to):
    return pltpu.make_async_remote_copy(
        src_ref=src,
        dst_ref=dst,
        send_sem=send,
        recv_sem=recv,
        device_id={"rep": to},
        device_id_type=MESH,
    )


def start_either(me, to, src, dst, send, recv):
    @pl.when(to == me)
    def _():
        pltpu.make_async_copy(src, dst, recv).start()

    @pl.when(to != me)
    def _():
        remote(src, dst, send, recv, to).start()


def end_either(me, to, src, dst, send, recv):
    @pl.when(to != me)
    def _():
        remote(src, dst, send, recv, to).wait_send()


def landed(ref, sem):
    pltpu.make_async_copy(ref, ref, sem).wait()


def scatter_tokens(plan, send, recv, send_sem, relay_sem, recv_sem):
    p = plan
    me = enter(p.R)
    w = me % p.W
    mine = p.worker_of(me)
    for u in range(p.U):
        start_either(me, u * p.W + mine, send.at[u], recv.at[me], send_sem.at[u], recv_sem.at[me])
    for j in range(p.J):
        r = p.source(j, w)
        landed(recv.at[r], recv_sem.at[r])
        for k in range(1, p.W):
            part = recv.at[r, pl.ds(p.F, 2 * p.F)]
            remote(
                part, part, relay_sem.at[k - 1, j], recv_sem.at[r], me - w + (w + k) % p.W
            ).start()
    for k in range(1, p.W):
        for j in range(p.J):
            r = p.source(j, (w + k) % p.W)
            landed(recv.at[r, pl.ds(p.F, 2 * p.F)], recv_sem.at[r])
    for u in range(p.U):
        end_either(me, u * p.W + mine, send.at[u], recv.at[me], send_sem.at[u], recv_sem.at[me])
    for k in range(1, p.W):
        for j in range(p.J):
            r = p.source(j, w)
            part = recv.at[r, pl.ds(p.F, 2 * p.F)]
            remote(
                part, part, relay_sem.at[k - 1, j], recv_sem.at[r], me - w + (w + k) % p.W
            ).wait_send()


def return_tokens(plan, send, recv, send_sem, recv_sem):
    p = plan
    me = enter(p.R)
    w = me % p.W
    unit = me // p.W
    for j in range(p.J):
        r = p.source(j, w)
        start_either(me, r, send.at[j], recv.at[unit], send_sem.at[j], recv_sem.at[unit])
    for u in range(p.U):
        landed(recv.at[u], recv_sem.at[u])
    for j in range(p.J):
        r = p.source(j, w)
        end_either(me, r, send.at[j], recv.at[unit], send_sem.at[j], recv_sem.at[unit])


def scatter_rows(plan, send, recv, send_sem, recv_sem):
    p = plan
    me = enter(p.R)
    mine = p.worker_of(me)
    slot = p.slot_of(me)
    for u in range(p.U):
        start_either(
            me, u * p.W + mine, send.at[u], recv.at[slot], send_sem.at[u], recv_sem.at[slot]
        )
    for j in range(p.J):
        landed(recv.at[j], recv_sem.at[j])
    for u in range(p.U):
        end_either(
            me, u * p.W + mine, send.at[u], recv.at[slot], send_sem.at[u], recv_sem.at[slot]
        )


def return_grads(plan, dq, dkv, recv, buf, out, send_sem, part_sem, got_sem, recv_sem):
    p = plan
    me = enter(p.R)
    w = me % p.W
    unit = me // p.W

    def give(k, j):
        to = (w + k) % p.W
        r = p.source(j, to)
        return remote(
            dkv.at[r],
            buf.at[k - 1, j],
            part_sem.at[k - 1, j],
            got_sem.at[k - 1, j],
            me - w + to,
        )

    for j in range(p.J):
        for k in range(1, p.W):
            give(k, j).start()
    for j in range(p.J):
        r = p.source(j, w)
        total = dkv[r].astype(F32)
        for k in range(1, p.W):
            landed(buf.at[k - 1, j], got_sem.at[k - 1, j])
            total = total + buf[k - 1, j].astype(F32)
        out[j, 0 : p.F, :] = dq[j]
        out[j, p.F : 3 * p.F, :] = total.astype(B16)
        start_either(me, r, out.at[j], recv.at[unit], send_sem.at[j], recv_sem.at[unit])
    for u in range(p.U):
        landed(recv.at[u], recv_sem.at[u])
    for j in range(p.J):
        r = p.source(j, w)
        end_either(me, r, out.at[j], recv.at[unit], send_sem.at[j], recv_sem.at[unit])
        for k in range(1, p.W):
            give(k, j).wait_send()


def comm_call(kernel, out, args, scratch, collective, name, space=pl.ANY):
    return pl.pallas_call(
        kernel,
        out_shape=jax.ShapeDtypeStruct(out, B16),
        in_specs=[pl.BlockSpec(memory_space=space)] * len(args),
        out_specs=pl.BlockSpec(memory_space=space),
        scratch_shapes=list(scratch),
        compiler_params=pltpu.CompilerParams(
            collective_id=collective, has_side_effects=True, vmem_limit_bytes=40 * 2**20
        ),
        name=name,
    )(*args)


def project_kernel(plan, hidden, gain, wq, wk, wv, a1_ref, send):
    p = plan
    x = hidden[...].reshape(p.S * p.T, D).astype(F32)
    a1 = (x * scale_of(x) * gain[...]).astype(B16)
    a1_ref[...] = a1
    for n, weight in enumerate((wq, wk, wv)):
        rows = dot(a1, weight[...])
        for s in range(p.S):
            turned = jnp.transpose(rows[s * p.T : (s + 1) * p.T]).astype(B16)
            for g in range(p.G):
                send[s * p.G + g, n * p.F : (n + 1) * p.F, :] = turned[g * p.F : (g + 1) * p.F]


def bias_tiles(plan, w, line, tiles):
    p = plan
    far = line[0:1, 2 * p.T - 1 : 2 * p.T]
    near = pltpu.roll(
        jnp.broadcast_to(line[0:1, :], (p.T, 2 * p.T)), 0, 1, stride=1, stride_axis=0
    )
    key = lax.broadcasted_iota(jnp.int32, (p.T, p.T), 0)
    query = lax.broadcasted_iota(jnp.int32, (p.T, p.T), 1)
    same = jnp.where(query >= key, near[:, : p.T], HIDE)
    next_ = near[:, p.T :]
    farb = jnp.broadcast_to(far, (p.T, p.T))
    tiles[0] = jnp.broadcast_to(far, (p.CK, 2 * p.T))
    for a in range(2):
        ahead = w if a == 0 else 2 * p.W - 1 - w
        for b in range(2 * p.W):
            diff = ahead - b
            tile = jnp.where(
                diff == 0, same, jnp.where(diff == 1, next_, jnp.where(diff < 0, HIDE, farb))
            )
            tiles[2, b * p.T : (b + 1) * p.T, a * p.T : (a + 1) * p.T] = tile
            back = diff + 2 * p.W
            tiles[1, b * p.T : (b + 1) * p.T, a * p.T : (a + 1) * p.T] = jnp.where(
                back == 1, next_, farb
            )


def block_pair(plan, ref, pair, w, row, count):
    p = plan
    return jnp.concatenate(
        [
            ref[p.source(2 * pair, w), pl.ds(row, count), :],
            ref[p.source(2 * pair + 1, w), pl.ds(row, count), :],
        ],
        axis=1,
    )


def attend_kernel(plan, recv, lines, o_ref, of_ref, rl_ref, kn, vt, tiles):
    p = plan
    me = lax.axis_index("rep")
    w = me % p.W
    group = (me // p.W) % p.G
    h = pl.program_id(0)
    row = pl.multiple_of(h * DH, DH)
    bias_tiles(p, w, lines.at[group * p.HG + h], tiles)
    for r in range(p.R):
        kn[r * p.T : (r + 1) * p.T, :] = jnp.transpose(
            recv[r, pl.ds(p.F + row, DH), :].astype(F32)
        ).astype(B16)
        vt[0:DH, r * p.T : (r + 1) * p.T] = recv[r, pl.ds(2 * p.F + row, DH), :]
    vt[DH : DH + ONES, :] = jnp.ones((ONES, p.L), B16)
    for pair in range(p.NP):
        qt = block_pair(p, recv, pair, w, row, DH)

        def step(i, acc, pair=pair, qt=qt):
            start = pl.multiple_of(i * p.CK, p.CK)
            s = dot(kn[pl.ds(start, p.CK), :], qt)
            e = jnp.exp(s + tiles[jnp.maximum(i - pair + 2, 0)])
            return acc + dot(vt[:, pl.ds(start, p.CK)], e.astype(B16))

        acc = lax.fori_loop(0, pair + 1, step, jnp.zeros((DH + ONES, 2 * p.T), F32))
        rl = 1.0 / acc[DH : DH + 1]
        of = acc[:DH] * rl
        rl_ref[h, pair] = rl
        for a in range(2):
            part = of[:, a * p.T : (a + 1) * p.T]
            of_ref[2 * pair + a, pl.ds(row, DH), :] = part
            o_ref[2 * pair + a, pl.ds(row, DH), :] = part.astype(B16)


def attend_back_kernel(
    plan, recv, lines, dout, of_ref, rl_ref, dq_ref, dkv_ref, line_ref, kn, vn, kt, dk, dv, tiles, near
):
    p = plan
    me = lax.axis_index("rep")
    w = me % p.W
    group = (me // p.W) % p.G
    h = pl.program_id(0)
    row = pl.multiple_of(h * DH, DH)
    bias_tiles(p, w, lines.at[group * p.HG + h], tiles)
    for r in range(p.R):
        kn[r * p.T : (r + 1) * p.T, :] = jnp.transpose(
            recv[r, pl.ds(p.F + row, DH), :].astype(F32)
        ).astype(B16)
        vn[r * p.T : (r + 1) * p.T, :] = jnp.transpose(
            recv[r, pl.ds(2 * p.F + row, DH), :].astype(F32)
        ).astype(B16)
        kt[0:DH, r * p.T : (r + 1) * p.T] = recv[r, pl.ds(p.F + row, DH), :]
    kt[DH : DH + ONES, :] = jnp.ones((ONES, p.L), B16)
    dk[...] = jnp.zeros_like(dk)
    dv[...] = jnp.zeros_like(dv)
    near[...] = jnp.zeros_like(near)
    total = jnp.zeros((1, 2 * p.T), F32)
    for pair in range(p.NP):
        qt = block_pair(p, recv, pair, w, row, DH)
        dot_rows = jnp.concatenate(
            [dout[2 * pair + a, pl.ds(row, DH), :] for a in range(2)], axis=1
        )
        of = jnp.concatenate([of_ref[2 * pair + a, pl.ds(row, DH), :] for a in range(2)], axis=1)
        delta = jnp.sum(dot_rows.astype(F32) * of, axis=0, keepdims=True)
        rl = rl_ref[h, pair]
        qn = jnp.transpose(qt.astype(F32)).astype(B16)
        don = jnp.transpose(dot_rows.astype(F32)).astype(B16)

        def step(i, acc, pair=pair, qt=qt, dot_rows=dot_rows, delta=delta, rl=rl, qn=qn, don=don):
            start = pl.multiple_of(i * p.CK, p.CK)
            kind = jnp.maximum(i - pair + 2, 0)
            keys = pl.ds(start, p.CK)
            prob = jnp.exp(dot(kn[keys, :], qt) + tiles[kind]) * rl
            ds = (prob * (dot(vn[keys, :], dot_rows) - delta)).astype(B16)
            near[kind] += ds.astype(F32)
            dk[keys, :] += dot(ds, qn)
            dv[keys, :] += dot(prob.astype(B16), don)
            return acc + dot(kt[:, keys], ds)

        acc = lax.fori_loop(0, pair + 1, step, jnp.zeros((DH + ONES, 2 * p.T), F32))
        total = total + acc[DH : DH + 1]
        for a in range(2):
            dq_ref[2 * pair + a, pl.ds(row, DH), :] = acc[:DH, a * p.T : (a + 1) * p.T].astype(B16)
    for r in range(p.R):
        dkv_ref[r, pl.ds(row, DH), :] = jnp.transpose(dk[r * p.T : (r + 1) * p.T, :]).astype(B16)
        dkv_ref[r, pl.ds(p.F + row, DH), :] = jnp.transpose(dv[r * p.T : (r + 1) * p.T, :]).astype(
            B16
        )
    same = jnp.zeros((p.T, p.T), F32)
    next_ = jnp.zeros((p.T, p.T), F32)
    for a in range(2):
        ahead = w if a == 0 else 2 * p.W - 1 - w
        for b in range(2 * p.W):
            diff = ahead - b
            spot = (slice(b * p.T, (b + 1) * p.T), slice(a * p.T, (a + 1) * p.T))
            tile = near[(2, *spot)]
            same = same + jnp.where(diff == 0, tile, 0.0)
            next_ = next_ + jnp.where(diff == 1, tile, 0.0)
            next_ = next_ + jnp.where(diff + 2 * p.W == 1, near[(1, *spot)], 0.0)
    both = jnp.concatenate([same, next_], axis=1)
    key = lax.broadcasted_iota(jnp.int32, (p.T, p.T), 0)
    other = lax.broadcasted_iota(jnp.int32, (p.T, p.T), 1)
    swap = (key + other == p.T - 1).astype(F32)
    turned = lax.dot_general(
        swap,
        both,
        (((1,), (0,)), ((), ())),
        precision=lax.Precision.HIGHEST,
        preferred_element_type=F32,
    )
    turned = pltpu.roll(turned, p.T + 1, 1, stride=1, stride_axis=0)
    by_distance = jnp.sum(turned, axis=0, keepdims=True)
    rest = jnp.sum(total) - jnp.sum(both)
    place = lax.broadcasted_iota(jnp.int32, (1, 2 * p.T), 1)
    line_ref[h] = by_distance + jnp.where(place == 2 * p.T - 1, rest, 0.0)


def encode_kernel(enc, wk, wv, kn, kt, vn, vt):
    rows = enc.shape[0]
    for weight, natural, turned in ((wk, kn, kt), (wv, vn, vt)):
        value = dot(enc[...], weight[...])
        for h in range(H):
            natural[h] = value[:, h * DH : (h + 1) * DH].astype(B16)
        flipped = jnp.transpose(value).astype(B16)
        for h in range(H):
            turned[h, 0:DH, :] = flipped[h * DH : (h + 1) * DH]
            turned[h, DH : DH + ONES, :] = jnp.ones((ONES, rows), B16)


def cross_kernel(
    seqs, hidden, ot, wo, gain, wcq, wco, kn, vt, x1_ref, x2_ref, a2_ref, qt_ref, of_ref, rl_ref
):
    toks = hidden.shape[1]
    span = kn.shape[1] // seqs
    x = hidden[...].reshape(seqs * toks, D).astype(F32)
    o = jnp.concatenate(
        [jnp.transpose(ot[s].astype(F32)) for s in range(seqs)], axis=0
    ).astype(B16)
    x1 = x + dot(o, wo[...])
    x1_ref[...] = x1
    a2 = (x1 * scale_of(x1) * gain[...]).astype(B16)
    a2_ref[...] = a2
    q2 = dot(a2, wcq[...])
    for s in range(seqs):
        qt_ref[s] = jnp.transpose(q2[s * toks : (s + 1) * toks]).astype(B16)

    def heads(i, carry):
        for sub in range(2):
            h = 2 * i + sub
            row = pl.multiple_of(h * DH, DH)
            for s in range(seqs):
                keys = slice(s * span, (s + 1) * span)
                e = jnp.exp(dot(kn[h, keys, :], qt_ref[s, pl.ds(row, DH), :]))
                acc = dot(vt[h, :, keys], e.astype(B16))
                rl = 1.0 / acc[DH : DH + 1]
                of_ref[s, pl.ds(row, DH), :] = acc[:DH] * rl
                rl_ref[s, h] = rl
        return carry

    lax.fori_loop(0, H // 2, heads, 0)
    o2 = jnp.concatenate([jnp.transpose(of_ref[s]) for s in range(seqs)], axis=0).astype(B16)
    x2_ref[...] = x1 + dot(o2, wco[...])


def ffn_kernel(
    x2_ref, og_ref, gain, wg, wu, wd, out_ref, dx2_ref, dgain_ref, dwg, dwu, dwd, a3, acc, da3
):
    step = pl.program_id(0)

    @pl.when(step == 0)
    def _():
        x2 = x2_ref[...]
        a3[...] = (x2 * scale_of(x2) * gain[...]).astype(B16)
        acc[...] = x2
        da3[...] = jnp.zeros_like(da3)

    rows = a3[...]
    og = og_ref[...]
    gate = dot(rows, wg[...])
    up = dot(rows, wu[...])
    square = gate * gate
    th = jnp.tanh(GELU_A * gate * (1.0 + GELU_B * square))
    half = 0.5 * (1.0 + th)
    value = gate * half
    slope = half + 0.5 * gate * (1.0 - th * th) * (GELU_A * (1.0 + 3.0 * GELU_B * square))
    inner = (value * up).astype(B16)
    acc[...] += dot(inner, wd[...])
    dwd[...] = t_dot(inner, og).astype(B16)
    dinner = dot_t(og, wd[...]).astype(B16).astype(F32)
    dgate = (dinner * up * slope).astype(B16)
    dup = (dinner * value).astype(B16)
    dwg[...] = t_dot(rows, dgate).astype(B16)
    dwu[...] = t_dot(rows, dup).astype(B16)
    da3[...] += dot_t(dgate, wg[...]) + dot_t(dup, wu[...])

    @pl.when(step == pl.num_programs(0) - 1)
    def _():
        out_ref[...] = acc[...].astype(B16)
        dv, dgain = norm_back(x2_ref[...], gain[...], da3[...])
        dx2_ref[...] = og_ref[...].astype(F32) + dv
        dgain_ref[...] = dgain


def cross_back_kernel(
    seqs,
    groups,
    dx2_ref,
    x1_ref,
    a2_ref,
    gain,
    qt_ref,
    of_ref,
    rl_ref,
    kn,
    kt,
    vn,
    enc,
    wco,
    wcq,
    wck,
    wcv,
    wo,
    ot,
    dx1_ref,
    dgain_ref,
    dot_ref,
    denc_ref,
    dwco,
    dwcq,
    dwck,
    dwcv,
    dwo,
    dt,
    dqt,
    dk,
    dv,
):
    toks = qt_ref.shape[2]
    span = kn.shape[1] // seqs
    dx2 = dx2_ref[...]
    dc = dx2.astype(B16)
    o2t = [of_ref[s].astype(B16) for s in range(seqs)]
    total = dot(o2t[0], dc[0:toks])
    for s in range(1, seqs):
        total = total + dot(o2t[s], dc[s * toks : (s + 1) * toks])
    dwco[...] = total.astype(B16)
    do2 = dot_t(dc, wco[...])
    for s in range(seqs):
        dt[s] = jnp.transpose(do2[s * toks : (s + 1) * toks]).astype(B16)

    def heads(i, carry):
        col = pl.multiple_of(2 * i * DH, 2 * DH)
        for s in range(seqs):
            keys = slice(s * span, (s + 1) * span)
            dks, dvs = [], []
            q_pair = jnp.transpose(qt_ref[s, pl.ds(col, 2 * DH), :].astype(F32)).astype(B16)
            d_pair = jnp.transpose(dt[s, pl.ds(col, 2 * DH), :].astype(F32)).astype(B16)
            for sub in range(2):
                h = 2 * i + sub
                row = pl.multiple_of(h * DH, DH)
                d_rows = dt[s, pl.ds(row, DH), :]
                prob = jnp.exp(dot(kn[h, keys, :], qt_ref[s, pl.ds(row, DH), :])) * rl_ref[s, h]
                delta = jnp.sum(
                    d_rows.astype(F32) * of_ref[s, pl.ds(row, DH), :], axis=0, keepdims=True
                )
                ds = (prob * (dot(vn[h, keys, :], d_rows) - delta)).astype(B16)
                dqt[s, pl.ds(row, DH), :] = dot(kt[h, 0:DH, keys], ds).astype(B16)
                dks.append(dot(ds, q_pair[:, sub * DH : (sub + 1) * DH]))
                dvs.append(dot(prob.astype(B16), d_pair[:, sub * DH : (sub + 1) * DH]))
            dk[keys, pl.ds(col, 2 * DH)] = jnp.concatenate(dks, axis=1).astype(B16)
            dv[keys, pl.ds(col, 2 * DH)] = jnp.concatenate(dvs, axis=1).astype(B16)
        return carry

    lax.fori_loop(0, H // 2, heads, 0)
    dwck[...] = t_dot(enc[...], dk[...]).astype(B16)
    dwcv[...] = t_dot(enc[...], dv[...]).astype(B16)
    denc_ref[...] = (dot_t(dk[...], wck[...]) + dot_t(dv[...], wcv[...])).astype(B16)
    dq2 = jnp.concatenate(
        [jnp.transpose(dqt[s].astype(F32)) for s in range(seqs)], axis=0
    ).astype(B16)
    dwcq[...] = t_dot(a2_ref[...], dq2).astype(B16)
    term, dgain = norm_back(x1_ref[...], gain[...], dot_t(dq2, wcq[...]))
    dgain_ref[...] = dgain
    dx1 = dx2 + term
    dx1_ref[...] = dx1
    db = dx1.astype(B16)
    total = dot(ot[0], db[0:toks])
    for s in range(1, seqs):
        total = total + dot(ot[s], db[s * toks : (s + 1) * toks])
    dwo[...] = total.astype(B16)
    do = dot_t(db, wo[...])
    width = D // groups
    for s in range(seqs):
        turned = jnp.transpose(do[s * toks : (s + 1) * toks]).astype(B16)
        for g in range(groups):
            dot_ref[s * groups + g] = turned[g * width : (g + 1) * width]


def last_kernel(plan, hidden, grads, a1, gain, dx1, wq, wk, wv, dh_ref, dgain_ref, dwq, dwk, dwv):
    p = plan
    x = hidden[...].reshape(p.S * p.T, D).astype(F32)
    da1 = jnp.zeros((p.S * p.T, D), F32)
    for n, (weight, dw) in enumerate(((wq, dwq), (wk, dwk), (wv, dwv))):
        rows = []
        for s in range(p.S):
            turned = jnp.concatenate(
                [grads[s * p.G + g, n * p.F : (n + 1) * p.F, :] for g in range(p.G)], axis=0
            )
            rows.append(jnp.transpose(turned.astype(F32)))
        d = jnp.concatenate(rows, axis=0).astype(B16)
        dw[...] = t_dot(a1[...], d).astype(B16)
        da1 = da1 + dot_t(d, weight[...])
    term, dgain = norm_back(x, gain[...], da1)
    dgain_ref[...] = dgain
    dh_ref[...] = (dx1[...] + term).astype(B16).reshape(dh_ref.shape)


def gather_rows(part):
    count = lax.axis_size("shard")
    rows, cols = part.shape
    half = rows // 2
    mine = lax.axis_index("shard")
    core = lax.axis_index("rep") % 2
    pairs = [(r, r ^ 1) for r in range(lax.axis_size("rep"))]
    own = lax.dynamic_slice(part, (core * half, 0), (half, cols))
    full = jnp.zeros((count, rows, cols), part.dtype)
    full = lax.dynamic_update_slice(full, part[None], (mine, 0, 0))
    for k in range(1, count):
        got = lax.ppermute(own, "shard", [(i, (i + k) % count) for i in range(count)])
        also = lax.ppermute(got, "rep", pairs)
        owner = (mine - k) % count
        full = lax.dynamic_update_slice(full, got[None], (owner, core * half, 0))
        full = lax.dynamic_update_slice(full, also[None], (owner, (1 - core) * half, 0))
    return full.reshape(count * rows, cols)


def reduce_grads(grads):
    owned = [lax.psum_scatter(g, "shard", scatter_dimension=0, tiled=True) for g in grads]
    summed = lax.psum(tuple(owned), "rep")
    return [s.astype(F32) for s in summed]


def local(
    hidden,
    encoded,
    out_grad,
    self_query,
    self_key,
    self_value,
    self_out,
    cross_query,
    cross_key,
    cross_value,
    cross_out,
    ffn_gate,
    ffn_up,
    ffn_down,
    gain_self,
    gain_cross,
    gain_ffn,
    bias_table,
    buckets,
):
    seqs, toks = hidden.shape[0], hidden.shape[1]
    p = Plan(seqs, toks, lax.axis_size("rep"))
    tokens = seqs * toks
    ff = ffn_gate.shape[1]
    enc_rows = seqs * encoded.shape[1] * p.R
    dma = pltpu.SemaphoreType.DMA

    small = jnp.concatenate(
        [
            jnp.stack([gain_self, gain_cross, gain_ffn]).reshape(-1),
            bias_table.reshape(-1),
        ]
    ).astype(B16)
    small = lax.all_gather(small, "shard", axis=0)
    part = gain_self.shape[0]
    gains = [
        small[:, i * part : (i + 1) * part].reshape(1, D).astype(F32) for i in range(3)
    ]
    table = small[:, 3 * part :].reshape(NB, H)
    near = buckets[: 2 * toks]
    onehot = (near[:, None] == jnp.arange(NB, dtype=jnp.int32)[None, :]).astype(B16)
    lines = jnp.einsum("lb,bh->hl", onehot, table, preferred_element_type=F32)[:, None, :]

    wq, wk, wv, wo, wcq, wck, wcv, wco, wg, wu, wd = [
        gather_rows(m.astype(B16))
        for m in (
            self_query,
            self_key,
            self_value,
            self_out,
            cross_query,
            cross_key,
            cross_value,
            cross_out,
            ffn_gate,
            ffn_up,
            ffn_down,
        )
    ]
    enc = lax.all_gather(encoded, "rep", axis=1, tiled=True).reshape(enc_rows, D)

    a1, send = plain_call(
        functools.partial(project_kernel, p),
        [((tokens, D), B16), ((p.U, 3 * p.F, toks), B16)],
        (hidden, gains[0], wq, wk, wv),
        "project",
    )
    recv = comm_call(
        functools.partial(scatter_tokens, p),
        (p.R, 3 * p.F, toks),
        (send,),
        [dma((p.U,)), dma((max(p.W - 1, 1), p.J)), dma((p.R,))],
        0,
        "scatter_tokens",
    )
    ckn, ckt, cvn, cvt = plain_call(
        encode_kernel,
        [
            ((H, enc_rows, DH), B16),
            ((H, DH + ONES, enc_rows), B16),
            ((H, enc_rows, DH), B16),
            ((H, DH + ONES, enc_rows), B16),
        ],
        (enc, wck, wcv),
        "encode",
    )
    o, of, rl = pl.pallas_call(
        functools.partial(attend_kernel, p),
        grid=(p.HG,),
        out_shape=[
            jax.ShapeDtypeStruct((p.J, p.F, toks), B16),
            jax.ShapeDtypeStruct((p.J, p.F, toks), F32),
            jax.ShapeDtypeStruct((p.HG, p.NP, 1, 2 * toks), F32),
        ],
        in_specs=[whole((p.R, 3 * p.F, toks)), whole((H, 1, 2 * toks))],
        out_specs=[
            whole((p.J, p.F, toks)),
            whole((p.J, p.F, toks)),
            whole((p.HG, p.NP, 1, 2 * toks)),
        ],
        scratch_shapes=[
            pltpu.VMEM((p.L, DH), B16),
            pltpu.VMEM((DH + ONES, p.L), B16),
            pltpu.VMEM((3, p.CK, 2 * toks), F32),
        ],
        compiler_params=pltpu.CompilerParams(vmem_limit_bytes=56 * 2**20),
        name="attend",
    )(recv, lines)
    ot = comm_call(
        functools.partial(return_tokens, p),
        (p.U, p.F, toks),
        (o,),
        [dma((p.J,)), dma((p.U,))],
        1,
        "return_tokens",
    ).reshape(seqs, D, toks)

    x1, x2, a2, qt2, of2, rl2 = plain_call(
        functools.partial(cross_kernel, seqs),
        [
            ((tokens, D), F32),
            ((tokens, D), F32),
            ((tokens, D), B16),
            ((seqs, D, toks), B16),
            ((seqs, D, toks), F32),
            ((seqs, H, 1, toks), F32),
        ],
        (hidden, ot, wo, gains[1], wcq, wco, ckn, cvt),
        "cross",
    )

    chunk = min(512, ff)
    const = lambda s: pl.BlockSpec(s, lambda i: (0, 0))
    output, dx2, dg_ffn, dwg, dwu, dwd = pl.pallas_call(
        ffn_kernel,
        grid=(ff // chunk,),
        out_shape=[
            jax.ShapeDtypeStruct((tokens, D), B16),
            jax.ShapeDtypeStruct((tokens, D), F32),
            jax.ShapeDtypeStruct((1, D), F32),
            jax.ShapeDtypeStruct((D, ff), B16),
            jax.ShapeDtypeStruct((D, ff), B16),
            jax.ShapeDtypeStruct((ff, D), B16),
        ],
        in_specs=[
            const((tokens, D)),
            const((tokens, D)),
            const((1, D)),
            pl.BlockSpec((D, chunk), lambda i: (0, i)),
            pl.BlockSpec((D, chunk), lambda i: (0, i)),
            pl.BlockSpec((chunk, D), lambda i: (i, 0)),
        ],
        out_specs=[
            const((tokens, D)),
            const((tokens, D)),
            const((1, D)),
            pl.BlockSpec((D, chunk), lambda i: (0, i)),
            pl.BlockSpec((D, chunk), lambda i: (0, i)),
            pl.BlockSpec((chunk, D), lambda i: (i, 0)),
        ],
        scratch_shapes=[
            pltpu.VMEM((tokens, D), B16),
            pltpu.VMEM((tokens, D), F32),
            pltpu.VMEM((tokens, D), F32),
        ],
        compiler_params=pltpu.CompilerParams(vmem_limit_bytes=56 * 2**20),
        name="ffn",
    )(x2, out_grad.reshape(tokens, D), gains[2], wg, wu, wd)

    dx1, dg_cross, dot_, denc, dwco, dwcq, dwck, dwcv, dwo = plain_call(
        functools.partial(cross_back_kernel, seqs, p.G),
        [
            ((tokens, D), F32),
            ((1, D), F32),
            ((p.U, p.F, toks), B16),
            ((enc_rows, D), B16),
        ]
        + [((D, D), B16)] * 5,
        (dx2, x1, a2, gains[1], qt2, of2, rl2, ckn, ckt, cvn, enc, wco, wcq, wck, wcv, wo, ot),
        "cross_back",
        scratch=[
            pltpu.VMEM((seqs, D, toks), B16),
            pltpu.VMEM((seqs, D, toks), B16),
            pltpu.VMEM((enc_rows, D), B16),
            pltpu.VMEM((enc_rows, D), B16),
        ],
    )
    encoded_grad = lax.psum_scatter(
        denc.reshape(seqs, enc_rows // seqs, D), "rep", scatter_dimension=1, tiled=True
    )
    dout = comm_call(
        functools.partial(scatter_rows, p),
        (p.J, p.F, toks),
        (dot_,),
        [dma((p.U,)), dma((p.J,))],
        2,
        "scatter_rows",
    )
    dq, dkv, line = pl.pallas_call(
        functools.partial(attend_back_kernel, p),
        grid=(p.HG,),
        out_shape=[
            jax.ShapeDtypeStruct((p.J, p.F, toks), B16),
            jax.ShapeDtypeStruct((p.R, 2 * p.F, toks), B16),
            jax.ShapeDtypeStruct((p.HG, 1, 2 * toks), F32),
        ],
        in_specs=[
            whole((p.R, 3 * p.F, toks)),
            whole((H, 1, 2 * toks)),
            whole((p.J, p.F, toks)),
            whole((p.J, p.F, toks)),
            whole((p.HG, p.NP, 1, 2 * toks)),
        ],
        out_specs=[
            whole((p.J, p.F, toks)),
            whole((p.R, 2 * p.F, toks)),
            whole((p.HG, 1, 2 * toks)),
        ],
        scratch_shapes=[
            pltpu.VMEM((p.L, DH), B16),
            pltpu.VMEM((p.L, DH), B16),
            pltpu.VMEM((DH + ONES, p.L), B16),
            pltpu.VMEM((p.L, DH), F32),
            pltpu.VMEM((p.L, DH), F32),
            pltpu.VMEM((3, p.CK, 2 * toks), F32),
            pltpu.VMEM((3, p.CK, 2 * toks), F32),
        ],
        compiler_params=pltpu.CompilerParams(vmem_limit_bytes=56 * 2**20),
        name="attend_back",
    )(recv, lines, dout, of, rl)
    grads = comm_call(
        functools.partial(return_grads, p),
        (p.U, 3 * p.F, toks),
        (dq, dkv),
        [
            pltpu.VMEM((max(p.W - 1, 1), p.J, 2 * p.F, toks), B16),
            pltpu.VMEM((p.J, 3 * p.F, toks), B16),
            dma((p.J,)),
            dma((max(p.W - 1, 1), p.J)),
            dma((max(p.W - 1, 1), p.J)),
            dma((p.U,)),
        ],
        3,
        "return_grads",
        space=pltpu.VMEM,
    )
    hidden_grad, dg_self, dwq, dwk, dwv = plain_call(
        functools.partial(last_kernel, p),
        [(hidden.shape, B16), ((1, D), F32)] + [((D, D), B16)] * 3,
        (hidden, grads, a1, gains[0], dx1, wq, wk, wv),
        "last",
    )

    group = (lax.axis_index("rep") // p.W) % p.G
    by_bucket = jnp.einsum(
        "hl,lb->bh", line[:, 0, :], onehot.astype(F32), precision=lax.Precision.HIGHEST
    )
    dtable = lax.dynamic_update_slice(jnp.zeros((NB, H), F32), by_bucket, (0, group * p.HG))

    mats = reduce_grads([dwq, dwk, dwv, dwo, dwcq, dwck, dwcv, dwco, dwg, dwu, dwd])
    n_shard = lax.axis_size("shard")
    lot = jnp.concatenate(
        [g.reshape(n_shard, part) for g in (dg_self, dg_cross, dg_ffn)]
        + [dtable.reshape(n_shard, -1)],
        axis=1,
    )
    lot = lax.psum(lot, ("shard", "rep"))
    lot = lax.dynamic_slice(lot, (lax.axis_index("shard"), 0), (1, lot.shape[1]))[0]
    dgains = [lot[i * part : (i + 1) * part] for i in range(3)]
    dtab = lot[3 * part :].reshape(bias_table.shape)
    return (
        output.reshape(hidden.shape),
        hidden_grad,
        encoded_grad,
        *mats,
        *dgains,
        dtab,
    )


def solution(mesh):
    tok = P("shard", "rep", None)
    mat = P("shard", None)
    in_specs = (tok,) * 3 + (mat,) * 11 + (P("shard"),) * 3 + (mat, P())
    out_specs = (tok,) * 3 + (mat,) * 11 + (P("shard"),) * 3 + (mat,)
    return jax.shard_map(local, mesh=mesh, in_specs=in_specs, out_specs=out_specs, check_vma=False)
```

time: 1680 us -> 926 us (0.55)
  waiting for transfers between devices: 926 us -> 543 us
  local copies, waits for them, and re-layouts: 433 us -> 65 us
  Pallas kernels: 0 us -> 193 us
  matrix products: 173 us -> 0.49 us
  other arithmetic: 58.2 us -> 26.3 us
    all_gather x15 -> x1, waiting for transfers between devices: 326 us -> 0.01 us  [local(): lax.all_gather(encoded, 'rep', axis=1, tiled=True).reshape(enc_rows, D)]
    pallas_call x0 -> x12, Pallas kernels: none -> 193 us  [the longest x4 85 us: comm_call(): pl.pallas_call(kernel, out_shape=jax.ShapeDtypeStruct(out, B16), in_specs...]
    dot_general x72 -> x2, matrix products: 173 us -> 0.49 us  [the longest x1 0.28 us: local(): jnp.einsum('hl,lb->bh', line[:, 0, :], onehot.astype(F32), precision=lax....]
    unnamed x37 -> x14, waiting for transfers between devices: 168 us -> 6.64 us
    reshape x16 -> x6, local copies, waits for them, and re-layouts: 95.9 us -> 0.89 us  [the longest x1 0.69 us: local(): dtab = lot[3 * part:].reshape(bias_table.shape)]
    reduce_scatter x11 -> x12, waiting for transfers between devices: 284 us -> 377 us  [the longest x11 330 us: reduce_grads(): lax.psum_scatter(g, 'shard', scatter_dimension=0, tiled=True)]
    unnamed x207 -> x91, local copies, waits for them, and re-layouts: 93.8 us -> 17.3 us
    slice x24 -> x4, local copies, waits for them, and re-layouts: 71.4 us -> 1.47 us  [the longest x1 0.69 us: local(): near = buckets[:2 * toks]]
  transfers between devices with their start and end apart: 32 -> 36, of which waited for: 25 -> 15; matrix products, arithmetic and copies ran while one was open for 37% -> 8% of each run, Pallas kernels for 0% -> 7%
where the time goes in v1:
time: 926 us; the launch traced here: 918 us
  waiting for transfers between devices  543 us (59%)
  Pallas kernels  193 us (21%)
  local copies, waits for them, and re-layouts  65 us (7%)
  blocking collectives  60.3 us (7%)
  other arithmetic  26.3 us (3%)
  starting transfers between devices  15.3 us (2%)
  between operations  15 us (2%)
    reduce_scatter x11, waiting for transfers between devices, reduce_grads(): lax.psum_scatter(g, 'shard', scatter_dimension=0, tiled=True)  330 us
    psum x1, waiting for transfers between devices, reduce_grads(): summed = lax.psum(tuple(owned), 'rep')  152 us
    pallas_call x4, Pallas kernels, comm_call(): pl.pallas_call(kernel, out_shape=jax.ShapeDtypeStruct(out, B16), in_specs...  85 us
    pallas_call x5, Pallas kernels, plain_call(): pl.pallas_call(kernel, out_shape=[jax.ShapeDtypeStruct(s, t) for s, t in...  57 us
    reduce_scatter x1, waiting for transfers between devices, local(): lax.psum_scatter(denc.reshape(seqs, enc_rows // seqs, D), 'rep', scatter_...  46.8 us
    psum x1, blocking collectives, local(): lot = lax.psum(lot, ('shard', 'rep'))  41.3 us
    pallas_call x1, Pallas kernels, local(): pl.pallas_call(functools.partial(attend_back_kernel, p), grid=(p.HG,), ou...  21.8 us
    all_gather x1, blocking collectives, local(): small = lax.all_gather(small, 'shard', axis=0)  19.1 us
  transfers between devices with their start and end apart: 36, of which 15 were waited for; matrix products, arithmetic and copies ran while one was open for 8% of the time, Pallas kernels for 7%

profile of v1, /device:TPU:0, one launch (start us, length us, event | category | flops | bytes accessed | tf_op | source)
XLA Modules:
  0.0 918.5 jit_solution(14331588520458200055)
XLA Ops:
  7.4 1.1 copy-done.18
  9.3 2.9 collective-permute-start.12
  12.3 1.1 broadcast.11.clone.7
  16.5 1.6 collective-permute-start.4
  18.1 1.1 broadcast.11.clone.1
  21.3 1.1 broadcast.11.clone
  24.0 1.6 collective-permute-start
  25.9 19.1 %all-gather = bf16[2,1,1344]{2,1,0:T(2,128)(2,1)S(1)} all-gather(bf16[1,1,1344]{2,1,0:T(2,128)(2,1)S(1)} %maximum_bitcast_fusion), channel_id=1, replica_groups=mesh['shard'=2,'rep'=16] {'shard'}, dimensions={0}, use_global_device_ids=true | all-gather | bytes 8064 | tf_op jit(solution)/shard_map/all_gather | solution.py:676
  45.8 1.1 broadcast.11.clone.3
  48.5 2.1 broadcast.12.clone
  51.5 1.4 bitcast_dynamic-update-slice_fusion.2
  53.9 2.1 broadcast.12.clone.1
  56.9 1.5 bitcast_dynamic-update-slice_fusion.1
  59.6 1.1 broadcast.11.clone.4
  64.6 1.7 copy-done.14
  66.2 1.4 bitcast_dynamic-update-slice_fusion
  68.4 2.1 constant_dynamic-slice_fusion.1
  73.6 1.7 collective-permute-start.6
  76.4 1.7 bitcast_dynamic-update-slice_fusion.18
  78.1 1.7 collective-permute-start.10
  79.8 1.7 bitcast_dynamic-update-slice_fusion.28
  81.8 1.7 bitcast_dynamic-update-slice_fusion.30
  83.5 1.7 collective-permute-start.18
  85.3 1.7 bitcast_dynamic-update-slice_fusion.32
  88.0 2.1 collective-permute-done.8
  90.9 5.6 collective-permute-done.10
  103.9 4.4 project.1
  108.2 1.3 copy-done.5
  109.5 24.9 %scatter_tokens.1.recv = bf16[16,576,128]{2,1,0:T(8,128)(2,1)S(1)} custom-call(bf16[8,576,128]{2,1,0:T(8,128)(2,1)S(1)} %copy-done.5), custom_call_target="tpu_custom_call" | custom-call | tf_op jit(solution)/shard_map/scatter_tokens/pallas_call | solution.py:238
  134.4 1.5 copy-done
  135.9 15.4 %attend.1 = (bf16[8,192,128]{2,1,0:T(8,128)(2,1)}, f32[8,192,128]{2,1,0:T(8,128)}, f32[3,4,1,256]{3,2,1,0:T(1,128)}) custom-call(bf16[16,576,128]{2,1,0:T(8,128)(2,1)} %copy-done, f32[12,1,256]{2,1,0:T(1,128)} %broadcast_in_dim.119.lines), custom_call_target="tpu_custom_call" | custom-call | tf_op jit(solution)/shard_map/attend/pallas_call | solution.py:729
  152.3 19.3 %return_tokens.1 = bf16[8,192,128]{2,1,0:T(8,128)(2,1)S(1)} custom-call(bf16[8,192,128]{2,1,0:T(8,128)(2,1)S(1)} %copy-done.8), custom_call_target="tpu_custom_call" | custom-call | tf_op jit(solution)/shard_map/return_tokens/pallas_call | solution.py:238
  173.0 2.1 bitcast_dynamic-update-slice_fusion.8
  175.2 2.1 bitcast_dynamic-update-slice_fusion.6
  177.3 1.2 bitcast_dynamic-update-slice_fusion.4
  179.6 1.2 bitcast_dynamic-update-slice_fusion.5
  180.8 9.5 %encode.1 = (bf16[12,1024,64]{2,1,0:T(8,128)(2,1)}, bf16[12,80,1024]{2,1,0:T(8,128)(2,1)}, bf16[12,1024,64]{2,1,0:T(8,128)(2,1)}, bf16[12,80,1024]{2,1,0:T(8,128)(2,1)}) custom-call(bf16[1024,768]{1,0:T(8,128)(2,1)} %bitcast.114, bf16[768,768]{1,0:T(8,128)(2,1)} %bitcast.112, bf16[768,768]{1,0:T(8,128)(2,1)} %bitcast.34.wv.wcv), custom_call_target="tpu_custom_call" | custom-call | tf_op jit(solution)/shard_map/encode/pallas_call | solution.py:53
  190.3 12.8 %cross.1 = (f32[256,768]{1,0:T(8,128)}, f32[256,768]{1,0:T(8,128)}, bf16[256,768]{1,0:T(8,128)(2,1)}, bf16[2,768,128]{2,1,0:T(8,128)(2,1)}, f32[2,768,128]{2,1,0:T(8,128)}, /*index=5*/f32[2,12,1,128]{3,2,1,0:T(1,128)}) custom-call(bf16[2,128,768]{2,1,0:T(8,128)(2,1)} %hidden.5, bf16[2,768,128]{2,1,0:T(8,128)(2,1)} %bitcast.107, ...), custom_call_target="tpu_custom_call" | custom-call | tf_op jit(solution)/shard_map/cross/pallas_call | solution.py:53
  203.1 14.2 %ffn.1 = (bf16[256,768]{1,0:T(8,128)(2,1)}, f32[256,768]{1,0:T(8,128)}, f32[1,768]{1,0:T(1,128)}, bf16[768,2048]{1,0:T(8,128)(2,1)}, bf16[768,2048]{1,0:T(8,128)(2,1)}, /*index=5*/bf16[2048,768]{1,0:T(8,128)(2,1)}) custom-call(f32[256,768]{1,0:T(8,128)} %get-tuple-element.60.x2_ref, bf16[256,768]{1,0:T(8,128)(2,1)} %bitcast.117, f32[1,768]{1,0:T(1,128)} %bitcast.125, ...), custom_call_target="tpu_custom_call" | custom-call | tf_op jit(solution)/shard_map/ffn/pallas_call | solution.py:776
  217.4 24.0 %cross_back.1 = (f32[256,768]{1,0:T(8,128)}, f32[1,768]{1,0:T(1,128)}, bf16[8,192,128]{2,1,0:T(8,128)(2,1)}, bf16[1024,768]{1,0:T(8,128)(2,1)}, bf16[768,768]{1,...) custom-call(f32[256,768]{1,0:T(8,128)} %get-tuple-element.62.dx2_ref, ...), custom_call_target="tpu_custom_call" | custom-call | tf_op jit(solution)/shard_map/cross_back/pallas_call | solution.py:53
  242.3 13.4 %scatter_rows.1.dout = bf16[8,192,128]{2,1,0:T(8,128)(2,1)S(1)} custom-call(bf16[8,192,128]{2,1,0:T(8,128)(2,1)S(1)} %copy-done.7), custom_call_target="tpu_custom_call" | custom-call | tf_op jit(solution)/shard_map/scatter_rows/pallas_call | solution.py:238
  256.5 21.8 %attend_back.1 = (bf16[8,192,128]{2,1,0:T(8,128)(2,1)}, bf16[16,384,128]{2,1,0:T(8,128)(2,1)}, f32[3,1,256]{2,1,0:T(1,128)}) custom-call(bf16[16,576,128]{2,1,0:T(8,128)(2,1)} %copy-done, f32[12,1,256]{2,1,0:T(1,128)} %broadcast_in_dim.119.lines, bf16[8,192,128]{2,1,0:T(8,128)(2,1)} %copy-done.4, f32[8,192,128]{2,1,0:T(8,128)} %get-tuple-element.71.of_ref, ...), custom_call_target="tpu_custom_call" | custom-call | tf_op jit(solution)/shard_map/attend_back/pallas_call | solution.py:841
  278.3 1.4 copy-done.3
  280.7 27.4 %return_grads.1.grads = bf16[8,576,128]{2,1,0:T(8,128)(2,1)S(1)} custom-call(bf16[8,192,128]{2,1,0:T(8,128)(2,1)S(1)} %copy-done.6, bf16[16,384,128]{2,1,0:T(8,128)(2,1)S(1)} %copy-done.3), custom_call_target="tpu_custom_call" | custom-call | tf_op jit(solution)/shard_map/return_grads/pallas_call | solution.py:238
  309.1 6.3 last.1
  322.1 22.5 %reduce-scatter.15.cloned.1.call-done = bf16[384,768]{1,0:T(8,128)(2,1)} async-done(((bf16[768,768]{1,0:T(8,128)(2,1)}), bf16[384,768]{1,0:T(8,128)(2,1)}) %reduce-scatter.15.cloned.1.call-update) | async-done | bytes 589840 | tf_op jit(solution)/shard_map/reduce_scatter | solution.py:637
  344.6 24.7 %reduce-scatter.17.cloned.1.call-done = bf16[384,768]{1,0:T(8,128)(2,1)} async-done(((bf16[768,768]{1,0:T(8,128)(2,1)}), bf16[384,768]{1,0:T(8,128)(2,1)}) %reduce-scatter.17.cloned.1.call-update) | async-done | bytes 589840 | tf_op jit(solution)/shard_map/reduce_scatter | solution.py:637
  369.4 24.5 %reduce-scatter.19.cloned.1.call-done = bf16[384,768]{1,0:T(8,128)(2,1)} async-done(((bf16[768,768]{1,0:T(8,128)(2,1)}), bf16[384,768]{1,0:T(8,128)(2,1)}) %reduce-scatter.19.cloned.1.call-update) | async-done | bytes 589840 | tf_op jit(solution)/shard_map/reduce_scatter | solution.py:637
  393.8 24.0 %reduce-scatter.21.cloned.1.call-done = bf16[384,768]{1,0:T(8,128)(2,1)} async-done(((bf16[768,768]{1,0:T(8,128)(2,1)}), bf16[384,768]{1,0:T(8,128)(2,1)}) %reduce-scatter.21.cloned.1.call-update) | async-done | bytes 589840 | tf_op jit(solution)/shard_map/reduce_scatter | solution.py:637
  417.8 24.5 %reduce-scatter.23.cloned.1.call-done = bf16[384,768]{1,0:T(8,128)(2,1)} async-done(((bf16[768,768]{1,0:T(8,128)(2,1)}), bf16[384,768]{1,0:T(8,128)(2,1)}) %reduce-scatter.23.cloned.1.call-update) | async-done | bytes 589840 | tf_op jit(solution)/shard_map/reduce_scatter | solution.py:637
  442.2 24.1 %reduce-scatter.25.cloned.1.call-done = bf16[384,768]{1,0:T(8,128)(2,1)} async-done(((bf16[768,768]{1,0:T(8,128)(2,1)}), bf16[384,768]{1,0:T(8,128)(2,1)}) %reduce-scatter.25.cloned.1.call-update) | async-done | bytes 589840 | tf_op jit(solution)/shard_map/reduce_scatter | solution.py:637
  466.4 24.0 %reduce-scatter.27.cloned.1.call-done = bf16[384,768]{1,0:T(8,128)(2,1)} async-done(((bf16[768,768]{1,0:T(8,128)(2,1)}), bf16[384,768]{1,0:T(8,128)(2,1)}) %reduce-scatter.27.cloned.1.call-update) | async-done | bytes 589840 | tf_op jit(solution)/shard_map/reduce_scatter | solution.py:637
  490.4 24.7 %reduce-scatter.29.cloned.1.call-done = bf16[384,768]{1,0:T(8,128)(2,1)} async-done(((bf16[768,768]{1,0:T(8,128)(2,1)}), bf16[384,768]{1,0:T(8,128)(2,1)}) %reduce-scatter.29.cloned.1.call-update) | async-done | bytes 589840 | tf_op jit(solution)/shard_map/reduce_scatter | solution.py:637
  515.1 45.5 %reduce-scatter.31.cloned.1.call-done = bf16[384,2048]{1,0:T(8,128)(2,1)} async-done(((bf16[768,2048]{1,0:T(8,128)(2,1)}), bf16[384,2048]{1,0:T(8,128)(2,1)}) %reduce-scatter.31.cloned.1.call-update) | async-done | bytes 1572880 | tf_op jit(solution)/shard_map/reduce_scatter | solution.py:637
  560.6 45.7 %reduce-scatter.33.cloned.1.call-done = bf16[384,2048]{1,0:T(8,128)(2,1)} async-done(((bf16[768,2048]{1,0:T(8,128)(2,1)}), bf16[384,2048]{1,0:T(8,128)(2,1)}) %reduce-scatter.33.cloned.1.call-update) | async-done | bytes 1572880 | tf_op jit(solution)/shard_map/reduce_scatter | solution.py:637
  606.3 45.5 %reduce-scatter.35.cloned.1.call-done = bf16[1024,768]{1,0:T(8,128)(2,1)} async-done(((bf16[2048,768]{1,0:T(8,128)(2,1)}), bf16[1024,768]{1,0:T(8,128)(2,1)}) %reduce-scatter.35.cloned.1.call-update) | async-done | bytes 1572880 | tf_op jit(solution)/shard_map/reduce_scatter | solution.py:637
  653.3 41.3 %psum.95 = f32[2,1344]{1,0:T(2,128)S(1)} all-reduce(f32[2,1344]{1,0:T(2,128)S(1)} %pad_maximum_fusion), channel_id=1, replica_groups=mesh['shard'=2,'rep'=16] {'shard','rep'}, use_global_device_ids=true, to_apply=%region_23.24 | all-reduce | flops 2688 | bytes 21504 | tf_op jit(solution)/shard_map/psum | solution.py:909
  696.0 151.7 %all-reduce.3.cloned.1.call-done = (bf16[384,768]{1,0:T(8,128)(2,1)}, bf16[384,768]{1,0:T(8,128)(2,1)}, bf16[384,768]{1,0:T(8,128)(2,1)}, bf16[384,768]{1,0:T(8,...) async-done(((bf16[384,768]{1,0:T(8,128)(2,1)}, ...) | async-done | bytes 9437200 | tf_op jit(solution)/shard_map/psum | solution.py:638
  847.7 3.6 convert_element_type.116
  851.3 2.0 convert_element_type.117
  853.3 1.9 convert_element_type.118
  857.6 1.1 convert_element_type.110
  859.9 1.1 convert_element_type.112
  864.7 46.8 %reduce-scatter.13.cloned.1.call-done = bf16[2,32,768]{2,1,0:T(8,128)(2,1)} async-done(((bf16[2,512,768]{2,1,0:T(8,128)(2,1)}), bf16[2,32,768]{2,1,0:T(8,128)(2,1)}) %reduce-scatter.13.cloned.1.call-update) | async-done | bytes 98320 | tf_op jit(solution)/shard_map/reduce_scatter | solution.py:830
  (223 shorter events, 56.6 us)
Async XLA Ops:
  7.2 173.6 %all-gather.3.cloned.1.call-start = ((), (), s32[]{:S(2)}) async-start(), calls=%async_computation.12 | async-start | bytes 1671168 | tf_op jit(solution)/shard_map/all_gather | solution.py:702
  8.5 5.8 copy-start.11
  8.6 4.8 copy-start.19
  9.3 64.3 %collective-permute-start.12 = (bf16[192,768]{1,0:T(8,128)(2,1)}, bf16[192,768]{1,0:T(8,128)(2,1)S(1)}, u32[]{:S(2)}, u32[]{:S(2)}) collective-permute-start(bf16[192,768]{1,0:T(8,128)(2,1)} %constant_dynamic-slice_fusion.5), channel_id=1, source_target_pairs={{0,16},{16,0},{1,17},{17,1},{2,18},{18,2},{3,19},{19,3},{4,20},{20... | collective-permute-start | bytes 884744 | tf_op jit(solution)/shard_map/ppermute | solution.py:628
  14.3 1.4 copy-start.20
  15.1 61.1 %collective-permute-start.14 = (bf16[192,768]{1,0:T(8,128)(2,1)}, bf16[192,768]{1,0:T(8,128)(2,1)}, u32[]{:S(2)}, u32[]{:S(2)}) collective-permute-start(bf16[192,768]{1,0:T(8,128)(2,1)} %constant_dynamic-slice_fusion.4), channel_id=1, source_target_pairs={{0,16},{16,0},{1,17},{17,1},{2,18},{18,2},{3,19},{19,3},{4,20},{20... | collective-permute-start | bytes 884744 | tf_op jit(solution)/shard_map/ppermute | solution.py:628
  15.1 329.6 %reduce-scatter.15.cloned.1.call-start = ((), (), s32[]{:S(2)}) async-start(), calls=%async_computation.14 | async-start | bytes 1769472 | tf_op jit(solution)/shard_map/reduce_scatter | solution.py:637
  15.8 4.3 copy-start.10
  15.8 3.4 copy-start.21
  16.5 61.6 %collective-permute-start.4 = (bf16[192,768]{1,0:T(8,128)(2,1)}, bf16[192,768]{1,0:T(8,128)(2,1)}, u32[]{:S(2)}, u32[]{:S(2)}) collective-permute-start(bf16[192,768]{1,0:T(8,128)(2,1)} %constant_dynamic-slice_fusion.9), channel_id=1, source_target_pairs={{0,16},{16,0},{1,17},{17,1},{2,18},{18,2},{3,19},{19,3},{4,20},{20... | collective-permute-start | bytes 884744 | tf_op jit(solution)/shard_map/ppermute | solution.py:628
  20.1 2.3 copy-start.22
  20.8 60.7 %collective-permute-start.2 = (bf16[192,768]{1,0:T(8,128)(2,1)}, bf16[192,768]{1,0:T(8,128)(2,1)}, u32[]{:S(2)}, u32[]{:S(2)}) collective-permute-start(bf16[192,768]{1,0:T(8,128)(2,1)} %constant_dynamic-slice_fusion.10), channel_id=1, source_target_pairs={{0,16},{16,0},{1,17},{17,1},{2,18},{18,2},{3,19},{19,3},{4,20},{20... | collective-permute-start | bytes 884744 | tf_op jit(solution)/shard_map/ppermute | solution.py:628
  22.4 3.2 copy-start.39
  22.4 3.2 copy-start.40
  22.4 3.3 copy-start.41
  22.4 3.3 copy-start.35
  23.3 23.5 %copy-start.23 = (f32[384,768]{1,0:T(8,128)S(1)}, f32[384,768]{1,0:T(8,128)}, u32[]{:S(2)}) copy-start(f32[384,768]{1,0:T(8,128)} %param.25) | copy-start | bytes 3538948
  24.0 59.5 %collective-permute-start = (bf16[192,768]{1,0:T(8,128)(2,1)}, bf16[192,768]{1,0:T(8,128)(2,1)}, u32[]{:S(2)}, u32[]{:S(2)}) collective-permute-start(bf16[192,768]{1,0:T(8,128)(2,1)} %constant_dynamic-slice_fusion.11), channel_id=1, source_target_pairs={{0,16},{16,0},{1,17},{17,1},{2,18},{18,2},{3,19},{19,3},{4,20},{20... | collective-permute-start | bytes 884744 | tf_op jit(solution)/shard_map/ppermute | solution.py:628
  48.5 3.0 copy-start.12
  53.9 3.0 copy-start.13
  58.4 2.3 copy-start.24
  61.6 1.7 copy-start.25
  64.4 1.9 copy-start.14
  68.4 2.2 copy-start.17
  73.6 4.5 copy-start.34
  73.6 13.3 %collective-permute-start.6 = (bf16[192,768]{1,0:T(8,128)(2,1)}, bf16[192,768]{1,0:T(8,128)(2,1)S(1)}, u32[]{:S(2)}, u32[]{:S(2)}) collective-permute-start(bf16[192,768]{1,0:T(8,128)(2,1)} %constant_dynamic-slice_fusion.8), channel_id=1, source_target_pairs={{0,16},{16,0},{1,17},{17,1},{2,18},{18,2},{3,19},{19,3},{4,20},{20... | collective-permute-start | bytes 884744 | tf_op jit(solution)/shard_map/ppermute | solution.py:628
  76.1 14.0 %collective-permute-start.8 = (bf16[192,768]{1,0:T(8,128)(2,1)}, bf16[192,768]{1,0:T(8,128)(2,1)S(1)}, u32[]{:S(2)}, u32[]{:S(2)}) collective-permute-start(bf16[192,768]{1,0:T(8,128)(2,1)} %constant_dynamic-slice_fusion.7), channel_id=1, source_target_pairs={{0,16},{16,0},{1,17},{17,1},{2,18},{18,2},{3,19},{19,3},{4,20},{20... | collective-permute-start | bytes 884744 | tf_op jit(solution)/shard_map/ppermute | solution.py:628
  78.1 18.3 %collective-permute-start.10 = (bf16[192,768]{1,0:T(8,128)(2,1)S(1)}, bf16[192,768]{1,0:T(8,128)(2,1)S(1)}, u32[]{:S(2)}, u32[]{:S(2)}) collective-permute-start(bf16[192,768]{1,0:T(8,128)(2,1)S(1)} %copy-done.34), channel_id=1, source_target_pairs={{0,16},{16,0},{1,17},{17,1},{2,18},{18,2},{3,19},{19,3},{4,20},{20... | collective-permute-start | bytes 884744 | tf_op jit(solution)/shard_map/ppermute | solution.py:628
  81.5 91.0 %collective-permute-start.16 = (bf16[192,2048]{1,0:T(8,128)(2,1)}, bf16[192,2048]{1,0:T(8,128)(2,1)}, u32[]{:S(2)}, u32[]{:S(2)}) collective-permute-start(bf16[192,2048]{1,0:T(8,128)(2,1)} %constant_dynamic-slice_fusion.3), channel_id=1, source_target_pairs={{0,16},{16,0},{1,17},{17,1},{2,18},{18,2},{3,19},{19,3},{4,20},{20... | collective-permute-start | bytes 2359304 | tf_op jit(solution)/shard_map/ppermute | solution.py:628
  83.5 91.6 %collective-permute-start.18 = (bf16[192,2048]{1,0:T(8,128)(2,1)}, bf16[192,2048]{1,0:T(8,128)(2,1)}, u32[]{:S(2)}, u32[]{:S(2)}) collective-permute-start(bf16[192,2048]{1,0:T(8,128)(2,1)} %constant_dynamic-slice_fusion.2), channel_id=1, source_target_pairs={{0,16},{16,0},{1,17},{17,1},{2,18},{18,2},{3,19},{19,3},{4,20},{20... | collective-permute-start | bytes 2359304 | tf_op jit(solution)/shard_map/ppermute | solution.py:628
  87.0 85.6 %collective-permute-start.20 = (bf16[512,768]{1,0:T(8,128)(2,1)}, bf16[512,768]{1,0:T(8,128)(2,1)}, u32[]{:S(2)}, u32[]{:S(2)}) collective-permute-start(bf16[512,768]{1,0:T(8,128)(2,1)} %constant_dynamic-slice_fusion.1), channel_id=1, source_target_pairs={{0,16},{16,0},{1,17},{17,1},{2,18},{18,2},{3,19},{19,3},{4,20},{20... | collective-permute-start | bytes 2359304 | tf_op jit(solution)/shard_map/ppermute | solution.py:628
  90.1 7.1 collective-permute-start.13
  96.4 2.0 collective-permute-start.15
  97.2 2.0 collective-permute-start.5
  98.4 2.0 collective-permute-start.3
  99.2 2.0 collective-permute-start.1
  100.4 2.0 collective-permute-start.7
  101.2 2.0 collective-permute-start.9
  102.4 69.3 %collective-permute-start.11 = (bf16[192,768]{1,0:T(8,128)(2,1)S(1)}, bf16[192,768]{1,0:T(8,128)(2,1)S(1)}, u32[]{:S(2)}, u32[]{:S(2)}) collective-permute-start(bf16[192,768]{1,0:T(8,128)(2,1)S(1)} %collective-permute-done.10), channel_id=1, source_target_pairs={{0,1},{1,0},{2,3},{3,2},{4,5},{5,4},{6,7},{7,6},{8,9},{9,8},{10,11... | collective-permute-start | bytes 884744 | tf_op jit(solution)/shard_map/ppermute | solution.py:629
  134.4 1.5 copy-start
  171.6 5.6 copy-start.2
  172.5 6.1 collective-permute-start.17
  172.5 6.0 collective-permute-start.21
  175.1 4.5 collective-permute-start.19
  178.6 2.2 copy-start.9
  278.3 1.4 copy-start.3
  315.4 53.9 %reduce-scatter.17.cloned.1.call-start = ((), (), s32[]{:S(2)}) async-start(), calls=%async_computation.15 | async-start | bytes 1769472 | tf_op jit(solution)/shard_map/reduce_scatter | solution.py:637
  316.2 77.6 %reduce-scatter.19.cloned.1.call-start = ((), (), s32[]{:S(2)}) async-start(), calls=%async_computation.16 | async-start | bytes 1769472 | tf_op jit(solution)/shard_map/reduce_scatter | solution.py:637
  316.8 101.0 %reduce-scatter.21.cloned.1.call-start = ((), (), s32[]{:S(2)}) async-start(), calls=%async_computation.17 | async-start | bytes 1769472 | tf_op jit(solution)/shard_map/reduce_scatter | solution.py:637
  317.3 124.9 %reduce-scatter.23.cloned.1.call-start = ((), (), s32[]{:S(2)}) async-start(), calls=%async_computation.18 | async-start | bytes 1769472 | tf_op jit(solution)/shard_map/reduce_scatter | solution.py:637
  317.9 148.5 %reduce-scatter.25.cloned.1.call-start = ((), (), s32[]{:S(2)}) async-start(), calls=%async_computation.19 | async-start | bytes 1769472 | tf_op jit(solution)/shard_map/reduce_scatter | solution.py:637
  318.7 171.7 %reduce-scatter.27.cloned.1.call-start = ((), (), s32[]{:S(2)}) async-start(), calls=%async_computation.20 | async-start | bytes 1769472 | tf_op jit(solution)/shard_map/reduce_scatter | solution.py:637
  319.4 195.7 %reduce-scatter.29.cloned.1.call-start = ((), (), s32[]{:S(2)}) async-start(), calls=%async_computation.21 | async-start | bytes 1769472 | tf_op jit(solution)/shard_map/reduce_scatter | solution.py:637
  320.2 240.4 %reduce-scatter.31.cloned.1.call-start = ((), (), s32[]{:S(2)}) async-start(), calls=%async_computation.22 | async-start | bytes 4718592 | tf_op jit(solution)/shard_map/reduce_scatter | solution.py:637
  320.7 285.6 %reduce-scatter.33.cloned.1.call-start = ((), (), s32[]{:S(2)}) async-start(), calls=%async_computation.23 | async-start | bytes 4718592 | tf_op jit(solution)/shard_map/reduce_scatter | solution.py:637
  321.5 330.3 %reduce-scatter.35.cloned.1.call-start = ((), (), s32[]{:S(2)}) async-start(), calls=%async_computation.24 | async-start | bytes 4718592 | tf_op jit(solution)/shard_map/reduce_scatter | solution.py:637
  322.1 525.7 %all-reduce.3.cloned.1.call-start = ((), (), s32[]{:S(2)}) async-start(), calls=%async_computation.25 | async-start | bytes 18874368 | tf_op jit(solution)/shard_map/psum | solution.py:638
  651.9 1.3 copy-start.37
  651.9 1.4 copy-start.36
  651.9 259.6 %reduce-scatter.13.cloned.1.call-start = ((), (), s32[]{:S(2)}) async-start(), calls=%async_computation.13 | async-start | bytes 1671168 | tf_op jit(solution)/shard_map/reduce_scatter | solution.py:830
  847.7 3.6 copy-start.16
  851.3 2.0 copy-start.15
  853.3 1.9 copy-start.33
  862.3 1.3 copy-start.26
  (15 other events, 16.3 us)
Sparse Core Ops, SparseCore 0:
  15.2 41.4 all-gather.2
  315.6 29.0 reduce-scatter.14
  347.5 21.7 reduce-scatter.16
  372.0 21.7 reduce-scatter.18
  396.0 21.7 reduce-scatter.20
  420.5 21.7 reduce-scatter.22
  444.6 21.7 reduce-scatter.24
  468.6 21.7 reduce-scatter.26
  493.3 21.7 reduce-scatter.28
  517.2 43.3 reduce-scatter.30
  562.9 43.3 reduce-scatter.32
  608.4 43.3 reduce-scatter.34
  657.7 189.9 all-reduce.2
  851.8 59.6 reduce-scatter.12

commit v2 on v1

--- a/solution.py
+++ b/solution.py
@@ -639,6 +639,219 @@
     return [s.astype(F32) for s in summed]
 
 
+BITS = 4
+
+
+class Job:
+    def __init__(self, source, result, rows, col, cols):
+        self.source, self.result = source, result
+        self.rows, self.col, self.cols = rows, col, cols
+
+
+def partner(bit):
+    me = lax.axis_index("rep")
+    half = 2**bit
+    mine = (me // half) % 2
+    return mine, me + half * (1 - 2 * mine)
+
+
+def to_rep(src, dst, send, recv, bit):
+    return remote(src, dst, send, recv, partner(bit)[1])
+
+
+def to_row(src, dst, send, recv):
+    x = lax.axis_index("shard")
+    return pltpu.make_async_remote_copy(
+        src_ref=src,
+        dst_ref=dst,
+        send_sem=send,
+        recv_sem=recv,
+        device_id={"shard": 1 - x},
+        device_id_type=MESH,
+    )
+
+
+def add_into(acc, term, rows):
+    step = 16 if rows % 32 else 32
+
+    def body(i, carry):
+        at = pl.ds(pl.multiple_of(i * step, step), step)
+        acc[at, :] = (acc[at, :].astype(F32) + term[at, :].astype(F32)).astype(B16)
+        return carry
+
+    lax.fori_loop(0, rows // step, body, 0)
+
+
+class JobRun:
+    STAGES = 10
+
+    def __init__(self, job, source, result, bufs, sems, index):
+        self.job, self.source, self.result = job, source, result
+        self.acc, self.core, self.row, *self.part = bufs
+        send, recv, local = sems
+        self.send = [send.at[index, i] for i in range(9)]
+        self.recv = [recv.at[index, i] for i in range(9)]
+        self.local = [local.at[index, i] for i in range(2)]
+        self.sent = []
+        self.x = lax.axis_index("shard")
+        self.bits = [partner(b)[0] for b in range(BITS)]
+        half = job.cols // 2
+        self.half = half
+        self.mine = pl.ds(pl.multiple_of(job.col + self.bits[0] * half, 128), half)
+        self.other = pl.ds(pl.multiple_of(job.col + (1 - self.bits[0]) * half, 128), half)
+        self.first = [0]
+        count = job.rows
+        for b in range(1, BITS):
+            count //= 2
+            self.first.append(self.first[-1] + self.bits[b] * count)
+
+    def count(self, level):
+        return self.job.rows // 2**level
+
+    def span(self, first, count):
+        return pl.ds(pl.multiple_of(first, 16), count)
+
+    def go(self, copy):
+        copy.start()
+        self.sent.append(copy)
+
+    def stage(self, n):
+        job = self.job
+        if n == 0:
+            pltpu.make_async_copy(
+                self.source.at[:, :, self.mine], self.acc, self.local[0]
+            ).start()
+            self.go(
+                to_rep(self.source.at[:, :, self.other], self.core, self.send[0], self.recv[0], 0)
+            )
+        elif n == 1:
+            landed(self.acc, self.local[0])
+            landed(self.core, self.recv[0])
+            for i in range(2):
+                add_into(self.acc.at[i], self.core.at[i], job.rows)
+            self.go(to_row(self.acc.at[1 - self.x], self.row, self.send[1], self.recv[1]))
+        elif n == 2:
+            landed(self.row, self.recv[1])
+            add_into(self.acc.at[self.x], self.row, job.rows)
+            self.give(1)
+        elif n in (3, 4):
+            self.take(n - 2)
+            self.give(n - 1)
+        elif n == 5:
+            self.take(3)
+            rows = self.span(self.first[3], self.count(3))
+            piece = self.acc.at[self.x, rows]
+            place = self.result.at[rows, self.mine]
+            pltpu.make_async_copy(piece, place, self.local[1]).start()
+            self.go(to_rep(piece, place, self.send[5], self.recv[5], 3))
+        elif n in (6, 7, 8):
+            level = 9 - n
+            if n == 6:
+                rows = self.span(self.first[3], self.count(3))
+                landed(self.result.at[rows, self.mine], self.local[1])
+            self.landed_at(level)
+            rows = self.span(self.first[level - 1], self.count(level - 1))
+            place = self.result.at[rows, self.mine]
+            self.go(to_rep(place, place, self.send[n], self.recv[n], level - 1))
+        else:
+            landed(self.result.at[:, self.other], self.recv[8])
+            for copy in self.sent:
+                copy.wait_send()
+
+    def give(self, level):
+        count = self.count(level)
+        first = self.first[level - 1] + (1 - self.bits[level]) * count
+        self.go(
+            to_rep(
+                self.acc.at[self.x, self.span(first, count)],
+                self.part[level - 1],
+                self.send[level + 1],
+                self.recv[level + 1],
+                level,
+            )
+        )
+
+    def take(self, level):
+        landed(self.part[level - 1], self.recv[level + 1])
+        count = self.count(level)
+        rows = self.span(self.first[level], count)
+        add_into(self.acc.at[self.x, rows], self.part[level - 1], count)
+
+    def landed_at(self, level):
+        count = self.count(level)
+        first = self.first[level - 1] + (1 - self.bits[level]) * count
+        landed(self.result.at[self.span(first, count), self.mine], self.recv[8 - level])
+
+
+def job_buffers(job):
+    half = job.cols // 2
+    return [
+        pltpu.VMEM((2, job.rows, half), B16),
+        pltpu.VMEM((2, job.rows, half), B16),
+        pltpu.VMEM((job.rows, half), B16),
+    ] + [pltpu.VMEM((job.rows // 2**b, half), B16) for b in range(1, BITS)]
+
+
+JOB_BUFFERS = 6
+
+
+def greet_partners():
+    barrier = pltpu.get_barrier_semaphore()
+    x = lax.axis_index("shard")
+    pl.semaphore_signal(barrier, inc=1, device_id={"shard": 1 - x}, device_id_type=MESH)
+    for b in range(BITS):
+        pl.semaphore_signal(
+            barrier, inc=1, device_id={"rep": partner(b)[1]}, device_id_type=MESH
+        )
+    pl.semaphore_wait(barrier, BITS + 1)
+
+
+def sum_kernel(jobs, arrays, *refs):
+    sources, results = refs[:arrays], refs[arrays : 2 * arrays]
+    scratch = refs[2 * arrays :]
+    sems = scratch[:3]
+    greet_partners()
+    runs = [
+        JobRun(
+            job,
+            sources[job.source],
+            results[job.result],
+            scratch[3 + i * JOB_BUFFERS : 3 + (i + 1) * JOB_BUFFERS],
+            sems,
+            i,
+        )
+        for i, job in enumerate(jobs)
+    ]
+    for tick in range(len(runs) + JobRun.STAGES - 1):
+        for n in reversed(range(JobRun.STAGES)):
+            if 0 <= tick - n < len(runs):
+                runs[tick - n].stage(n)
+
+
+def sum_call(grads, collective):
+    jobs = []
+    for i, g in enumerate(grads):
+        rows, cols = g.shape[1:]
+        wide = cols // 2 if cols > 1024 else cols
+        for col in range(0, cols, wide):
+            jobs.append(Job(i, i, rows, col, wide))
+    dma = pltpu.SemaphoreType.DMA
+    scratch = [dma((len(jobs), 9)), dma((len(jobs), 9)), dma((len(jobs), 2))]
+    for job in jobs:
+        scratch += job_buffers(job)
+    return pl.pallas_call(
+        functools.partial(sum_kernel, jobs, len(grads)),
+        out_shape=[jax.ShapeDtypeStruct(g.shape[1:], B16) for g in grads],
+        in_specs=[pl.BlockSpec(memory_space=pl.ANY)] * len(grads),
+        out_specs=[pl.BlockSpec(memory_space=pl.ANY)] * len(grads),
+        scratch_shapes=scratch,
+        compiler_params=pltpu.CompilerParams(
+            collective_id=collective, has_side_effects=True, vmem_limit_bytes=56 * 2**20
+        ),
+        name="sum_gradients",
+    )(*grads)
+
+
 def local(
     hidden,
     encoded,
@@ -899,15 +1112,29 @@
     )
     dtable = lax.dynamic_update_slice(jnp.zeros((NB, H), F32), by_bucket, (0, group * p.HG))
 
-    mats = reduce_grads([dwq, dwk, dwv, dwo, dwcq, dwck, dwcv, dwco, dwg, dwu, dwd])
+    mats = [dwg, dwu, dwd, dwo, dwcq, dwck, dwcv, dwco, dwq, dwk, dwv]
     n_shard = lax.axis_size("shard")
     lot = jnp.concatenate(
         [g.reshape(n_shard, part) for g in (dg_self, dg_cross, dg_ffn)]
         + [dtable.reshape(n_shard, -1)],
         axis=1,
     )
-    lot = lax.psum(lot, ("shard", "rep"))
-    lot = lax.dynamic_slice(lot, (lax.axis_index("shard"), 0), (1, lot.shape[1]))[0]
+    size = lot.shape[1]
+    if n_shard == 2 and p.R == 2**BITS:
+        lines_in = 16 * 2 ** (BITS - 1)
+        lot = jnp.pad(lot.astype(B16), ((0, 0), (0, lines_in * D - size)))
+        *sums, lot = sum_call(
+            [g.reshape(2, g.shape[0] // 2, g.shape[1]) for g in mats]
+            + [lot.reshape(2, lines_in, D)],
+            4,
+        )
+        lot = lot.reshape(-1)[:size].astype(F32)
+        mats = [g.astype(F32) for g in sums]
+    else:
+        mats = reduce_grads(mats)
+        lot = lax.psum(lot, ("shard", "rep"))
+        lot = lax.dynamic_slice(lot, (lax.axis_index("shard"), 0), (1, size))[0]
+    mats = mats[8:] + mats[3:8] + mats[:3]
     dgains = [lot[i * part : (i + 1) * part] for i in range(3)]
     dtab = lot[3 * part :].reshape(bias_table.shape)
     return (

time: 926 us -> 530 us (0.57)
  waiting for transfers between devices: 543 us -> 7.81 us
  Pallas kernels: 193 us -> 366 us
  blocking collectives: 60.3 us -> 19 us
    reduce_scatter x11 -> x0, waiting for transfers between devices: 330 us -> none  [reduce_grads(): lax.psum_scatter(g, 'shard', scatter_dimension=0, tiled=True)]
    pallas_call x0 -> x1, Pallas kernels: none -> 173 us  [sum_call(): pl.pallas_call(functools.partial(sum_kernel, jobs, len(grads)), out_shape...]
    psum x1 -> x0, waiting for transfers between devices: 152 us -> none  [reduce_grads(): summed = lax.psum(tuple(owned), 'rep')]
    reduce_scatter x1, waiting for transfers between devices: 46.8 us -> 0.01 us  [local(): lax.psum_scatter(denc.reshape(seqs, enc_rows // seqs, D), 'rep', scatter_...]
    psum x1 -> x0, blocking collectives: 41.3 us -> none  [local(): lot = lax.psum(lot, ('shard', 'rep'))]
  transfers between devices with their start and end apart: 36 -> 24, of which waited for: 15 -> 2; matrix products, arithmetic and copies ran while one was open for 8% -> 16% of each run, Pallas kernels for 7% -> 45%
where the time goes in v2:
time: 530 us; the launch traced here: 522 us
  Pallas kernels  366 us (69%)
  local copies, waits for them, and re-layouts  70.9 us (13%)
  other arithmetic  27.8 us (5%)
  blocking collectives  19 us (4%)
  starting transfers between devices  14.8 us (3%)
  between operations  14.8 us (3%)
  waiting for transfers between devices  7.81 us (1%)
    pallas_call x1, Pallas kernels, sum_call(): pl.pallas_call(functools.partial(sum_kernel, jobs, len(grads)), out_shape...  173 us
    pallas_call x4, Pallas kernels, comm_call(): pl.pallas_call(kernel, out_shape=jax.ShapeDtypeStruct(out, B16), in_specs...  85.1 us
    pallas_call x5, Pallas kernels, plain_call(): pl.pallas_call(kernel, out_shape=[jax.ShapeDtypeStruct(s, t) for s, t in...  56.9 us
    pallas_call x1, Pallas kernels, local(): pl.pallas_call(functools.partial(attend_back_kernel, p), grid=(p.HG,), ou...  21.8 us
    all_gather x1, blocking collectives, local(): small = lax.all_gather(small, 'shard', axis=0)  19 us
    unnamed x92, local copies, waits for them, and re-layouts  18 us
    convert_element_type x11, other arithmetic, local(): mats = [g.astype(F32) for g in sums]  16.2 us
    pallas_call x1, Pallas kernels, local(): pl.pallas_call(functools.partial(attend_kernel, p), grid=(p.HG,), out_sha...  15.4 us
  transfers between devices with their start and end apart: 24, of which 2 were waited for; matrix products, arithmetic and copies ran while one was open for 16% of the time, Pallas kernels for 45%

profile of v2, /device:TPU:0, one launch (start us, length us, event | category | flops | bytes accessed | tf_op | source)
XLA Modules:
  0.0 521.9 jit_solution(7063699391775435384)
XLA Ops:
  7.4 1.1 copy-done.18
  9.3 2.9 collective-permute-start.12
  12.3 1.1 broadcast.13.clone.7
  16.6 1.6 collective-permute-start.4
  18.2 1.1 broadcast.13.clone.1
  21.3 1.1 broadcast.13.clone
  24.1 1.6 collective-permute-start
  25.9 19.0 %all-gather = bf16[2,1,1344]{2,1,0:T(2,128)(2,1)S(1)} all-gather(bf16[1,1,1344]{2,1,0:T(2,128)(2,1)S(1)} %maximum_bitcast_fusion), channel_id=1, replica_groups=mesh['shard'=2,'rep'=16] {'shard'}, dimensions={0}, use_global_device_ids=true | all-gather | bytes 8064 | tf_op jit(solution)/shard_map/all_gather | solution.py:889
  45.8 1.1 broadcast.13.clone.3
  48.5 2.1 broadcast.14.clone
  51.5 1.4 bitcast_dynamic-update-slice_fusion.2
  53.9 2.1 broadcast.14.clone.1
  56.9 1.4 bitcast_dynamic-update-slice_fusion.1
  59.6 1.1 broadcast.13.clone.4
  61.6 1.1 broadcast.13.clone.5
  63.3 1.1 bitcast_dynamic-update-slice_fusion.11
  64.6 1.7 copy-done.14
  66.2 1.4 bitcast_dynamic-update-slice_fusion
  68.4 2.1 constant_dynamic-slice_fusion
  73.6 1.8 collective-permute-start.6
  76.4 1.7 bitcast_dynamic-update-slice_fusion.18
  78.1 1.8 collective-permute-start.10
  79.8 1.7 bitcast_dynamic-update-slice_fusion.28
  81.8 1.7 bitcast_dynamic-update-slice_fusion.30
  83.5 1.8 collective-permute-start.18
  85.3 1.7 bitcast_dynamic-update-slice_fusion.32
  87.9 2.1 collective-permute-done.8
  90.8 5.6 %collective-permute-done.10 = bf16[192,768]{1,0:T(8,128)(2,1)S(1)} collective-permute-done((bf16[192,768]{1,0:T(8,128)(2,1)S(1)}, bf16[192,768]{1,0:T(8,128)(2,1)S(1)}, u32[]{:S(2)}, u32[]{:S(2)}) %collective-permute-start.10) | collective-permute-done | bytes 294944 | tf_op jit(solution)/shard_map/ppermute | solution.py:628
  103.8 4.4 project.1
  108.2 1.3 copy-done.5
  109.5 24.9 %scatter_tokens.1.recv = bf16[16,576,128]{2,1,0:T(8,128)(2,1)S(1)} custom-call(bf16[8,576,128]{2,1,0:T(8,128)(2,1)S(1)} %copy-done.5), custom_call_target="tpu_custom_call" | custom-call | tf_op jit(solution)/shard_map/scatter_tokens/pallas_call | solution.py:238
  134.4 1.5 copy-done
  135.9 15.4 %attend.1 = (bf16[8,192,128]{2,1,0:T(8,128)(2,1)}, f32[8,192,128]{2,1,0:T(8,128)}, f32[3,4,1,256]{3,2,1,0:T(1,128)}) custom-call(bf16[16,576,128]{2,1,0:T(8,128)(2,1)} %copy-done, f32[12,1,256]{2,1,0:T(1,128)} %broadcast_in_dim.119.lines), custom_call_target="tpu_custom_call" | custom-call | tf_op jit(solution)/shard_map/attend/pallas_call | solution.py:942
  151.3 1.0 copy-done.8
  152.3 19.3 %return_tokens.1 = bf16[8,192,128]{2,1,0:T(8,128)(2,1)S(1)} custom-call(bf16[8,192,128]{2,1,0:T(8,128)(2,1)S(1)} %copy-done.8), custom_call_target="tpu_custom_call" | custom-call | tf_op jit(solution)/shard_map/return_tokens/pallas_call | solution.py:238
  173.0 2.1 bitcast_dynamic-update-slice_fusion.8
  175.2 2.1 bitcast_dynamic-update-slice_fusion.6
  177.3 1.2 bitcast_dynamic-update-slice_fusion.4
  178.5 1.1 bitcast_dynamic-update-slice_fusion.7
  179.6 1.2 bitcast_dynamic-update-slice_fusion.5
  180.8 9.4 %encode.1 = (bf16[12,1024,64]{2,1,0:T(8,128)(2,1)}, bf16[12,80,1024]{2,1,0:T(8,128)(2,1)}, bf16[12,1024,64]{2,1,0:T(8,128)(2,1)}, bf16[12,80,1024]{2,1,0:T(8,128)(2,1)}) custom-call(bf16[1024,768]{1,0:T(8,128)(2,1)} %bitcast.129, bf16[768,768]{1,0:T(8,128)(2,1)} %bitcast.127, bf16[768,768]{1,0:T(8,128)(2,1)} %bitcast.34.wv.wcv), custom_call_target="tpu_custom_call" | custom-call | tf_op jit(solution)/shard_map/encode/pallas_call | solution.py:53
  190.2 12.8 %cross.1 = (f32[256,768]{1,0:T(8,128)}, f32[256,768]{1,0:T(8,128)}, bf16[256,768]{1,0:T(8,128)(2,1)}, bf16[2,768,128]{2,1,0:T(8,128)(2,1)}, f32[2,768,128]{2,1,0:T(8,128)}, /*index=5*/f32[2,12,1,128]{3,2,1,0:T(1,128)}) custom-call(bf16[2,128,768]{2,1,0:T(8,128)(2,1)} %hidden.5, bf16[2,768,128]{2,1,0:T(8,128)(2,1)} %bitcast.122, ...), custom_call_target="tpu_custom_call" | custom-call | tf_op jit(solution)/shard_map/cross/pallas_call | solution.py:53
  203.0 14.2 %ffn.1 = (bf16[256,768]{1,0:T(8,128)(2,1)}, f32[256,768]{1,0:T(8,128)}, f32[1,768]{1,0:T(1,128)}, bf16[768,2048]{1,0:T(8,128)(2,1)}, bf16[768,2048]{1,0:T(8,128)(2,1)}, /*index=5*/bf16[2048,768]{1,0:T(8,128)(2,1)}) custom-call(f32[256,768]{1,0:T(8,128)} %get-tuple-element.72.x2_ref, bf16[256,768]{1,0:T(8,128)(2,1)} %bitcast.145, f32[1,768]{1,0:T(1,128)} %bitcast.153, ...), custom_call_target="tpu_custom_call" | custom-call | tf_op jit(solution)/shard_map/ffn/pallas_call | solution.py:989
  217.2 24.0 %cross_back.1 = (f32[256,768]{1,0:T(8,128)}, f32[1,768]{1,0:T(1,128)}, bf16[8,192,128]{2,1,0:T(8,128)(2,1)}, bf16[1024,768]{1,0:T(8,128)(2,1)}, bf16[768,768]{1,...) custom-call(f32[256,768]{1,0:T(8,128)} %get-tuple-element.74.dx2_ref, ...), custom_call_target="tpu_custom_call" | custom-call | tf_op jit(solution)/shard_map/cross_back/pallas_call | solution.py:53
  242.2 13.4 %scatter_rows.1.dout = bf16[8,192,128]{2,1,0:T(8,128)(2,1)S(1)} custom-call(bf16[8,192,128]{2,1,0:T(8,128)(2,1)S(1)} %copy-done.7), custom_call_target="tpu_custom_call" | custom-call | tf_op jit(solution)/shard_map/scatter_rows/pallas_call | solution.py:238
  256.4 21.8 %attend_back.1 = (bf16[8,192,128]{2,1,0:T(8,128)(2,1)}, bf16[16,384,128]{2,1,0:T(8,128)(2,1)}, f32[3,1,256]{2,1,0:T(1,128)}) custom-call(bf16[16,576,128]{2,1,0:T(8,128)(2,1)} %copy-done, f32[12,1,256]{2,1,0:T(1,128)} %broadcast_in_dim.119.lines, bf16[8,192,128]{2,1,0:T(8,128)(2,1)} %copy-done.4, f32[8,192,128]{2,1,0:T(8,128)} %get-tuple-element.83.of_ref, ...), custom_call_target="tpu_custom_call" | custom-call | tf_op jit(solution)/shard_map/attend_back/pallas_call | solution.py:1054
  278.2 1.4 copy-done.3
  279.6 1.0 copy-done.6
  280.6 27.4 %return_grads.1.grads = bf16[8,576,128]{2,1,0:T(8,128)(2,1)S(1)} custom-call(bf16[8,192,128]{2,1,0:T(8,128)(2,1)S(1)} %copy-done.6, bf16[16,384,128]{2,1,0:T(8,128)(2,1)S(1)} %copy-done.3), custom_call_target="tpu_custom_call" | custom-call | tf_op jit(solution)/shard_map/return_grads/pallas_call | solution.py:238
  308.0 1.0 copy-done.1
  309.0 6.3 %last.1 = (bf16[2,128,768]{2,1,0:T(8,128)(2,1)}, f32[1,768]{1,0:T(1,128)}, bf16[768,768]{1,0:T(8,128)(2,1)}, bf16[768,768]{1,0:T(8,128)(2,1)}, bf16[768,768]{1,0:T(8,128)(2,1)}) custom-call(bf16[2,128,768]{2,1,0:T(8,128)(2,1)} %hidden.5, bf16[8,576,128]{2,1,0:T(8,128)(2,1)} %copy-done.1, bf16[256,768]{1,0:T(8,128)(2,1)} %get-tuple-element.87.a1, ...), custom_call_target="tpu_custom_call" | custom-call | tf_op jit(solution)/shard_map/last/pallas_call | solution.py:53
  318.0 172.7 %sum_gradients.1 = (bf16[384,2048]{1,0:T(8,128)(2,1)}, bf16[384,2048]{1,0:T(8,128)(2,1)}, bf16[1024,768]{1,0:T(8,128)(2,1)}, bf16[384,768]{1,0:T(8,128)(2,1)}, b...) custom-call(bf16[2,384,2048]{2,1,0:T(8,128)(2,1)} %bitcast.131, ...), custom_call_target="tpu_custom_call" | custom-call | tf_op jit(solution)/shard_map/sum_gradients/pallas_call | solution.py:842
  490.7 5.7 %slice.47 = bf16[8192,12]{1,0:T(8,128)(2,1)S(1)} reshape(bf16[128,768]{1,0:T(8,128)(2,1)} %get-tuple-element.117) | data formatting | bytes 393216 | tf_op jit(solution)/shard_map/slice | solution.py:1131
  496.7 3.6 convert_element_type.123
  500.2 2.0 convert_element_type.124
  502.3 1.9 convert_element_type.125
  504.2 1.1 convert_element_type.115
  505.4 1.1 convert_element_type.116
  506.5 1.1 convert_element_type.117
  507.8 1.1 convert_element_type.118
  508.9 1.1 convert_element_type.119
  510.1 1.1 convert_element_type.120
  511.2 1.1 convert_element_type.121
  512.5 1.1 convert_element_type.122
  (190 shorter events, 38.3 us)
Async XLA Ops:
  7.2 1.3 copy-start.18
  7.2 173.6 %all-gather.3.cloned.1.call-start = ((), (), s32[]{:S(2)}) async-start(), calls=%async_computation.1 | async-start | bytes 1671168 | tf_op jit(solution)/shard_map/all_gather | solution.py:915
  8.5 5.8 %copy-start.11 = (bf16[2,384,768]{2,1,0:T(8,128)(2,1)}, bf16[2,384,768]{2,1,0:T(8,128)(2,1)S(1)}, u32[]{:S(2)}) copy-start(bf16[2,384,768]{2,1,0:T(8,128)(2,1)S(1)} %get-tuple-element.126) | copy-start | bytes 3538948
  8.6 4.8 copy-start.19
  9.3 64.3 %collective-permute-start.12 = (bf16[192,768]{1,0:T(8,128)(2,1)}, bf16[192,768]{1,0:T(8,128)(2,1)S(1)}, u32[]{:S(2)}, u32[]{:S(2)}) collective-permute-start(bf16[192,768]{1,0:T(8,128)(2,1)} %constant_dynamic-slice_fusion.4), channel_id=1, source_target_pairs={{0,16},{16,0},{1,17},{17,1},{2,18},{18,2},{3,19},{19,3},{4,20},{20... | collective-permute-start | bytes 884744 | tf_op jit(solution)/shard_map/ppermute | solution.py:628
  14.3 1.4 copy-start.20
  15.1 61.0 %collective-permute-start.14 = (bf16[192,768]{1,0:T(8,128)(2,1)}, bf16[192,768]{1,0:T(8,128)(2,1)}, u32[]{:S(2)}, u32[]{:S(2)}) collective-permute-start(bf16[192,768]{1,0:T(8,128)(2,1)} %constant_dynamic-slice_fusion.3), channel_id=1, source_target_pairs={{0,16},{16,0},{1,17},{17,1},{2,18},{18,2},{3,19},{19,3},{4,20},{20... | collective-permute-start | bytes 884744 | tf_op jit(solution)/shard_map/ppermute | solution.py:628
  15.1 499.6 %reduce-scatter.2.cloned.1.call-start = ((), (), s32[]{:S(2)}) async-start(), calls=%async_computation.2 | async-start | bytes 1671168 | tf_op jit(solution)/shard_map/reduce_scatter | solution.py:1043
  15.8 4.4 copy-start.10
  15.8 3.5 copy-start.21
  16.6 61.5 %collective-permute-start.4 = (bf16[192,768]{1,0:T(8,128)(2,1)}, bf16[192,768]{1,0:T(8,128)(2,1)}, u32[]{:S(2)}, u32[]{:S(2)}) collective-permute-start(bf16[192,768]{1,0:T(8,128)(2,1)} %constant_dynamic-slice_fusion.8), channel_id=1, source_target_pairs={{0,16},{16,0},{1,17},{17,1},{2,18},{18,2},{3,19},{19,3},{4,20},{20... | collective-permute-start | bytes 884744 | tf_op jit(solution)/shard_map/ppermute | solution.py:628
  20.1 2.3 copy-start.22
  20.9 60.7 %collective-permute-start.2 = (bf16[192,768]{1,0:T(8,128)(2,1)}, bf16[192,768]{1,0:T(8,128)(2,1)}, u32[]{:S(2)}, u32[]{:S(2)}) collective-permute-start(bf16[192,768]{1,0:T(8,128)(2,1)} %constant_dynamic-slice_fusion.9), channel_id=1, source_target_pairs={{0,16},{16,0},{1,17},{17,1},{2,18},{18,2},{3,19},{19,3},{4,20},{20... | collective-permute-start | bytes 884744 | tf_op jit(solution)/shard_map/ppermute | solution.py:628
  22.4 3.3 copy-start.39
  22.4 3.3 copy-start.40
  22.4 3.3 copy-start.41
  22.4 3.4 copy-start.36
  23.3 23.5 %copy-start.23 = (f32[384,768]{1,0:T(8,128)S(1)}, f32[384,768]{1,0:T(8,128)}, u32[]{:S(2)}) copy-start(f32[384,768]{1,0:T(8,128)} %param.25) | copy-start | bytes 3538948
  24.1 59.4 %collective-permute-start = (bf16[192,768]{1,0:T(8,128)(2,1)}, bf16[192,768]{1,0:T(8,128)(2,1)}, u32[]{:S(2)}, u32[]{:S(2)}) collective-permute-start(bf16[192,768]{1,0:T(8,128)(2,1)} %constant_dynamic-slice_fusion.10), channel_id=1, source_target_pairs={{0,16},{16,0},{1,17},{17,1},{2,18},{18,2},{3,19},{19,3},{4,20},{20... | collective-permute-start | bytes 884744 | tf_op jit(solution)/shard_map/ppermute | solution.py:628
  48.5 3.0 copy-start.12
  53.9 3.0 copy-start.13
  58.4 2.3 copy-start.24
  61.6 1.7 copy-start.25
  64.3 1.9 copy-start.14
  68.4 2.1 copy-start.17
  73.6 4.5 copy-start.35
  73.6 13.4 %collective-permute-start.6 = (bf16[192,768]{1,0:T(8,128)(2,1)}, bf16[192,768]{1,0:T(8,128)(2,1)S(1)}, u32[]{:S(2)}, u32[]{:S(2)}) collective-permute-start(bf16[192,768]{1,0:T(8,128)(2,1)} %constant_dynamic-slice_fusion.7), channel_id=1, source_target_pairs={{0,16},{16,0},{1,17},{17,1},{2,18},{18,2},{3,19},{19,3},{4,20},{20... | collective-permute-start | bytes 884744 | tf_op jit(solution)/shard_map/ppermute | solution.py:628
  76.1 14.0 %collective-permute-start.8 = (bf16[192,768]{1,0:T(8,128)(2,1)}, bf16[192,768]{1,0:T(8,128)(2,1)S(1)}, u32[]{:S(2)}, u32[]{:S(2)}) collective-permute-start(bf16[192,768]{1,0:T(8,128)(2,1)} %constant_dynamic-slice_fusion.6), channel_id=1, source_target_pairs={{0,16},{16,0},{1,17},{17,1},{2,18},{18,2},{3,19},{19,3},{4,20},{20... | collective-permute-start | bytes 884744 | tf_op jit(solution)/shard_map/ppermute | solution.py:628
  78.1 18.3 %collective-permute-start.10 = (bf16[192,768]{1,0:T(8,128)(2,1)S(1)}, bf16[192,768]{1,0:T(8,128)(2,1)S(1)}, u32[]{:S(2)}, u32[]{:S(2)}) collective-permute-start(bf16[192,768]{1,0:T(8,128)(2,1)S(1)} %copy-done.35), channel_id=1, source_target_pairs={{0,16},{16,0},{1,17},{17,1},{2,18},{18,2},{3,19},{19,3},{4,20},{20... | collective-permute-start | bytes 884744 | tf_op jit(solution)/shard_map/ppermute | solution.py:628
  81.5 90.9 %collective-permute-start.16 = (bf16[192,2048]{1,0:T(8,128)(2,1)}, bf16[192,2048]{1,0:T(8,128)(2,1)}, u32[]{:S(2)}, u32[]{:S(2)}) collective-permute-start(bf16[192,2048]{1,0:T(8,128)(2,1)} %constant_dynamic-slice_fusion.2), channel_id=1, source_target_pairs={{0,16},{16,0},{1,17},{17,1},{2,18},{18,2},{3,19},{19,3},{4,20},{20... | collective-permute-start | bytes 2359304 | tf_op jit(solution)/shard_map/ppermute | solution.py:628
  83.5 91.6 %collective-permute-start.18 = (bf16[192,2048]{1,0:T(8,128)(2,1)}, bf16[192,2048]{1,0:T(8,128)(2,1)}, u32[]{:S(2)}, u32[]{:S(2)}) collective-permute-start(bf16[192,2048]{1,0:T(8,128)(2,1)} %constant_dynamic-slice_fusion.1), channel_id=1, source_target_pairs={{0,16},{16,0},{1,17},{17,1},{2,18},{18,2},{3,19},{19,3},{4,20},{20... | collective-permute-start | bytes 2359304 | tf_op jit(solution)/shard_map/ppermute | solution.py:628
  87.0 85.5 %collective-permute-start.20 = (bf16[512,768]{1,0:T(8,128)(2,1)}, bf16[512,768]{1,0:T(8,128)(2,1)}, u32[]{:S(2)}, u32[]{:S(2)}) collective-permute-start(bf16[512,768]{1,0:T(8,128)(2,1)} %constant_dynamic-slice_fusion), channel_id=1, source_target_pairs={{0,16},{16,0},{1,17},{17,1},{2,18},{18,2},{3,19},{19,3},{4,20},{20... | collective-permute-start | bytes 2359304 | tf_op jit(solution)/shard_map/ppermute | solution.py:628
  90.1 7.1 %collective-permute-start.13 = (bf16[192,768]{1,0:T(8,128)(2,1)S(1)}, bf16[192,768]{1,0:T(8,128)(2,1)S(1)}, u32[]{:S(2)}, u32[]{:S(2)}) collective-permute-start(bf16[192,768]{1,0:T(8,128)(2,1)S(1)} %collective-permute-done.12), channel_id=1, source_target_pairs={{0,1},{1,0},{2,3},{3,2},{4,5},{5,4},{6,7},{7,6},{8,9},{9,8},{10,11... | collective-permute-start | bytes 884744 | tf_op jit(solution)/shard_map/ppermute | solution.py:629
  96.4 2.0 collective-permute-start.15
  97.1 2.0 collective-permute-start.5
  98.4 2.0 collective-permute-start.3
  99.1 2.0 collective-permute-start.1
  100.4 2.0 collective-permute-start.7
  101.1 2.0 collective-permute-start.9
  102.3 69.3 %collective-permute-start.11 = (bf16[192,768]{1,0:T(8,128)(2,1)S(1)}, bf16[192,768]{1,0:T(8,128)(2,1)S(1)}, u32[]{:S(2)}, u32[]{:S(2)}) collective-permute-start(bf16[192,768]{1,0:T(8,128)(2,1)S(1)} %collective-permute-done.10), channel_id=1, source_target_pairs={{0,1},{1,0},{2,3},{3,2},{4,5},{5,4},{6,7},{7,6},{8,9},{9,8},{10,11... | collective-permute-start | bytes 884744 | tf_op jit(solution)/shard_map/ppermute | solution.py:629
  108.2 1.3 copy-start.5
  134.4 1.5 copy-start
  151.3 1.0 copy-start.8
  171.6 5.6 %copy-start.2 = (bf16[8,192,128]{2,1,0:T(8,128)(2,1)}, bf16[8,192,128]{2,1,0:T(8,128)(2,1)S(1)}, u32[]{:S(2)}) copy-start(bf16[8,192,128]{2,1,0:T(8,128)(2,1)S(1)} %return_tokens.1) | copy-start | bytes 1179652
  172.5 6.1 %collective-permute-start.17 = (bf16[192,2048]{1,0:T(8,128)(2,1)}, bf16[192,2048]{1,0:T(8,128)(2,1)S(1)}, u32[]{:S(2)}, u32[]{:S(2)}) collective-permute-start(bf16[192,2048]{1,0:T(8,128)(2,1)} %collective-permute-done.16), channel_id=1, source_target_pairs={{0,1},{1,0},{2,3},{3,2},{4,5},{5,4},{6,7},{7,6},{8,9},{9,8},{10,11... | collective-permute-start | bytes 2359304 | tf_op jit(solution)/shard_map/ppermute | solution.py:629
  172.5 6.0 %collective-permute-start.21 = (bf16[512,768]{1,0:T(8,128)(2,1)}, bf16[512,768]{1,0:T(8,128)(2,1)S(1)}, u32[]{:S(2)}, u32[]{:S(2)}) collective-permute-start(bf16[512,768]{1,0:T(8,128)(2,1)} %collective-permute-done.20), channel_id=1, source_target_pairs={{0,1},{1,0},{2,3},{3,2},{4,5},{5,4},{6,7},{7,6},{8,9},{9,8},{10,11... | collective-permute-start | bytes 2359304 | tf_op jit(solution)/shard_map/ppermute | solution.py:629
  175.1 4.5 collective-permute-start.19
  178.5 2.3 copy-start.9
  278.2 1.4 copy-start.3
  308.0 1.0 copy-start.1
  309.0 7.0 %copy-start.42 = (f32[3,1,256]{2,1,0:T(1,128)S(1)}, f32[3,1,256]{2,1,0:T(1,128)}, u32[]{:S(2)}) copy-start(f32[3,1,256]{2,1,0:T(1,128)} %get-tuple-element.105) | copy-start | bytes 9220
  309.0 7.8 %copy-start.38 = (f32[1,768]{1,0:T(1,128)S(1)}, f32[1,768]{1,0:T(1,128)}, u32[]{:S(2)}) copy-start(f32[1,768]{1,0:T(1,128)} %get-tuple-element.103) | copy-start | bytes 9220
  309.0 7.9 %copy-start.37 = (f32[1,768]{1,0:T(1,128)S(1)}, f32[1,768]{1,0:T(1,128)}, u32[]{:S(2)}) copy-start(f32[1,768]{1,0:T(1,128)} %get-tuple-element.104) | copy-start | bytes 9220
  490.7 5.7 %copy-start.26 = (bf16[128,768]{1,0:T(8,128)(2,1)S(1)}, bf16[128,768]{1,0:T(8,128)(2,1)}, u32[]{:S(2)}) copy-start(bf16[128,768]{1,0:T(8,128)(2,1)} %get-tuple-element.117) | copy-start | bytes 589828
  496.6 3.6 copy-start.16
  500.2 2.0 copy-start.15
  502.3 1.9 copy-start.34
  504.2 1.3 copy-start.33
  505.3 1.3 copy-start.32
  506.5 1.3 copy-start.31
  507.6 1.3 copy-start.30
  508.9 1.3 copy-start.29
  510.0 1.3 copy-start.28
  511.2 1.3 copy-start.27
  (3 other events, 2.7 us)
Sparse Core Ops, SparseCore 0:
  15.2 41.4 all-gather.2
  317.1 70.0 reduce-scatter.1

commit v3 on v2

--- a/solution.py
+++ b/solution.py
@@ -87,9 +87,12 @@
         return 2 * (r // (2 * self.W)) + (r % (2 * self.W)) // self.W
 
     def source(self, j, w):
-        if j % 2 == 0:
-            return 2 * self.W * (j // 2) + w
-        return 2 * self.W * (j // 2) + 2 * self.W - 1 - w
+        return self.source_in(j // 2, j % 2, w)
+
+    def source_in(self, pair, late, w):
+        if late:
+            return 2 * self.W * pair + 2 * self.W - 1 - w
+        return 2 * self.W * pair + w
 
 
 def enter(rows):
@@ -291,8 +294,8 @@
     p = plan
     return jnp.concatenate(
         [
-            ref[p.source(2 * pair, w), pl.ds(row, count), :],
-            ref[p.source(2 * pair + 1, w), pl.ds(row, count), :],
+            ref[p.source_in(pair, 0, w), pl.ds(row, count), :],
+            ref[p.source_in(pair, 1, w), pl.ds(row, count), :],
         ],
         axis=1,
     )
@@ -331,16 +334,10 @@
             o_ref[2 * pair + a, pl.ds(row, DH), :] = part.astype(B16)
 
 
-def attend_back_kernel(
-    plan, recv, lines, dout, of_ref, rl_ref, dq_ref, dkv_ref, line_ref, kn, vn, kt, dk, dv, tiles, near
+def back_head(
+    p, w, row, line, recv, dout, of_ref, rl, dq_ref, dkv_ref, kn, vn, kt, dk, dv, tiles, near
 ):
-    p = plan
-    me = lax.axis_index("rep")
-    w = me % p.W
-    group = (me // p.W) % p.G
-    h = pl.program_id(0)
-    row = pl.multiple_of(h * DH, DH)
-    bias_tiles(p, w, lines.at[group * p.HG + h], tiles)
+    bias_tiles(p, w, line, tiles)
     for r in range(p.R):
         kn[r * p.T : (r + 1) * p.T, :] = jnp.transpose(
             recv[r, pl.ds(p.F + row, DH), :].astype(F32)
@@ -353,23 +350,23 @@
     dk[...] = jnp.zeros_like(dk)
     dv[...] = jnp.zeros_like(dv)
     near[...] = jnp.zeros_like(near)
-    total = jnp.zeros((1, 2 * p.T), F32)
-    for pair in range(p.NP):
+
+    def one_pair(pair, total):
         qt = block_pair(p, recv, pair, w, row, DH)
         dot_rows = jnp.concatenate(
             [dout[2 * pair + a, pl.ds(row, DH), :] for a in range(2)], axis=1
         )
         of = jnp.concatenate([of_ref[2 * pair + a, pl.ds(row, DH), :] for a in range(2)], axis=1)
         delta = jnp.sum(dot_rows.astype(F32) * of, axis=0, keepdims=True)
-        rl = rl_ref[h, pair]
+        scale = rl[pair]
         qn = jnp.transpose(qt.astype(F32)).astype(B16)
         don = jnp.transpose(dot_rows.astype(F32)).astype(B16)
 
-        def step(i, acc, pair=pair, qt=qt, dot_rows=dot_rows, delta=delta, rl=rl, qn=qn, don=don):
+        def step(i, acc):
             start = pl.multiple_of(i * p.CK, p.CK)
             kind = jnp.maximum(i - pair + 2, 0)
             keys = pl.ds(start, p.CK)
-            prob = jnp.exp(dot(kn[keys, :], qt) + tiles[kind]) * rl
+            prob = jnp.exp(dot(kn[keys, :], qt) + tiles[kind]) * scale
             ds = (prob * (dot(vn[keys, :], dot_rows) - delta)).astype(B16)
             near[kind] += ds.astype(F32)
             dk[keys, :] += dot(ds, qn)
@@ -377,9 +374,11 @@
             return acc + dot(kt[:, keys], ds)
 
         acc = lax.fori_loop(0, pair + 1, step, jnp.zeros((DH + ONES, 2 * p.T), F32))
-        total = total + acc[DH : DH + 1]
         for a in range(2):
             dq_ref[2 * pair + a, pl.ds(row, DH), :] = acc[:DH, a * p.T : (a + 1) * p.T].astype(B16)
+        return total + acc[DH : DH + 1]
+
+    total = lax.fori_loop(0, p.NP, one_pair, jnp.zeros((1, 2 * p.T), F32))
     for r in range(p.R):
         dkv_ref[r, pl.ds(row, DH), :] = jnp.transpose(dk[r * p.T : (r + 1) * p.T, :]).astype(B16)
         dkv_ref[r, pl.ds(p.F + row, DH), :] = jnp.transpose(dv[r * p.T : (r + 1) * p.T, :]).astype(
@@ -411,7 +410,41 @@
     by_distance = jnp.sum(turned, axis=0, keepdims=True)
     rest = jnp.sum(total) - jnp.sum(both)
     place = lax.broadcasted_iota(jnp.int32, (1, 2 * p.T), 1)
-    line_ref[h] = by_distance + jnp.where(place == 2 * p.T - 1, rest, 0.0)
+    return by_distance + jnp.where(place == 2 * p.T - 1, rest, 0.0)
+
+
+def back_scratch(p):
+    return [
+        pltpu.VMEM((p.L, DH), B16),
+        pltpu.VMEM((p.L, DH), B16),
+        pltpu.VMEM((DH + ONES, p.L), B16),
+        pltpu.VMEM((p.L, DH), F32),
+        pltpu.VMEM((p.L, DH), F32),
+        pltpu.VMEM((3, p.CK, 2 * p.T), F32),
+        pltpu.VMEM((3, p.CK, 2 * p.T), F32),
+    ]
+
+
+def attend_back_kernel(plan, recv, lines, dout, of_ref, rl_ref, dq_ref, dkv_ref, line_ref, *scratch):
+    p = plan
+    me = lax.axis_index("rep")
+    w = me % p.W
+    group = (me // p.W) % p.G
+    h = pl.program_id(0)
+    row = pl.multiple_of(h * DH, DH)
+    line_ref[h] = back_head(
+        p,
+        w,
+        row,
+        lines.at[group * p.HG + h],
+        recv,
+        dout,
+        of_ref,
+        rl_ref.at[h],
+        dq_ref,
+        dkv_ref,
+        *scratch,
+    )
 
 
 def encode_kernel(enc, wk, wv, kn, kt, vn, vt):
@@ -596,7 +629,12 @@
 
 
 def last_kernel(plan, hidden, grads, a1, gain, dx1, wq, wk, wv, dh_ref, dgain_ref, dwq, dwk, dwv):
-    p = plan
+    dgain_ref[...] = last_products(
+        plan, hidden, grads, a1, gain, dx1, wq, wk, wv, dh_ref, dwq, dwk, dwv
+    )
+
+
+def last_products(p, hidden, grads, a1, gain, dx1, wq, wk, wv, dh_ref, dwq, dwk, dwv):
     x = hidden[...].reshape(p.S * p.T, D).astype(F32)
     da1 = jnp.zeros((p.S * p.T, D), F32)
     for n, (weight, dw) in enumerate(((wq, dwq), (wk, dwk), (wv, dwv))):
@@ -607,11 +645,11 @@
             )
             rows.append(jnp.transpose(turned.astype(F32)))
         d = jnp.concatenate(rows, axis=0).astype(B16)
-        dw[...] = t_dot(a1[...], d).astype(B16)
+        dw[...] = t_dot(a1[...], d).astype(B16).reshape(dw.shape)
         da1 = da1 + dot_t(d, weight[...])
     term, dgain = norm_back(x, gain[...], da1)
-    dgain_ref[...] = dgain
     dh_ref[...] = (dx1[...] + term).astype(B16).reshape(dh_ref.shape)
+    return dgain
 
 
 def gather_rows(part):
@@ -643,9 +681,9 @@
 
 
 class Job:
-    def __init__(self, source, result, rows, col, cols):
+    def __init__(self, source, result, row, rows, col, cols):
         self.source, self.result = source, result
-        self.rows, self.col, self.cols = rows, col, cols
+        self.row, self.rows, self.col, self.cols = row, rows, col, cols
 
 
 def partner(bit):
@@ -699,6 +737,7 @@
         self.half = half
         self.mine = pl.ds(pl.multiple_of(job.col + self.bits[0] * half, 128), half)
         self.other = pl.ds(pl.multiple_of(job.col + (1 - self.bits[0]) * half, 128), half)
+        self.all = pl.ds(job.row, job.rows)
         self.first = [0]
         count = job.rows
         for b in range(1, BITS):
@@ -711,6 +750,9 @@
     def span(self, first, count):
         return pl.ds(pl.multiple_of(first, 16), count)
 
+    def out(self, first, count):
+        return self.result.at[self.span(self.job.row + first, count), self.mine]
+
     def go(self, copy):
         copy.start()
         self.sent.append(copy)
@@ -719,10 +761,16 @@
         job = self.job
         if n == 0:
             pltpu.make_async_copy(
-                self.source.at[:, :, self.mine], self.acc, self.local[0]
+                self.source.at[:, self.all, self.mine], self.acc, self.local[0]
             ).start()
             self.go(
-                to_rep(self.source.at[:, :, self.other], self.core, self.send[0], self.recv[0], 0)
+                to_rep(
+                    self.source.at[:, self.all, self.other],
+                    self.core,
+                    self.send[0],
+                    self.recv[0],
+                    0,
+                )
             )
         elif n == 1:
             landed(self.acc, self.local[0])
@@ -739,22 +787,19 @@
             self.give(n - 1)
         elif n == 5:
             self.take(3)
-            rows = self.span(self.first[3], self.count(3))
-            piece = self.acc.at[self.x, rows]
-            place = self.result.at[rows, self.mine]
+            piece = self.acc.at[self.x, self.span(self.first[3], self.count(3))]
+            place = self.out(self.first[3], self.count(3))
             pltpu.make_async_copy(piece, place, self.local[1]).start()
             self.go(to_rep(piece, place, self.send[5], self.recv[5], 3))
         elif n in (6, 7, 8):
             level = 9 - n
             if n == 6:
-                rows = self.span(self.first[3], self.count(3))
-                landed(self.result.at[rows, self.mine], self.local[1])
+                landed(self.out(self.first[3], self.count(3)), self.local[1])
             self.landed_at(level)
-            rows = self.span(self.first[level - 1], self.count(level - 1))
-            place = self.result.at[rows, self.mine]
+            place = self.out(self.first[level - 1], self.count(level - 1))
             self.go(to_rep(place, place, self.send[n], self.recv[n], level - 1))
         else:
-            landed(self.result.at[:, self.other], self.recv[8])
+            landed(self.result.at[self.all, self.other], self.recv[8])
             for copy in self.sent:
                 copy.wait_send()
 
@@ -780,7 +825,7 @@
     def landed_at(self, level):
         count = self.count(level)
         first = self.first[level - 1] + (1 - self.bits[level]) * count
-        landed(self.result.at[self.span(first, count), self.mine], self.recv[8 - level])
+        landed(self.out(first, count), self.recv[8 - level])
 
 
 def job_buffers(job):
@@ -795,61 +840,243 @@
 JOB_BUFFERS = 6
 
 
-def greet_partners():
+class SmallRun:
+    STAGES = BITS + 2
+
+    def __init__(self, sums, terms, send, recv):
+        self.sums, self.terms, self.send, self.recv = sums, terms, send, recv
+
+    def copy(self, n):
+        args = (self.sums.at[n], self.terms.at[n], self.send.at[n], self.recv.at[n])
+        return to_row(*args) if n == BITS else to_rep(*args, n)
+
+    def stage(self, n):
+        if n > 0:
+            landed(self.terms.at[n - 1], self.recv.at[n - 1])
+            self.sums[n] = self.sums[n - 1] + self.terms[n - 1]
+        if n <= BITS:
+            self.copy(n).start()
+        else:
+            for i in range(BITS + 1):
+                self.copy(i).wait_send()
+
+
+def in_ticks(runs):
+    last = max(i + run.STAGES for i, run in enumerate(runs))
+    for tick in range(last):
+        for n in range(max(run.STAGES for run in runs)):
+            if 0 <= tick - n < len(runs) and n < runs[tick - n].STAGES:
+                runs[tick - n].stage(n)
+        yield
+
+
+def jobs_of(shapes):
+    jobs = []
+    for i, (rows, cols) in enumerate(shapes):
+        wide = cols // 2 if cols > 1024 else cols
+        tall = rows // 2 if rows > 512 else rows
+        for row in range(0, rows, tall):
+            for col in range(0, cols, wide):
+                jobs.append(Job(i, i, row, tall, col, wide))
+    return jobs
+
+
+SMALL_ROWS = 16
+
+
+def tail_kernel(p, jobs, early, arrays, *refs):
+    refs = list(refs)
+    take = lambda n: [refs.pop(0) for _ in range(n)]
+    sources = take(early)
+    (dot_,) = take(1)
+    recv, lines, of_ref, rl_ref, hidden, a1, gain, dx1, dgc, dgf, wq, wk, wv = take(13)
+    results = take(arrays)
+    small, dh_ref = take(2)
+    dout, dq, dkv, part, out, grads = take(6)
+    late = take(arrays - early)
+    small_sums, small_terms = take(2)
+    back = take(7)
+    rows_send, rows_recv, part_sem, got_sem, ret_send, ret_recv = take(6)
+    small_send, small_recv = take(2)
+    sems = take(3)
+    sources = sources + late
+    runs = [
+        JobRun(job, sources[job.source], results[job.result], take(JOB_BUFFERS), sems, i)
+        for i, job in enumerate(jobs)
+    ]
+    ready = sum(1 for job in jobs if job.source < early)
+    runs.insert(ready, SmallRun(small_sums, small_terms, small_send, small_recv))
+
+    me = lax.axis_index("rep")
+    w = me % p.W
+    unit = me // p.W
+    group = unit % p.G
+    mine = p.worker_of(me)
+    slot = p.slot_of(me)
     barrier = pltpu.get_barrier_semaphore()
+    for k in range(1, p.R):
+        pl.semaphore_signal(
+            barrier, inc=1, device_id={"rep": (me + k) % p.R}, device_id_type=MESH
+        )
     x = lax.axis_index("shard")
     pl.semaphore_signal(barrier, inc=1, device_id={"shard": 1 - x}, device_id_type=MESH)
-    for b in range(BITS):
-        pl.semaphore_signal(
-            barrier, inc=1, device_id={"rep": partner(b)[1]}, device_id_type=MESH
-        )
-    pl.semaphore_wait(barrier, BITS + 1)
-
-
-def sum_kernel(jobs, arrays, *refs):
-    sources, results = refs[:arrays], refs[arrays : 2 * arrays]
-    scratch = refs[2 * arrays :]
-    sems = scratch[:3]
-    greet_partners()
-    runs = [
-        JobRun(
-            job,
-            sources[job.source],
-            results[job.result],
-            scratch[3 + i * JOB_BUFFERS : 3 + (i + 1) * JOB_BUFFERS],
-            sems,
-            i,
-        )
-        for i, job in enumerate(jobs)
+    pl.semaphore_wait(barrier, p.R)
+
+    pipeline = in_ticks(runs)
+    passed = 0
+
+    def tick(count=1):
+        nonlocal passed
+        for _ in range(count):
+            next(pipeline)
+        passed += count
+
+    for u in range(p.U):
+        start_either(
+            me, u * p.W + mine, dot_.at[u], dout.at[slot], rows_send.at[u], rows_recv.at[slot]
+        )
+    tick(2)
+    for j in range(p.J):
+        landed(dout.at[j], rows_recv.at[j])
+    lines_at = lax.broadcasted_iota(jnp.int32, (SMALL_ROWS, D), 0)
+    block = jnp.zeros((SMALL_ROWS, D), F32)
+    for h in range(p.HG):
+        sums = back_head(
+            p,
+            w,
+            h * DH,
+            lines.at[group * p.HG + h],
+            recv,
+            dout,
+            of_ref,
+            rl_ref.at[h],
+            dq,
+            dkv,
+            *back,
+        )
+        sums = jnp.concatenate([sums, jnp.zeros((1, D - 2 * p.T), F32)], axis=1)
+        block = jnp.where(lines_at == 3 + group * p.HG + h, sums, block)
+        tick()
+
+    def give(k, j):
+        to = (w + k) % p.W
+        return remote(
+            dkv.at[p.source(j, to)],
+            part.at[k - 1, j],
+            part_sem.at[k - 1, j],
+            got_sem.at[k - 1, j],
+            me - w + to,
+        )
+
+    for j in range(p.J):
+        for k in range(1, p.W):
+            give(k, j).start()
+    tick()
+    for j in range(p.J):
+        r = p.source(j, w)
+        total = dkv[r].astype(F32)
+        for k in range(1, p.W):
+            landed(part.at[k - 1, j], got_sem.at[k - 1, j])
+            total = total + part[k - 1, j].astype(F32)
+        out[j, 0 : p.F, :] = dq[j]
+        out[j, p.F : 3 * p.F, :] = total.astype(B16)
+        start_either(me, r, out.at[j], grads.at[unit], ret_send.at[j], ret_recv.at[unit])
+    tick(2)
+    for u in range(p.U):
+        landed(grads.at[u], ret_recv.at[u])
+    dgain = last_products(p, hidden, grads, a1, gain, dx1, wq, wk, wv, dh_ref, *late)
+    for i, row in enumerate((dgain, dgc[...], dgf[...])):
+        block = jnp.where(lines_at == i, row, block)
+    small_sums[0] = block
+    assert passed <= ready
+    for _ in pipeline:
+        pass
+    small[...] = small_sums[BITS + 1]
+    for u in range(p.U):
+        end_either(
+            me, u * p.W + mine, dot_.at[u], dout.at[slot], rows_send.at[u], rows_recv.at[slot]
+        )
+    for j in range(p.J):
+        r = p.source(j, w)
+        end_either(me, r, out.at[j], grads.at[unit], ret_send.at[j], ret_recv.at[unit])
+        for k in range(1, p.W):
+            give(k, j).wait_send()
+
+
+def tail_call(p, mats, dot_, held, hidden, collective):
+    half = D // 2
+    shapes = [m.shape[1:] for m in mats] + [(half, D)] * 3
+    jobs = jobs_of(shapes)
+    dma = pltpu.SemaphoreType.DMA
+    others = max(p.W - 1, 1)
+    scratch = [
+        pltpu.VMEM((p.J, p.F, p.T), B16),
+        pltpu.VMEM((p.J, p.F, p.T), B16),
+        pltpu.VMEM((p.R, 2 * p.F, p.T), B16),
+        pltpu.VMEM((others, p.J, 2 * p.F, p.T), B16),
+        pltpu.VMEM((p.J, 3 * p.F, p.T), B16),
+        pltpu.VMEM((p.U, 3 * p.F, p.T), B16),
     ]
-    for tick in range(len(runs) + JobRun.STAGES - 1):
-        for n in reversed(range(JobRun.STAGES)):
-            if 0 <= tick - n < len(runs):
-                runs[tick - n].stage(n)
-
-
-def sum_call(grads, collective):
-    jobs = []
-    for i, g in enumerate(grads):
-        rows, cols = g.shape[1:]
-        wide = cols // 2 if cols > 1024 else cols
-        for col in range(0, cols, wide):
-            jobs.append(Job(i, i, rows, col, wide))
-    dma = pltpu.SemaphoreType.DMA
-    scratch = [dma((len(jobs), 9)), dma((len(jobs), 9)), dma((len(jobs), 2))]
+    scratch += [pltpu.VMEM((2, half, D), B16)] * 3
+    scratch += [
+        pltpu.VMEM((BITS + 2, SMALL_ROWS, D), F32),
+        pltpu.VMEM((BITS + 1, SMALL_ROWS, D), F32),
+    ]
+    scratch += back_scratch(p)
+    scratch += [
+        dma((p.U,)),
+        dma((p.J,)),
+        dma((others, p.J)),
+        dma((others, p.J)),
+        dma((p.J,)),
+        dma((p.U,)),
+        dma((BITS + 1,)),
+        dma((BITS + 1,)),
+        dma((len(jobs), 9)),
+        dma((len(jobs), 9)),
+        dma((len(jobs), 2)),
+    ]
     for job in jobs:
         scratch += job_buffers(job)
-    return pl.pallas_call(
-        functools.partial(sum_kernel, jobs, len(grads)),
-        out_shape=[jax.ShapeDtypeStruct(g.shape[1:], B16) for g in grads],
-        in_specs=[pl.BlockSpec(memory_space=pl.ANY)] * len(grads),
-        out_specs=[pl.BlockSpec(memory_space=pl.ANY)] * len(grads),
+    anywhere = pl.BlockSpec(memory_space=pl.ANY)
+    near = pl.BlockSpec(memory_space=pltpu.VMEM)
+    *sums, small, dh = pl.pallas_call(
+        functools.partial(tail_kernel, p, jobs, len(mats), len(shapes)),
+        out_shape=[jax.ShapeDtypeStruct(s, B16) for s in shapes]
+        + [
+            jax.ShapeDtypeStruct((SMALL_ROWS, D), F32),
+            jax.ShapeDtypeStruct(hidden.shape, B16),
+        ],
+        in_specs=[anywhere] * (len(mats) + 1) + [near] * len(held),
+        out_specs=[anywhere] * len(shapes) + [near] * 2,
         scratch_shapes=scratch,
         compiler_params=pltpu.CompilerParams(
-            collective_id=collective, has_side_effects=True, vmem_limit_bytes=56 * 2**20
+            collective_id=collective, has_side_effects=True, vmem_limit_bytes=60 * 2**20
         ),
-        name="sum_gradients",
-    )(*grads)
+        name="tail",
+    )(*mats, dot_, *held)
+    return sums, small, dh
+
+
+def widen_kernel(count, *refs):
+    for i in range(count):
+        refs[count + i][...] = refs[i][...].astype(F32)
+
+
+def widen(mats):
+    parts = 8
+    blocks = [
+        pl.BlockSpec((m.shape[0] // parts, m.shape[1]), lambda i: (i, 0)) for m in mats
+    ]
+    return pl.pallas_call(
+        functools.partial(widen_kernel, len(mats)),
+        grid=(parts,),
+        out_shape=[jax.ShapeDtypeStruct(m.shape, F32) for m in mats],
+        in_specs=blocks,
+        out_specs=blocks,
+        compiler_params=pltpu.CompilerParams(vmem_limit_bytes=40 * 2**20),
+        name="widen",
+    )(*mats)
 
 
 def local(
@@ -1043,100 +1270,100 @@
     encoded_grad = lax.psum_scatter(
         denc.reshape(seqs, enc_rows // seqs, D), "rep", scatter_dimension=1, tiled=True
     )
-    dout = comm_call(
-        functools.partial(scatter_rows, p),
-        (p.J, p.F, toks),
-        (dot_,),
-        [dma((p.U,)), dma((p.J,))],
-        2,
-        "scatter_rows",
-    )
-    dq, dkv, line = pl.pallas_call(
-        functools.partial(attend_back_kernel, p),
-        grid=(p.HG,),
-        out_shape=[
-            jax.ShapeDtypeStruct((p.J, p.F, toks), B16),
-            jax.ShapeDtypeStruct((p.R, 2 * p.F, toks), B16),
-            jax.ShapeDtypeStruct((p.HG, 1, 2 * toks), F32),
-        ],
-        in_specs=[
-            whole((p.R, 3 * p.F, toks)),
-            whole((H, 1, 2 * toks)),
-            whole((p.J, p.F, toks)),
-            whole((p.J, p.F, toks)),
-            whole((p.HG, p.NP, 1, 2 * toks)),
-        ],
-        out_specs=[
-            whole((p.J, p.F, toks)),
-            whole((p.R, 2 * p.F, toks)),
-            whole((p.HG, 1, 2 * toks)),
-        ],
-        scratch_shapes=[
-            pltpu.VMEM((p.L, DH), B16),
-            pltpu.VMEM((p.L, DH), B16),
-            pltpu.VMEM((DH + ONES, p.L), B16),
-            pltpu.VMEM((p.L, DH), F32),
-            pltpu.VMEM((p.L, DH), F32),
-            pltpu.VMEM((3, p.CK, 2 * toks), F32),
-            pltpu.VMEM((3, p.CK, 2 * toks), F32),
-        ],
-        compiler_params=pltpu.CompilerParams(vmem_limit_bytes=56 * 2**20),
-        name="attend_back",
-    )(recv, lines, dout, of, rl)
-    grads = comm_call(
-        functools.partial(return_grads, p),
-        (p.U, 3 * p.F, toks),
-        (dq, dkv),
-        [
-            pltpu.VMEM((max(p.W - 1, 1), p.J, 2 * p.F, toks), B16),
-            pltpu.VMEM((p.J, 3 * p.F, toks), B16),
-            dma((p.J,)),
-            dma((max(p.W - 1, 1), p.J)),
-            dma((max(p.W - 1, 1), p.J)),
-            dma((p.U,)),
-        ],
-        3,
-        "return_grads",
-        space=pltpu.VMEM,
-    )
-    hidden_grad, dg_self, dwq, dwk, dwv = plain_call(
-        functools.partial(last_kernel, p),
-        [(hidden.shape, B16), ((1, D), F32)] + [((D, D), B16)] * 3,
-        (hidden, grads, a1, gains[0], dx1, wq, wk, wv),
-        "last",
-    )
-
-    group = (lax.axis_index("rep") // p.W) % p.G
-    by_bucket = jnp.einsum(
-        "hl,lb->bh", line[:, 0, :], onehot.astype(F32), precision=lax.Precision.HIGHEST
-    )
-    dtable = lax.dynamic_update_slice(jnp.zeros((NB, H), F32), by_bucket, (0, group * p.HG))
-
-    mats = [dwg, dwu, dwd, dwo, dwcq, dwck, dwcv, dwco, dwq, dwk, dwv]
     n_shard = lax.axis_size("shard")
-    lot = jnp.concatenate(
-        [g.reshape(n_shard, part) for g in (dg_self, dg_cross, dg_ffn)]
-        + [dtable.reshape(n_shard, -1)],
-        axis=1,
-    )
-    size = lot.shape[1]
-    if n_shard == 2 and p.R == 2**BITS:
-        lines_in = 16 * 2 ** (BITS - 1)
-        lot = jnp.pad(lot.astype(B16), ((0, 0), (0, lines_in * D - size)))
-        *sums, lot = sum_call(
-            [g.reshape(2, g.shape[0] // 2, g.shape[1]) for g in mats]
-            + [lot.reshape(2, lines_in, D)],
-            4,
-        )
-        lot = lot.reshape(-1)[:size].astype(F32)
-        mats = [g.astype(F32) for g in sums]
+    mine = lax.axis_index("shard")
+    if n_shard == 2 and p.R == 2**BITS and 3 + H <= SMALL_ROWS:
+        early = [
+            g.reshape(2, g.shape[0] // 2, g.shape[1])
+            for g in (dwd, dwg, dwu, dwo, dwcq, dwck, dwcv, dwco)
+        ]
+        held = (recv, lines, of, rl, hidden, a1, gains[0], dx1, dg_cross, dg_ffn, wq, wk, wv)
+        sums, block, hidden_grad = tail_call(p, early, dot_, held, hidden, 2)
+        dwd, dwg, dwu, dwo, dwcq, dwck, dwcv, dwco, dwq, dwk, dwv = widen(sums)
+        mats = [dwq, dwk, dwv, dwo, dwcq, dwck, dwcv, dwco, dwg, dwu, dwd]
+        dgains = lax.dynamic_slice(block, (0, mine * part), (3, part))
+        by_bucket = jnp.einsum(
+            "hl,lb->bh",
+            block[3 : 3 + H, : 2 * toks],
+            onehot.astype(F32),
+            precision=lax.Precision.HIGHEST,
+        )
+        dtab = lax.dynamic_slice(
+            by_bucket, (mine * bias_table.shape[0], 0), bias_table.shape
+        )
     else:
-        mats = reduce_grads(mats)
+        dout = comm_call(
+            functools.partial(scatter_rows, p),
+            (p.J, p.F, toks),
+            (dot_,),
+            [dma((p.U,)), dma((p.J,))],
+            2,
+            "scatter_rows",
+        )
+        dq, dkv, line = pl.pallas_call(
+            functools.partial(attend_back_kernel, p),
+            grid=(p.HG,),
+            out_shape=[
+                jax.ShapeDtypeStruct((p.J, p.F, toks), B16),
+                jax.ShapeDtypeStruct((p.R, 2 * p.F, toks), B16),
+                jax.ShapeDtypeStruct((p.HG, 1, 2 * toks), F32),
+            ],
+            in_specs=[
+                whole((p.R, 3 * p.F, toks)),
+                whole((H, 1, 2 * toks)),
+                whole((p.J, p.F, toks)),
+                whole((p.J, p.F, toks)),
+                whole((p.HG, p.NP, 1, 2 * toks)),
+            ],
+            out_specs=[
+                whole((p.J, p.F, toks)),
+                whole((p.R, 2 * p.F, toks)),
+                whole((p.HG, 1, 2 * toks)),
+            ],
+            scratch_shapes=back_scratch(p),
+            compiler_params=pltpu.CompilerParams(vmem_limit_bytes=56 * 2**20),
+            name="attend_back",
+        )(recv, lines, dout, of, rl)
+        grads = comm_call(
+            functools.partial(return_grads, p),
+            (p.U, 3 * p.F, toks),
+            (dq, dkv),
+            [
+                pltpu.VMEM((max(p.W - 1, 1), p.J, 2 * p.F, toks), B16),
+                pltpu.VMEM((p.J, 3 * p.F, toks), B16),
+                dma((p.J,)),
+                dma((max(p.W - 1, 1), p.J)),
+                dma((max(p.W - 1, 1), p.J)),
+                dma((p.U,)),
+            ],
+            3,
+            "return_grads",
+            space=pltpu.VMEM,
+        )
+        hidden_grad, dg_self, dwq, dwk, dwv = plain_call(
+            functools.partial(last_kernel, p),
+            [(hidden.shape, B16), ((1, D), F32)] + [((D, D), B16)] * 3,
+            (hidden, grads, a1, gains[0], dx1, wq, wk, wv),
+            "last",
+        )
+
+        group = (lax.axis_index("rep") // p.W) % p.G
+        by_bucket = jnp.einsum(
+            "hl,lb->bh", line[:, 0, :], onehot.astype(F32), precision=lax.Precision.HIGHEST
+        )
+        dtable = lax.dynamic_update_slice(jnp.zeros((NB, H), F32), by_bucket, (0, group * p.HG))
+
+        mats = reduce_grads([dwq, dwk, dwv, dwo, dwcq, dwck, dwcv, dwco, dwg, dwu, dwd])
+        lot = jnp.concatenate(
+            [g.reshape(n_shard, part) for g in (dg_self, dg_cross, dg_ffn)]
+            + [dtable.reshape(n_shard, -1)],
+            axis=1,
+        )
+        size = lot.shape[1]
         lot = lax.psum(lot, ("shard", "rep"))
-        lot = lax.dynamic_slice(lot, (lax.axis_index("shard"), 0), (1, size))[0]
-    mats = mats[8:] + mats[3:8] + mats[:3]
-    dgains = [lot[i * part : (i + 1) * part] for i in range(3)]
-    dtab = lot[3 * part :].reshape(bias_table.shape)
+        lot = lax.dynamic_slice(lot, (mine, 0), (1, size))[0]
+        dgains = [lot[i * part : (i + 1) * part] for i in range(3)]
+        dtab = lot[3 * part :].reshape(bias_table.shape)
     return (
         output.reshape(hidden.shape),
         hidden_grad,

time: 530 us -> 463 us (0.87)
  Pallas kernels: 366 us -> 315 us
  other arithmetic: 27.8 us -> 10.1 us
    pallas_call x4 -> x2, Pallas kernels: 85.1 us -> 44.2 us  [comm_call(): pl.pallas_call(kernel, out_shape=jax.ShapeDtypeStruct(out, B16), in_specs...]
    convert_element_type x12 -> x0, other arithmetic: 16.2 us -> none  [the longest x11 16.2 us: local(): mats = [g.astype(F32) for g in sums]]
    unnamed x92 -> x78, local copies, waits for them, and re-layouts: 18 us -> 24.8 us
    slice x2 -> x0, local copies, waits for them, and re-layouts: 6.29 us -> none  [the longest x1 5.7 us: local(): lot = lot.reshape(-1)[:size].astype(F32)]
    pallas_call x5 -> x4, Pallas kernels: 56.9 us -> 50.7 us  [plain_call(): pl.pallas_call(kernel, out_shape=[jax.ShapeDtypeStruct(s, t) for s, t in...]
    another operation x10 -> x11, local copies, waits for them, and re-layouts: 10.8 us -> 12.4 us
  transfers between devices with their start and end apart: 24 -> 24, of which waited for: 2 -> 2; matrix products, arithmetic and copies ran while one was open for 16% -> 13% of each run, Pallas kernels for 45% -> 56%
where the time goes in v3:
time: 463 us; the launch traced here: 455 us
  Pallas kernels  315 us (68%)
  local copies, waits for them, and re-layouts  72.8 us (16%)
  blocking collectives  19 us (4%)
  between operations  14.9 us (3%)
  starting transfers between devices  14.8 us (3%)
  other arithmetic  10.1 us (2%)
  waiting for transfers between devices  7.81 us (2%)
    pallas_call x1, Pallas kernels, tail_call(): pl.pallas_call(functools.partial(tail_kernel, p, jobs, len(mats), len(sha...  183 us
    pallas_call x4, Pallas kernels, plain_call(): pl.pallas_call(kernel, out_shape=[jax.ShapeDtypeStruct(s, t) for s, t in...  50.7 us
    pallas_call x2, Pallas kernels, comm_call(): pl.pallas_call(kernel, out_shape=jax.ShapeDtypeStruct(out, B16), in_specs...  44.2 us
    unnamed x78, local copies, waits for them, and re-layouts  24.8 us
    all_gather x1, blocking collectives, local(): small = lax.all_gather(small, 'shard', axis=0)  19 us
    pallas_call x1, Pallas kernels, local(): pl.pallas_call(functools.partial(attend_kernel, p), grid=(p.HG,), out_sha...  15.4 us
    dynamic_update_slice x11, local copies, waits for them, and re-layouts, gather_rows(): full = lax.dynamic_update_slice(full, got[None], (owner, core * half, 0))  15.2 us
    pallas_call x1, Pallas kernels, local(): pl.pallas_call(ffn_kernel, grid=(ff // chunk,), out_shape=[jax.ShapeDtype...  14.3 us
  transfers between devices with their start and end apart: 24, of which 2 were waited for; matrix products, arithmetic and copies ran while one was open for 13% of the time, Pallas kernels for 56%

profile of v3, /device:TPU:0, one launch (start us, length us, event | category | flops | bytes accessed | tf_op | source)
XLA Modules:
  0.0 455.2 jit_solution(12626068754543022060)
XLA Ops:
  7.3 1.1 copy-done.22
  9.3 2.9 collective-permute-start.12
  12.2 1.1 broadcast.9.clone.7
  13.4 1.0 bitcast_dynamic-update-slice_fusion.9
  16.6 1.6 collective-permute-start.4
  18.2 1.1 broadcast.9.clone.1
  21.3 1.1 broadcast.9.clone
  24.1 1.6 collective-permute-start
  25.9 19.0 %all-gather = bf16[2,1,1344]{2,1,0:T(2,128)(2,1)S(1)} all-gather(bf16[1,1,1344]{2,1,0:T(2,128)(2,1)S(1)} %maximum_bitcast_fusion), channel_id=1, replica_groups=mesh['shard'=2,'rep'=16] {'shard'}, dimensions={0}, use_global_device_ids=true | all-gather | bytes 8064 | tf_op jit(solution)/shard_map/all_gather | solution.py:1116
  45.7 1.1 broadcast.9.clone.3
  48.5 2.1 broadcast.10.clone
  50.5 1.0 copy-done.18
  51.5 1.4 bitcast_dynamic-update-slice_fusion.2
  52.9 1.0 constant_dynamic-slice_fusion.4
  53.9 2.1 broadcast.10.clone.1
  56.0 0.9 copy-done.19
  56.9 1.5 bitcast_dynamic-update-slice_fusion.1
  58.4 1.0 constant_dynamic-slice_fusion.3
  59.6 1.1 broadcast.9.clone.4
  61.6 1.1 broadcast.9.clone.5
  63.3 1.1 bitcast_dynamic-update-slice_fusion.11
  64.6 1.7 copy-done.20
  66.3 1.4 bitcast_dynamic-update-slice_fusion
  68.4 2.1 constant_dynamic-slice_fusion.2
  73.6 1.8 collective-permute-start.6
  76.4 1.7 bitcast_dynamic-update-slice_fusion.18
  78.1 1.8 collective-permute-start.10
  79.9 1.7 bitcast_dynamic-update-slice_fusion.28
  81.8 1.7 bitcast_dynamic-update-slice_fusion.30
  83.5 1.8 collective-permute-start.18
  85.3 1.7 bitcast_dynamic-update-slice_fusion.32
  88.0 2.1 collective-permute-done.8
  90.8 5.6 %collective-permute-done.10 = bf16[192,768]{1,0:T(8,128)(2,1)S(1)} collective-permute-done((bf16[192,768]{1,0:T(8,128)(2,1)S(1)}, bf16[192,768]{1,0:T(8,128)(2,1)S(1)}, u32[]{:S(2)}, u32[]{:S(2)}) %collective-permute-start.10) | collective-permute-done | bytes 294944 | tf_op jit(solution)/shard_map/ppermute | solution.py:666
  103.9 4.4 project.1
  108.2 1.3 copy-done.5
  109.5 24.9 %scatter_tokens.1.recv.refs_9_ = bf16[16,576,128]{2,1,0:T(8,128)(2,1)S(1)} custom-call(bf16[8,576,128]{2,1,0:T(8,128)(2,1)S(1)} %copy-done.5), custom_call_target="tpu_custom_call" | custom-call | tf_op jit(solution)/shard_map/scatter_tokens/pallas_call | solution.py:241
  134.4 1.4 copy-done
  135.8 15.4 %attend.1 = (bf16[8,192,128]{2,1,0:T(8,128)(2,1)}, f32[8,192,128]{2,1,0:T(8,128)}, f32[3,4,1,256]{3,2,1,0:T(1,128)}) custom-call(bf16[16,576,128]{2,1,0:T(8,128)(2,1)} %copy-done, f32[12,1,256]{2,1,0:T(1,128)} %broadcast_in_dim.116.lines.refs_10_), custom_call_target="tpu_custom_call" | custom-call | tf_op jit(solution)/shard_map/attend/pallas_call | solution.py:1169
  151.3 1.0 copy-done.14
  152.2 19.3 %return_tokens.1 = bf16[8,192,128]{2,1,0:T(8,128)(2,1)S(1)} custom-call(bf16[8,192,128]{2,1,0:T(8,128)(2,1)S(1)} %copy-done.14), custom_call_target="tpu_custom_call" | custom-call | tf_op jit(solution)/shard_map/return_tokens/pallas_call | solution.py:241
  172.9 2.1 bitcast_dynamic-update-slice_fusion.8
  175.1 2.2 bitcast_dynamic-update-slice_fusion.6
  177.3 1.2 bitcast_dynamic-update-slice_fusion.4
  178.6 1.1 bitcast_dynamic-update-slice_fusion.7
  179.6 1.1 bitcast_dynamic-update-slice_fusion.5
  180.8 9.4 %encode.1 = (bf16[12,1024,64]{2,1,0:T(8,128)(2,1)}, bf16[12,80,1024]{2,1,0:T(8,128)(2,1)}, bf16[12,1024,64]{2,1,0:T(8,128)(2,1)}, bf16[12,80,1024]{2,1,0:T(8,128)(2,1)}) custom-call(bf16[1024,768]{1,0:T(8,128)(2,1)} %bitcast.119, bf16[768,768]{1,0:T(8,128)(2,1)} %bitcast.117, bf16[768,768]{1,0:T(8,128)(2,1)} %bitcast.34.wv.wcv), custom_call_target="tpu_custom_call" | custom-call | tf_op jit(solution)/shard_map/encode/pallas_call | solution.py:53
  190.2 12.8 %cross.1 = (f32[256,768]{1,0:T(8,128)}, f32[256,768]{1,0:T(8,128)}, bf16[256,768]{1,0:T(8,128)(2,1)}, bf16[2,768,128]{2,1,0:T(8,128)(2,1)}, f32[2,768,128]{2,1,0:T(8,128)}, /*index=5*/f32[2,12,1,128]{3,2,1,0:T(1,128)}) custom-call(bf16[2,128,768]{2,1,0:T(8,128)(2,1)} %refs_13_.1, bf16[2,768,128]{2,1,0:T(8,128)(2,1)} %bitcast.112, ...), custom_call_target="tpu_custom_call" | custom-call | tf_op jit(solution)/shard_map/cross/pallas_call | solution.py:53
  203.0 14.3 %ffn.1 = (bf16[256,768]{1,0:T(8,128)(2,1)}, f32[256,768]{1,0:T(8,128)}, f32[1,768]{1,0:T(1,128)}, bf16[768,2048]{1,0:T(8,128)(2,1)}, bf16[768,2048]{1,0:T(8,128)(2,1)}, /*index=5*/bf16[2048,768]{1,0:T(8,128)(2,1)}) custom-call(f32[256,768]{1,0:T(8,128)} %get-tuple-element.76.x2_ref, bf16[256,768]{1,0:T(8,128)(2,1)} %bitcast.130, f32[1,768]{1,0:T(1,128)} %bitcast.138, ...), custom_call_target="tpu_custom_call" | custom-call | tf_op jit(solution)/shard_map/ffn/pallas_call | solution.py:1216
  217.3 24.1 %cross_back.1 = (f32[256,768]{1,0:T(8,128)}, f32[1,768]{1,0:T(1,128)}, bf16[8,192,128]{2,1,0:T(8,128)(2,1)}, bf16[1024,768]{1,0:T(8,128)(2,1)}, bf16[768,768]{1,...) custom-call(f32[256,768]{1,0:T(8,128)} %get-tuple-element.81.dx2_ref, ...), custom_call_target="tpu_custom_call" | custom-call | tf_op jit(solution)/shard_map/cross_back/pallas_call | solution.py:53
  241.4 183.3 %tail.1 = (bf16[1024,768]{1,0:T(8,128)(2,1)}, bf16[384,2048]{1,0:T(8,128)(2,1)}, bf16[384,2048]{1,0:T(8,128)(2,1)}, bf16[384,768]{1,0:T(8,128)(2,1)}, bf16[384,7...) custom-call(bf16[2,1024,768]{2,1,0:T(8,128)(2,1)} %bitcast.123, ...), custom_call_target="tpu_custom_call" | custom-call | tf_op jit(solution)/shard_map/tail/pallas_call | solution.py:1043
  424.8 1.4 copy-done.2
  426.2 1.4 copy-done.3
  427.6 1.4 copy-done.4
  429.0 1.1 copy-done.6
  430.1 1.1 copy-done.7
  431.1 1.1 copy-done.8
  432.2 1.1 copy-done.9
  433.3 1.1 copy-done.10
  434.3 1.1 copy-done.11
  435.4 1.1 copy-done.12
  436.5 1.1 copy-done.13
  437.5 6.6 %widen.1 = (f32[1024,768]{1,0:T(8,128)}, f32[384,2048]{1,0:T(8,128)}, f32[384,2048]{1,0:T(8,128)}, f32[384,768]{1,0:T(8,128)}, f32[384,768]{1,0:T(8,128)}, /*ind...) custom-call(bf16[1024,768]{1,0:T(8,128)(2,1)S(1)} %copy-done.2, ...), custom_call_target="tpu_custom_call" | custom-call | tf_op jit(solution)/shard_map/widen/pallas_call | solution.py:1071
  444.1 1.5 dynamic-slice_reduce_fusion
  445.6 1.0 fusion.2
  (149 shorter events, 28.5 us)
Async XLA Ops:
  7.2 1.3 copy-start.22
  7.2 173.6 %all-gather.3.cloned.1.call-start = ((), (), s32[]{:S(2)}) async-start(), calls=%async_computation.1 | async-start | bytes 1671168 | tf_op jit(solution)/shard_map/all_gather | solution.py:1142
  8.5 5.8 %copy-start.17 = (bf16[2,384,768]{2,1,0:T(8,128)(2,1)}, bf16[2,384,768]{2,1,0:T(8,128)(2,1)S(1)}, u32[]{:S(2)}) copy-start(bf16[2,384,768]{2,1,0:T(8,128)(2,1)S(1)} %get-tuple-element.137) | copy-start | bytes 3538948
  8.6 4.8 %copy-start.23 = (f32[384,768]{1,0:T(8,128)S(1)}, f32[384,768]{1,0:T(8,128)}, u32[]{:S(2)}) copy-start(f32[384,768]{1,0:T(8,128)} %param.28) | copy-start | bytes 3538948
  9.3 64.3 %collective-permute-start.12 = (bf16[192,768]{1,0:T(8,128)(2,1)}, bf16[192,768]{1,0:T(8,128)(2,1)S(1)}, u32[]{:S(2)}, u32[]{:S(2)}) collective-permute-start(bf16[192,768]{1,0:T(8,128)(2,1)} %constant_dynamic-slice_fusion.6), channel_id=1, source_target_pairs={{0,16},{16,0},{1,17},{17,1},{2,18},{18,2},{3,19},{19,3},{4,20},{20... | collective-permute-start | bytes 884744 | tf_op jit(solution)/shard_map/ppermute | solution.py:666
  14.3 1.4 copy-start.24
  15.1 61.1 %collective-permute-start.14 = (bf16[192,768]{1,0:T(8,128)(2,1)}, bf16[192,768]{1,0:T(8,128)(2,1)}, u32[]{:S(2)}, u32[]{:S(2)}) collective-permute-start(bf16[192,768]{1,0:T(8,128)(2,1)} %constant_dynamic-slice_fusion.5), channel_id=1, source_target_pairs={{0,16},{16,0},{1,17},{17,1},{2,18},{18,2},{3,19},{19,3},{4,20},{20... | collective-permute-start | bytes 884744 | tf_op jit(solution)/shard_map/ppermute | solution.py:666
  15.1 432.1 %reduce-scatter.2.cloned.1.call-start = ((), (), s32[]{:S(2)}) async-start(), calls=%async_computation.2 | async-start | bytes 1671168 | tf_op jit(solution)/shard_map/reduce_scatter | solution.py:1270
  15.8 4.4 copy-start.16
  15.8 3.5 copy-start.25
  16.6 61.5 %collective-permute-start.4 = (bf16[192,768]{1,0:T(8,128)(2,1)}, bf16[192,768]{1,0:T(8,128)(2,1)}, u32[]{:S(2)}, u32[]{:S(2)}) collective-permute-start(bf16[192,768]{1,0:T(8,128)(2,1)} %constant_dynamic-slice_fusion.10), channel_id=1, source_target_pairs={{0,16},{16,0},{1,17},{17,1},{2,18},{18,2},{3,19},{19,3},{4,20},{20... | collective-permute-start | bytes 884744 | tf_op jit(solution)/shard_map/ppermute | solution.py:666
  20.2 2.3 copy-start.26
  20.9 60.7 %collective-permute-start.2 = (bf16[192,768]{1,0:T(8,128)(2,1)}, bf16[192,768]{1,0:T(8,128)(2,1)}, u32[]{:S(2)}, u32[]{:S(2)}) collective-permute-start(bf16[192,768]{1,0:T(8,128)(2,1)} %constant_dynamic-slice_fusion.11), channel_id=1, source_target_pairs={{0,16},{16,0},{1,17},{17,1},{2,18},{18,2},{3,19},{19,3},{4,20},{20... | collective-permute-start | bytes 884744 | tf_op jit(solution)/shard_map/ppermute | solution.py:666
  22.4 3.2 copy-start.33
  22.4 3.3 copy-start.34
  22.4 3.3 copy-start.35
  22.4 3.3 copy-start.32
  23.4 23.5 %copy-start.27 = (f32[384,768]{1,0:T(8,128)S(1)}, f32[384,768]{1,0:T(8,128)}, u32[]{:S(2)}) copy-start(f32[384,768]{1,0:T(8,128)} %param.25) | copy-start | bytes 3538948
  24.1 59.4 %collective-permute-start = (bf16[192,768]{1,0:T(8,128)(2,1)}, bf16[192,768]{1,0:T(8,128)(2,1)}, u32[]{:S(2)}, u32[]{:S(2)}) collective-permute-start(bf16[192,768]{1,0:T(8,128)(2,1)} %constant_dynamic-slice_fusion.12), channel_id=1, source_target_pairs={{0,16},{16,0},{1,17},{17,1},{2,18},{18,2},{3,19},{19,3},{4,20},{20... | collective-permute-start | bytes 884744 | tf_op jit(solution)/shard_map/ppermute | solution.py:666
  48.5 3.0 copy-start.18
  53.9 3.0 copy-start.19
  58.4 2.3 copy-start.28
  61.6 1.7 copy-start.29
  64.4 1.9 copy-start.20
  68.4 2.1 copy-start.21
  73.6 4.5 copy-start.31
  73.6 13.4 %collective-permute-start.6 = (bf16[192,768]{1,0:T(8,128)(2,1)}, bf16[192,768]{1,0:T(8,128)(2,1)S(1)}, u32[]{:S(2)}, u32[]{:S(2)}) collective-permute-start(bf16[192,768]{1,0:T(8,128)(2,1)} %constant_dynamic-slice_fusion.9), channel_id=1, source_target_pairs={{0,16},{16,0},{1,17},{17,1},{2,18},{18,2},{3,19},{19,3},{4,20},{20... | collective-permute-start | bytes 884744 | tf_op jit(solution)/shard_map/ppermute | solution.py:666
  76.1 14.0 %collective-permute-start.8 = (bf16[192,768]{1,0:T(8,128)(2,1)}, bf16[192,768]{1,0:T(8,128)(2,1)S(1)}, u32[]{:S(2)}, u32[]{:S(2)}) collective-permute-start(bf16[192,768]{1,0:T(8,128)(2,1)} %constant_dynamic-slice_fusion.8), channel_id=1, source_target_pairs={{0,16},{16,0},{1,17},{17,1},{2,18},{18,2},{3,19},{19,3},{4,20},{20... | collective-permute-start | bytes 884744 | tf_op jit(solution)/shard_map/ppermute | solution.py:666
  78.1 18.3 %collective-permute-start.10 = (bf16[192,768]{1,0:T(8,128)(2,1)S(1)}, bf16[192,768]{1,0:T(8,128)(2,1)S(1)}, u32[]{:S(2)}, u32[]{:S(2)}) collective-permute-start(bf16[192,768]{1,0:T(8,128)(2,1)S(1)} %copy-done.31), channel_id=1, source_target_pairs={{0,16},{16,0},{1,17},{17,1},{2,18},{18,2},{3,19},{19,3},{4,20},{20... | collective-permute-start | bytes 884744 | tf_op jit(solution)/shard_map/ppermute | solution.py:666
  81.6 90.8 %collective-permute-start.16 = (bf16[192,2048]{1,0:T(8,128)(2,1)}, bf16[192,2048]{1,0:T(8,128)(2,1)}, u32[]{:S(2)}, u32[]{:S(2)}) collective-permute-start(bf16[192,2048]{1,0:T(8,128)(2,1)} %constant_dynamic-slice_fusion.4), channel_id=1, source_target_pairs={{0,16},{16,0},{1,17},{17,1},{2,18},{18,2},{3,19},{19,3},{4,20},{20... | collective-permute-start | bytes 2359304 | tf_op jit(solution)/shard_map/ppermute | solution.py:666
  83.5 91.5 %collective-permute-start.18 = (bf16[192,2048]{1,0:T(8,128)(2,1)}, bf16[192,2048]{1,0:T(8,128)(2,1)}, u32[]{:S(2)}, u32[]{:S(2)}) collective-permute-start(bf16[192,2048]{1,0:T(8,128)(2,1)} %constant_dynamic-slice_fusion.3), channel_id=1, source_target_pairs={{0,16},{16,0},{1,17},{17,1},{2,18},{18,2},{3,19},{19,3},{4,20},{20... | collective-permute-start | bytes 2359304 | tf_op jit(solution)/shard_map/ppermute | solution.py:666
  87.0 85.4 %collective-permute-start.20 = (bf16[512,768]{1,0:T(8,128)(2,1)}, bf16[512,768]{1,0:T(8,128)(2,1)}, u32[]{:S(2)}, u32[]{:S(2)}) collective-permute-start(bf16[512,768]{1,0:T(8,128)(2,1)} %constant_dynamic-slice_fusion.2), channel_id=1, source_target_pairs={{0,16},{16,0},{1,17},{17,1},{2,18},{18,2},{3,19},{19,3},{4,20},{20... | collective-permute-start | bytes 2359304 | tf_op jit(solution)/shard_map/ppermute | solution.py:666
  90.1 7.1 %collective-permute-start.13 = (bf16[192,768]{1,0:T(8,128)(2,1)S(1)}, bf16[192,768]{1,0:T(8,128)(2,1)S(1)}, u32[]{:S(2)}, u32[]{:S(2)}) collective-permute-start(bf16[192,768]{1,0:T(8,128)(2,1)S(1)} %collective-permute-done.12), channel_id=1, source_target_pairs={{0,1},{1,0},{2,3},{3,2},{4,5},{5,4},{6,7},{7,6},{8,9},{9,8},{10,11... | collective-permute-start | bytes 884744 | tf_op jit(solution)/shard_map/ppermute | solution.py:667
  96.4 2.0 collective-permute-start.15
  97.2 2.0 collective-permute-start.5
  98.4 2.0 collective-permute-start.3
  99.2 2.0 collective-permute-start.1
  100.4 2.0 collective-permute-start.7
  101.2 2.0 collective-permute-start.9
  102.4 69.2 %collective-permute-start.11 = (bf16[192,768]{1,0:T(8,128)(2,1)S(1)}, bf16[192,768]{1,0:T(8,128)(2,1)S(1)}, u32[]{:S(2)}, u32[]{:S(2)}) collective-permute-start(bf16[192,768]{1,0:T(8,128)(2,1)S(1)} %collective-permute-done.10), channel_id=1, source_target_pairs={{0,1},{1,0},{2,3},{3,2},{4,5},{5,4},{6,7},{7,6},{8,9},{9,8},{10,11... | collective-permute-start | bytes 884744 | tf_op jit(solution)/shard_map/ppermute | solution.py:667
  108.2 1.3 copy-start.5
  134.4 1.4 copy-start
  151.2 1.0 copy-start.14
  171.6 5.7 %copy-start.1 = (bf16[8,192,128]{2,1,0:T(8,128)(2,1)}, bf16[8,192,128]{2,1,0:T(8,128)(2,1)S(1)}, u32[]{:S(2)}) copy-start(bf16[8,192,128]{2,1,0:T(8,128)(2,1)S(1)} %return_tokens.1) | copy-start | bytes 1179652
  172.4 6.1 %collective-permute-start.17 = (bf16[192,2048]{1,0:T(8,128)(2,1)}, bf16[192,2048]{1,0:T(8,128)(2,1)S(1)}, u32[]{:S(2)}, u32[]{:S(2)}) collective-permute-start(bf16[192,2048]{1,0:T(8,128)(2,1)} %collective-permute-done.16), channel_id=1, source_target_pairs={{0,1},{1,0},{2,3},{3,2},{4,5},{5,4},{6,7},{7,6},{8,9},{9,8},{10,11... | collective-permute-start | bytes 2359304 | tf_op jit(solution)/shard_map/ppermute | solution.py:667
  172.4 6.0 %collective-permute-start.21 = (bf16[512,768]{1,0:T(8,128)(2,1)}, bf16[512,768]{1,0:T(8,128)(2,1)S(1)}, u32[]{:S(2)}, u32[]{:S(2)}) collective-permute-start(bf16[512,768]{1,0:T(8,128)(2,1)} %collective-permute-done.20), channel_id=1, source_target_pairs={{0,1},{1,0},{2,3},{3,2},{4,5},{5,4},{6,7},{7,6},{8,9},{9,8},{10,11... | collective-permute-start | bytes 2359304 | tf_op jit(solution)/shard_map/ppermute | solution.py:667
  175.0 4.6 %collective-permute-start.19 = (bf16[192,2048]{1,0:T(8,128)(2,1)}, bf16[192,2048]{1,0:T(8,128)(2,1)S(1)}, u32[]{:S(2)}, u32[]{:S(2)}) collective-permute-start(bf16[192,2048]{1,0:T(8,128)(2,1)} %collective-permute-done.18), channel_id=1, source_target_pairs={{0,1},{1,0},{2,3},{3,2},{4,5},{5,4},{6,7},{7,6},{8,9},{9,8},{10,11... | collective-permute-start | bytes 2359304 | tf_op jit(solution)/shard_map/ppermute | solution.py:667
  178.5 2.2 copy-start.15
  424.8 1.4 copy-start.2
  426.2 1.4 copy-start.3
  427.6 1.4 copy-start.4
  429.0 1.1 copy-start.6
  430.1 1.1 copy-start.7
  431.1 1.1 copy-start.8
  432.2 1.1 copy-start.9
  433.3 1.1 copy-start.10
  434.3 1.1 copy-start.11
  435.4 1.1 copy-start.12
  436.5 1.1 copy-start.13
  437.5 9.7 %copy-start.30 = (bf16[2,128,768]{2,1,0:T(8,128)(2,1)S(1)}, bf16[2,128,768]{2,1,0:T(8,128)(2,1)}, u32[]{:S(2)}) copy-start(bf16[2,128,768]{2,1,0:T(8,128)(2,1)} %get-tuple-element.173) | copy-start | bytes 1179652
Sparse Core Ops, SparseCore 0:
  15.2 41.4 all-gather.2
  241.5 73.9 reduce-scatter.1

commit v4 on v3

--- a/solution.py
+++ b/solution.py
@@ -31,6 +31,10 @@
 
 def t_dot(a, b):
     return lax.dot_general(a, b, (((0,), (0,)), ((), ())), preferred_element_type=F32)
+
+
+def mat(ref):
+    return ref[...].reshape(-1, ref.shape[-1])
 
 
 def scale_of(v):
@@ -254,10 +258,10 @@
 def project_kernel(plan, hidden, gain, wq, wk, wv, a1_ref, send):
     p = plan
     x = hidden[...].reshape(p.S * p.T, D).astype(F32)
-    a1 = (x * scale_of(x) * gain[...]).astype(B16)
+    a1 = (x * scale_of(x) * gain[0:1, :]).astype(B16)
     a1_ref[...] = a1
     for n, weight in enumerate((wq, wk, wv)):
-        rows = dot(a1, weight[...])
+        rows = dot(a1, mat(weight))
         for s in range(p.S):
             turned = jnp.transpose(rows[s * p.T : (s + 1) * p.T]).astype(B16)
             for g in range(p.G):
@@ -266,10 +270,8 @@
 
 def bias_tiles(plan, w, line, tiles):
     p = plan
-    far = line[0:1, 2 * p.T - 1 : 2 * p.T]
-    near = pltpu.roll(
-        jnp.broadcast_to(line[0:1, :], (p.T, 2 * p.T)), 0, 1, stride=1, stride_axis=0
-    )
+    far = line[:, 2 * p.T - 1 : 2 * p.T]
+    near = pltpu.roll(jnp.broadcast_to(line, (p.T, 2 * p.T)), 0, 1, stride=1, stride_axis=0)
     key = lax.broadcasted_iota(jnp.int32, (p.T, p.T), 0)
     query = lax.broadcasted_iota(jnp.int32, (p.T, p.T), 1)
     same = jnp.where(query >= key, near[:, : p.T], HIDE)
@@ -301,37 +303,57 @@
     )
 
 
-def attend_kernel(plan, recv, lines, o_ref, of_ref, rl_ref, kn, vt, tiles):
+def line_of(p, block, head):
+    return block[pl.ds(3 + head, 1), 0 : 2 * p.T]
+
+
+def attend_head(p, w, row, line, recv, o_ref, of_ref, rl, kn, vt, tiles):
+    bias_tiles(p, w, line, tiles)
+    for r in range(p.R):
+        kn[r * p.T : (r + 1) * p.T, :] = jnp.transpose(
+            recv[r, pl.ds(p.F + row, DH), :].astype(F32)
+        ).astype(B16)
+        vt[0:DH, r * p.T : (r + 1) * p.T] = recv[r, pl.ds(2 * p.F + row, DH), :]
+    vt[DH : DH + ONES, :] = jnp.ones((ONES, p.L), B16)
+
+    def one_pair(pair, carry):
+        qt = block_pair(p, recv, pair, w, row, DH)
+
+        def step(i, acc):
+            start = pl.multiple_of(i * p.CK, p.CK)
+            e = jnp.exp(dot(kn[pl.ds(start, p.CK), :], qt) + tiles[jnp.maximum(i - pair + 2, 0)])
+            return acc + dot(vt[:, pl.ds(start, p.CK)], e.astype(B16))
+
+        acc = lax.fori_loop(0, pair + 1, step, jnp.zeros((DH + ONES, 2 * p.T), F32))
+        scale = 1.0 / acc[DH : DH + 1]
+        of = acc[:DH] * scale
+        rl[pair] = scale
+        for a in range(2):
+            part = of[:, a * p.T : (a + 1) * p.T]
+            of_ref[2 * pair + a, pl.ds(row, DH), :] = part
+            o_ref[2 * pair + a, pl.ds(row, DH), :] = part.astype(B16)
+        return carry
+
+    lax.fori_loop(0, p.NP, one_pair, 0)
+
+
+def attend_scratch(p):
+    return [
+        pltpu.VMEM((p.L, DH), B16),
+        pltpu.VMEM((DH + ONES, p.L), B16),
+        pltpu.VMEM((3, p.CK, 2 * p.T), F32),
+    ]
+
+
+def attend_kernel(plan, recv, block, o_ref, of_ref, rl_ref, *scratch):
     p = plan
     me = lax.axis_index("rep")
     w = me % p.W
     group = (me // p.W) % p.G
     h = pl.program_id(0)
     row = pl.multiple_of(h * DH, DH)
-    bias_tiles(p, w, lines.at[group * p.HG + h], tiles)
-    for r in range(p.R):
-        kn[r * p.T : (r + 1) * p.T, :] = jnp.transpose(
-            recv[r, pl.ds(p.F + row, DH), :].astype(F32)
-        ).astype(B16)
-        vt[0:DH, r * p.T : (r + 1) * p.T] = recv[r, pl.ds(2 * p.F + row, DH), :]
-    vt[DH : DH + ONES, :] = jnp.ones((ONES, p.L), B16)
-    for pair in range(p.NP):
-        qt = block_pair(p, recv, pair, w, row, DH)
-
-        def step(i, acc, pair=pair, qt=qt):
-            start = pl.multiple_of(i * p.CK, p.CK)
-            s = dot(kn[pl.ds(start, p.CK), :], qt)
-            e = jnp.exp(s + tiles[jnp.maximum(i - pair + 2, 0)])
-            return acc + dot(vt[:, pl.ds(start, p.CK)], e.astype(B16))
-
-        acc = lax.fori_loop(0, pair + 1, step, jnp.zeros((DH + ONES, 2 * p.T), F32))
-        rl = 1.0 / acc[DH : DH + 1]
-        of = acc[:DH] * rl
-        rl_ref[h, pair] = rl
-        for a in range(2):
-            part = of[:, a * p.T : (a + 1) * p.T]
-            of_ref[2 * pair + a, pl.ds(row, DH), :] = part
-            o_ref[2 * pair + a, pl.ds(row, DH), :] = part.astype(B16)
+    line = line_of(p, block, group * p.HG + h)
+    attend_head(p, w, row, line, recv, o_ref, of_ref, rl_ref.at[h], *scratch)
 
 
 def back_head(
@@ -425,7 +447,7 @@
     ]
 
 
-def attend_back_kernel(plan, recv, lines, dout, of_ref, rl_ref, dq_ref, dkv_ref, line_ref, *scratch):
+def attend_back_kernel(plan, recv, block, dout, of_ref, rl_ref, dq_ref, dkv_ref, line_ref, *scratch):
     p = plan
     me = lax.axis_index("rep")
     w = me % p.W
@@ -436,7 +458,7 @@
         p,
         w,
         row,
-        lines.at[group * p.HG + h],
+        line_of(p, block, group * p.HG + h),
         recv,
         dout,
         of_ref,
@@ -448,33 +470,58 @@
 
 
 def encode_kernel(enc, wk, wv, kn, kt, vn, vt):
-    rows = enc.shape[0]
-    for weight, natural, turned in ((wk, kn, kt), (wv, vn, vt)):
-        value = dot(enc[...], weight[...])
-        for h in range(H):
-            natural[h] = value[:, h * DH : (h + 1) * DH].astype(B16)
-        flipped = jnp.transpose(value).astype(B16)
-        for h in range(H):
-            turned[h, 0:DH, :] = flipped[h * DH : (h + 1) * DH]
-            turned[h, DH : DH + ONES, :] = jnp.ones((ONES, rows), B16)
+    encode_one(enc, wk, kn, kt)
+    encode_one(enc, wv, vn, vt)
+
+
+def encode_one(enc, weight, natural, turned):
+    rows = turned.shape[2]
+    value = dot(mat(enc), mat(weight))
+    for h in range(H):
+        natural[h] = value[:, h * DH : (h + 1) * DH].astype(B16)
+    flipped = jnp.transpose(value).astype(B16)
+    for h in range(H):
+        turned[h, 0:DH, :] = flipped[h * DH : (h + 1) * DH]
+        turned[h, DH : DH + ONES, :] = jnp.ones((ONES, rows), B16)
+
+
+def rows_of(units, s, seqs):
+    groups = units.shape[0] // seqs
+    return units[s * groups : (s + 1) * groups].reshape(-1, units.shape[-1])
 
 
 def cross_kernel(
-    seqs, hidden, ot, wo, gain, wcq, wco, kn, vt, x1_ref, x2_ref, a2_ref, qt_ref, of_ref, rl_ref
+    seqs,
+    hidden,
+    ot,
+    wo,
+    gain,
+    wcq,
+    wco,
+    kn,
+    vt,
+    x1_ref,
+    x2_ref,
+    a2_ref,
+    qt_ref,
+    of_ref,
+    rl_ref,
+    pause=lambda: None,
 ):
     toks = hidden.shape[1]
     span = kn.shape[1] // seqs
     x = hidden[...].reshape(seqs * toks, D).astype(F32)
     o = jnp.concatenate(
-        [jnp.transpose(ot[s].astype(F32)) for s in range(seqs)], axis=0
+        [jnp.transpose(rows_of(ot, s, seqs).astype(F32)) for s in range(seqs)], axis=0
     ).astype(B16)
-    x1 = x + dot(o, wo[...])
+    x1 = x + dot(o, mat(wo))
     x1_ref[...] = x1
-    a2 = (x1 * scale_of(x1) * gain[...]).astype(B16)
+    a2 = (x1 * scale_of(x1) * gain[1:2, :]).astype(B16)
     a2_ref[...] = a2
-    q2 = dot(a2, wcq[...])
+    q2 = dot(a2, mat(wcq))
     for s in range(seqs):
         qt_ref[s] = jnp.transpose(q2[s * toks : (s + 1) * toks]).astype(B16)
+    pause()
 
     def heads(i, carry):
         for sub in range(2):
@@ -490,8 +537,9 @@
         return carry
 
     lax.fori_loop(0, H // 2, heads, 0)
+    pause()
     o2 = jnp.concatenate([jnp.transpose(of_ref[s]) for s in range(seqs)], axis=0).astype(B16)
-    x2_ref[...] = x1 + dot(o2, wco[...])
+    x2_ref[...] = x1_ref[...] + dot(o2, mat(wco))
 
 
 def ffn_kernel(
@@ -502,7 +550,7 @@
     @pl.when(step == 0)
     def _():
         x2 = x2_ref[...]
-        a3[...] = (x2 * scale_of(x2) * gain[...]).astype(B16)
+        a3[...] = (x2 * scale_of(x2) * gain[2:3, :]).astype(B16)
         acc[...] = x2
         da3[...] = jnp.zeros_like(da3)
 
@@ -528,7 +576,7 @@
     @pl.when(step == pl.num_programs(0) - 1)
     def _():
         out_ref[...] = acc[...].astype(B16)
-        dv, dgain = norm_back(x2_ref[...], gain[...], da3[...])
+        dv, dgain = norm_back(x2_ref[...], gain[2:3, :], da3[...])
         dx2_ref[...] = og_ref[...].astype(F32) + dv
         dgain_ref[...] = dgain
 
@@ -576,7 +624,7 @@
     for s in range(1, seqs):
         total = total + dot(o2t[s], dc[s * toks : (s + 1) * toks])
     dwco[...] = total.astype(B16)
-    do2 = dot_t(dc, wco[...])
+    do2 = dot_t(dc, mat(wco))
     for s in range(seqs):
         dt[s] = jnp.transpose(do2[s * toks : (s + 1) * toks]).astype(B16)
 
@@ -604,23 +652,23 @@
         return carry
 
     lax.fori_loop(0, H // 2, heads, 0)
-    dwck[...] = t_dot(enc[...], dk[...]).astype(B16)
-    dwcv[...] = t_dot(enc[...], dv[...]).astype(B16)
-    denc_ref[...] = (dot_t(dk[...], wck[...]) + dot_t(dv[...], wcv[...])).astype(B16)
+    dwck[...] = t_dot(mat(enc), dk[...]).astype(B16)
+    dwcv[...] = t_dot(mat(enc), dv[...]).astype(B16)
+    denc_ref[...] = (dot_t(dk[...], mat(wck)) + dot_t(dv[...], mat(wcv))).astype(B16)
     dq2 = jnp.concatenate(
         [jnp.transpose(dqt[s].astype(F32)) for s in range(seqs)], axis=0
     ).astype(B16)
     dwcq[...] = t_dot(a2_ref[...], dq2).astype(B16)
-    term, dgain = norm_back(x1_ref[...], gain[...], dot_t(dq2, wcq[...]))
+    term, dgain = norm_back(x1_ref[...], gain[1:2, :], dot_t(dq2, mat(wcq)))
     dgain_ref[...] = dgain
     dx1 = dx2 + term
     dx1_ref[...] = dx1
     db = dx1.astype(B16)
-    total = dot(ot[0], db[0:toks])
+    total = dot(rows_of(ot, 0, seqs), db[0:toks])
     for s in range(1, seqs):
-        total = total + dot(ot[s], db[s * toks : (s + 1) * toks])
+        total = total + dot(rows_of(ot, s, seqs), db[s * toks : (s + 1) * toks])
     dwo[...] = total.astype(B16)
-    do = dot_t(db, wo[...])
+    do = dot_t(db, mat(wo))
     width = D // groups
     for s in range(seqs):
         turned = jnp.transpose(do[s * toks : (s + 1) * toks]).astype(B16)
@@ -646,8 +694,8 @@
             rows.append(jnp.transpose(turned.astype(F32)))
         d = jnp.concatenate(rows, axis=0).astype(B16)
         dw[...] = t_dot(a1[...], d).astype(B16).reshape(dw.shape)
-        da1 = da1 + dot_t(d, weight[...])
-    term, dgain = norm_back(x, gain[...], da1)
+        da1 = da1 + dot_t(d, mat(weight))
+    term, dgain = norm_back(x, gain[0:1, :], da1)
     dh_ref[...] = (dx1[...] + term).astype(B16).reshape(dh_ref.shape)
     return dgain
 
@@ -889,7 +937,7 @@
     take = lambda n: [refs.pop(0) for _ in range(n)]
     sources = take(early)
     (dot_,) = take(1)
-    recv, lines, of_ref, rl_ref, hidden, a1, gain, dx1, dgc, dgf, wq, wk, wv = take(13)
+    recv, lines, of_ref, rl_ref, hidden, a1, dx1, dgc, dgf, wq, wk, wv = take(12)
     results = take(arrays)
     small, dh_ref = take(2)
     dout, dq, dkv, part, out, grads = take(6)
@@ -945,7 +993,7 @@
             p,
             w,
             h * DH,
-            lines.at[group * p.HG + h],
+            line_of(p, lines, group * p.HG + h),
             recv,
             dout,
             of_ref,
@@ -984,7 +1032,7 @@
     tick(2)
     for u in range(p.U):
         landed(grads.at[u], ret_recv.at[u])
-    dgain = last_products(p, hidden, grads, a1, gain, dx1, wq, wk, wv, dh_ref, *late)
+    dgain = last_products(p, hidden, grads, a1, lines, dx1, wq, wk, wv, dh_ref, *late)
     for i, row in enumerate((dgain, dgc[...], dgf[...])):
         block = jnp.where(lines_at == i, row, block)
     small_sums[0] = block
@@ -1079,6 +1127,336 @@
     )(*mats)
 
 
+class Fetch:
+    def __init__(self, master, held, staged, out, first, rows, col, cols, stage, own, sems, index):
+        self.x = lax.axis_index("shard")
+        self.core = lax.axis_index("rep") % 2
+        self.rows, self.staged = rows, staged
+        self.master = master.at[pl.ds(first, rows), pl.ds(col, cols)]
+        self.stage_ref = stage.at[pl.ds(0, rows), pl.ds(0, cols)]
+        self.own = own
+        self.out, self.first, self.col, self.cols = out, first, col, cols
+        load, send, recv, relay_send, relay_recv, keep = sems
+        self.load, self.keep = load.at[index], keep.at[index]
+        self.send, self.recv = send.at[index], recv.at[index]
+        self.relay_send, self.relay_recv = relay_send.at[index], relay_recv.at[index]
+
+    def place(self, owner, core):
+        half = self.rows // 2
+        first = pl.multiple_of(self.first + core * half, 16)
+        return self.out.at[owner, pl.ds(first, half), pl.ds(self.col, self.cols)]
+
+    def read(self):
+        pltpu.make_async_copy(self.master, self.stage_ref, self.load).start()
+
+    def kept(self):
+        return self.out.at[self.x, pl.ds(self.first, self.rows), pl.ds(self.col, self.cols)]
+
+    def across(self):
+        half = self.rows // 2
+        first = pl.multiple_of(self.core * half, 16)
+        return to_row(self.own.at[pl.ds(first, half)], self.place(self.x, self.core), self.send, self.recv)
+
+    def start(self):
+        landed(self.stage_ref, self.load)
+        step = 32
+
+        def body(i, carry):
+            at = pl.ds(pl.multiple_of(i * step, step), step)
+            self.own[at, :] = self.stage_ref[at, :].astype(B16)
+            return carry
+
+        lax.fori_loop(0, self.rows // step, body, 0)
+        self.across().start()
+        if self.staged:
+            pltpu.make_async_copy(self.own, self.kept(), self.keep).start()
+
+    def over(self):
+        place = self.place(1 - self.x, self.core)
+        return to_rep(place, place, self.relay_send, self.relay_recv, 0)
+
+    def relay(self):
+        landed(self.place(1 - self.x, self.core), self.recv)
+        self.over().start()
+
+    def finish(self):
+        landed(self.place(1 - self.x, 1 - self.core), self.relay_recv)
+
+    def end(self):
+        self.across().wait_send()
+        self.over().wait_send()
+        if self.staged:
+            landed(self.kept(), self.keep)
+
+
+def small_block(p, gains, table, buckets, x):
+    at = lax.broadcasted_iota(jnp.int32, (SMALL_ROWS, D), 0)
+    block = jnp.zeros((SMALL_ROWS, D), F32)
+    for i, gain in enumerate(gains):
+        part = gain[...].astype(B16).astype(F32)
+        none = jnp.zeros_like(part)
+        row = jnp.where(
+            x == 0,
+            jnp.concatenate([part, none], axis=1),
+            jnp.concatenate([none, part], axis=1),
+        )
+        block = jnp.where(at == i, row, block)
+    held = table.shape[0]
+    bucket = lax.broadcasted_iota(jnp.int32, (held, 2 * p.T), 0) + x * held
+    onehot = (buckets[...] == bucket).astype(F32).astype(B16)
+    lines = t_dot(table[...].astype(B16), onehot)
+    lines = jnp.concatenate([lines, jnp.zeros((H, D - 2 * p.T), F32)], axis=1)
+    lines = jnp.concatenate(
+        [jnp.zeros((3, D), F32), lines, jnp.zeros((SMALL_ROWS - 3 - H, D), F32)], axis=0
+    )
+    return block + lines
+
+
+def head_kernel(p, *refs):
+    refs = list(refs)
+    take = lambda n: [refs.pop(0) for _ in range(n)]
+    masters = take(11)
+    hidden, encoded, g1, g2, g3, table, buckets = take(7)
+    mats = take(8)
+    wide = take(3)
+    small, a1, recv, of_ref, rl_ref, enc, kn, kt, vn, vt, ot = take(11)
+    x1, x2, a2, qt2, of2, rl2 = take(6)
+    send, o_ref, mine_small, their_small = take(4)
+    stages = take(4)
+    owns = take(6)
+    att = take(3)
+    fetch_sems = take(6)
+    small_send, small_recv, enc_send, enc_recv = take(4)
+    tok_send, relay_sem, tok_recv, back_send, back_recv = take(5)
+
+    me = lax.axis_index("rep")
+    x = lax.axis_index("shard")
+    w = me % p.W
+    unit = me // p.W
+    group = unit % p.G
+    mine = p.worker_of(me)
+    bits = [(me // 2**b) % 2 for b in range(BITS)]
+
+    half = D // 2
+    jobs = []
+    for i in range(8):
+        jobs.append((masters[i], mats[i], 0, half, 0, D))
+    for i, ref in enumerate(wide):
+        rows, cols = ref.shape[1:]
+        tall = rows // 2 if rows > 512 else rows
+        part = cols // 2 if cols > 1024 else cols
+        for row in range(0, rows, tall):
+            for col in range(0, cols, part):
+                jobs.append((masters[8 + i], ref, row, tall, col, part))
+    fetches = []
+    for i, (master, out, row, rows, col, cols) in enumerate(jobs):
+        staged = i >= 8
+        own = owns[i - 8] if staged else out.at[x]
+        fetches.append(
+            Fetch(
+                master, out, staged, out, row, rows, col, cols, stages[i % 4], own, fetch_sems, i
+            )
+        )
+
+    barrier = pltpu.get_barrier_semaphore()
+    for k in range(1, p.R):
+        pl.semaphore_signal(
+            barrier, inc=1, device_id={"rep": (me + k) % p.R}, device_id_type=MESH
+        )
+    pl.semaphore_signal(barrier, inc=1, device_id={"shard": 1 - x}, device_id_type=MESH)
+    for fetch in fetches[:4]:
+        fetch.read()
+    mine_small[...] = small_block(p, (g1, g2, g3), table, buckets, x)
+    enc[:, bits[3], bits[2], bits[1], bits[0]] = encoded[...]
+    pl.semaphore_wait(barrier, p.R)
+
+    share = to_row(mine_small, their_small, small_send, small_recv)
+    share.start()
+
+    def enc_copy(n):
+        at = (slice(None),) * (1 + n) + tuple(bits[b] for b in range(BITS - 1 - n, -1, -1))
+        part = enc.at[at]
+        return to_rep(part, part, enc_send.at[n], enc_recv.at[n], BITS - 1 - n)
+
+    def enc_landed(n):
+        b = [bits[i] for i in range(BITS - 1 - n, -1, -1)]
+        b[0] = 1 - b[0]
+        landed(enc.at[(slice(None),) * (1 + n) + tuple(b)], enc_recv.at[n])
+
+    started = 0
+    relayed = 0
+
+    def begin(count=1):
+        nonlocal started
+        for _ in range(count):
+            if started < len(fetches):
+                fetches[started].start()
+                if started + 4 < len(fetches):
+                    fetches[started + 4].read()
+                started += 1
+
+    def pass_on(count=1):
+        nonlocal relayed
+        for _ in range(count):
+            if relayed < started:
+                fetches[relayed].relay()
+                relayed += 1
+
+    begin(3)
+    enc_copy(0).start()
+    landed(their_small, small_recv)
+    small[...] = mine_small[...] + their_small[...]
+    enc_landed(0)
+    enc_copy(1).start()
+    pass_on()
+    begin()
+    enc_landed(1)
+    enc_copy(2).start()
+    pass_on()
+    begin()
+    pass_on()
+    for fetch in fetches[:3]:
+        fetch.finish()
+    project_kernel(p, hidden, small, *mats[:3], a1, send)
+    for u in range(p.U):
+        start_either(
+            me, u * p.W + mine, send.at[u], recv.at[me], tok_send.at[u], tok_recv.at[me]
+        )
+    enc_landed(2)
+    enc_copy(3).start()
+    begin()
+    pass_on(2)
+    enc_landed(3)
+    for fetch, natural, turned in ((fetches[3], kn, kt), (fetches[4], vn, vt)):
+        fetch.finish()
+        encode_one(enc, fetch.out, natural, turned)
+        begin()
+        pass_on()
+
+    def relay(k, j):
+        part = recv.at[p.source(j, w), pl.ds(p.F, 2 * p.F)]
+        to = me - w + (w + k) % p.W
+        return remote(part, part, relay_sem.at[k - 1, j], tok_recv.at[p.source(j, w)], to)
+
+    for j in range(p.J):
+        landed(recv.at[p.source(j, w)], tok_recv.at[p.source(j, w)])
+        for k in range(1, p.W):
+            relay(k, j).start()
+    begin()
+    pass_on()
+    for k in range(1, p.W):
+        for j in range(p.J):
+            r = p.source(j, (w + k) % p.W)
+            landed(recv.at[r, pl.ds(p.F, 2 * p.F)], tok_recv.at[r])
+    for h in range(p.HG):
+        line = line_of(p, small, group * p.HG + h)
+        attend_head(p, w, h * DH, line, recv, o_ref, of_ref, rl_ref.at[h], *att)
+        begin()
+        pass_on()
+    for j in range(p.J):
+        r = p.source(j, w)
+        start_either(me, r, o_ref.at[j], ot.at[unit], back_send.at[j], back_recv.at[unit])
+    begin()
+    pass_on(2)
+    for u in range(p.U):
+        landed(ot.at[u], back_recv.at[u])
+    for fetch in fetches[5:8]:
+        fetch.finish()
+
+    def pause():
+        begin()
+        pass_on()
+
+    cross_kernel(
+        p.S, hidden, ot, mats[5], small, mats[6], mats[7], kn, vt, x1, x2, a2, qt2, of2, rl2, pause
+    )
+    begin(len(fetches))
+    pass_on(len(fetches))
+    for fetch in fetches[8:]:
+        fetch.finish()
+    for fetch in fetches:
+        fetch.end()
+    share.wait_send()
+    for n in range(BITS):
+        enc_copy(n).wait_send()
+    for u in range(p.U):
+        end_either(
+            me, u * p.W + mine, send.at[u], recv.at[me], tok_send.at[u], tok_recv.at[me]
+        )
+    for j in range(p.J):
+        r = p.source(j, w)
+        end_either(me, r, o_ref.at[j], ot.at[unit], back_send.at[j], back_recv.at[unit])
+        for k in range(1, p.W):
+            relay(k, j).wait_send()
+
+
+def head_call(p, masters, hidden, encoded, gains, table, buckets, collective):
+    half, tokens = D // 2, p.S * p.T
+    piece = encoded.shape[1]
+    enc_rows = p.S * piece * p.R
+    wides = [m.shape for m in masters[8:]]
+    near = pl.BlockSpec(memory_space=pltpu.VMEM)
+    anywhere = pl.BlockSpec(memory_space=pl.ANY)
+    outs = [((2, half, D), B16)] * 8 + [((2, *s), B16) for s in wides]
+    outs += [
+        ((SMALL_ROWS, D), F32),
+        ((tokens, D), B16),
+        ((p.R, 3 * p.F, p.T), B16),
+        ((p.J, p.F, p.T), F32),
+        ((p.HG, p.NP, 1, 2 * p.T), F32),
+        ((p.S,) + (2,) * BITS + (piece, D), B16),
+        ((H, enc_rows, DH), B16),
+        ((H, DH + ONES, enc_rows), B16),
+        ((H, enc_rows, DH), B16),
+        ((H, DH + ONES, enc_rows), B16),
+        ((p.U, p.F, p.T), B16),
+        ((tokens, D), F32),
+        ((tokens, D), F32),
+        ((tokens, D), B16),
+        ((p.S, D, p.T), B16),
+        ((p.S, D, p.T), F32),
+        ((p.S, H, 1, p.T), F32),
+    ]
+    parts = [(half, D)] * 8
+    for rows, cols in wides:
+        tall = rows // 2 if rows > 512 else rows
+        part = cols // 2 if cols > 1024 else cols
+        parts += [(tall, part)] * ((rows // tall) * (cols // part))
+    count = len(parts)
+    dma = pltpu.SemaphoreType.DMA
+    scratch = [
+        pltpu.VMEM((p.U, 3 * p.F, p.T), B16),
+        pltpu.VMEM((p.J, p.F, p.T), B16),
+        pltpu.VMEM((SMALL_ROWS, D), F32),
+        pltpu.VMEM((SMALL_ROWS, D), F32),
+    ]
+    tallest = max(r for r, _ in parts)
+    widest = max(c for _, c in parts)
+    scratch += [pltpu.VMEM((tallest, widest), F32)] * 4
+    scratch += [pltpu.VMEM(s, B16) for s in parts[8:]]
+    scratch += attend_scratch(p)
+    scratch += [dma((count,))] * 6
+    scratch += [dma, dma, dma((BITS,)), dma((BITS,))]
+    scratch += [
+        dma((p.U,)),
+        dma((max(p.W - 1, 1), p.J)),
+        dma((p.R,)),
+        dma((p.J,)),
+        dma((p.U,)),
+    ]
+    return pl.pallas_call(
+        functools.partial(head_kernel, p),
+        out_shape=[jax.ShapeDtypeStruct(s, t) for s, t in outs],
+        in_specs=[anywhere] * 11 + [near] * 7,
+        out_specs=[near] * 8 + [anywhere] * 3 + [near] * 17,
+        scratch_shapes=scratch,
+        compiler_params=pltpu.CompilerParams(
+            collective_id=collective, has_side_effects=True, vmem_limit_bytes=62 * 2**20
+        ),
+        name="head",
+    )(*masters, hidden, encoded, *gains, table, buckets)
+
+
 def local(
     hidden,
     encoded,
@@ -1107,109 +1485,133 @@
     enc_rows = seqs * encoded.shape[1] * p.R
     dma = pltpu.SemaphoreType.DMA
 
-    small = jnp.concatenate(
-        [
-            jnp.stack([gain_self, gain_cross, gain_ffn]).reshape(-1),
-            bias_table.reshape(-1),
-        ]
-    ).astype(B16)
-    small = lax.all_gather(small, "shard", axis=0)
+    n_shard = lax.axis_size("shard")
+    mine = lax.axis_index("shard")
     part = gain_self.shape[0]
-    gains = [
-        small[:, i * part : (i + 1) * part].reshape(1, D).astype(F32) for i in range(3)
-    ]
-    table = small[:, 3 * part :].reshape(NB, H)
     near = buckets[: 2 * toks]
     onehot = (near[:, None] == jnp.arange(NB, dtype=jnp.int32)[None, :]).astype(B16)
-    lines = jnp.einsum("lb,bh->hl", onehot, table, preferred_element_type=F32)[:, None, :]
-
-    wq, wk, wv, wo, wcq, wck, wcv, wco, wg, wu, wd = [
-        gather_rows(m.astype(B16))
-        for m in (
+    paired = n_shard == 2 and p.R == 2**BITS and 3 + H <= SMALL_ROWS
+    if paired:
+        masters = (
             self_query,
             self_key,
             self_value,
+            cross_key,
+            cross_value,
             self_out,
             cross_query,
-            cross_key,
-            cross_value,
             cross_out,
             ffn_gate,
             ffn_up,
             ffn_down,
         )
-    ]
-    enc = lax.all_gather(encoded, "rep", axis=1, tiled=True).reshape(enc_rows, D)
-
-    a1, send = plain_call(
-        functools.partial(project_kernel, p),
-        [((tokens, D), B16), ((p.U, 3 * p.F, toks), B16)],
-        (hidden, gains[0], wq, wk, wv),
-        "project",
-    )
-    recv = comm_call(
-        functools.partial(scatter_tokens, p),
-        (p.R, 3 * p.F, toks),
-        (send,),
-        [dma((p.U,)), dma((max(p.W - 1, 1), p.J)), dma((p.R,))],
-        0,
-        "scatter_tokens",
-    )
-    ckn, ckt, cvn, cvt = plain_call(
-        encode_kernel,
-        [
-            ((H, enc_rows, DH), B16),
-            ((H, DH + ONES, enc_rows), B16),
-            ((H, enc_rows, DH), B16),
-            ((H, DH + ONES, enc_rows), B16),
-        ],
-        (enc, wck, wcv),
-        "encode",
-    )
-    o, of, rl = pl.pallas_call(
-        functools.partial(attend_kernel, p),
-        grid=(p.HG,),
-        out_shape=[
-            jax.ShapeDtypeStruct((p.J, p.F, toks), B16),
-            jax.ShapeDtypeStruct((p.J, p.F, toks), F32),
-            jax.ShapeDtypeStruct((p.HG, p.NP, 1, 2 * toks), F32),
-        ],
-        in_specs=[whole((p.R, 3 * p.F, toks)), whole((H, 1, 2 * toks))],
-        out_specs=[
-            whole((p.J, p.F, toks)),
-            whole((p.J, p.F, toks)),
-            whole((p.HG, p.NP, 1, 2 * toks)),
-        ],
-        scratch_shapes=[
-            pltpu.VMEM((p.L, DH), B16),
-            pltpu.VMEM((DH + ONES, p.L), B16),
-            pltpu.VMEM((3, p.CK, 2 * toks), F32),
-        ],
-        compiler_params=pltpu.CompilerParams(vmem_limit_bytes=56 * 2**20),
-        name="attend",
-    )(recv, lines)
-    ot = comm_call(
-        functools.partial(return_tokens, p),
-        (p.U, p.F, toks),
-        (o,),
-        [dma((p.J,)), dma((p.U,))],
-        1,
-        "return_tokens",
-    ).reshape(seqs, D, toks)
-
-    x1, x2, a2, qt2, of2, rl2 = plain_call(
-        functools.partial(cross_kernel, seqs),
-        [
-            ((tokens, D), F32),
-            ((tokens, D), F32),
-            ((tokens, D), B16),
-            ((seqs, D, toks), B16),
-            ((seqs, D, toks), F32),
-            ((seqs, H, 1, toks), F32),
-        ],
-        (hidden, ot, wo, gains[1], wcq, wco, ckn, cvt),
-        "cross",
-    )
+        gains = [g.reshape(1, part) for g in (gain_self, gain_cross, gain_ffn)]
+        got = head_call(
+            p, masters, hidden, encoded, gains, bias_table, near.reshape(1, -1), 0
+        )
+        wq, wk, wv, wck, wcv, wo, wcq, wco = got[:8]
+        wg, wu, wd = [g.reshape(-1, g.shape[-1]) for g in got[8:11]]
+        small, a1, recv, of, rl, enc, ckn, ckt, cvn, cvt, ot = got[11:22]
+        x1, x2, a2, qt2, of2, rl2 = got[22:]
+    else:
+        lot = jnp.concatenate(
+            [
+                jnp.stack([gain_self, gain_cross, gain_ffn]).reshape(-1),
+                bias_table.reshape(-1),
+            ]
+        ).astype(B16)
+        lot = lax.all_gather(lot, "shard", axis=0)
+        gains = [
+            lot[:, i * part : (i + 1) * part].reshape(1, D).astype(F32) for i in range(3)
+        ]
+        table = lot[:, 3 * part :].reshape(NB, H)
+        lines = jnp.einsum("lb,bh->hl", onehot, table, preferred_element_type=F32)
+        lines = jnp.pad(lines, ((0, SMALL_ROWS - 3 - H), (0, D - 2 * toks)))
+        small = jnp.concatenate([*gains, lines], axis=0)
+
+        wq, wk, wv, wo, wcq, wck, wcv, wco, wg, wu, wd = [
+            gather_rows(m.astype(B16))
+            for m in (
+                self_query,
+                self_key,
+                self_value,
+                self_out,
+                cross_query,
+                cross_key,
+                cross_value,
+                cross_out,
+                ffn_gate,
+                ffn_up,
+                ffn_down,
+            )
+        ]
+        enc = lax.all_gather(encoded, "rep", axis=1, tiled=True).reshape(enc_rows, D)
+
+        a1, send = plain_call(
+            functools.partial(project_kernel, p),
+            [((tokens, D), B16), ((p.U, 3 * p.F, toks), B16)],
+            (hidden, small, wq, wk, wv),
+            "project",
+        )
+        recv = comm_call(
+            functools.partial(scatter_tokens, p),
+            (p.R, 3 * p.F, toks),
+            (send,),
+            [dma((p.U,)), dma((max(p.W - 1, 1), p.J)), dma((p.R,))],
+            0,
+            "scatter_tokens",
+        )
+        ckn, ckt, cvn, cvt = plain_call(
+            encode_kernel,
+            [
+                ((H, enc_rows, DH), B16),
+                ((H, DH + ONES, enc_rows), B16),
+                ((H, enc_rows, DH), B16),
+                ((H, DH + ONES, enc_rows), B16),
+            ],
+            (enc, wck, wcv),
+            "encode",
+        )
+        o, of, rl = pl.pallas_call(
+            functools.partial(attend_kernel, p),
+            grid=(p.HG,),
+            out_shape=[
+                jax.ShapeDtypeStruct((p.J, p.F, toks), B16),
+                jax.ShapeDtypeStruct((p.J, p.F, toks), F32),
+                jax.ShapeDtypeStruct((p.HG, p.NP, 1, 2 * toks), F32),
+            ],
+            in_specs=[whole((p.R, 3 * p.F, toks)), whole((SMALL_ROWS, D))],
+            out_specs=[
+                whole((p.J, p.F, toks)),
+                whole((p.J, p.F, toks)),
+                whole((p.HG, p.NP, 1, 2 * toks)),
+            ],
+            scratch_shapes=attend_scratch(p),
+            compiler_params=pltpu.CompilerParams(vmem_limit_bytes=56 * 2**20),
+            name="attend",
+        )(recv, small)
+        ot = comm_call(
+            functools.partial(return_tokens, p),
+            (p.U, p.F, toks),
+            (o,),
+            [dma((p.J,)), dma((p.U,))],
+            1,
+            "return_tokens",
+        )
+
+        x1, x2, a2, qt2, of2, rl2 = plain_call(
+            functools.partial(cross_kernel, seqs),
+            [
+                ((tokens, D), F32),
+                ((tokens, D), F32),
+                ((tokens, D), B16),
+                ((seqs, D, toks), B16),
+                ((seqs, D, toks), F32),
+                ((seqs, H, 1, toks), F32),
+            ],
+            (hidden, ot, wo, small, wcq, wco, ckn, cvt),
+            "cross",
+        )
 
     chunk = min(512, ff)
     const = lambda s: pl.BlockSpec(s, lambda i: (0, 0))
@@ -1227,7 +1629,7 @@
         in_specs=[
             const((tokens, D)),
             const((tokens, D)),
-            const((1, D)),
+            const((SMALL_ROWS, D)),
             pl.BlockSpec((D, chunk), lambda i: (0, i)),
             pl.BlockSpec((D, chunk), lambda i: (0, i)),
             pl.BlockSpec((chunk, D), lambda i: (i, 0)),
@@ -1247,7 +1649,7 @@
         ],
         compiler_params=pltpu.CompilerParams(vmem_limit_bytes=56 * 2**20),
         name="ffn",
-    )(x2, out_grad.reshape(tokens, D), gains[2], wg, wu, wd)
+    )(x2, out_grad.reshape(tokens, D), small, wg, wu, wd)
 
     dx1, dg_cross, dot_, denc, dwco, dwcq, dwck, dwcv, dwo = plain_call(
         functools.partial(cross_back_kernel, seqs, p.G),
@@ -1258,7 +1660,7 @@
             ((enc_rows, D), B16),
         ]
         + [((D, D), B16)] * 5,
-        (dx2, x1, a2, gains[1], qt2, of2, rl2, ckn, ckt, cvn, enc, wco, wcq, wck, wcv, wo, ot),
+        (dx2, x1, a2, small, qt2, of2, rl2, ckn, ckt, cvn, enc, wco, wcq, wck, wcv, wo, ot),
         "cross_back",
         scratch=[
             pltpu.VMEM((seqs, D, toks), B16),
@@ -1270,14 +1672,12 @@
     encoded_grad = lax.psum_scatter(
         denc.reshape(seqs, enc_rows // seqs, D), "rep", scatter_dimension=1, tiled=True
     )
-    n_shard = lax.axis_size("shard")
-    mine = lax.axis_index("shard")
-    if n_shard == 2 and p.R == 2**BITS and 3 + H <= SMALL_ROWS:
+    if paired:
         early = [
             g.reshape(2, g.shape[0] // 2, g.shape[1])
             for g in (dwd, dwg, dwu, dwo, dwcq, dwck, dwcv, dwco)
         ]
-        held = (recv, lines, of, rl, hidden, a1, gains[0], dx1, dg_cross, dg_ffn, wq, wk, wv)
+        held = (recv, small, of, rl, hidden, a1, dx1, dg_cross, dg_ffn, wq, wk, wv)
         sums, block, hidden_grad = tail_call(p, early, dot_, held, hidden, 2)
         dwd, dwg, dwu, dwo, dwcq, dwck, dwcv, dwco, dwq, dwk, dwv = widen(sums)
         mats = [dwq, dwk, dwv, dwo, dwcq, dwck, dwcv, dwco, dwg, dwu, dwd]
@@ -1310,7 +1710,7 @@
             ],
             in_specs=[
                 whole((p.R, 3 * p.F, toks)),
-                whole((H, 1, 2 * toks)),
+                whole((SMALL_ROWS, D)),
                 whole((p.J, p.F, toks)),
                 whole((p.J, p.F, toks)),
                 whole((p.HG, p.NP, 1, 2 * toks)),
@@ -1323,7 +1723,7 @@
             scratch_shapes=back_scratch(p),
             compiler_params=pltpu.CompilerParams(vmem_limit_bytes=56 * 2**20),
             name="attend_back",
-        )(recv, lines, dout, of, rl)
+        )(recv, small, dout, of, rl)
         grads = comm_call(
             functools.partial(return_grads, p),
             (p.U, 3 * p.F, toks),
@@ -1343,7 +1743,7 @@
         hidden_grad, dg_self, dwq, dwk, dwv = plain_call(
             functools.partial(last_kernel, p),
             [(hidden.shape, B16), ((1, D), F32)] + [((D, D), B16)] * 3,
-            (hidden, grads, a1, gains[0], dx1, wq, wk, wv),
+            (hidden, grads, a1, small, dx1, wq, wk, wv),
             "last",
         )
 

time: 463 us -> 394 us (0.85); the launches traced: 455 us -> 393 us
  local copies, waits for them, and re-layouts: 72.8 us -> 20.6 us
  Pallas kernels: 315 us -> 357 us
  blocking collectives: 19 us -> 0 us
  starting transfers between devices: 14.8 us -> 0.04 us
  other arithmetic: 10.1 us -> 0 us
  waiting for transfers between devices: 7.81 us -> 0.02 us
    pallas_call x3 -> x1, Pallas kernels: 59.7 us -> 132 us  [head_call(): pl.pallas_call(functools.partial(head_kernel, p), out_shape=[jax.ShapeDty...]
    pallas_call x4 -> x1, Pallas kernels: 50.7 us -> 24.2 us  [plain_call(): pl.pallas_call(kernel, out_shape=[jax.ShapeDtypeStruct(s, t) for s, t in...]
    dynamic_update_slice x22 -> x0, local copies, waits for them, and re-layouts: 23.4 us -> none  [the longest x11 15.2 us: gather_rows(): full = lax.dynamic_update_slice(full, got[None], (owner, core * half, 0))]
    all_gather x1 -> x0, blocking collectives: 19 us -> none  [local(): small = lax.all_gather(small, 'shard', axis=0)]
    ppermute x22 -> x0, starting transfers between devices: 14.7 us -> none  [the longest x11 12.6 us: gather_rows(): lax.ppermute(own, 'shard', [(i, (i + k) % count) for i in range(count)])]
    unnamed x78 -> x27, local copies, waits for them, and re-layouts: 24.8 us -> 13.5 us
    another operation x13 -> x0, local copies, waits for them, and re-layouts: 10.9 us -> none
    dynamic_update_slice x11 -> x0, other arithmetic: 10 us -> none  [gather_rows(): full = lax.dynamic_update_slice(full, part[None], (mine, 0, 0))]
  transfers between devices with their start and end apart: 24 -> 1, of which waited for: 2 -> 0; matrix products, arithmetic and copies ran while one was open for 13% -> 1% of each run, Pallas kernels for 56% -> 48%
where the time goes in v4:
time: 394 us; the launch traced here: 393 us
  Pallas kernels  357 us (91%)
  local copies, waits for them, and re-layouts  20.6 us (5%)
  between operations  14.1 us (4%)
    pallas_call x1, Pallas kernels, tail_call(): pl.pallas_call(functools.partial(tail_kernel, p, jobs, len(mats), len(sha...  181 us
    pallas_call x1, Pallas kernels, head_call(): pl.pallas_call(functools.partial(head_kernel, p), out_shape=[jax.ShapeDty...  132 us
    pallas_call x1, Pallas kernels, plain_call(): pl.pallas_call(kernel, out_shape=[jax.ShapeDtypeStruct(s, t) for s, t in...  24.2 us
    pallas_call x1, Pallas kernels, local(): pl.pallas_call(ffn_kernel, grid=(ff // chunk,), out_shape=[jax.ShapeDtype...  14.2 us
    unnamed x27, local copies, waits for them, and re-layouts  13.5 us
  transfers between devices with their start and end apart: 1, of which 0 were waited for; matrix products, arithmetic and copies ran while one was open for 1% of the time, Pallas kernels for 48%

profile of v4, /device:TPU:0, one launch (start us, length us, event | category | flops | bytes accessed | tf_op | source)
XLA Modules:
  0.0 392.9 jit_solution(3606305979123392009)
XLA Ops:
  7.2 0.0 reduce-scatter.2.cloned.1.call-start
  7.2 1.3 slice.6
  8.5 1.2 reshape.91.refs_13_
  9.7 1.2 reshape.92.refs_14_
  11.0 1.2 reshape.93.refs_15_
  12.2 131.6 %head.1 = (bf16[2,384,768]{2,1,0:T(8,128)(2,1)}, bf16[2,384,768]{2,1,0:T(8,128)(2,1)}, bf16[2,384,768]{2,1,0:T(8,128)(2,1)}, bf16[2,384,768]{2,1,0:T(8,128)(2,1)...) custom-call(f32[384,768]{1,0:T(8,128)} %refs_0_.1, ...), custom_call_target="tpu_custom_call" | custom-call | tf_op jit(solution)/shard_map/head/pallas_call | solution.py:1447
  143.9 14.2 %ffn.1 = (bf16[256,768]{1,0:T(8,128)(2,1)}, f32[256,768]{1,0:T(8,128)}, f32[1,768]{1,0:T(1,128)}, bf16[768,2048]{1,0:T(8,128)(2,1)}, bf16[768,2048]{1,0:T(8,128)(2,1)}, /*index=5*/bf16[2048,768]{1,0:T(8,128)(2,1)}) custom-call(f32[256,768]{1,0:T(8,128)} %get-tuple-element.84.x2_ref, bf16[256,768]{1,0:T(8,128)(2,1)} %bitcast.27, ...), custom_call_target="tpu_custom_call" | custom-call | tf_op jit(solution)/shard_map/ffn/pallas_call | solution.py:1618
  158.1 24.2 %cross_back.1 = (f32[256,768]{1,0:T(8,128)}, f32[1,768]{1,0:T(1,128)}, bf16[8,192,128]{2,1,0:T(8,128)(2,1)}, bf16[1024,768]{1,0:T(8,128)(2,1)}, bf16[768,768]{1,...) custom-call(f32[256,768]{1,0:T(8,128)} %get-tuple-element.93.dx2_ref, ...), custom_call_target="tpu_custom_call" | custom-call | tf_op jit(solution)/shard_map/cross_back/pallas_call | solution.py:57
  182.3 0.0 reduce-scatter.2.cloned.1.call-update
  182.3 180.6 %tail.1 = (bf16[1024,768]{1,0:T(8,128)(2,1)}, bf16[384,2048]{1,0:T(8,128)(2,1)}, bf16[384,2048]{1,0:T(8,128)(2,1)}, bf16[384,768]{1,0:T(8,128)(2,1)}, bf16[384,7...) custom-call(bf16[2,1024,768]{2,1,0:T(8,128)(2,1)} %bitcast.17, ...), custom_call_target="tpu_custom_call" | custom-call | tf_op jit(solution)/shard_map/tail/pallas_call | solution.py:1091
  362.9 0.0 copy-start
  362.9 1.4 copy-done
  364.3 0.0 copy-start.1
  364.3 1.4 copy-done.1
  365.7 0.0 copy-start.2
  365.7 1.4 copy-done.2
  367.1 0.0 copy-start.3
  367.1 1.1 copy-done.3
  368.2 0.0 copy-start.4
  368.2 1.1 copy-done.4
  369.2 0.0 copy-start.5
  369.3 1.1 copy-done.5
  370.3 0.0 copy-start.6
  370.3 1.1 copy-done.6
  371.4 0.0 copy-start.7
  371.4 1.1 copy-done.7
  372.4 0.0 copy-start.8
  372.4 1.1 copy-done.8
  373.5 0.0 copy-start.9
  373.5 1.1 copy-done.9
  374.6 0.0 copy-start.10
  374.6 1.1 copy-done.10
  375.6 0.0 copy-start.12
  375.6 0.0 copy-start.11
  375.6 6.6 %widen.1 = (f32[1024,768]{1,0:T(8,128)}, f32[384,2048]{1,0:T(8,128)}, f32[384,2048]{1,0:T(8,128)}, f32[384,768]{1,0:T(8,128)}, f32[384,768]{1,0:T(8,128)}, /*ind...) custom-call(bf16[1024,768]{1,0:T(8,128)(2,1)S(1)} %copy-done, ...), custom_call_target="tpu_custom_call" | custom-call | tf_op jit(solution)/shard_map/widen/pallas_call | solution.py:1119
  382.2 1.5 dynamic-slice_reduce_fusion
  383.7 0.0 copy-done.12
  383.7 1.0 fusion.1
  384.7 0.6 constant_dynamic-slice_fusion
  385.3 0.0 reduce-scatter.2.cloned.1.call-done
  385.3 0.0 copy-done.11
  385.3 0.7 copy.38
Async XLA Ops:
  7.2 378.1 %reduce-scatter.2.cloned.1.call-start = ((), (), s32[]{:S(2)}) async-start(), calls=%async_computation.1 | async-start | bytes 1671168 | tf_op jit(solution)/shard_map/reduce_scatter | solution.py:1672
  362.9 1.4 copy-start
  364.3 1.4 copy-start.1
  365.7 1.4 copy-start.2
  367.1 1.1 copy-start.3
  368.2 1.1 copy-start.4
  369.2 1.1 copy-start.5
  370.3 1.1 copy-start.6
  371.4 1.1 copy-start.7
  372.4 1.1 copy-start.8
  373.5 1.1 copy-start.9
  374.6 1.1 copy-start.10
  375.6 8.1 %copy-start.12 = (s32[256]{0:T(256)S(1)}, s32[256]{0:T(256)}, u32[]{:S(2)}) copy-start(s32[256]{0:T(256)} %slice.6) | copy-start | bytes 3076
  375.6 9.7 %copy-start.11 = (bf16[2,128,768]{2,1,0:T(8,128)(2,1)S(1)}, bf16[2,128,768]{2,1,0:T(8,128)(2,1)}, u32[]{:S(2)}) copy-start(bf16[2,128,768]{2,1,0:T(8,128)(2,1)} %get-tuple-element.172) | copy-start | bytes 1179652
Sparse Core Ops, SparseCore 0:
  182.4 70.9 reduce-scatter.1

commit v5 on v4

--- a/solution.py
+++ b/solution.py
@@ -542,20 +542,7 @@
     x2_ref[...] = x1_ref[...] + dot(o2, mat(wco))
 
 
-def ffn_kernel(
-    x2_ref, og_ref, gain, wg, wu, wd, out_ref, dx2_ref, dgain_ref, dwg, dwu, dwd, a3, acc, da3
-):
-    step = pl.program_id(0)
-
-    @pl.when(step == 0)
-    def _():
-        x2 = x2_ref[...]
-        a3[...] = (x2 * scale_of(x2) * gain[2:3, :]).astype(B16)
-        acc[...] = x2
-        da3[...] = jnp.zeros_like(da3)
-
-    rows = a3[...]
-    og = og_ref[...]
+def ffn_products(rows, og, wg, wu, wd, acc, da3):
     gate = dot(rows, wg[...])
     up = dot(rows, wu[...])
     square = gate * gate
@@ -565,13 +552,147 @@
     slope = half + 0.5 * gate * (1.0 - th * th) * (GELU_A * (1.0 + 3.0 * GELU_B * square))
     inner = (value * up).astype(B16)
     acc[...] += dot(inner, wd[...])
-    dwd[...] = t_dot(inner, og).astype(B16)
+    dwd = t_dot(inner, og).astype(B16)
     dinner = dot_t(og, wd[...]).astype(B16).astype(F32)
     dgate = (dinner * up * slope).astype(B16)
     dup = (dinner * value).astype(B16)
-    dwg[...] = t_dot(rows, dgate).astype(B16)
-    dwu[...] = t_dot(rows, dup).astype(B16)
     da3[...] += dot_t(dgate, wg[...]) + dot_t(dup, wu[...])
+    return t_dot(rows, dgate).astype(B16), t_dot(rows, dup).astype(B16), dwd
+
+
+def ffn_pair_kernel(x2_ref, og_ref, gain, wg, wu, wd, out_ref, dx2_ref, dgain_ref, *refs):
+    kept, theirs = refs[0:6], refs[6:12]
+    a3, acc, da3, own, give, got, own_d, give_d, got_d, send, recv = refs[12:]
+    step = pl.program_id(0)
+    x = lax.axis_index("shard")
+    core = lax.axis_index("rep") % 2
+    slot = step // 2
+    half = D // 2
+
+    @pl.when(step == 0)
+    def _():
+        barrier = pltpu.get_barrier_semaphore()
+        pl.semaphore_signal(
+            barrier, inc=1, device_id={"rep": partner(0)[1]}, device_id_type=MESH
+        )
+        x2 = x2_ref[...]
+        a3[...] = (x2 * scale_of(x2) * gain[2:3, :]).astype(B16)
+        acc[...] = x2
+        da3[...] = jnp.zeros_like(da3)
+        pl.semaphore_wait(barrier, 1)
+
+    def pass_wide(i, at):
+        return to_rep(give.at[i, at], got.at[i, at], send.at[i, at], recv.at[i, at], 0)
+
+    def pass_down(at):
+        return to_rep(give_d.at[at], got_d.at[at], send.at[2, at], recv.at[2, at], 0)
+
+    *wide, down = ffn_products(a3[...], og_ref[...], wg, wu, wd, acc, da3)
+    for i, dw in enumerate(wide):
+        dw = dw.reshape(2, half, dw.shape[1])
+
+        @pl.when(step % 2 == core)
+        def _(i=i, dw=dw):
+            own[i, slot] = dw
+
+        @pl.when(step % 2 != core)
+        def _(i=i, dw=dw):
+            give[i, slot] = dw
+            pass_wide(i, slot).start()
+
+    @pl.when(core == 0)
+    def _():
+        own_d[step] = down[:, :half]
+        give_d[step] = down[:, half:]
+
+    @pl.when(core != 0)
+    def _():
+        own_d[step] = down[:, half:]
+        give_d[step] = down[:, :half]
+
+    pass_down(step).start()
+
+    def both(a, b):
+        return (a.astype(F32) + b.astype(F32)).astype(B16)
+
+    def finish_wide(at):
+        for i in range(2):
+            landed(got.at[i, at], recv.at[i, at])
+            kept[2 * i + at][...] = both(own[i, at, x], got[i, at, x])
+            theirs[2 * i + at][...] = both(own[i, at, 1 - x], got[i, at, 1 - x])
+
+    @pl.when(step == 2)
+    def _():
+        finish_wide(0)
+
+    @pl.when(step == 3)
+    def _():
+        out_ref[...] = acc[...].astype(B16)
+        dv, dgain = norm_back(x2_ref[...], gain[2:3, :], da3[...])
+        dx2_ref[...] = og_ref[...].astype(F32) + dv
+        dgain_ref[...] = dgain
+        finish_wide(1)
+        for at in range(4):
+            landed(got_d.at[at], recv.at[2, at])
+        for at in range(2):
+            kept[4 + at][...] = both(own_d[2 * x + at], got_d[2 * x + at])
+            theirs[4 + at][...] = both(own_d[2 - 2 * x + at], got_d[2 - 2 * x + at])
+        for at in range(4):
+            pass_down(at).wait_send()
+        for at in range(2):
+            for i in range(2):
+                pass_wide(i, at).wait_send()
+
+
+def ffn_pair_call(x2, og, small, wg, wu, wd, collective):
+    tokens, ff = x2.shape[0], wg.shape[1]
+    half, chunk = D // 2, ff // 4
+    const = lambda s: pl.BlockSpec(s, lambda i: (0, 0))
+    parts = [(half, chunk)] * 4 + [(chunk, half)] * 2
+    outs = [((tokens, D), B16), ((tokens, D), F32), ((1, D), F32)]
+    outs += [(s, B16) for s in parts + parts]
+    dma = pltpu.SemaphoreType.DMA
+    return pl.pallas_call(
+        ffn_pair_kernel,
+        grid=(4,),
+        out_shape=[jax.ShapeDtypeStruct(s, t) for s, t in outs],
+        in_specs=[
+            const((tokens, D)),
+            const((tokens, D)),
+            const((SMALL_ROWS, D)),
+            pl.BlockSpec((D, chunk), lambda i: (0, i)),
+            pl.BlockSpec((D, chunk), lambda i: (0, i)),
+            pl.BlockSpec((chunk, D), lambda i: (i, 0)),
+        ],
+        out_specs=[const(s) for s, _ in outs],
+        scratch_shapes=[
+            pltpu.VMEM((tokens, D), B16),
+            pltpu.VMEM((tokens, D), F32),
+            pltpu.VMEM((tokens, D), F32),
+        ]
+        + [pltpu.VMEM((2, 2, 2, half, chunk), B16)] * 3
+        + [pltpu.VMEM((4, chunk, half), B16)] * 3
+        + [dma((3, 4)), dma((3, 4))],
+        compiler_params=pltpu.CompilerParams(
+            collective_id=collective, has_side_effects=True, vmem_limit_bytes=60 * 2**20
+        ),
+        name="ffn",
+    )(x2, og, small, wg, wu, wd)
+
+
+def ffn_kernel(
+    x2_ref, og_ref, gain, wg, wu, wd, out_ref, dx2_ref, dgain_ref, dwg, dwu, dwd, a3, acc, da3
+):
+    step = pl.program_id(0)
+
+    @pl.when(step == 0)
+    def _():
+        x2 = x2_ref[...]
+        a3[...] = (x2 * scale_of(x2) * gain[2:3, :]).astype(B16)
+        acc[...] = x2
+        da3[...] = jnp.zeros_like(da3)
+
+    dwg[...], dwu[...], dwd[...] = ffn_products(a3[...], og_ref[...], wg, wu, wd, acc, da3)
 
     @pl.when(step == pl.num_programs(0) - 1)
     def _():
@@ -614,6 +735,8 @@
     dqt,
     dk,
     dv,
+    need=lambda *refs: None,
+    done=lambda ref: None,
 ):
     toks = qt_ref.shape[2]
     span = kn.shape[1] // seqs
@@ -624,9 +747,13 @@
     for s in range(1, seqs):
         total = total + dot(o2t[s], dc[s * toks : (s + 1) * toks])
     dwco[...] = total.astype(B16)
+    done(dwco)
+    need(wco)
     do2 = dot_t(dc, mat(wco))
     for s in range(seqs):
         dt[s] = jnp.transpose(do2[s * toks : (s + 1) * toks]).astype(B16)
+
+    need(kn, kt, vn)
 
     def heads(i, carry):
         col = pl.multiple_of(2 * i * DH, 2 * DH)
@@ -652,13 +779,18 @@
         return carry
 
     lax.fori_loop(0, H // 2, heads, 0)
+    need(enc, wck, wcv, wcq, wo)
     dwck[...] = t_dot(mat(enc), dk[...]).astype(B16)
+    done(dwck)
     dwcv[...] = t_dot(mat(enc), dv[...]).astype(B16)
+    done(dwcv)
     denc_ref[...] = (dot_t(dk[...], mat(wck)) + dot_t(dv[...], mat(wcv))).astype(B16)
+    done(denc_ref)
     dq2 = jnp.concatenate(
         [jnp.transpose(dqt[s].astype(F32)) for s in range(seqs)], axis=0
     ).astype(B16)
     dwcq[...] = t_dot(a2_ref[...], dq2).astype(B16)
+    done(dwcq)
     term, dgain = norm_back(x1_ref[...], gain[1:2, :], dot_t(dq2, mat(wcq)))
     dgain_ref[...] = dgain
     dx1 = dx2 + term
@@ -668,12 +800,81 @@
     for s in range(1, seqs):
         total = total + dot(rows_of(ot, s, seqs), db[s * toks : (s + 1) * toks])
     dwo[...] = total.astype(B16)
+    done(dwo)
     do = dot_t(db, mat(wo))
     width = D // groups
     for s in range(seqs):
         turned = jnp.transpose(do[s * toks : (s + 1) * toks]).astype(B16)
         for g in range(groups):
             dot_ref[s * groups + g] = turned[g * width : (g + 1) * width]
+
+
+def cross_back_pair_kernel(kernel, ins, outs, far_ins, far_outs, count, *refs):
+    refs = list(refs)
+    take = lambda n: [refs.pop(0) for _ in range(n)]
+    args, sources, results_, crossed = take(ins), take(count), take(outs), take(count)
+    scratch = take(4)
+    near_in, near_out = take(len(far_ins)), take(len(far_outs))
+    sems, *cross_sems = refs
+    moves = Moves(sems)
+    moves.bring([(args[i], near) for i, near in zip(far_ins, near_in)])
+    if count:
+        send, recv = cross_sems
+        barrier = pltpu.get_barrier_semaphore()
+        x = lax.axis_index("shard")
+        pl.semaphore_signal(barrier, inc=1, device_id={"shard": 1 - x}, device_id_type=MESH)
+        pl.semaphore_wait(barrier, 1)
+    copies = [
+        to_row(sources[i], crossed[i], send.at[i], recv.at[i]) for i in range(count)
+    ]
+    for copy in copies:
+        copy.start()
+    for i, near in zip(far_ins, near_in):
+        args[i] = near
+    made = {}
+    for i, near in zip(far_outs, near_out):
+        made[id(near)] = (near, results_[i])
+        results_[i] = near
+
+    def done(ref):
+        moves.take(*made[id(ref)])
+
+    kernel(*args, *results_, *scratch, need=moves.need, done=done)
+    moves.end()
+    for copy in copies:
+        copy.wait()
+
+
+def cross_back_pair_call(kernel, outs, args, scratch, sources, collective):
+    near = pl.BlockSpec(memory_space=pltpu.VMEM)
+    anywhere = pl.BlockSpec(memory_space=pl.ANY)
+    count = len(sources)
+    far_ins = [11, 7, 8, 9, 10, 13, 14, 12, 15]
+    far_outs = [3, 4, 5, 6, 7, 8]
+    dma = pltpu.SemaphoreType.DMA
+    scratch = [*scratch]
+    scratch += [pltpu.VMEM(args[i].shape, args[i].dtype) for i in far_ins]
+    scratch += [pltpu.VMEM(*outs[i]) for i in far_outs]
+    scratch += [dma((len(far_ins) + len(far_outs),))]
+    if count:
+        scratch += [dma((count,)), dma((count,))]
+        params = dict(collective_id=collective, has_side_effects=True)
+    else:
+        params = {}
+    return pl.pallas_call(
+        functools.partial(
+            cross_back_pair_kernel, kernel, len(args), len(outs), far_ins, far_outs, count
+        ),
+        out_shape=[jax.ShapeDtypeStruct(s, t) for s, t in outs]
+        + [jax.ShapeDtypeStruct(s.shape, s.dtype) for s in sources],
+        in_specs=[anywhere if i in far_ins else near for i in range(len(args))]
+        + [anywhere] * count,
+        out_specs=[anywhere if i in far_outs else near for i in range(len(outs))]
+        + [anywhere] * count,
+        scratch_shapes=scratch,
+        compiler_params=pltpu.CompilerParams(vmem_limit_bytes=60 * 2**20, **params),
+        name="cross_back",
+    )(*args, *sources)
 
 
 def last_kernel(plan, hidden, grads, a1, gain, dx1, wq, wk, wv, dh_ref, dgain_ref, dwq, dwk, dwv):
@@ -725,12 +926,42 @@
     return [s.astype(F32) for s in summed]
 
 
+class Moves:
+    def __init__(self, sems):
+        self.sems, self.used, self.coming, self.going = sems, 0, {}, []
+
+    def sem(self):
+        self.used += 1
+        return self.sems.at[self.used - 1]
+
+    def bring(self, pairs):
+        for far, near in pairs:
+            sem = self.sem()
+            pltpu.make_async_copy(far, near, sem).start()
+            self.coming[id(near)] = (near, sem)
+
+    def need(self, *refs):
+        for ref in refs:
+            if id(ref) in self.coming:
+                near, sem = self.coming.pop(id(ref))
+                landed(near, sem)
+
+    def take(self, near, far):
+        sem = self.sem()
+        pltpu.make_async_copy(near, far, sem).start()
+        self.going.append((near, sem))
+
+    def end(self):
+        for near, sem in self.going:
+            landed(near, sem)
+
+
 BITS = 4
 
 
 class Job:
-    def __init__(self, source, result, row, rows, col, cols):
-        self.source, self.result = source, result
+    def __init__(self, result, row, rows, col, cols, taken=None):
+        self.result, self.taken = result, taken
         self.row, self.rows, self.col, self.cols = row, rows, col, cols
 
 
@@ -769,20 +1000,27 @@
 
 
 class JobRun:
-    STAGES = 10
-
-    def __init__(self, job, source, result, bufs, sems, index):
-        self.job, self.source, self.result = job, source, result
-        self.acc, self.core, self.row, *self.part = bufs
+    def __init__(self, job, sources, result, bufs, sems, index, order, depth):
+        self.order = (0, *order)
+        self.job, self.sources, self.result = job, sources, result
+        bufs = list(bufs)
+        self.x = lax.axis_index("shard")
+        if job.taken is None:
+            self.acc, self.core = bufs.pop(0), bufs.pop(0)
+            self.kept = self.acc.at[self.x]
+            self.steps = [(0, 1), (1, depth)]
+        else:
+            self.kept = bufs.pop(0)
+            self.steps = [(0, depth if job.taken == "sent" else 1)]
+        self.steps += [(n, LAG) for n in range(2, 10)]
+        self.row, *self.part = bufs
         send, recv, local = sems
         self.send = [send.at[index, i] for i in range(9)]
         self.recv = [recv.at[index, i] for i in range(9)]
         self.local = [local.at[index, i] for i in range(2)]
         self.sent = []
-        self.x = lax.axis_index("shard")
-        self.bits = [partner(b)[0] for b in range(BITS)]
+        self.bits = [partner(b)[0] for b in self.order]
         half = job.cols // 2
-        self.half = half
         self.mine = pl.ds(pl.multiple_of(job.col + self.bits[0] * half, 128), half)
         self.other = pl.ds(pl.multiple_of(job.col + (1 - self.bits[0]) * half, 128), half)
         self.all = pl.ds(job.row, job.rows)
@@ -805,21 +1043,26 @@
         copy.start()
         self.sent.append(copy)
 
+    def begin(self):
+        if self.job.taken is None:
+            (source,) = self.sources
+            pltpu.make_async_copy(
+                source.at[:, self.all, self.mine], self.acc, self.local[0]
+            ).start()
+            theirs = source.at[:, self.all, self.other]
+            self.go(to_rep(theirs, self.core, self.send[0], self.recv[0], 0))
+            return
+        mine, theirs = self.sources
+        pltpu.make_async_copy(mine, self.kept, self.local[0]).start()
+        if self.job.taken == "sent":
+            self.go(to_row(theirs, self.row, self.send[1], self.recv[1]))
+        else:
+            pltpu.make_async_copy(theirs, self.row, self.recv[1]).start()
+
     def stage(self, n):
         job = self.job
         if n == 0:
-            pltpu.make_async_copy(
-                self.source.at[:, self.all, self.mine], self.acc, self.local[0]
-            ).start()
-            self.go(
-                to_rep(
-                    self.source.at[:, self.all, self.other],
-                    self.core,
-                    self.send[0],
-                    self.recv[0],
-                    0,
-                )
-            )
+            self.begin()
         elif n == 1:
             landed(self.acc, self.local[0])
             landed(self.core, self.recv[0])
@@ -827,25 +1070,29 @@
                 add_into(self.acc.at[i], self.core.at[i], job.rows)
             self.go(to_row(self.acc.at[1 - self.x], self.row, self.send[1], self.recv[1]))
         elif n == 2:
+            if job.taken is not None:
+                landed(self.kept, self.local[0])
             landed(self.row, self.recv[1])
-            add_into(self.acc.at[self.x], self.row, job.rows)
+            add_into(self.kept, self.row, job.rows)
             self.give(1)
         elif n in (3, 4):
             self.take(n - 2)
             self.give(n - 1)
         elif n == 5:
             self.take(3)
-            piece = self.acc.at[self.x, self.span(self.first[3], self.count(3))]
+            piece = self.kept.at[self.span(self.first[3], self.count(3))]
             place = self.out(self.first[3], self.count(3))
             pltpu.make_async_copy(piece, place, self.local[1]).start()
-            self.go(to_rep(piece, place, self.send[5], self.recv[5], 3))
+            self.go(to_rep(piece, place, self.send[5], self.recv[5], self.order[3]))
         elif n in (6, 7, 8):
             level = 9 - n
             if n == 6:
                 landed(self.out(self.first[3], self.count(3)), self.local[1])
             self.landed_at(level)
             place = self.out(self.first[level - 1], self.count(level - 1))
-            self.go(to_rep(place, place, self.send[n], self.recv[n], level - 1))
+            self.go(
+                to_rep(place, place, self.send[n], self.recv[n], self.order[level - 1])
+            )
         else:
             landed(self.result.at[self.all, self.other], self.recv[8])
             for copy in self.sent:
@@ -856,11 +1103,11 @@
         first = self.first[level - 1] + (1 - self.bits[level]) * count
         self.go(
             to_rep(
-                self.acc.at[self.x, self.span(first, count)],
+                self.kept.at[self.span(first, count)],
                 self.part[level - 1],
                 self.send[level + 1],
                 self.recv[level + 1],
-                level,
+                self.order[level],
             )
         )
 
@@ -868,7 +1115,7 @@
         landed(self.part[level - 1], self.recv[level + 1])
         count = self.count(level)
         rows = self.span(self.first[level], count)
-        add_into(self.acc.at[self.x, rows], self.part[level - 1], count)
+        add_into(self.kept.at[rows], self.part[level - 1], count)
 
     def landed_at(self, level):
         count = self.count(level)
@@ -878,18 +1125,16 @@
 
 def job_buffers(job):
     half = job.cols // 2
-    return [
-        pltpu.VMEM((2, job.rows, half), B16),
-        pltpu.VMEM((2, job.rows, half), B16),
-        pltpu.VMEM((job.rows, half), B16),
-    ] + [pltpu.VMEM((job.rows // 2**b, half), B16) for b in range(1, BITS)]
-
-
-JOB_BUFFERS = 6
+    if job.taken is None:
+        shapes = [(2, job.rows, half)] * 2
+    else:
+        shapes = [(job.rows, half)]
+    shapes += [(job.rows // 2**b, half) for b in range(BITS)]
+    return [pltpu.VMEM(s, B16) for s in shapes]
 
 
 class SmallRun:
-    STAGES = BITS + 2
+    steps = [(n, 1) for n in range(BITS + 2)]
 
     def __init__(self, sums, terms, send, recv):
         self.sums, self.terms, self.send, self.recv = sums, terms, send, recv
@@ -909,51 +1154,139 @@
                 self.copy(i).wait_send()
 
 
-def in_ticks(runs):
-    last = max(i + run.STAGES for i, run in enumerate(runs))
-    for tick in range(last):
-        for n in range(max(run.STAGES for run in runs)):
-            if 0 <= tick - n < len(runs) and n < runs[tick - n].STAGES:
-                runs[tick - n].stage(n)
-        yield
-
-
-def jobs_of(shapes):
-    jobs = []
-    for i, (rows, cols) in enumerate(shapes):
-        wide = cols // 2 if cols > 1024 else cols
-        tall = rows // 2 if rows > 512 else rows
-        for row in range(0, rows, tall):
-            for col in range(0, cols, wide):
-                jobs.append(Job(i, i, row, tall, col, wide))
-    return jobs
+class EncodedRun:
+    def __init__(self, source, result, bufs, send, recv, load, lag):
+        self.source, self.result, self.send, self.recv, self.load = source, result, send, recv, load
+        self.acc, self.terms = bufs[0], bufs[1:]
+        self.bits = [partner(b)[0] for b in range(BITS)]
+        self.steps = [(0, 1)] + [(n + 1, lag) for n in range(1, BITS + 1)]
+        self.sent = []
+
+    def part(self, ref, n, bit):
+        at = (slice(None),) * (BITS - n) + (bit,)
+        return ref.at[at]
+
+    def go(self, n, source):
+        copy = to_rep(source, self.terms[n], self.send.at[n], self.recv.at[n], n)
+        copy.start()
+        self.sent.append(copy)
+
+    def fixed(self, n):
+        return self.acc.at[
+            (slice(None),) * (BITS + 1 - n) + tuple(self.bits[b] for b in range(n - 1, 0, -1))
+        ]
+
+    def add(self, n):
+        left = self.fixed(n + 1)
+        terms = self.terms[n]
+        lead = left.shape[:-2]
+        count = 1
+        for d in lead:
+            count *= d
+
+        def body(i, carry):
+            at, rest = [], i
+            for d in reversed(lead):
+                at.insert(0, rest % d)
+                rest = rest // d
+            at = tuple(at)
+            left[at] = (left[at].astype(F32) + terms[at].astype(F32)).astype(B16)
+            return carry
+
+        lax.fori_loop(0, count, body, 0)
+
+    def stage(self, step):
+        if step == 0:
+            pltpu.make_async_copy(
+                self.part(self.source, 0, self.bits[0]), self.acc, self.load
+            ).start()
+            self.go(0, self.part(self.source, 0, 1 - self.bits[0]))
+            return
+        n = step - 1
+        if n == 1:
+            landed(self.acc, self.load)
+        landed(self.terms[n - 1], self.recv.at[n - 1])
+        self.add(n - 1)
+        if n < BITS:
+            self.go(n, self.part(self.fixed(n), n, 1 - self.bits[n]))
+        else:
+            self.result[...] = self.fixed(BITS)[...]
+            for copy in self.sent:
+                copy.wait_send()
+
+
+class Pipeline:
+    def __init__(self):
+        self.waiting, self.active, self.now = [], [], 0
+
+    def add(self, runs):
+        self.waiting += runs
+
+    def tick(self, count=1):
+        for _ in range(count):
+            if self.waiting:
+                self.active.insert(0, [self.waiting.pop(0), 0, self.now])
+            early = [e for e in self.active if e[0].steps[e[1]][0] < 2]
+            late = [e for e in self.active if e[0].steps[e[1]][0] >= 2]
+            for entry in early + late:
+                run, at, due = entry
+                if due <= self.now:
+                    stage, wait = run.steps[at]
+                    run.stage(stage)
+                    entry[1:] = [at + 1, self.now + wait]
+            self.active = [e for e in self.active if e[1] < len(e[0].steps)]
+            self.now += 1
+
+    def finish(self):
+        while self.waiting or self.active:
+            self.tick()
+
+
+def jobs_of(result, rows, cols):
+    wide = cols // 2 if cols > 1024 else cols
+    tall = rows // 2 if rows > 512 else rows
+    return [
+        Job(result, row, tall, col, wide)
+        for row in range(0, rows, tall)
+        for col in range(0, cols, wide)
+    ]
 
 
 SMALL_ROWS = 16
-
-
-def tail_kernel(p, jobs, early, arrays, *refs):
+HOSTED = None
+X_DEPTH = 3
+LAG = 2
+TICKS = (4, 1, 1, 2)
+
+
+def tail_kernel(p, jobs, counts, arrays, *refs):
     refs = list(refs)
     take = lambda n: [refs.pop(0) for _ in range(n)]
-    sources = take(early)
-    (dot_,) = take(1)
-    recv, lines, of_ref, rl_ref, hidden, a1, dx1, dgc, dgf, wq, wk, wv = take(12)
+    given = [take(n) for n in counts]
+    dot_, denc, *far = take(7)
+    lines, rl_ref, hidden, a1, dx1, dgc, dgf = take(7)
     results = take(arrays)
-    small, dh_ref = take(2)
+    small, dh_ref, denc_out = take(3)
     dout, dq, dkv, part, out, grads = take(6)
-    late = take(arrays - early)
+    late = take(3)
+    recv, of_ref, wq, wk, wv = held = take(5)
+    enc_bufs = take(BITS + 1)
+    enc_send, enc_recv, enc_load, move_sems = take(4)
     small_sums, small_terms = take(2)
     back = take(7)
     rows_send, rows_recv, part_sem, got_sem, ret_send, ret_recv = take(6)
     small_send, small_recv = take(2)
     sems = take(3)
-    sources = sources + late
-    runs = [
-        JobRun(job, sources[job.source], results[job.result], take(JOB_BUFFERS), sems, i)
-        for i, job in enumerate(jobs)
-    ]
-    ready = sum(1 for job in jobs if job.source < early)
-    runs.insert(ready, SmallRun(small_sums, small_terms, small_send, small_recv))
+    moves = Moves(move_sems)
+    moves.bring(zip(far, held))
+    ready = len(given)
+    given += [[ref] for ref in late]
+    runs = []
+    for i, (job, pair) in enumerate(zip(jobs, given)):
+        bufs = take(len(job_buffers(job)))
+        order = (2, 1, 3) if i % 4 == 1 else (1, 2, 3)
+        runs.append(JobRun(job, pair, results[job.result], bufs, sems, i, order, X_DEPTH))
+    enc_run = EncodedRun(denc, denc_out, enc_bufs, enc_send, enc_recv, enc_load.at[0], LAG)
 
     me = lax.axis_index("rep")
     w = me % p.W
@@ -970,24 +1303,19 @@
     pl.semaphore_signal(barrier, inc=1, device_id={"shard": 1 - x}, device_id_type=MESH)
     pl.semaphore_wait(barrier, p.R)
 
-    pipeline = in_ticks(runs)
-    passed = 0
-
-    def tick(count=1):
-        nonlocal passed
-        for _ in range(count):
-            next(pipeline)
-        passed += count
-
+    pipeline = Pipeline()
+    pipeline.add([*runs[:2], enc_run, *runs[2:ready]])
+    tick = pipeline.tick
     for u in range(p.U):
         start_either(
             me, u * p.W + mine, dot_.at[u], dout.at[slot], rows_send.at[u], rows_recv.at[slot]
         )
-    tick(2)
+    tick(TICKS[0])
     for j in range(p.J):
         landed(dout.at[j], rows_recv.at[j])
     lines_at = lax.broadcasted_iota(jnp.int32, (SMALL_ROWS, D), 0)
     block = jnp.zeros((SMALL_ROWS, D), F32)
+    moves.need(recv, of_ref)
     for h in range(p.HG):
         sums = back_head(
             p,
@@ -1004,7 +1332,7 @@
         )
         sums = jnp.concatenate([sums, jnp.zeros((1, D - 2 * p.T), F32)], axis=1)
         block = jnp.where(lines_at == 3 + group * p.HG + h, sums, block)
-        tick()
+        tick(TICKS[1])
 
     def give(k, j):
         to = (w + k) % p.W
@@ -1019,7 +1347,7 @@
     for j in range(p.J):
         for k in range(1, p.W):
             give(k, j).start()
-    tick()
+    tick(TICKS[2])
     for j in range(p.J):
         r = p.source(j, w)
         total = dkv[r].astype(F32)
@@ -1029,16 +1357,16 @@
         out[j, 0 : p.F, :] = dq[j]
         out[j, p.F : 3 * p.F, :] = total.astype(B16)
         start_either(me, r, out.at[j], grads.at[unit], ret_send.at[j], ret_recv.at[unit])
-    tick(2)
+    tick(TICKS[3])
     for u in range(p.U):
         landed(grads.at[u], ret_recv.at[u])
+    moves.need(wq, wk, wv)
     dgain = last_products(p, hidden, grads, a1, lines, dx1, wq, wk, wv, dh_ref, *late)
     for i, row in enumerate((dgain, dgc[...], dgf[...])):
         block = jnp.where(lines_at == i, row, block)
     small_sums[0] = block
-    assert passed <= ready
-    for _ in pipeline:
-        pass
+    pipeline.add([*runs[ready:], SmallRun(small_sums, small_terms, small_send, small_recv)])
+    pipeline.finish()
     small[...] = small_sums[BITS + 1]
     for u in range(p.U):
         end_either(
@@ -1051,10 +1379,19 @@
             give(k, j).wait_send()
 
 
-def tail_call(p, mats, dot_, held, hidden, collective):
+def tail_call(p, work, dot_, denc, far, held, collective):
     half = D // 2
-    shapes = [m.shape[1:] for m in mats] + [(half, D)] * 3
-    jobs = jobs_of(shapes)
+    jobs = [job for job, _ in work]
+    shapes = []
+    for result in range(1 + max(job.result for job in jobs)):
+        parts = [job for job in jobs if job.result == result]
+        shapes.append((max(j.row + j.rows for j in parts), max(j.col + j.cols for j in parts)))
+    for _ in range(3):
+        jobs.append(Job(len(shapes), 0, half, 0, D))
+        shapes.append((half, D))
+    sources = [s for _, pair in work for s in pair]
+    piece = denc.shape[0] // (p.S * p.R)
+    denc = denc.reshape((p.S,) + (2,) * BITS + (piece, D))
     dma = pltpu.SemaphoreType.DMA
     others = max(p.W - 1, 1)
     scratch = [
@@ -1066,6 +1403,12 @@
         pltpu.VMEM((p.U, 3 * p.F, p.T), B16),
     ]
     scratch += [pltpu.VMEM((2, half, D), B16)] * 3
+    scratch += [pltpu.VMEM(a.shape, a.dtype) for a in far]
+    scratch += [pltpu.VMEM((p.S,) + (2,) * (BITS - 1) + (piece, D), B16)]
+    scratch += [
+        pltpu.VMEM((p.S,) + (2,) * (BITS - 1 - n) + (piece, D), B16) for n in range(BITS)
+    ]
+    scratch += [dma((BITS,)), dma((BITS,)), dma((1,)), dma((len(far),))]
     scratch += [
         pltpu.VMEM((BITS + 2, SMALL_ROWS, D), F32),
         pltpu.VMEM((BITS + 1, SMALL_ROWS, D), F32),
@@ -1088,22 +1431,23 @@
         scratch += job_buffers(job)
     anywhere = pl.BlockSpec(memory_space=pl.ANY)
     near = pl.BlockSpec(memory_space=pltpu.VMEM)
-    *sums, small, dh = pl.pallas_call(
-        functools.partial(tail_kernel, p, jobs, len(mats), len(shapes)),
+    *sums, small, dh, denc = pl.pallas_call(
+        functools.partial(tail_kernel, p, jobs, [len(pair) for _, pair in work], len(shapes)),
         out_shape=[jax.ShapeDtypeStruct(s, B16) for s in shapes]
         + [
             jax.ShapeDtypeStruct((SMALL_ROWS, D), F32),
-            jax.ShapeDtypeStruct(hidden.shape, B16),
+            jax.ShapeDtypeStruct((p.S, p.T, D), B16),
+            jax.ShapeDtypeStruct((p.S, piece, D), B16),
         ],
-        in_specs=[anywhere] * (len(mats) + 1) + [near] * len(held),
-        out_specs=[anywhere] * len(shapes) + [near] * 2,
+        in_specs=[anywhere] * (len(sources) + 2 + len(far)) + [near] * len(held),
+        out_specs=[anywhere] * len(shapes) + [near] * 3,
         scratch_shapes=scratch,
         compiler_params=pltpu.CompilerParams(
             collective_id=collective, has_side_effects=True, vmem_limit_bytes=60 * 2**20
         ),
         name="tail",
-    )(*mats, dot_, *held)
-    return sums, small, dh
+    )(*sources, dot_, denc, *far, *held)
+    return sums, small, dh, denc
 
 
 def widen_kernel(count, *refs):
@@ -1122,29 +1466,38 @@
         out_shape=[jax.ShapeDtypeStruct(m.shape, F32) for m in mats],
         in_specs=blocks,
         out_specs=blocks,
-        compiler_params=pltpu.CompilerParams(vmem_limit_bytes=40 * 2**20),
+        compiler_params=pltpu.CompilerParams(vmem_limit_bytes=63 * 2**20),
         name="widen",
     )(*mats)
 
 
 class Fetch:
-    def __init__(self, master, held, staged, out, first, rows, col, cols, stage, own, sems, index):
+    def __init__(self, master, staged, out, first, rows, col, cols, stage, own, sems, index, wide):
         self.x = lax.axis_index("shard")
-        self.core = lax.axis_index("rep") % 2
-        self.rows, self.staged = rows, staged
+        self.core, self.y = [partner(b)[0] for b in range(2)]
+        self.rows, self.staged, self.wide = rows, staged, wide
         self.master = master.at[pl.ds(first, rows), pl.ds(col, cols)]
         self.stage_ref = stage.at[pl.ds(0, rows), pl.ds(0, cols)]
         self.own = own
         self.out, self.first, self.col, self.cols = out, first, col, cols
-        load, send, recv, relay_send, relay_recv, keep = sems
+        load, keep, self.send, self.recv = sems
         self.load, self.keep = load.at[index], keep.at[index]
-        self.send, self.recv = send.at[index], recv.at[index]
-        self.relay_send, self.relay_recv = relay_send.at[index], relay_recv.at[index]
-
-    def place(self, owner, core):
+        self.send = [self.send.at[index, i] for i in range(3)]
+        self.recv = [self.recv.at[index, i] for i in range(3)]
+
+    def span(self, core, y=None):
         half = self.rows // 2
-        first = pl.multiple_of(self.first + core * half, 16)
-        return self.out.at[owner, pl.ds(first, half), pl.ds(self.col, self.cols)]
+        if y is None:
+            return core * half, half
+        return core * half + y * (half // 2), half // 2
+
+    def place(self, owner, *share):
+        first, count = self.span(*share)
+        first = pl.multiple_of(self.first + first, 16)
+        return self.out.at[owner, pl.ds(first, count), pl.ds(self.col, self.cols)]
+
+    def share(self):
+        return (self.core, self.y) if self.wide else (self.core,)
 
     def read(self):
         pltpu.make_async_copy(self.master, self.stage_ref, self.load).start()
@@ -1153,9 +1506,9 @@
         return self.out.at[self.x, pl.ds(self.first, self.rows), pl.ds(self.col, self.cols)]
 
     def across(self):
-        half = self.rows // 2
-        first = pl.multiple_of(self.core * half, 16)
-        return to_row(self.own.at[pl.ds(first, half)], self.place(self.x, self.core), self.send, self.recv)
+        first, count = self.span(*self.share())
+        part = self.own.at[pl.ds(pl.multiple_of(first, 16), count)]
+        return to_row(part, self.place(self.x, *self.share()), self.send[0], self.recv[0])
 
     def start(self):
         landed(self.stage_ref, self.load)
@@ -1171,20 +1524,34 @@
         if self.staged:
             pltpu.make_async_copy(self.own, self.kept(), self.keep).start()
 
+    def beside(self):
+        place = self.place(1 - self.x, self.core, self.y)
+        return to_rep(place, place, self.send[2], self.recv[2], 1)
+
     def over(self):
         place = self.place(1 - self.x, self.core)
-        return to_rep(place, place, self.relay_send, self.relay_recv, 0)
+        return to_rep(place, place, self.send[1], self.recv[1], 0)
 
     def relay(self):
-        landed(self.place(1 - self.x, self.core), self.recv)
-        self.over().start()
+        landed(self.place(1 - self.x, *self.share()), self.recv[0])
+        if self.wide:
+            self.beside().start()
+        else:
+            self.over().start()
+
+    def relay_more(self):
+        if self.wide:
+            landed(self.place(1 - self.x, self.core, 1 - self.y), self.recv[2])
+            self.over().start()
 
     def finish(self):
-        landed(self.place(1 - self.x, 1 - self.core), self.relay_recv)
+        landed(self.place(1 - self.x, 1 - self.core), self.recv[1])
 
     def end(self):
         self.across().wait_send()
         self.over().wait_send()
+        if self.wide:
+            self.beside().wait_send()
         if self.staged:
             landed(self.kept(), self.keep)
 
@@ -1193,7 +1560,7 @@
     at = lax.broadcasted_iota(jnp.int32, (SMALL_ROWS, D), 0)
     block = jnp.zeros((SMALL_ROWS, D), F32)
     for i, gain in enumerate(gains):
-        part = gain[...].astype(B16).astype(F32)
+        part = gain[...].astype(B16).astype(F32).reshape(1, -1)
         none = jnp.zeros_like(part)
         row = jnp.where(
             x == 0,
@@ -1203,7 +1570,8 @@
         block = jnp.where(at == i, row, block)
     held = table.shape[0]
     bucket = lax.broadcasted_iota(jnp.int32, (held, 2 * p.T), 0) + x * held
-    onehot = (buckets[...] == bucket).astype(F32).astype(B16)
+    near = buckets[...].reshape(1, -1)[:, : 2 * p.T]
+    onehot = (near == bucket).astype(F32).astype(B16)
     lines = t_dot(table[...].astype(B16), onehot)
     lines = jnp.concatenate([lines, jnp.zeros((H, D - 2 * p.T), F32)], axis=1)
     lines = jnp.concatenate(
@@ -1217,15 +1585,19 @@
     take = lambda n: [refs.pop(0) for _ in range(n)]
     masters = take(11)
     hidden, encoded, g1, g2, g3, table, buckets = take(7)
+    far_mats = take(8)
+    wide = take(3)
+    far_recv, far_enc, far_kn, far_kt, far_vn = take(5)
+    small, a1, of_ref, rl_ref, ot = take(5)
+    x1, x2, a2, qt2, of2, rl2 = take(6)
     mats = take(8)
-    wide = take(3)
-    small, a1, recv, of_ref, rl_ref, enc, kn, kt, vn, vt, ot = take(11)
-    x1, x2, a2, qt2, of2, rl2 = take(6)
+    recv, enc, kn, kt, vn, vt = take(6)
+    moves = Moves(take(1)[0])
     send, o_ref, mine_small, their_small = take(4)
     stages = take(4)
     owns = take(6)
     att = take(3)
-    fetch_sems = take(6)
+    fetch_sems = take(4)
     small_send, small_recv, enc_send, enc_recv = take(4)
     tok_send, relay_sem, tok_recv, back_send, back_recv = take(5)
 
@@ -1254,7 +1626,18 @@
         own = owns[i - 8] if staged else out.at[x]
         fetches.append(
             Fetch(
-                master, out, staged, out, row, rows, col, cols, stages[i % 4], own, fetch_sems, i
+                master,
+                staged,
+                out,
+                row,
+                rows,
+                col,
+                cols,
+                stages[i % 4],
+                own,
+                fetch_sems,
+                i,
+                i < 5 or i % 2 == 0,
             )
         )
 
@@ -1283,8 +1666,7 @@
         b[0] = 1 - b[0]
         landed(enc.at[(slice(None),) * (1 + n) + tuple(b)], enc_recv.at[n])
 
-    started = 0
-    relayed = 0
+    started, relayed, more = 0, 0, 0
 
     def begin(count=1):
         nonlocal started
@@ -1296,8 +1678,11 @@
                 started += 1
 
     def pass_on(count=1):
-        nonlocal relayed
+        nonlocal relayed, more
         for _ in range(count):
+            if more < relayed:
+                fetches[more].relay_more()
+                more += 1
             if relayed < started:
                 fetches[relayed].relay()
                 relayed += 1
@@ -1311,12 +1696,16 @@
     pass_on()
     begin()
     enc_landed(1)
+    pass_on()
+    begin()
     enc_copy(2).start()
     pass_on()
     begin()
-    pass_on()
-    for fetch in fetches[:3]:
+    fetches[2].relay_more()
+    more = 3
+    for fetch, far in zip(fetches[:3], far_mats):
         fetch.finish()
+        moves.take(fetch.out, far)
     project_kernel(p, hidden, small, *mats[:3], a1, send)
     for u in range(p.U):
         start_either(
@@ -1326,12 +1715,17 @@
     enc_copy(3).start()
     begin()
     pass_on(2)
+    begin()
     enc_landed(3)
-    for fetch, natural, turned in ((fetches[3], kn, kt), (fetches[4], vn, vt)):
-        fetch.finish()
-        encode_one(enc, fetch.out, natural, turned)
+    moves.take(enc, far_enc)
+    fetches[4].relay_more()
+    more = 5
+    for i, natural, turned in ((3, kn, kt), (4, vn, vt)):
+        fetches[i].finish()
+        moves.take(mats[i], far_mats[i])
+        encode_one(enc, mats[i], natural, turned)
+        pass_on()
         begin()
-        pass_on()
 
     def relay(k, j):
         part = recv.at[p.source(j, w), pl.ds(p.F, 2 * p.F)]
@@ -1342,40 +1736,45 @@
         landed(recv.at[p.source(j, w)], tok_recv.at[p.source(j, w)])
         for k in range(1, p.W):
             relay(k, j).start()
+    pass_on()
     begin()
-    pass_on()
     for k in range(1, p.W):
         for j in range(p.J):
             r = p.source(j, (w + k) % p.W)
             landed(recv.at[r, pl.ds(p.F, 2 * p.F)], tok_recv.at[r])
+    for made, far in ((recv, far_recv), (kn, far_kn), (kt, far_kt), (vn, far_vn)):
+        moves.take(made, far)
     for h in range(p.HG):
         line = line_of(p, small, group * p.HG + h)
         attend_head(p, w, h * DH, line, recv, o_ref, of_ref, rl_ref.at[h], *att)
+        pass_on()
         begin()
-        pass_on()
     for j in range(p.J):
         r = p.source(j, w)
         start_either(me, r, o_ref.at[j], ot.at[unit], back_send.at[j], back_recv.at[unit])
+    pass_on()
     begin()
-    pass_on(2)
+    for fetch, far in zip(fetches[5:8], far_mats[5:]):
+        fetch.finish()
+        moves.take(fetch.out, far)
     for u in range(p.U):
         landed(ot.at[u], back_recv.at[u])
-    for fetch in fetches[5:8]:
-        fetch.finish()
 
     def pause():
+        pass_on()
         begin()
-        pass_on()
 
     cross_kernel(
         p.S, hidden, ot, mats[5], small, mats[6], mats[7], kn, vt, x1, x2, a2, qt2, of2, rl2, pause
     )
     begin(len(fetches))
-    pass_on(len(fetches))
+    while more < len(fetches):
+        pass_on()
     for fetch in fetches[8:]:
         fetch.finish()
     for fetch in fetches:
         fetch.end()
+    moves.end()
     share.wait_send()
     for n in range(BITS):
         enc_copy(n).wait_send()
@@ -1398,17 +1797,20 @@
     near = pl.BlockSpec(memory_space=pltpu.VMEM)
     anywhere = pl.BlockSpec(memory_space=pl.ANY)
     outs = [((2, half, D), B16)] * 8 + [((2, *s), B16) for s in wides]
-    outs += [
-        ((SMALL_ROWS, D), F32),
-        ((tokens, D), B16),
+    inner = [
         ((p.R, 3 * p.F, p.T), B16),
-        ((p.J, p.F, p.T), F32),
-        ((p.HG, p.NP, 1, 2 * p.T), F32),
         ((p.S,) + (2,) * BITS + (piece, D), B16),
         ((H, enc_rows, DH), B16),
         ((H, DH + ONES, enc_rows), B16),
         ((H, enc_rows, DH), B16),
-        ((H, DH + ONES, enc_rows), B16),
+    ]
+    outs += inner
+    inner = [((2, half, D), B16)] * 8 + inner + [inner[3]]
+    outs += [
+        ((SMALL_ROWS, D), F32),
+        ((tokens, D), B16),
+        ((p.J, p.F, p.T), F32),
+        ((p.HG, p.NP, 1, 2 * p.T), F32),
         ((p.U, p.F, p.T), B16),
         ((tokens, D), F32),
         ((tokens, D), F32),
@@ -1424,7 +1826,8 @@
         parts += [(tall, part)] * ((rows // tall) * (cols // part))
     count = len(parts)
     dma = pltpu.SemaphoreType.DMA
-    scratch = [
+    scratch = [pltpu.VMEM(s, t) for s, t in inner] + [dma((13,))]
+    scratch += [
         pltpu.VMEM((p.U, 3 * p.F, p.T), B16),
         pltpu.VMEM((p.J, p.F, p.T), B16),
         pltpu.VMEM((SMALL_ROWS, D), F32),
@@ -1435,7 +1838,7 @@
     scratch += [pltpu.VMEM((tallest, widest), F32)] * 4
     scratch += [pltpu.VMEM(s, B16) for s in parts[8:]]
     scratch += attend_scratch(p)
-    scratch += [dma((count,))] * 6
+    scratch += [dma((count,)), dma((count,)), dma((count, 3)), dma((count, 3))]
     scratch += [dma, dma, dma((BITS,)), dma((BITS,))]
     scratch += [
         dma((p.U,)),
@@ -1448,7 +1851,7 @@
         functools.partial(head_kernel, p),
         out_shape=[jax.ShapeDtypeStruct(s, t) for s, t in outs],
         in_specs=[anywhere] * 11 + [near] * 7,
-        out_specs=[near] * 8 + [anywhere] * 3 + [near] * 17,
+        out_specs=[anywhere] * 16 + [near] * 11,
         scratch_shapes=scratch,
         compiler_params=pltpu.CompilerParams(
             collective_id=collective, has_side_effects=True, vmem_limit_bytes=62 * 2**20
@@ -1505,14 +1908,14 @@
             ffn_up,
             ffn_down,
         )
-        gains = [g.reshape(1, part) for g in (gain_self, gain_cross, gain_ffn)]
+        gains = [gain_self, gain_cross, gain_ffn]
         got = head_call(
-            p, masters, hidden, encoded, gains, bias_table, near.reshape(1, -1), 0
+            p, masters, hidden, encoded, gains, bias_table, buckets, 0
         )
         wq, wk, wv, wck, wcv, wo, wcq, wco = got[:8]
         wg, wu, wd = [g.reshape(-1, g.shape[-1]) for g in got[8:11]]
-        small, a1, recv, of, rl, enc, ckn, ckt, cvn, cvt, ot = got[11:22]
-        x1, x2, a2, qt2, of2, rl2 = got[22:]
+        recv, enc, ckn, ckt, cvn, small, a1, of, rl, ot = got[11:21]
+        x1, x2, a2, qt2, of2, rl2 = got[21:]
     else:
         lot = jnp.concatenate(
             [
@@ -1613,73 +2016,102 @@
             "cross",
         )
 
-    chunk = min(512, ff)
-    const = lambda s: pl.BlockSpec(s, lambda i: (0, 0))
-    output, dx2, dg_ffn, dwg, dwu, dwd = pl.pallas_call(
-        ffn_kernel,
-        grid=(ff // chunk,),
-        out_shape=[
-            jax.ShapeDtypeStruct((tokens, D), B16),
-            jax.ShapeDtypeStruct((tokens, D), F32),
-            jax.ShapeDtypeStruct((1, D), F32),
-            jax.ShapeDtypeStruct((D, ff), B16),
-            jax.ShapeDtypeStruct((D, ff), B16),
-            jax.ShapeDtypeStruct((ff, D), B16),
-        ],
-        in_specs=[
-            const((tokens, D)),
-            const((tokens, D)),
-            const((SMALL_ROWS, D)),
-            pl.BlockSpec((D, chunk), lambda i: (0, i)),
-            pl.BlockSpec((D, chunk), lambda i: (0, i)),
-            pl.BlockSpec((chunk, D), lambda i: (i, 0)),
-        ],
-        out_specs=[
-            const((tokens, D)),
-            const((tokens, D)),
-            const((1, D)),
-            pl.BlockSpec((D, chunk), lambda i: (0, i)),
-            pl.BlockSpec((D, chunk), lambda i: (0, i)),
-            pl.BlockSpec((chunk, D), lambda i: (i, 0)),
-        ],
-        scratch_shapes=[
-            pltpu.VMEM((tokens, D), B16),
-            pltpu.VMEM((tokens, D), F32),
-            pltpu.VMEM((tokens, D), F32),
-        ],
-        compiler_params=pltpu.CompilerParams(vmem_limit_bytes=56 * 2**20),
-        name="ffn",
-    )(x2, out_grad.reshape(tokens, D), small, wg, wu, wd)
-
-    dx1, dg_cross, dot_, denc, dwco, dwcq, dwck, dwcv, dwo = plain_call(
-        functools.partial(cross_back_kernel, seqs, p.G),
-        [
-            ((tokens, D), F32),
-            ((1, D), F32),
-            ((p.U, p.F, toks), B16),
-            ((enc_rows, D), B16),
+    if paired and HOSTED is not None:
+        output, dx2, dg_ffn, *parts = ffn_pair_call(
+            x2, out_grad.reshape(tokens, D), small, wg, wu, wd, 1
+        )
+        kept, theirs = parts[:6], parts[6:]
+        half, wide = D // 2, ff // 2
+        jobs = [Job(i // 2, 0, half, (i % 2) * wide, wide) for i in range(4)]
+        jobs += [Job(2, i * (ff // 4), ff // 4, 0, D) for i in range(2)]
+        for i, job in enumerate(jobs):
+            job.taken = "here" if i < HOSTED else "sent"
+    else:
+        chunk = min(512, ff)
+        const = lambda s: pl.BlockSpec(s, lambda i: (0, 0))
+        output, dx2, dg_ffn, dwg, dwu, dwd = pl.pallas_call(
+            ffn_kernel,
+            grid=(ff // chunk,),
+            out_shape=[
+                jax.ShapeDtypeStruct((tokens, D), B16),
+                jax.ShapeDtypeStruct((tokens, D), F32),
+                jax.ShapeDtypeStruct((1, D), F32),
+                jax.ShapeDtypeStruct((D, ff), B16),
+                jax.ShapeDtypeStruct((D, ff), B16),
+                jax.ShapeDtypeStruct((ff, D), B16),
+            ],
+            in_specs=[
+                const((tokens, D)),
+                const((tokens, D)),
+                const((SMALL_ROWS, D)),
+                pl.BlockSpec((D, chunk), lambda i: (0, i)),
+                pl.BlockSpec((D, chunk), lambda i: (0, i)),
+                pl.BlockSpec((chunk, D), lambda i: (i, 0)),
+            ],
+            out_specs=[
+                const((tokens, D)),
+                const((tokens, D)),
+                const((1, D)),
+                pl.BlockSpec((D, chunk), lambda i: (0, i)),
+                pl.BlockSpec((D, chunk), lambda i: (0, i)),
+                pl.BlockSpec((chunk, D), lambda i: (i, 0)),
+            ],
+            scratch_shapes=[
+                pltpu.VMEM((tokens, D), B16),
+                pltpu.VMEM((tokens, D), F32),
+                pltpu.VMEM((tokens, D), F32),
+            ],
+            compiler_params=pltpu.CompilerParams(vmem_limit_bytes=56 * 2**20),
+            name="ffn",
+        )(x2, out_grad.reshape(tokens, D), small, wg, wu, wd)
+
+    back_outs = [
+        ((tokens, D), F32),
+        ((1, D), F32),
+        ((p.U, p.F, toks), B16),
+        ((enc_rows, D), B16),
+    ] + [((D, D), B16)] * 5
+    back_args = (dx2, x1, a2, small, qt2, of2, rl2, ckn, ckt, cvn, enc, wco, wcq, wck, wcv, wo, ot)
+    back_scratch_ = [
+        pltpu.VMEM((seqs, D, toks), B16),
+        pltpu.VMEM((seqs, D, toks), B16),
+        pltpu.VMEM((enc_rows, D), B16),
+        pltpu.VMEM((enc_rows, D), B16),
+    ]
+    back_kernel = functools.partial(cross_back_kernel, seqs, p.G)
+    if paired:
+        hosted = [] if HOSTED is None else theirs[:HOSTED]
+        got = cross_back_pair_call(back_kernel, back_outs, back_args, back_scratch_, hosted, 2)
+        crossed = got[9:]
+        got = got[:9]
+    else:
+        got = plain_call(back_kernel, back_outs, back_args, "cross_back", scratch=back_scratch_)
+    dx1, dg_cross, dot_, denc, dwco, dwcq, dwck, dwcv, dwo = got
+    if paired:
+        half = D // 2
+        if HOSTED is None:
+            work = []
+            for i, g in enumerate((dwg, dwu, dwd)):
+                g = g.reshape(2, g.shape[0] // 2, g.shape[1])
+                work += [(job, [g]) for job in jobs_of(i, *g.shape[1:])]
+        else:
+            work = list(zip(jobs, zip(kept, [*crossed, *theirs[HOSTED:]])))
+            if HOSTED == 3:
+                work = [work[i] for i in (3, 0, 4, 1, 5, 2)]
+        work += [
+            (Job(3 + i, 0, half, 0, D), [g.reshape(2, half, D)])
+            for i, g in enumerate((dwo, dwcq, dwck, dwcv, dwco))
         ]
-        + [((D, D), B16)] * 5,
-        (dx2, x1, a2, small, qt2, of2, rl2, ckn, ckt, cvn, enc, wco, wcq, wck, wcv, wo, ot),
-        "cross_back",
-        scratch=[
-            pltpu.VMEM((seqs, D, toks), B16),
-            pltpu.VMEM((seqs, D, toks), B16),
-            pltpu.VMEM((enc_rows, D), B16),
-            pltpu.VMEM((enc_rows, D), B16),
-        ],
-    )
-    encoded_grad = lax.psum_scatter(
-        denc.reshape(seqs, enc_rows // seqs, D), "rep", scatter_dimension=1, tiled=True
-    )
-    if paired:
-        early = [
-            g.reshape(2, g.shape[0] // 2, g.shape[1])
-            for g in (dwd, dwg, dwu, dwo, dwcq, dwck, dwcv, dwco)
-        ]
-        held = (recv, small, of, rl, hidden, a1, dx1, dg_cross, dg_ffn, wq, wk, wv)
-        sums, block, hidden_grad = tail_call(p, early, dot_, held, hidden, 2)
-        dwd, dwg, dwu, dwo, dwcq, dwck, dwcv, dwco, dwq, dwk, dwv = widen(sums)
+        sums, block, hidden_grad, encoded_grad = tail_call(
+            p,
+            work,
+            dot_,
+            denc,
+            (recv, of, wq, wk, wv),
+            (small, rl, hidden, a1, dx1, dg_cross, dg_ffn),
+            3,
+        )
+        dwg, dwu, dwd, dwo, dwcq, dwck, dwcv, dwco, dwq, dwk, dwv = widen(sums)
         mats = [dwq, dwk, dwv, dwo, dwcq, dwck, dwcv, dwco, dwg, dwu, dwd]
         dgains = lax.dynamic_slice(block, (0, mine * part), (3, part))
         by_bucket = jnp.einsum(
@@ -1692,6 +2124,9 @@
             by_bucket, (mine * bias_table.shape[0], 0), bias_table.shape
         )
     else:
+        encoded_grad = lax.psum_scatter(
+            denc.reshape(seqs, enc_rows // seqs, D), "rep", scatter_dimension=1, tiled=True
+        )
         dout = comm_call(
             functools.partial(scatter_rows, p),
             (p.J, p.F, toks),

time: 394 us -> 330 us (0.84)
  Pallas kernels: 357 us -> 324 us
  local copies, waits for them, and re-layouts: 20.6 us -> 3.5 us
  between operations: 14.1 us -> 0.74 us
    pallas_call x1, Pallas kernels: 132 us -> 107 us  [head_call(): pl.pallas_call(functools.partial(head_kernel, p), out_shape=[jax.ShapeDty...]
    pallas_call x2, Pallas kernels: 205 us -> 191 us  [the longest x1 167 us: tail_call(): pl.pallas_call(functools.partial(tail_kernel, p, jobs, [len(pair) for _,...]
    unnamed x27 -> x6, local copies, waits for them, and re-layouts: 13.5 us -> 1.39 us
    pallas_call x1, Pallas kernels: 6.58 us -> 11 us  [widen(): pl.pallas_call(functools.partial(widen_kernel, len(mats)), grid=(parts,),...]
  transfers between devices with their start and end apart: 1 -> 0, of which waited for: 0 -> 0; matrix products, arithmetic and copies ran while one was open for 1% -> 0% of each run, Pallas kernels for 48% -> 0%
where the time goes in v5:
time: 330 us; the launch traced here: 329 us
  Pallas kernels  324 us (98%)
  local copies, waits for them, and re-layouts  3.5 us (1%)
    pallas_call x1, Pallas kernels, tail_call(): pl.pallas_call(functools.partial(tail_kernel, p, jobs, [len(pair) for _,...  167 us
    pallas_call x1, Pallas kernels, head_call(): pl.pallas_call(functools.partial(head_kernel, p), out_shape=[jax.ShapeDty...  107 us
    pallas_call x1, Pallas kernels, cross_back_pair_call(): pl.pallas_call(functools.partial(cross_back_pair_kernel, kernel, len(args...  23.5 us
    pallas_call x1, Pallas kernels, local(): pl.pallas_call(ffn_kernel, grid=(ff // chunk,), out_shape=[jax.ShapeDtype...  14.3 us
    pallas_call x1, Pallas kernels, widen(): pl.pallas_call(functools.partial(widen_kernel, len(mats)), grid=(parts,),...  11 us

profile of v5, /device:TPU:0, one launch (start us, length us, event | category | flops | bytes accessed | tf_op | source)
XLA Modules:
  0.0 328.8 jit_solution(1614206455270730603)
XLA Ops:
  0.7 107.4 %head.1 = (bf16[2,384,768]{2,1,0:T(8,128)(2,1)}, bf16[2,384,768]{2,1,0:T(8,128)(2,1)}, bf16[2,384,768]{2,1,0:T(8,128)(2,1)}, bf16[2,384,768]{2,1,0:T(8,128)(2,1)...) custom-call(f32[384,768]{1,0:T(8,128)} %refs_0_.1, ...), custom_call_target="tpu_custom_call" | custom-call | tf_op jit(solution)/shard_map/head/pallas_call | solution.py:1850
  108.1 14.3 %ffn.1 = (bf16[256,768]{1,0:T(8,128)(2,1)}, f32[256,768]{1,0:T(8,128)}, f32[1,768]{1,0:T(1,128)}, bf16[768,2048]{1,0:T(8,128)(2,1)}, bf16[768,2048]{1,0:T(8,128)(2,1)}, /*index=5*/bf16[2048,768]{1,0:T(8,128)(2,1)}) custom-call(f32[256,768]{1,0:T(8,128)} %get-tuple-element.85.x2_ref, bf16[256,768]{1,0:T(8,128)(2,1)} %bitcast.29, ...), custom_call_target="tpu_custom_call" | custom-call | tf_op jit(solution)/shard_map/ffn/pallas_call | solution.py:2032
  122.4 23.5 %cross_back.1 = (f32[256,768]{1,0:T(8,128)}, f32[1,768]{1,0:T(1,128)}, bf16[8,192,128]{2,1,0:T(8,128)(2,1)}, bf16[1024,768]{1,0:T(8,128)(2,1)}, bf16[768,768]{1,...) custom-call(f32[256,768]{1,0:T(8,128)} %get-tuple-element.94.refs_0_, ...), custom_call_target="tpu_custom_call" | custom-call | tf_op jit(solution)/shard_map/cross_back/pallas_call | solution.py:864
  145.9 167.4 %tail.1 = (bf16[384,2048]{1,0:T(8,128)(2,1)}, bf16[384,2048]{1,0:T(8,128)(2,1)}, bf16[1024,768]{1,0:T(8,128)(2,1)}, bf16[384,768]{1,0:T(8,128)(2,1)}, bf16[384,7...) custom-call(bf16[2,384,2048]{2,1,0:T(8,128)(2,1)} %bitcast.14, ...), custom_call_target="tpu_custom_call" | custom-call | tf_op jit(solution)/shard_map/tail/pallas_call | solution.py:1434
  313.3 0.0 slice-start
  313.4 0.0 copy-start
  313.4 0.0 copy-start.1
  313.4 11.0 %widen.1 = (f32[384,2048]{1,0:T(8,128)}, f32[384,2048]{1,0:T(8,128)}, f32[1024,768]{1,0:T(8,128)}, f32[384,768]{1,0:T(8,128)}, f32[384,768]{1,0:T(8,128)}, /*ind...) custom-call(bf16[384,2048]{1,0:T(8,128)(2,1)} %get-tuple-element.129, ...), custom_call_target="tpu_custom_call" | custom-call | tf_op jit(solution)/shard_map/widen/pallas_call | solution.py:1463
  324.3 0.0 slice-done
  324.3 1.0 fusion.1
  325.4 0.6 constant_dynamic-slice_fusion
  326.0 1.5 dynamic-slice_reduce_fusion
  327.5 0.0 copy-done
  327.5 0.7 copy.39
  328.2 0.0 copy-done.1
  328.2 0.6 copy.40
Async XLA Ops:
  313.3 11.0 %slice-start = ((s32[2048]{0:T(1024)}), s32[256]{0:T(256)S(1)}, s32[]{:S(2)}) async-start(s32[2048]{0:T(1024)} %refs_17_.1), calls=%async_computation | async-start | bytes 2048 | tf_op jit(solution)/shard_map/slice | solution.py:1894
  313.4 14.1 %copy-start = (bf16[2,128,768]{2,1,0:T(8,128)(2,1)S(1)}, bf16[2,128,768]{2,1,0:T(8,128)(2,1)}, u32[]{:S(2)}) copy-start(bf16[2,128,768]{2,1,0:T(8,128)(2,1)} %get-tuple-element.174) | copy-start | bytes 1179652
  313.4 14.8 %copy-start.1 = (bf16[2,32,768]{2,1,0:T(8,128)(2,1)S(1)}, bf16[2,32,768]{2,1,0:T(8,128)(2,1)}, u32[]{:S(2)}) copy-start(bf16[2,32,768]{2,1,0:T(8,128)(2,1)} %get-tuple-element.175) | copy-start | bytes 294916

commit v6 on v5

--- a/solution.py
+++ b/solution.py
@@ -1,4 +1,5 @@
 import functools
+import itertools
 
 import jax
 import jax.numpy as jnp
@@ -152,20 +153,20 @@
         r = p.source(j, w)
         landed(recv.at[r], recv_sem.at[r])
         for k in range(1, p.W):
-            part = recv.at[r, pl.ds(p.F, 2 * p.F)]
+            part = recv.at[r, :, pl.ds(DH, 2 * DH)]
             remote(
                 part, part, relay_sem.at[k - 1, j], recv_sem.at[r], me - w + (w + k) % p.W
             ).start()
     for k in range(1, p.W):
         for j in range(p.J):
             r = p.source(j, (w + k) % p.W)
-            landed(recv.at[r, pl.ds(p.F, 2 * p.F)], recv_sem.at[r])
+            landed(recv.at[r, :, pl.ds(DH, 2 * DH)], recv_sem.at[r])
     for u in range(p.U):
         end_either(me, u * p.W + mine, send.at[u], recv.at[me], send_sem.at[u], recv_sem.at[me])
     for k in range(1, p.W):
         for j in range(p.J):
             r = p.source(j, w)
-            part = recv.at[r, pl.ds(p.F, 2 * p.F)]
+            part = recv.at[r, :, pl.ds(DH, 2 * DH)]
             remote(
                 part, part, relay_sem.at[k - 1, j], recv_sem.at[r], me - w + (w + k) % p.W
             ).wait_send()
@@ -229,8 +230,8 @@
         for k in range(1, p.W):
             landed(buf.at[k - 1, j], got_sem.at[k - 1, j])
             total = total + buf[k - 1, j].astype(F32)
-        out[j, 0 : p.F, :] = dq[j]
-        out[j, p.F : 3 * p.F, :] = total.astype(B16)
+        out[j, :, 0:DH, :] = dq[j]
+        out[j, :, DH : 3 * DH, :] = total.astype(B16)
         start_either(me, r, out.at[j], recv.at[unit], send_sem.at[j], recv_sem.at[unit])
     for u in range(p.U):
         landed(recv.at[u], recv_sem.at[u])
@@ -264,8 +265,10 @@
         rows = dot(a1, mat(weight))
         for s in range(p.S):
             turned = jnp.transpose(rows[s * p.T : (s + 1) * p.T]).astype(B16)
-            for g in range(p.G):
-                send[s * p.G + g, n * p.F : (n + 1) * p.F, :] = turned[g * p.F : (g + 1) * p.F]
+            for i in range(H):
+                send[s * p.G + i // p.HG, i % p.HG, n * DH : (n + 1) * DH, :] = turned[
+                    i * DH : (i + 1) * DH
+                ]
 
 
 def bias_tiles(plan, w, line, tiles):
@@ -292,32 +295,36 @@
             )
 
 
-def block_pair(plan, ref, pair, w, row, count):
+def block_pair(plan, ref, pair, w, h):
     p = plan
     return jnp.concatenate(
-        [
-            ref[p.source_in(pair, 0, w), pl.ds(row, count), :],
-            ref[p.source_in(pair, 1, w), pl.ds(row, count), :],
-        ],
-        axis=1,
+        [ref[p.source_in(pair, late, w), h, 0:DH, :] for late in range(2)], axis=1
     )
+
+
+def in_two(count, body, carry, between):
+    if between is None:
+        return lax.fori_loop(0, count, body, carry)
+    carry = lax.fori_loop(0, count - 1, body, carry)
+    between()
+    return lax.fori_loop(count - 1, count, body, carry)
 
 
 def line_of(p, block, head):
     return block[pl.ds(3 + head, 1), 0 : 2 * p.T]
 
 
-def attend_head(p, w, row, line, recv, o_ref, of_ref, rl, kn, vt, tiles):
+def attend_head(p, w, h, line, recv, o_ref, of_ref, rl, kn, vt, tiles, between=None):
     bias_tiles(p, w, line, tiles)
     for r in range(p.R):
         kn[r * p.T : (r + 1) * p.T, :] = jnp.transpose(
-            recv[r, pl.ds(p.F + row, DH), :].astype(F32)
+            recv[r, h, DH : 2 * DH, :].astype(F32)
         ).astype(B16)
-        vt[0:DH, r * p.T : (r + 1) * p.T] = recv[r, pl.ds(2 * p.F + row, DH), :]
+        vt[0:DH, r * p.T : (r + 1) * p.T] = recv[r, h, 2 * DH : 3 * DH, :]
     vt[DH : DH + ONES, :] = jnp.ones((ONES, p.L), B16)
 
     def one_pair(pair, carry):
-        qt = block_pair(p, recv, pair, w, row, DH)
+        qt = block_pair(p, recv, pair, w, h)
 
         def step(i, acc):
             start = pl.multiple_of(i * p.CK, p.CK)
@@ -330,11 +337,11 @@
         rl[pair] = scale
         for a in range(2):
             part = of[:, a * p.T : (a + 1) * p.T]
-            of_ref[2 * pair + a, pl.ds(row, DH), :] = part
-            o_ref[2 * pair + a, pl.ds(row, DH), :] = part.astype(B16)
+            of_ref[2 * pair + a, h] = part
+            o_ref[2 * pair + a, h] = part.astype(B16)
         return carry
 
-    lax.fori_loop(0, p.NP, one_pair, 0)
+    in_two(p.NP, one_pair, 0, between)
 
 
 def attend_scratch(p):
@@ -351,34 +358,48 @@
     w = me % p.W
     group = (me // p.W) % p.G
     h = pl.program_id(0)
-    row = pl.multiple_of(h * DH, DH)
     line = line_of(p, block, group * p.HG + h)
-    attend_head(p, w, row, line, recv, o_ref, of_ref, rl_ref.at[h], *scratch)
+    attend_head(p, w, h, line, recv, o_ref, of_ref, rl_ref.at[h], *scratch)
 
 
 def back_head(
-    p, w, row, line, recv, dout, of_ref, rl, dq_ref, dkv_ref, kn, vn, kt, dk, dv, tiles, near
+    p,
+    w,
+    h,
+    line,
+    recv,
+    dout,
+    of_ref,
+    rl,
+    dq_ref,
+    dkv_ref,
+    kn,
+    vn,
+    kt,
+    dk,
+    dv,
+    tiles,
+    near,
+    between=None,
 ):
     bias_tiles(p, w, line, tiles)
     for r in range(p.R):
         kn[r * p.T : (r + 1) * p.T, :] = jnp.transpose(
-            recv[r, pl.ds(p.F + row, DH), :].astype(F32)
+            recv[r, h, DH : 2 * DH, :].astype(F32)
         ).astype(B16)
         vn[r * p.T : (r + 1) * p.T, :] = jnp.transpose(
-            recv[r, pl.ds(2 * p.F + row, DH), :].astype(F32)
+            recv[r, h, 2 * DH : 3 * DH, :].astype(F32)
         ).astype(B16)
-        kt[0:DH, r * p.T : (r + 1) * p.T] = recv[r, pl.ds(p.F + row, DH), :]
+        kt[0:DH, r * p.T : (r + 1) * p.T] = recv[r, h, DH : 2 * DH, :]
     kt[DH : DH + ONES, :] = jnp.ones((ONES, p.L), B16)
     dk[...] = jnp.zeros_like(dk)
     dv[...] = jnp.zeros_like(dv)
     near[...] = jnp.zeros_like(near)
 
     def one_pair(pair, total):
-        qt = block_pair(p, recv, pair, w, row, DH)
-        dot_rows = jnp.concatenate(
-            [dout[2 * pair + a, pl.ds(row, DH), :] for a in range(2)], axis=1
-        )
-        of = jnp.concatenate([of_ref[2 * pair + a, pl.ds(row, DH), :] for a in range(2)], axis=1)
+        qt = block_pair(p, recv, pair, w, h)
+        dot_rows = jnp.concatenate([dout[2 * pair + a, h] for a in range(2)], axis=1)
+        of = jnp.concatenate([of_ref[2 * pair + a, h] for a in range(2)], axis=1)
         delta = jnp.sum(dot_rows.astype(F32) * of, axis=0, keepdims=True)
         scale = rl[pair]
         qn = jnp.transpose(qt.astype(F32)).astype(B16)
@@ -397,15 +418,13 @@
 
         acc = lax.fori_loop(0, pair + 1, step, jnp.zeros((DH + ONES, 2 * p.T), F32))
         for a in range(2):
-            dq_ref[2 * pair + a, pl.ds(row, DH), :] = acc[:DH, a * p.T : (a + 1) * p.T].astype(B16)
+            dq_ref[2 * pair + a, h] = acc[:DH, a * p.T : (a + 1) * p.T].astype(B16)
         return total + acc[DH : DH + 1]
 
-    total = lax.fori_loop(0, p.NP, one_pair, jnp.zeros((1, 2 * p.T), F32))
+    total = in_two(p.NP, one_pair, jnp.zeros((1, 2 * p.T), F32), between)
     for r in range(p.R):
-        dkv_ref[r, pl.ds(row, DH), :] = jnp.transpose(dk[r * p.T : (r + 1) * p.T, :]).astype(B16)
-        dkv_ref[r, pl.ds(p.F + row, DH), :] = jnp.transpose(dv[r * p.T : (r + 1) * p.T, :]).astype(
-            B16
-        )
+        dkv_ref[r, h, 0:DH, :] = jnp.transpose(dk[r * p.T : (r + 1) * p.T, :]).astype(B16)
+        dkv_ref[r, h, DH : 2 * DH, :] = jnp.transpose(dv[r * p.T : (r + 1) * p.T, :]).astype(B16)
     same = jnp.zeros((p.T, p.T), F32)
     next_ = jnp.zeros((p.T, p.T), F32)
     for a in range(2):
@@ -453,11 +472,10 @@
     w = me % p.W
     group = (me // p.W) % p.G
     h = pl.program_id(0)
-    row = pl.multiple_of(h * DH, DH)
     line_ref[h] = back_head(
         p,
         w,
-        row,
+        h,
         line_of(p, block, group * p.HG + h),
         recv,
         dout,
@@ -475,14 +493,23 @@
 
 
 def encode_one(enc, weight, natural, turned):
-    rows = turned.shape[2]
     value = dot(mat(enc), mat(weight))
-    for h in range(H):
-        natural[h] = value[:, h * DH : (h + 1) * DH].astype(B16)
+    natural[...] = value.astype(B16)
     flipped = jnp.transpose(value).astype(B16)
-    for h in range(H):
-        turned[h, 0:DH, :] = flipped[h * DH : (h + 1) * DH]
-        turned[h, DH : DH + ONES, :] = jnp.ones((ONES, rows), B16)
+    if len(turned.shape) == 2:
+        turned[...] = flipped
+        return
+    for i in range(H // 2):
+        turned[i, 0 : 2 * DH, :] = flipped[2 * i * DH : 2 * (i + 1) * DH]
+        turned[i, 2 * DH : 2 * DH + ONES, :] = jnp.ones((ONES, turned.shape[2]), B16)
+
+
+def apart(pair, axis, other):
+    twice = jnp.concatenate([pair, pair], axis=axis)
+    half = (pair.shape[axis], pair.shape[other] // 2)
+    one = lax.broadcasted_iota(jnp.int32, twice.shape, axis) < half[0]
+    two = lax.broadcasted_iota(jnp.int32, twice.shape, other) < half[1]
+    return jnp.where(one == two, twice, jnp.zeros_like(twice))
 
 
 def rows_of(units, s, seqs):
@@ -509,7 +536,7 @@
     pause=lambda: None,
 ):
     toks = hidden.shape[1]
-    span = kn.shape[1] // seqs
+    span = kn.shape[0] // seqs
     x = hidden[...].reshape(seqs * toks, D).astype(F32)
     o = jnp.concatenate(
         [jnp.transpose(rows_of(ot, s, seqs).astype(F32)) for s in range(seqs)], axis=0
@@ -524,16 +551,17 @@
     pause()
 
     def heads(i, carry):
-        for sub in range(2):
-            h = 2 * i + sub
-            row = pl.multiple_of(h * DH, DH)
-            for s in range(seqs):
-                keys = slice(s * span, (s + 1) * span)
-                e = jnp.exp(dot(kn[h, keys, :], qt_ref[s, pl.ds(row, DH), :]))
-                acc = dot(vt[h, :, keys], e.astype(B16))
-                rl = 1.0 / acc[DH : DH + 1]
-                of_ref[s, pl.ds(row, DH), :] = acc[:DH] * rl
-                rl_ref[s, h] = rl
+        col = pl.multiple_of(2 * i * DH, 2 * DH)
+        for s in range(seqs):
+            keys = slice(s * span, (s + 1) * span)
+            q_pair = apart(qt_ref[s, pl.ds(col, 2 * DH), :], 1, 0)
+            e = jnp.exp(dot(kn[keys, pl.ds(col, 2 * DH)], q_pair))
+            acc = dot(vt[i, :, keys], e.astype(B16))
+            rl = 1.0 / acc[2 * DH : 2 * DH + 1]
+            both = acc * rl
+            of_ref[s, pl.ds(col, DH), :] = both[:DH, :toks]
+            of_ref[s, pl.ds(col + DH, DH), :] = both[DH : 2 * DH, toks:]
+            rl_ref[s, i] = rl
         return carry
 
     lax.fori_loop(0, H // 2, heads, 0)
@@ -558,126 +586,6 @@
     dup = (dinner * value).astype(B16)
     da3[...] += dot_t(dgate, wg[...]) + dot_t(dup, wu[...])
     return t_dot(rows, dgate).astype(B16), t_dot(rows, dup).astype(B16), dwd
-
-
-def ffn_pair_kernel(x2_ref, og_ref, gain, wg, wu, wd, out_ref, dx2_ref, dgain_ref, *refs):
-    kept, theirs = refs[0:6], refs[6:12]
-    a3, acc, da3, own, give, got, own_d, give_d, got_d, send, recv = refs[12:]
-    step = pl.program_id(0)
-    x = lax.axis_index("shard")
-    core = lax.axis_index("rep") % 2
-    slot = step // 2
-    half = D // 2
-
-    @pl.when(step == 0)
-    def _():
-        barrier = pltpu.get_barrier_semaphore()
-        pl.semaphore_signal(
-            barrier, inc=1, device_id={"rep": partner(0)[1]}, device_id_type=MESH
-        )
-        x2 = x2_ref[...]
-        a3[...] = (x2 * scale_of(x2) * gain[2:3, :]).astype(B16)
-        acc[...] = x2
-        da3[...] = jnp.zeros_like(da3)
-        pl.semaphore_wait(barrier, 1)
-
-    def pass_wide(i, at):
-        return to_rep(give.at[i, at], got.at[i, at], send.at[i, at], recv.at[i, at], 0)
-
-    def pass_down(at):
-        return to_rep(give_d.at[at], got_d.at[at], send.at[2, at], recv.at[2, at], 0)
-
-    *wide, down = ffn_products(a3[...], og_ref[...], wg, wu, wd, acc, da3)
-    for i, dw in enumerate(wide):
-        dw = dw.reshape(2, half, dw.shape[1])
-
-        @pl.when(step % 2 == core)
-        def _(i=i, dw=dw):
-            own[i, slot] = dw
-
-        @pl.when(step % 2 != core)
-        def _(i=i, dw=dw):
-            give[i, slot] = dw
-            pass_wide(i, slot).start()
-
-    @pl.when(core == 0)
-    def _():
-        own_d[step] = down[:, :half]
-        give_d[step] = down[:, half:]
-
-    @pl.when(core != 0)
-    def _():
-        own_d[step] = down[:, half:]
-        give_d[step] = down[:, :half]
-
-    pass_down(step).start()
-
-    def both(a, b):
-        return (a.astype(F32) + b.astype(F32)).astype(B16)
-
-    def finish_wide(at):
-        for i in range(2):
-            landed(got.at[i, at], recv.at[i, at])
-            kept[2 * i + at][...] = both(own[i, at, x], got[i, at, x])
-            theirs[2 * i + at][...] = both(own[i, at, 1 - x], got[i, at, 1 - x])
-
-    @pl.when(step == 2)
-    def _():
-        finish_wide(0)
-
-    @pl.when(step == 3)
-    def _():
-        out_ref[...] = acc[...].astype(B16)
-        dv, dgain = norm_back(x2_ref[...], gain[2:3, :], da3[...])
-        dx2_ref[...] = og_ref[...].astype(F32) + dv
-        dgain_ref[...] = dgain
-        finish_wide(1)
-        for at in range(4):
-            landed(got_d.at[at], recv.at[2, at])
-        for at in range(2):
-            kept[4 + at][...] = both(own_d[2 * x + at], got_d[2 * x + at])
-            theirs[4 + at][...] = both(own_d[2 - 2 * x + at], got_d[2 - 2 * x + at])
-        for at in range(4):
-            pass_down(at).wait_send()
-        for at in range(2):
-            for i in range(2):
-                pass_wide(i, at).wait_send()
-
-
-def ffn_pair_call(x2, og, small, wg, wu, wd, collective):
-    tokens, ff = x2.shape[0], wg.shape[1]
-    half, chunk = D // 2, ff // 4
-    const = lambda s: pl.BlockSpec(s, lambda i: (0, 0))
-    parts = [(half, chunk)] * 4 + [(chunk, half)] * 2
-    outs = [((tokens, D), B16), ((tokens, D), F32), ((1, D), F32)]
-    outs += [(s, B16) for s in parts + parts]
-    dma = pltpu.SemaphoreType.DMA
-    return pl.pallas_call(
-        ffn_pair_kernel,
-        grid=(4,),
-        out_shape=[jax.ShapeDtypeStruct(s, t) for s, t in outs],
-        in_specs=[
-            const((tokens, D)),
-            const((tokens, D)),
-            const((SMALL_ROWS, D)),
-            pl.BlockSpec((D, chunk), lambda i: (0, i)),
-            pl.BlockSpec((D, chunk), lambda i: (0, i)),
-            pl.BlockSpec((chunk, D), lambda i: (i, 0)),
-        ],
-        out_specs=[const(s) for s, _ in outs],
-        scratch_shapes=[
-            pltpu.VMEM((tokens, D), B16),
-            pltpu.VMEM((tokens, D), F32),
-            pltpu.VMEM((tokens, D), F32),
-        ]
-        + [pltpu.VMEM((2, 2, 2, half, chunk), B16)] * 3
-        + [pltpu.VMEM((4, chunk, half), B16)] * 3
-        + [dma((3, 4)), dma((3, 4))],
-        compiler_params=pltpu.CompilerParams(
-            collective_id=collective, has_side_effects=True, vmem_limit_bytes=60 * 2**20
-        ),
-        name="ffn",
-    )(x2, og, small, wg, wu, wd)
 
 
 def ffn_kernel(
@@ -739,7 +647,7 @@
     done=lambda ref: None,
 ):
     toks = qt_ref.shape[2]
-    span = kn.shape[1] // seqs
+    span = kn.shape[0] // seqs
     dx2 = dx2_ref[...]
     dc = dx2.astype(B16)
     o2t = [of_ref[s].astype(B16) for s in range(seqs)]
@@ -757,25 +665,24 @@
 
     def heads(i, carry):
         col = pl.multiple_of(2 * i * DH, 2 * DH)
+        pair = pl.ds(col, 2 * DH)
         for s in range(seqs):
             keys = slice(s * span, (s + 1) * span)
-            dks, dvs = [], []
-            q_pair = jnp.transpose(qt_ref[s, pl.ds(col, 2 * DH), :].astype(F32)).astype(B16)
-            d_pair = jnp.transpose(dt[s, pl.ds(col, 2 * DH), :].astype(F32)).astype(B16)
-            for sub in range(2):
-                h = 2 * i + sub
-                row = pl.multiple_of(h * DH, DH)
-                d_rows = dt[s, pl.ds(row, DH), :]
-                prob = jnp.exp(dot(kn[h, keys, :], qt_ref[s, pl.ds(row, DH), :])) * rl_ref[s, h]
-                delta = jnp.sum(
-                    d_rows.astype(F32) * of_ref[s, pl.ds(row, DH), :], axis=0, keepdims=True
-                )
-                ds = (prob * (dot(vn[h, keys, :], d_rows) - delta)).astype(B16)
-                dqt[s, pl.ds(row, DH), :] = dot(kt[h, 0:DH, keys], ds).astype(B16)
-                dks.append(dot(ds, q_pair[:, sub * DH : (sub + 1) * DH]))
-                dvs.append(dot(prob.astype(B16), d_pair[:, sub * DH : (sub + 1) * DH]))
-            dk[keys, pl.ds(col, 2 * DH)] = jnp.concatenate(dks, axis=1).astype(B16)
-            dv[keys, pl.ds(col, 2 * DH)] = jnp.concatenate(dvs, axis=1).astype(B16)
+            q_rows, d_rows = qt_ref[s, pair, :], dt[s, pair, :]
+            q_pair = apart(jnp.transpose(q_rows.astype(F32)), 0, 1).astype(B16)
+            d_pair = apart(jnp.transpose(d_rows.astype(F32)), 0, 1).astype(B16)
+            prob = jnp.exp(dot(kn[keys, pair], apart(q_rows, 1, 0))) * rl_ref[s, i]
+            terms = d_rows.astype(F32) * of_ref[s, pair, :]
+            delta = jnp.concatenate(
+                [jnp.sum(terms[n * DH : (n + 1) * DH], axis=0, keepdims=True) for n in range(2)],
+                axis=1,
+            )
+            ds = (prob * (dot(vn[keys, pair], apart(d_rows, 1, 0)) - delta)).astype(B16)
+            dq = dot(kt[pair, keys], ds).astype(B16)
+            dqt[s, pl.ds(col, DH), :] = dq[:DH, :toks]
+            dqt[s, pl.ds(col + DH, DH), :] = dq[DH:, toks:]
+            dk[keys, pair] = dot(ds, q_pair).astype(B16)
+            dv[keys, pair] = dot(prob.astype(B16), d_pair).astype(B16)
         return carry
 
     lax.fori_loop(0, H // 2, heads, 0)
@@ -806,75 +713,52 @@
     for s in range(seqs):
         turned = jnp.transpose(do[s * toks : (s + 1) * toks]).astype(B16)
         for g in range(groups):
-            dot_ref[s * groups + g] = turned[g * width : (g + 1) * width]
-
-
-def cross_back_pair_kernel(kernel, ins, outs, far_ins, far_outs, count, *refs):
+            dot_ref[s * groups + g] = turned[g * width : (g + 1) * width].reshape(
+                dot_ref.shape[1:]
+            )
+
+
+def cross_back_moves_kernel(kernel, ins, outs, far_ins, far_outs, *refs):
     refs = list(refs)
     take = lambda n: [refs.pop(0) for _ in range(n)]
-    args, sources, results_, crossed = take(ins), take(count), take(outs), take(count)
-    scratch = take(4)
+    args, results, scratch = take(ins), take(outs), take(4)
     near_in, near_out = take(len(far_ins)), take(len(far_outs))
-    sems, *cross_sems = refs
-    moves = Moves(sems)
+    moves = Moves(refs[0])
     moves.bring([(args[i], near) for i, near in zip(far_ins, near_in)])
-    if count:
-        send, recv = cross_sems
-        barrier = pltpu.get_barrier_semaphore()
-        x = lax.axis_index("shard")
-        pl.semaphore_signal(barrier, inc=1, device_id={"shard": 1 - x}, device_id_type=MESH)
-        pl.semaphore_wait(barrier, 1)
-    copies = [
-        to_row(sources[i], crossed[i], send.at[i], recv.at[i]) for i in range(count)
-    ]
-    for copy in copies:
-        copy.start()
     for i, near in zip(far_ins, near_in):
         args[i] = near
     made = {}
     for i, near in zip(far_outs, near_out):
-        made[id(near)] = (near, results_[i])
-        results_[i] = near
+        made[id(near)] = (near, results[i])
+        results[i] = near
 
     def done(ref):
         moves.take(*made[id(ref)])
 
-    kernel(*args, *results_, *scratch, need=moves.need, done=done)
+    kernel(*args, *results, *scratch, need=moves.need, done=done)
     moves.end()
-    for copy in copies:
-        copy.wait()
-
-
-def cross_back_pair_call(kernel, outs, args, scratch, sources, collective):
+
+
+def cross_back_moves_call(kernel, outs, args, scratch):
     near = pl.BlockSpec(memory_space=pltpu.VMEM)
     anywhere = pl.BlockSpec(memory_space=pl.ANY)
-    count = len(sources)
     far_ins = [11, 7, 8, 9, 10, 13, 14, 12, 15]
     far_outs = [3, 4, 5, 6, 7, 8]
-    dma = pltpu.SemaphoreType.DMA
     scratch = [*scratch]
     scratch += [pltpu.VMEM(args[i].shape, args[i].dtype) for i in far_ins]
     scratch += [pltpu.VMEM(*outs[i]) for i in far_outs]
-    scratch += [dma((len(far_ins) + len(far_outs),))]
-    if count:
-        scratch += [dma((count,)), dma((count,))]
-        params = dict(collective_id=collective, has_side_effects=True)
-    else:
-        params = {}
+    scratch += [pltpu.SemaphoreType.DMA((len(far_ins) + len(far_outs),))]
     return pl.pallas_call(
         functools.partial(
-            cross_back_pair_kernel, kernel, len(args), len(outs), far_ins, far_outs, count
+            cross_back_moves_kernel, kernel, len(args), len(outs), far_ins, far_outs
         ),
-        out_shape=[jax.ShapeDtypeStruct(s, t) for s, t in outs]
-        + [jax.ShapeDtypeStruct(s.shape, s.dtype) for s in sources],
-        in_specs=[anywhere if i in far_ins else near for i in range(len(args))]
-        + [anywhere] * count,
-        out_specs=[anywhere if i in far_outs else near for i in range(len(outs))]
-        + [anywhere] * count,
+        out_shape=[jax.ShapeDtypeStruct(s, t) for s, t in outs],
+        in_specs=[anywhere if i in far_ins else near for i in range(len(args))],
+        out_specs=[anywhere if i in far_outs else near for i in range(len(outs))],
         scratch_shapes=scratch,
-        compiler_params=pltpu.CompilerParams(vmem_limit_bytes=60 * 2**20, **params),
+        compiler_params=pltpu.CompilerParams(vmem_limit_bytes=60 * 2**20),
         name="cross_back",
-    )(*args, *sources)
+    )(*args)
 
 
 def last_kernel(plan, hidden, grads, a1, gain, dx1, wq, wk, wv, dh_ref, dgain_ref, dwq, dwk, dwv):
@@ -890,7 +774,11 @@
         rows = []
         for s in range(p.S):
             turned = jnp.concatenate(
-                [grads[s * p.G + g, n * p.F : (n + 1) * p.F, :] for g in range(p.G)], axis=0
+                [
+                    grads[s * p.G + i // p.HG, i % p.HG, n * DH : (n + 1) * DH, :]
+                    for i in range(H)
+                ],
+                axis=0,
             )
             rows.append(jnp.transpose(turned.astype(F32)))
         d = jnp.concatenate(rows, axis=0).astype(B16)
@@ -957,12 +845,24 @@
 
 
 BITS = 4
+ROW = -1
 
 
 class Job:
-    def __init__(self, result, row, rows, col, cols, taken=None):
-        self.result, self.taken = result, taken
+    def __init__(self, result, row, rows, col, cols, order):
+        self.result, self.order = result, order
         self.row, self.rows, self.col, self.cols = row, rows, col, cols
+
+    def buffers(self):
+        half, rows, lead = self.cols // 2, self.rows, (2,)
+        shapes = [(2, rows, half)] * 2
+        for axis in self.order:
+            if axis == ROW:
+                lead = ()
+            else:
+                rows //= 2
+            shapes.append((*lead, rows, half))
+        return shapes
 
 
 def partner(bit):
@@ -1000,38 +900,35 @@
 
 
 class JobRun:
-    def __init__(self, job, sources, result, bufs, sems, index, order, depth):
-        self.order = (0, *order)
-        self.job, self.sources, self.result = job, sources, result
-        bufs = list(bufs)
-        self.x = lax.axis_index("shard")
-        if job.taken is None:
-            self.acc, self.core = bufs.pop(0), bufs.pop(0)
-            self.kept = self.acc.at[self.x]
-            self.steps = [(0, 1), (1, depth)]
-        else:
-            self.kept = bufs.pop(0)
-            self.steps = [(0, depth if job.taken == "sent" else 1)]
-        self.steps += [(n, LAG) for n in range(2, 10)]
-        self.row, *self.part = bufs
+    def __init__(self, job, source, result, bufs, sems, index):
+        self.job, self.source, self.result = job, source, result
+        self.acc, self.core, *self.part = bufs
+        self.steps = [(0, 1), (1, FIRST_LAG)] + [(n, LAG) for n in range(2, 10)]
         send, recv, local = sems
         self.send = [send.at[index, i] for i in range(9)]
         self.recv = [recv.at[index, i] for i in range(9)]
         self.local = [local.at[index, i] for i in range(2)]
         self.sent = []
-        self.bits = [partner(b)[0] for b in self.order]
+        self.x = lax.axis_index("shard")
         half = job.cols // 2
-        self.mine = pl.ds(pl.multiple_of(job.col + self.bits[0] * half, 128), half)
-        self.other = pl.ds(pl.multiple_of(job.col + (1 - self.bits[0]) * half, 128), half)
+        core = partner(0)[0]
+        self.mine = pl.ds(pl.multiple_of(job.col + core * half, 128), half)
+        self.other = pl.ds(pl.multiple_of(job.col + (1 - core) * half, 128), half)
         self.all = pl.ds(job.row, job.rows)
-        self.first = [0]
-        count = job.rows
-        for b in range(1, BITS):
-            count //= 2
-            self.first.append(self.first[-1] + self.bits[b] * count)
-
-    def count(self, level):
-        return self.job.rows // 2**level
+        self.plan, self.back = [], []
+        owners, first, count = (0, 1), 0, job.rows
+        for axis in job.order:
+            if axis == ROW:
+                keep = give = (first, count)
+                owners, others = (self.x,), (1 - self.x,)
+            else:
+                count //= 2
+                bit = partner(axis)[0]
+                keep, give = (first + bit * count, count), (first + (1 - bit) * count, count)
+                self.back.insert(0, (axis, (first, 2 * count), give))
+                first, others = keep[0], owners
+            self.plan.append((axis, owners, keep, others, give))
+        self.last = (first, count)
 
     def span(self, first, count):
         return pl.ds(pl.multiple_of(first, 16), count)
@@ -1039,98 +936,62 @@
     def out(self, first, count):
         return self.result.at[self.span(self.job.row + first, count), self.mine]
 
-    def go(self, copy):
+    def held(self, owners, rows):
+        at = slice(None) if len(owners) == 2 else owners[0]
+        return self.acc.at[at, self.span(*rows)]
+
+    def go(self, n, source, target, axis):
+        copy = (to_row if axis == ROW else to_rep)(
+            source, target, self.send[n], self.recv[n], *(() if axis == ROW else (axis,))
+        )
         copy.start()
         self.sent.append(copy)
-
-    def begin(self):
-        if self.job.taken is None:
-            (source,) = self.sources
-            pltpu.make_async_copy(
-                source.at[:, self.all, self.mine], self.acc, self.local[0]
-            ).start()
-            theirs = source.at[:, self.all, self.other]
-            self.go(to_rep(theirs, self.core, self.send[0], self.recv[0], 0))
-            return
-        mine, theirs = self.sources
-        pltpu.make_async_copy(mine, self.kept, self.local[0]).start()
-        if self.job.taken == "sent":
-            self.go(to_row(theirs, self.row, self.send[1], self.recv[1]))
-        else:
-            pltpu.make_async_copy(theirs, self.row, self.recv[1]).start()
 
     def stage(self, n):
         job = self.job
         if n == 0:
-            self.begin()
-        elif n == 1:
-            landed(self.acc, self.local[0])
-            landed(self.core, self.recv[0])
-            for i in range(2):
-                add_into(self.acc.at[i], self.core.at[i], job.rows)
-            self.go(to_row(self.acc.at[1 - self.x], self.row, self.send[1], self.recv[1]))
-        elif n == 2:
-            if job.taken is not None:
-                landed(self.kept, self.local[0])
-            landed(self.row, self.recv[1])
-            add_into(self.kept, self.row, job.rows)
-            self.give(1)
-        elif n in (3, 4):
-            self.take(n - 2)
-            self.give(n - 1)
-        elif n == 5:
-            self.take(3)
-            piece = self.kept.at[self.span(self.first[3], self.count(3))]
-            place = self.out(self.first[3], self.count(3))
-            pltpu.make_async_copy(piece, place, self.local[1]).start()
-            self.go(to_rep(piece, place, self.send[5], self.recv[5], self.order[3]))
-        elif n in (6, 7, 8):
-            level = 9 - n
+            pltpu.make_async_copy(
+                self.source.at[:, self.all, self.mine], self.acc, self.local[0]
+            ).start()
+            self.go(0, self.source.at[:, self.all, self.other], self.core, 0)
+        elif n <= 5:
+            if n == 1:
+                landed(self.acc, self.local[0])
+                landed(self.core, self.recv[0])
+                for i in range(2):
+                    add_into(self.acc.at[i], self.core.at[i], job.rows)
+            else:
+                _, owners, keep, _, _ = self.plan[n - 2]
+                terms = self.part[n - 2]
+                landed(terms, self.recv[n - 1])
+                for i, owner in enumerate(owners):
+                    add_into(
+                        self.held((owner,), keep),
+                        terms.at[i] if len(owners) == 2 else terms,
+                        keep[1],
+                    )
+            if n < 5:
+                axis, _, _, others, give = self.plan[n - 1]
+                self.go(n, self.held(others, give), self.part[n - 1], axis)
+            else:
+                piece, place = self.held((self.x,), self.last), self.out(*self.last)
+                pltpu.make_async_copy(piece, place, self.local[1]).start()
+                self.go(5, piece, place, self.back[0][0])
+        elif n <= 8:
             if n == 6:
-                landed(self.out(self.first[3], self.count(3)), self.local[1])
-            self.landed_at(level)
-            place = self.out(self.first[level - 1], self.count(level - 1))
-            self.go(
-                to_rep(place, place, self.send[n], self.recv[n], self.order[level - 1])
-            )
+                landed(self.out(*self.last), self.local[1])
+            _, rows, came = self.back[n - 6]
+            landed(self.out(*came), self.recv[n - 1])
+            place = self.out(*rows)
+            self.go(n, place, place, self.back[n - 5][0] if n < 8 else 0)
         else:
             landed(self.result.at[self.all, self.other], self.recv[8])
             for copy in self.sent:
                 copy.wait_send()
 
-    def give(self, level):
-        count = self.count(level)
-        first = self.first[level - 1] + (1 - self.bits[level]) * count
-        self.go(
-            to_rep(
-                self.kept.at[self.span(first, count)],
-                self.part[level - 1],
-                self.send[level + 1],
-                self.recv[level + 1],
-                self.order[level],
-            )
-        )
-
-    def take(self, level):
-        landed(self.part[level - 1], self.recv[level + 1])
-        count = self.count(level)
-        rows = self.span(self.first[level], count)
-        add_into(self.kept.at[rows], self.part[level - 1], count)
-
-    def landed_at(self, level):
-        count = self.count(level)
-        first = self.first[level - 1] + (1 - self.bits[level]) * count
-        landed(self.out(first, count), self.recv[8 - level])
-
 
 def job_buffers(job):
-    half = job.cols // 2
-    if job.taken is None:
-        shapes = [(2, job.rows, half)] * 2
-    else:
-        shapes = [(job.rows, half)]
-    shapes += [(job.rows // 2**b, half) for b in range(BITS)]
-    return [pltpu.VMEM(s, B16) for s in shapes]
+    return [pltpu.VMEM(shape, B16) for shape in job.buffers()]
 
 
 class SmallRun:
@@ -1242,27 +1103,29 @@
             self.tick()
 
 
-def jobs_of(result, rows, cols):
+def jobs_of(result, rows, cols, orders):
     wide = cols // 2 if cols > 1024 else cols
     tall = rows // 2 if rows > 512 else rows
     return [
-        Job(result, row, tall, col, wide)
+        Job(result, row, tall, col, wide, next(orders))
         for row in range(0, rows, tall)
         for col in range(0, cols, wide)
     ]
 
 
+EARLY = [(ROW, 1, 2, 3), (ROW, 2, 1, 3), (ROW, 1, 2, 3), (ROW, 1, 2, 3)]
+LATE = [(ROW, 1, 2, 3)] * 3
 SMALL_ROWS = 16
-HOSTED = None
-X_DEPTH = 3
+FETCH_LAG = 3
+FIRST_LAG = 3
 LAG = 2
 TICKS = (4, 1, 1, 2)
 
 
-def tail_kernel(p, jobs, counts, arrays, *refs):
+def tail_kernel(p, jobs, early, arrays, *refs):
     refs = list(refs)
     take = lambda n: [refs.pop(0) for _ in range(n)]
-    given = [take(n) for n in counts]
+    sources = take(early)
     dot_, denc, *far = take(7)
     lines, rl_ref, hidden, a1, dx1, dgc, dgf = take(7)
     results = take(arrays)
@@ -1279,13 +1142,12 @@
     sems = take(3)
     moves = Moves(move_sems)
     moves.bring(zip(far, held))
-    ready = len(given)
-    given += [[ref] for ref in late]
+    sources = sources + late
     runs = []
-    for i, (job, pair) in enumerate(zip(jobs, given)):
-        bufs = take(len(job_buffers(job)))
-        order = (2, 1, 3) if i % 4 == 1 else (1, 2, 3)
-        runs.append(JobRun(job, pair, results[job.result], bufs, sems, i, order, X_DEPTH))
+    for i, job in enumerate(jobs):
+        bufs = take(len(job.buffers()))
+        runs.append(JobRun(job, sources[job.result], results[job.result], bufs, sems, i))
+    ready = len(jobs) - 3
     enc_run = EncodedRun(denc, denc_out, enc_bufs, enc_send, enc_recv, enc_load.at[0], LAG)
 
     me = lax.axis_index("rep")
@@ -1306,21 +1168,49 @@
     pipeline = Pipeline()
     pipeline.add([*runs[:2], enc_run, *runs[2:ready]])
     tick = pipeline.tick
-    for u in range(p.U):
-        start_either(
-            me, u * p.W + mine, dot_.at[u], dout.at[slot], rows_send.at[u], rows_recv.at[slot]
-        )
+    def outward(u, h):
+        to, sem = u * p.W + mine, rows_recv.at[slot, h]
+        return me, to, dot_.at[u, h], dout.at[slot, h], rows_send.at[u, h], sem
+
+    def give(k, j, h):
+        to = (w + k) % p.W
+        return remote(
+            dkv.at[p.source(j, to), h],
+            part.at[k - 1, j, h],
+            part_sem.at[k - 1, j, h],
+            got_sem.at[k - 1, j, h],
+            me - w + to,
+        )
+
+    def returned(j, h):
+        r, sem = p.source(j, w), ret_recv.at[unit, h]
+        return me, r, out.at[j, h], grads.at[unit, h], ret_send.at[j, h], sem
+
+    def return_all(h):
+        for j in range(p.J):
+            total = dkv[p.source(j, w), h].astype(F32)
+            for k in range(1, p.W):
+                landed(part.at[k - 1, j, h], got_sem.at[k - 1, j, h])
+                total = total + part[k - 1, j, h].astype(F32)
+            out[j, h, 0:DH, :] = dq[j, h]
+            out[j, h, DH : 3 * DH, :] = total.astype(B16)
+            start_either(*returned(j, h))
+
+    for h in range(p.HG):
+        for u in range(p.U):
+            start_either(*outward(u, h))
     tick(TICKS[0])
-    for j in range(p.J):
-        landed(dout.at[j], rows_recv.at[j])
     lines_at = lax.broadcasted_iota(jnp.int32, (SMALL_ROWS, D), 0)
     block = jnp.zeros((SMALL_ROWS, D), F32)
     moves.need(recv, of_ref)
     for h in range(p.HG):
+        for j in range(p.J):
+            landed(dout.at[j, h], rows_recv.at[j, h])
+        between = functools.partial(return_all, h - 1) if h > 0 else None
         sums = back_head(
             p,
             w,
-            h * DH,
+            h,
             line_of(p, lines, group * p.HG + h),
             recv,
             dout,
@@ -1329,37 +1219,20 @@
             dq,
             dkv,
             *back,
-        )
+            between=between,
+        )
+        for j in range(p.J):
+            for k in range(1, p.W):
+                give(k, j, h).start()
         sums = jnp.concatenate([sums, jnp.zeros((1, D - 2 * p.T), F32)], axis=1)
         block = jnp.where(lines_at == 3 + group * p.HG + h, sums, block)
         tick(TICKS[1])
-
-    def give(k, j):
-        to = (w + k) % p.W
-        return remote(
-            dkv.at[p.source(j, to)],
-            part.at[k - 1, j],
-            part_sem.at[k - 1, j],
-            got_sem.at[k - 1, j],
-            me - w + to,
-        )
-
-    for j in range(p.J):
-        for k in range(1, p.W):
-            give(k, j).start()
     tick(TICKS[2])
-    for j in range(p.J):
-        r = p.source(j, w)
-        total = dkv[r].astype(F32)
-        for k in range(1, p.W):
-            landed(part.at[k - 1, j], got_sem.at[k - 1, j])
-            total = total + part[k - 1, j].astype(F32)
-        out[j, 0 : p.F, :] = dq[j]
-        out[j, p.F : 3 * p.F, :] = total.astype(B16)
-        start_either(me, r, out.at[j], grads.at[unit], ret_send.at[j], ret_recv.at[unit])
+    return_all(p.HG - 1)
     tick(TICKS[3])
     for u in range(p.U):
-        landed(grads.at[u], ret_recv.at[u])
+        for h in range(p.HG):
+            landed(grads.at[u, h], ret_recv.at[u, h])
     moves.need(wq, wk, wv)
     dgain = last_products(p, hidden, grads, a1, lines, dx1, wq, wk, wv, dh_ref, *late)
     for i, row in enumerate((dgain, dgc[...], dgf[...])):
@@ -1368,39 +1241,34 @@
     pipeline.add([*runs[ready:], SmallRun(small_sums, small_terms, small_send, small_recv)])
     pipeline.finish()
     small[...] = small_sums[BITS + 1]
-    for u in range(p.U):
-        end_either(
-            me, u * p.W + mine, dot_.at[u], dout.at[slot], rows_send.at[u], rows_recv.at[slot]
-        )
-    for j in range(p.J):
-        r = p.source(j, w)
-        end_either(me, r, out.at[j], grads.at[unit], ret_send.at[j], ret_recv.at[unit])
-        for k in range(1, p.W):
-            give(k, j).wait_send()
-
-
-def tail_call(p, work, dot_, denc, far, held, collective):
+    moves.end()
+    for h in range(p.HG):
+        for u in range(p.U):
+            end_either(*outward(u, h))
+        for j in range(p.J):
+            end_either(*returned(j, h))
+            for k in range(1, p.W):
+                give(k, j, h).wait_send()
+
+
+def tail_call(p, early, dot_, denc, far, held, collective):
     half = D // 2
-    jobs = [job for job, _ in work]
-    shapes = []
-    for result in range(1 + max(job.result for job in jobs)):
-        parts = [job for job in jobs if job.result == result]
-        shapes.append((max(j.row + j.rows for j in parts), max(j.col + j.cols for j in parts)))
-    for _ in range(3):
-        jobs.append(Job(len(shapes), 0, half, 0, D))
-        shapes.append((half, D))
-    sources = [s for _, pair in work for s in pair]
+    shapes = [g.shape[1:] for g in early] + [(half, D)] * 3
+    turn = itertools.cycle(EARLY)
+    jobs = [job for i in range(len(early)) for job in jobs_of(i, *shapes[i], turn)]
+    jobs += [Job(len(early) + i, 0, half, 0, D, order) for i, order in enumerate(LATE)]
+    sources = early
     piece = denc.shape[0] // (p.S * p.R)
     denc = denc.reshape((p.S,) + (2,) * BITS + (piece, D))
     dma = pltpu.SemaphoreType.DMA
     others = max(p.W - 1, 1)
     scratch = [
-        pltpu.VMEM((p.J, p.F, p.T), B16),
-        pltpu.VMEM((p.J, p.F, p.T), B16),
-        pltpu.VMEM((p.R, 2 * p.F, p.T), B16),
-        pltpu.VMEM((others, p.J, 2 * p.F, p.T), B16),
-        pltpu.VMEM((p.J, 3 * p.F, p.T), B16),
-        pltpu.VMEM((p.U, 3 * p.F, p.T), B16),
+        pltpu.VMEM((p.J, p.HG, DH, p.T), B16),
+        pltpu.VMEM((p.J, p.HG, DH, p.T), B16),
+        pltpu.VMEM((p.R, p.HG, 2 * DH, p.T), B16),
+        pltpu.VMEM((others, p.J, p.HG, 2 * DH, p.T), B16),
+        pltpu.VMEM((p.J, p.HG, 3 * DH, p.T), B16),
+        pltpu.VMEM((p.U, p.HG, 3 * DH, p.T), B16),
     ]
     scratch += [pltpu.VMEM((2, half, D), B16)] * 3
     scratch += [pltpu.VMEM(a.shape, a.dtype) for a in far]
@@ -1415,12 +1283,12 @@
     ]
     scratch += back_scratch(p)
     scratch += [
-        dma((p.U,)),
-        dma((p.J,)),
-        dma((others, p.J)),
-        dma((others, p.J)),
-        dma((p.J,)),
-        dma((p.U,)),
+        dma((p.U, p.HG)),
+        dma((p.J, p.HG)),
+        dma((others, p.J, p.HG)),
+        dma((others, p.J, p.HG)),
+        dma((p.J, p.HG)),
+        dma((p.U, p.HG)),
         dma((BITS + 1,)),
         dma((BITS + 1,)),
         dma((len(jobs), 9)),
@@ -1432,7 +1300,7 @@
     anywhere = pl.BlockSpec(memory_space=pl.ANY)
     near = pl.BlockSpec(memory_space=pltpu.VMEM)
     *sums, small, dh, denc = pl.pallas_call(
-        functools.partial(tail_kernel, p, jobs, [len(pair) for _, pair in work], len(shapes)),
+        functools.partial(tail_kernel, p, jobs, len(early), len(shapes)),
         out_shape=[jax.ShapeDtypeStruct(s, B16) for s in shapes]
         + [
             jax.ShapeDtypeStruct((SMALL_ROWS, D), F32),
@@ -1687,83 +1555,108 @@
                 fetches[relayed].relay()
                 relayed += 1
 
+    def slot():
+        begin()
+        if started - relayed > FETCH_LAG or started == len(fetches):
+            pass_on()
+
     begin(3)
     enc_copy(0).start()
     landed(their_small, small_recv)
     small[...] = mine_small[...] + their_small[...]
     enc_landed(0)
     enc_copy(1).start()
-    pass_on()
-    begin()
+    pass_on(2)
     enc_landed(1)
-    pass_on()
-    begin()
     enc_copy(2).start()
     pass_on()
-    begin()
+    begin(2)
     fetches[2].relay_more()
     more = 3
     for fetch, far in zip(fetches[:3], far_mats):
         fetch.finish()
         moves.take(fetch.out, far)
     project_kernel(p, hidden, small, *mats[:3], a1, send)
-    for u in range(p.U):
-        start_either(
-            me, u * p.W + mine, send.at[u], recv.at[me], tok_send.at[u], tok_recv.at[me]
-        )
+
+    def token(u, h):
+        to, sem = u * p.W + mine, tok_recv.at[me, h]
+        return me, to, send.at[u, h], recv.at[me, h], tok_send.at[u, h], sem
+
+    def relay(k, j, h):
+        r = p.source(j, w)
+        part = recv.at[r, h, pl.ds(DH, 2 * DH)]
+        to = me - w + (w + k) % p.W
+        return remote(part, part, relay_sem.at[k - 1, j, h], tok_recv.at[r, h], to)
+
+    def returned(j, h):
+        r, sem = p.source(j, w), back_recv.at[unit, h]
+        return me, r, o_ref.at[j, h], ot.at[unit, h], back_send.at[j, h], sem
+
+    def relay_all(h):
+        for j in range(p.J):
+            r = p.source(j, w)
+            landed(recv.at[r, h], tok_recv.at[r, h])
+            for k in range(1, p.W):
+                relay(k, j, h).start()
+
+    def relayed_all(h):
+        for k in range(1, p.W):
+            for j in range(p.J):
+                r = p.source(j, (w + k) % p.W)
+                landed(recv.at[r, h, pl.ds(DH, 2 * DH)], tok_recv.at[r, h])
+
+    def send_all(h):
+        for u in range(p.U):
+            start_either(*token(u, h))
+
+    send_all(0)
     enc_landed(2)
     enc_copy(3).start()
     begin()
     pass_on(2)
-    begin()
     enc_landed(3)
     moves.take(enc, far_enc)
     fetches[4].relay_more()
     more = 5
-    for i, natural, turned in ((3, kn, kt), (4, vn, vt)):
+
+    def encode(i, natural, turned):
         fetches[i].finish()
         moves.take(mats[i], far_mats[i])
         encode_one(enc, mats[i], natural, turned)
-        pass_on()
-        begin()
-
-    def relay(k, j):
-        part = recv.at[p.source(j, w), pl.ds(p.F, 2 * p.F)]
-        to = me - w + (w + k) % p.W
-        return remote(part, part, relay_sem.at[k - 1, j], tok_recv.at[p.source(j, w)], to)
-
-    for j in range(p.J):
-        landed(recv.at[p.source(j, w)], tok_recv.at[p.source(j, w)])
-        for k in range(1, p.W):
-            relay(k, j).start()
-    pass_on()
-    begin()
-    for k in range(1, p.W):
-        for j in range(p.J):
-            r = p.source(j, (w + k) % p.W)
-            landed(recv.at[r, pl.ds(p.F, 2 * p.F)], tok_recv.at[r])
-    for made, far in ((recv, far_recv), (kn, far_kn), (kt, far_kt), (vn, far_vn)):
+        slot()
+
+    encode(3, kn, kt)
+    if p.HG > 1:
+        send_all(1)
+    relay_all(0)
+    encode(4, vn, vt)
+    for h in range(2, p.HG):
+        send_all(h)
+    for made, far in ((kn, far_kn), (kt, far_kt), (vn, far_vn)):
         moves.take(made, far)
+    slot()
+    relayed_all(0)
     for h in range(p.HG):
         line = line_of(p, small, group * p.HG + h)
-        attend_head(p, w, h * DH, line, recv, o_ref, of_ref, rl_ref.at[h], *att)
+        between = functools.partial(relay_all, h + 1) if h + 1 < p.HG else None
+        attend_head(p, w, h, line, recv, o_ref, of_ref, rl_ref.at[h], *att, between=between)
+        for j in range(p.J):
+            start_either(*returned(j, h))
+        slot()
+        if h + 1 < p.HG:
+            relayed_all(h + 1)
+    moves.take(recv, far_recv)
+    slot()
+    while more < 8:
         pass_on()
-        begin()
-    for j in range(p.J):
-        r = p.source(j, w)
-        start_either(me, r, o_ref.at[j], ot.at[unit], back_send.at[j], back_recv.at[unit])
-    pass_on()
-    begin()
     for fetch, far in zip(fetches[5:8], far_mats[5:]):
         fetch.finish()
         moves.take(fetch.out, far)
     for u in range(p.U):
-        landed(ot.at[u], back_recv.at[u])
-
-    def pause():
-        pass_on()
-        begin()
-
+        for h in range(p.HG):
+            landed(ot.at[u, h], back_recv.at[u, h])
+
+    pause = slot
     cross_kernel(
         p.S, hidden, ot, mats[5], small, mats[6], mats[7], kn, vt, x1, x2, a2, qt2, of2, rl2, pause
     )
@@ -1778,15 +1671,13 @@
     share.wait_send()
     for n in range(BITS):
         enc_copy(n).wait_send()
-    for u in range(p.U):
-        end_either(
-            me, u * p.W + mine, send.at[u], recv.at[me], tok_send.at[u], tok_recv.at[me]
-        )
-    for j in range(p.J):
-        r = p.source(j, w)
-        end_either(me, r, o_ref.at[j], ot.at[unit], back_send.at[j], back_recv.at[unit])
-        for k in range(1, p.W):
-            relay(k, j).wait_send()
+    for h in range(p.HG):
+        for u in range(p.U):
+            end_either(*token(u, h))
+        for j in range(p.J):
+            end_either(*returned(j, h))
+            for k in range(1, p.W):
+                relay(k, j, h).wait_send()
 
 
 def head_call(p, masters, hidden, encoded, gains, table, buckets, collective):
@@ -1798,26 +1689,26 @@
     anywhere = pl.BlockSpec(memory_space=pl.ANY)
     outs = [((2, half, D), B16)] * 8 + [((2, *s), B16) for s in wides]
     inner = [
-        ((p.R, 3 * p.F, p.T), B16),
+        ((p.R, p.HG, 3 * DH, p.T), B16),
         ((p.S,) + (2,) * BITS + (piece, D), B16),
-        ((H, enc_rows, DH), B16),
-        ((H, DH + ONES, enc_rows), B16),
-        ((H, enc_rows, DH), B16),
+        ((enc_rows, D), B16),
+        ((D, enc_rows), B16),
+        ((enc_rows, D), B16),
     ]
     outs += inner
-    inner = [((2, half, D), B16)] * 8 + inner + [inner[3]]
+    inner = [((2, half, D), B16)] * 8 + inner + [((H // 2, 2 * DH + ONES, enc_rows), B16)]
     outs += [
         ((SMALL_ROWS, D), F32),
         ((tokens, D), B16),
-        ((p.J, p.F, p.T), F32),
+        ((p.J, p.HG, DH, p.T), F32),
         ((p.HG, p.NP, 1, 2 * p.T), F32),
-        ((p.U, p.F, p.T), B16),
+        ((p.U, p.HG, DH, p.T), B16),
         ((tokens, D), F32),
         ((tokens, D), F32),
         ((tokens, D), B16),
         ((p.S, D, p.T), B16),
         ((p.S, D, p.T), F32),
-        ((p.S, H, 1, p.T), F32),
+        ((p.S, H // 2, 1, 2 * p.T), F32),
     ]
     parts = [(half, D)] * 8
     for rows, cols in wides:
@@ -1828,8 +1719,8 @@
     dma = pltpu.SemaphoreType.DMA
     scratch = [pltpu.VMEM(s, t) for s, t in inner] + [dma((13,))]
     scratch += [
-        pltpu.VMEM((p.U, 3 * p.F, p.T), B16),
-        pltpu.VMEM((p.J, p.F, p.T), B16),
+        pltpu.VMEM((p.U, p.HG, 3 * DH, p.T), B16),
+        pltpu.VMEM((p.J, p.HG, DH, p.T), B16),
         pltpu.VMEM((SMALL_ROWS, D), F32),
         pltpu.VMEM((SMALL_ROWS, D), F32),
     ]
@@ -1841,11 +1732,11 @@
     scratch += [dma((count,)), dma((count,)), dma((count, 3)), dma((count, 3))]
     scratch += [dma, dma, dma((BITS,)), dma((BITS,))]
     scratch += [
-        dma((p.U,)),
-        dma((max(p.W - 1, 1), p.J)),
-        dma((p.R,)),
-        dma((p.J,)),
-        dma((p.U,)),
+        dma((p.U, p.HG)),
+        dma((max(p.W - 1, 1), p.J, p.HG)),
+        dma((p.R, p.HG)),
+        dma((p.J, p.HG)),
+        dma((p.U, p.HG)),
     ]
     return pl.pallas_call(
         functools.partial(head_kernel, p),
@@ -1952,13 +1843,13 @@
 
         a1, send = plain_call(
             functools.partial(project_kernel, p),
-            [((tokens, D), B16), ((p.U, 3 * p.F, toks), B16)],
+            [((tokens, D), B16), ((p.U, p.HG, 3 * DH, toks), B16)],
             (hidden, small, wq, wk, wv),
             "project",
         )
         recv = comm_call(
             functools.partial(scatter_tokens, p),
-            (p.R, 3 * p.F, toks),
+            (p.R, p.HG, 3 * DH, toks),
             (send,),
             [dma((p.U,)), dma((max(p.W - 1, 1), p.J)), dma((p.R,))],
             0,
@@ -1967,10 +1858,10 @@
         ckn, ckt, cvn, cvt = plain_call(
             encode_kernel,
             [
-                ((H, enc_rows, DH), B16),
-                ((H, DH + ONES, enc_rows), B16),
-                ((H, enc_rows, DH), B16),
-                ((H, DH + ONES, enc_rows), B16),
+                ((enc_rows, D), B16),
+                ((D, enc_rows), B16),
+                ((enc_rows, D), B16),
+                ((H // 2, 2 * DH + ONES, enc_rows), B16),
             ],
             (enc, wck, wcv),
             "encode",
@@ -1979,14 +1870,14 @@
             functools.partial(attend_kernel, p),
             grid=(p.HG,),
             out_shape=[
-                jax.ShapeDtypeStruct((p.J, p.F, toks), B16),
-                jax.ShapeDtypeStruct((p.J, p.F, toks), F32),
+                jax.ShapeDtypeStruct((p.J, p.HG, DH, toks), B16),
+                jax.ShapeDtypeStruct((p.J, p.HG, DH, toks), F32),
                 jax.ShapeDtypeStruct((p.HG, p.NP, 1, 2 * toks), F32),
             ],
-            in_specs=[whole((p.R, 3 * p.F, toks)), whole((SMALL_ROWS, D))],
+            in_specs=[whole((p.R, p.HG, 3 * DH, toks)), whole((SMALL_ROWS, D))],
             out_specs=[
-                whole((p.J, p.F, toks)),
-                whole((p.J, p.F, toks)),
+                whole((p.J, p.HG, DH, toks)),
+                whole((p.J, p.HG, DH, toks)),
                 whole((p.HG, p.NP, 1, 2 * toks)),
             ],
             scratch_shapes=attend_scratch(p),
@@ -1995,7 +1886,7 @@
         )(recv, small)
         ot = comm_call(
             functools.partial(return_tokens, p),
-            (p.U, p.F, toks),
+            (p.U, p.HG, DH, toks),
             (o,),
             [dma((p.J,)), dma((p.U,))],
             1,
@@ -2010,65 +1901,54 @@
                 ((tokens, D), B16),
                 ((seqs, D, toks), B16),
                 ((seqs, D, toks), F32),
-                ((seqs, H, 1, toks), F32),
+                ((seqs, H // 2, 1, 2 * toks), F32),
             ],
             (hidden, ot, wo, small, wcq, wco, ckn, cvt),
             "cross",
         )
 
-    if paired and HOSTED is not None:
-        output, dx2, dg_ffn, *parts = ffn_pair_call(
-            x2, out_grad.reshape(tokens, D), small, wg, wu, wd, 1
-        )
-        kept, theirs = parts[:6], parts[6:]
-        half, wide = D // 2, ff // 2
-        jobs = [Job(i // 2, 0, half, (i % 2) * wide, wide) for i in range(4)]
-        jobs += [Job(2, i * (ff // 4), ff // 4, 0, D) for i in range(2)]
-        for i, job in enumerate(jobs):
-            job.taken = "here" if i < HOSTED else "sent"
-    else:
-        chunk = min(512, ff)
-        const = lambda s: pl.BlockSpec(s, lambda i: (0, 0))
-        output, dx2, dg_ffn, dwg, dwu, dwd = pl.pallas_call(
-            ffn_kernel,
-            grid=(ff // chunk,),
-            out_shape=[
-                jax.ShapeDtypeStruct((tokens, D), B16),
-                jax.ShapeDtypeStruct((tokens, D), F32),
-                jax.ShapeDtypeStruct((1, D), F32),
-                jax.ShapeDtypeStruct((D, ff), B16),
-                jax.ShapeDtypeStruct((D, ff), B16),
-                jax.ShapeDtypeStruct((ff, D), B16),
-            ],
-            in_specs=[
-                const((tokens, D)),
-                const((tokens, D)),
-                const((SMALL_ROWS, D)),
-                pl.BlockSpec((D, chunk), lambda i: (0, i)),
-                pl.BlockSpec((D, chunk), lambda i: (0, i)),
-                pl.BlockSpec((chunk, D), lambda i: (i, 0)),
-            ],
-            out_specs=[
-                const((tokens, D)),
-                const((tokens, D)),
-                const((1, D)),
-                pl.BlockSpec((D, chunk), lambda i: (0, i)),
-                pl.BlockSpec((D, chunk), lambda i: (0, i)),
-                pl.BlockSpec((chunk, D), lambda i: (i, 0)),
-            ],
-            scratch_shapes=[
-                pltpu.VMEM((tokens, D), B16),
-                pltpu.VMEM((tokens, D), F32),
-                pltpu.VMEM((tokens, D), F32),
-            ],
-            compiler_params=pltpu.CompilerParams(vmem_limit_bytes=56 * 2**20),
-            name="ffn",
-        )(x2, out_grad.reshape(tokens, D), small, wg, wu, wd)
+    chunk = min(512, ff)
+    const = lambda s: pl.BlockSpec(s, lambda i: (0, 0))
+    output, dx2, dg_ffn, dwg, dwu, dwd = pl.pallas_call(
+        ffn_kernel,
+        grid=(ff // chunk,),
+        out_shape=[
+            jax.ShapeDtypeStruct((tokens, D), B16),
+            jax.ShapeDtypeStruct((tokens, D), F32),
+            jax.ShapeDtypeStruct((1, D), F32),
+            jax.ShapeDtypeStruct((D, ff), B16),
+            jax.ShapeDtypeStruct((D, ff), B16),
+            jax.ShapeDtypeStruct((ff, D), B16),
+        ],
+        in_specs=[
+            const((tokens, D)),
+            const((tokens, D)),
+            const((SMALL_ROWS, D)),
+            pl.BlockSpec((D, chunk), lambda i: (0, i)),
+            pl.BlockSpec((D, chunk), lambda i: (0, i)),
+            pl.BlockSpec((chunk, D), lambda i: (i, 0)),
+        ],
+        out_specs=[
+            const((tokens, D)),
+            const((tokens, D)),
+            const((1, D)),
+            pl.BlockSpec((D, chunk), lambda i: (0, i)),
+            pl.BlockSpec((D, chunk), lambda i: (0, i)),
+            pl.BlockSpec((chunk, D), lambda i: (i, 0)),
+        ],
+        scratch_shapes=[
+            pltpu.VMEM((tokens, D), B16),
+            pltpu.VMEM((tokens, D), F32),
+            pltpu.VMEM((tokens, D), F32),
+        ],
+        compiler_params=pltpu.CompilerParams(vmem_limit_bytes=56 * 2**20),
+        name="ffn",
+    )(x2, out_grad.reshape(tokens, D), small, wg, wu, wd)
 
     back_outs = [
         ((tokens, D), F32),
         ((1, D), F32),
-        ((p.U, p.F, toks), B16),
+        ((p.U, p.HG, DH, toks), B16),
         ((enc_rows, D), B16),
     ] + [((D, D), B16)] * 5
     back_args = (dx2, x1, a2, small, qt2, of2, rl2, ckn, ckt, cvn, enc, wco, wcq, wck, wcv, wo, ot)
@@ -2080,31 +1960,18 @@
     ]
     back_kernel = functools.partial(cross_back_kernel, seqs, p.G)
     if paired:
-        hosted = [] if HOSTED is None else theirs[:HOSTED]
-        got = cross_back_pair_call(back_kernel, back_outs, back_args, back_scratch_, hosted, 2)
-        crossed = got[9:]
-        got = got[:9]
+        got = cross_back_moves_call(back_kernel, back_outs, back_args, back_scratch_)
     else:
         got = plain_call(back_kernel, back_outs, back_args, "cross_back", scratch=back_scratch_)
     dx1, dg_cross, dot_, denc, dwco, dwcq, dwck, dwcv, dwo = got
     if paired:
-        half = D // 2
-        if HOSTED is None:
-            work = []
-            for i, g in enumerate((dwg, dwu, dwd)):
-                g = g.reshape(2, g.shape[0] // 2, g.shape[1])
-                work += [(job, [g]) for job in jobs_of(i, *g.shape[1:])]
-        else:
-            work = list(zip(jobs, zip(kept, [*crossed, *theirs[HOSTED:]])))
-            if HOSTED == 3:
-                work = [work[i] for i in (3, 0, 4, 1, 5, 2)]
-        work += [
-            (Job(3 + i, 0, half, 0, D), [g.reshape(2, half, D)])
-            for i, g in enumerate((dwo, dwcq, dwck, dwcv, dwco))
+        early = [
+            g.reshape(2, g.shape[0] // 2, g.shape[1])
+            for g in (dwg, dwu, dwd, dwo, dwcq, dwck, dwcv, dwco)
         ]
         sums, block, hidden_grad, encoded_grad = tail_call(
             p,
-            work,
+            early,
             dot_,
             denc,
             (recv, of, wq, wk, wv),
@@ -2129,7 +1996,7 @@
         )
         dout = comm_call(
             functools.partial(scatter_rows, p),
-            (p.J, p.F, toks),
+            (p.J, p.HG, DH, toks),
             (dot_,),
             [dma((p.U,)), dma((p.J,))],
             2,
@@ -2139,20 +2006,20 @@
             functools.partial(attend_back_kernel, p),
             grid=(p.HG,),
             out_shape=[
-                jax.ShapeDtypeStruct((p.J, p.F, toks), B16),
-                jax.ShapeDtypeStruct((p.R, 2 * p.F, toks), B16),
+                jax.ShapeDtypeStruct((p.J, p.HG, DH, toks), B16),
+                jax.ShapeDtypeStruct((p.R, p.HG, 2 * DH, toks), B16),
                 jax.ShapeDtypeStruct((p.HG, 1, 2 * toks), F32),
             ],
             in_specs=[
-                whole((p.R, 3 * p.F, toks)),
+                whole((p.R, p.HG, 3 * DH, toks)),
                 whole((SMALL_ROWS, D)),
-                whole((p.J, p.F, toks)),
-                whole((p.J, p.F, toks)),
+                whole((p.J, p.HG, DH, toks)),
+                whole((p.J, p.HG, DH, toks)),
                 whole((p.HG, p.NP, 1, 2 * toks)),
             ],
             out_specs=[
-                whole((p.J, p.F, toks)),
-                whole((p.R, 2 * p.F, toks)),
+                whole((p.J, p.HG, DH, toks)),
+                whole((p.R, p.HG, 2 * DH, toks)),
                 whole((p.HG, 1, 2 * toks)),
             ],
             scratch_shapes=back_scratch(p),
@@ -2161,11 +2028,11 @@
         )(recv, small, dout, of, rl)
         grads = comm_call(
             functools.partial(return_grads, p),
-            (p.U, 3 * p.F, toks),
+            (p.U, p.HG, 3 * DH, toks),
             (dq, dkv),
             [
-                pltpu.VMEM((max(p.W - 1, 1), p.J, 2 * p.F, toks), B16),
-                pltpu.VMEM((p.J, 3 * p.F, toks), B16),
+                pltpu.VMEM((max(p.W - 1, 1), p.J, p.HG, 2 * DH, toks), B16),
+                pltpu.VMEM((p.J, p.HG, 3 * DH, toks), B16),
                 dma((p.J,)),
                 dma((max(p.W - 1, 1), p.J)),
                 dma((max(p.W - 1, 1), p.J)),

time: 330 us -> 320 us (0.970)
  Pallas kernels: 324 us -> 314 us
    pallas_call x2, Pallas kernels: 191 us -> 181 us  [the longest x1 160 us: tail_call(): pl.pallas_call(functools.partial(tail_kernel, p, jobs, len(early), len(sh...]
where the time goes in v6:
time: 320 us; the launch traced here: 319 us
  Pallas kernels  314 us (98%)
  local copies, waits for them, and re-layouts  3.5 us (1%)
    pallas_call x1, Pallas kernels, tail_call(): pl.pallas_call(functools.partial(tail_kernel, p, jobs, len(early), len(sh...  160 us
    pallas_call x1, Pallas kernels, head_call(): pl.pallas_call(functools.partial(head_kernel, p), out_shape=[jax.ShapeDty...  108 us
    pallas_call x1, Pallas kernels, cross_back_moves_call(): pl.pallas_call(functools.partial(cross_back_moves_kernel, kernel, len(arg...  20.4 us
    pallas_call x1, Pallas kernels, local(): pl.pallas_call(ffn_kernel, grid=(ff // chunk,), out_shape=[jax.ShapeDtype...  14.3 us
    pallas_call x1, Pallas kernels, widen(): pl.pallas_call(functools.partial(widen_kernel, len(mats)), grid=(parts,),...  11 us

profile of v6, /device:TPU:0, one launch (start us, length us, event | category | flops | bytes accessed | tf_op | source)
XLA Modules:
  0.0 319.3 jit_solution(15615574261864328314)
XLA Ops:
  0.7 108.2 %head.1 = (bf16[2,384,768]{2,1,0:T(8,128)(2,1)}, bf16[2,384,768]{2,1,0:T(8,128)(2,1)}, bf16[2,384,768]{2,1,0:T(8,128)(2,1)}, bf16[2,384,768]{2,1,0:T(8,128)(2,1)...) custom-call(f32[384,768]{1,0:T(8,128)} %refs_0_.1, ...), custom_call_target="tpu_custom_call" | custom-call | tf_op jit(solution)/shard_map/head/pallas_call | solution.py:1741
  108.9 14.3 %ffn.1 = (bf16[256,768]{1,0:T(8,128)(2,1)}, f32[256,768]{1,0:T(8,128)}, f32[1,768]{1,0:T(1,128)}, bf16[768,2048]{1,0:T(8,128)(2,1)}, bf16[768,2048]{1,0:T(8,128)(2,1)}, /*index=5*/bf16[2048,768]{1,0:T(8,128)(2,1)}) custom-call(f32[256,768]{1,0:T(8,128)} %get-tuple-element.85.x2_ref, bf16[256,768]{1,0:T(8,128)(2,1)} %bitcast.26, ...), custom_call_target="tpu_custom_call" | custom-call | tf_op jit(solution)/shard_map/ffn/pallas_call | solution.py:1912
  123.2 20.4 %cross_back.1 = (f32[256,768]{1,0:T(8,128)}, f32[1,768]{1,0:T(1,128)}, bf16[8,3,64,128]{3,2,1,0:T(8,128)(2,1)}, bf16[1024,768]{1,0:T(8,128)(2,1)}, bf16[768,768]...) custom-call(f32[256,768]{1,0:T(8,128)} %get-tuple-element.94.refs_0_, ...), custom_call_target="tpu_custom_call" | custom-call | tf_op jit(solution)/shard_map/cross_back/pallas_call | solution.py:751
  143.6 160.2 %tail.1 = (bf16[384,2048]{1,0:T(8,128)(2,1)}, bf16[384,2048]{1,0:T(8,128)(2,1)}, bf16[1024,768]{1,0:T(8,128)(2,1)}, bf16[384,768]{1,0:T(8,128)(2,1)}, bf16[384,7...) custom-call(bf16[2,384,2048]{2,1,0:T(8,128)(2,1)} %bitcast.14, ...), custom_call_target="tpu_custom_call" | custom-call | tf_op jit(solution)/shard_map/tail/pallas_call | solution.py:1302
  303.8 0.0 slice-start
  303.8 0.0 copy-start
  303.8 0.0 copy-start.1
  303.9 11.0 %widen.1 = (f32[384,2048]{1,0:T(8,128)}, f32[384,2048]{1,0:T(8,128)}, f32[1024,768]{1,0:T(8,128)}, f32[384,768]{1,0:T(8,128)}, f32[384,768]{1,0:T(8,128)}, /*ind...) custom-call(bf16[384,2048]{1,0:T(8,128)(2,1)} %get-tuple-element.129, ...), custom_call_target="tpu_custom_call" | custom-call | tf_op jit(solution)/shard_map/widen/pallas_call | solution.py:1331
  314.8 0.0 slice-done
  314.8 1.0 fusion.1
  315.8 0.6 constant_dynamic-slice_fusion
  316.4 1.5 dynamic-slice_reduce_fusion
  317.9 0.0 copy-done
  317.9 0.7 copy.39
  318.7 0.0 copy-done.1
  318.7 0.6 copy.40
Async XLA Ops:
  303.8 11.0 %slice-start = ((s32[2048]{0:T(1024)}), s32[256]{0:T(256)S(1)}, s32[]{:S(2)}) async-start(s32[2048]{0:T(1024)} %refs_17_.2), calls=%async_computation | async-start | bytes 2048 | tf_op jit(solution)/shard_map/slice | solution.py:1785
  303.8 14.1 %copy-start = (bf16[2,128,768]{2,1,0:T(8,128)(2,1)S(1)}, bf16[2,128,768]{2,1,0:T(8,128)(2,1)}, u32[]{:S(2)}) copy-start(bf16[2,128,768]{2,1,0:T(8,128)(2,1)} %get-tuple-element.174) | copy-start | bytes 1179652
  303.8 14.8 %copy-start.1 = (bf16[2,32,768]{2,1,0:T(8,128)(2,1)S(1)}, bf16[2,32,768]{2,1,0:T(8,128)(2,1)}, u32[]{:S(2)}) copy-start(bf16[2,32,768]{2,1,0:T(8,128)(2,1)} %get-tuple-element.175) | copy-start | bytes 294916

commit v7 on v6

--- a/solution.py
+++ b/solution.py
@@ -1113,7 +1113,7 @@
     ]
 
 
-EARLY = [(ROW, 1, 2, 3), (ROW, 2, 1, 3), (ROW, 1, 2, 3), (ROW, 1, 2, 3)]
+EARLY = [(ROW, 1, 2, 3), (2, ROW, 1, 3), (ROW, 1, 2, 3), (ROW, 1, 2, 3)]
 LATE = [(ROW, 1, 2, 3)] * 3
 SMALL_ROWS = 16
 FETCH_LAG = 3
@@ -1324,7 +1324,7 @@
 
 
 def widen(mats):
-    parts = 8
+    parts = 2
     blocks = [
         pl.BlockSpec((m.shape[0] // parts, m.shape[1]), lambda i: (i, 0)) for m in mats
     ]
@@ -1505,7 +1505,7 @@
                 own,
                 fetch_sems,
                 i,
-                i < 5 or i % 2 == 0,
+                3 <= i < 5 or (i > 4 and i % 2 == 0),
             )
         )
 

time: 320 us -> 313 us (0.978)
  Pallas kernels: 314 us -> 307 us
    pallas_call x1, Pallas kernels: 108 us -> 103 us  [head_call(): pl.pallas_call(functools.partial(head_kernel, p), out_shape=[jax.ShapeDty...]
where the time goes in v7:
time: 313 us; the launch traced here: 312 us
  Pallas kernels  307 us (98%)
  local copies, waits for them, and re-layouts  3.5 us (1%)
    pallas_call x1, Pallas kernels, tail_call(): pl.pallas_call(functools.partial(tail_kernel, p, jobs, len(early), len(sh...  160 us
    pallas_call x1, Pallas kernels, head_call(): pl.pallas_call(functools.partial(head_kernel, p), out_shape=[jax.ShapeDty...  103 us
    pallas_call x1, Pallas kernels, cross_back_moves_call(): pl.pallas_call(functools.partial(cross_back_moves_kernel, kernel, len(arg...  20.4 us
    pallas_call x1, Pallas kernels, local(): pl.pallas_call(ffn_kernel, grid=(ff // chunk,), out_shape=[jax.ShapeDtype...  14.3 us
    pallas_call x1, Pallas kernels, widen(): pl.pallas_call(functools.partial(widen_kernel, len(mats)), grid=(parts,),...  9.33 us

profile of v7, /device:TPU:0, one launch (start us, length us, event | category | flops | bytes accessed | tf_op | source)
XLA Modules:
  0.0 312.2 jit_solution(9167369251588765468)
XLA Ops:
  0.7 102.6 %head.1 = (bf16[2,384,768]{2,1,0:T(8,128)(2,1)}, bf16[2,384,768]{2,1,0:T(8,128)(2,1)}, bf16[2,384,768]{2,1,0:T(8,128)(2,1)}, bf16[2,384,768]{2,1,0:T(8,128)(2,1)...) custom-call(f32[384,768]{1,0:T(8,128)} %refs_0_.1, ...), custom_call_target="tpu_custom_call" | custom-call | tf_op jit(solution)/shard_map/head/pallas_call | solution.py:1741
  103.3 14.3 %ffn.1 = (bf16[256,768]{1,0:T(8,128)(2,1)}, f32[256,768]{1,0:T(8,128)}, f32[1,768]{1,0:T(1,128)}, bf16[768,2048]{1,0:T(8,128)(2,1)}, bf16[768,2048]{1,0:T(8,128)(2,1)}, /*index=5*/bf16[2048,768]{1,0:T(8,128)(2,1)}) custom-call(f32[256,768]{1,0:T(8,128)} %get-tuple-element.85.x2_ref, bf16[256,768]{1,0:T(8,128)(2,1)} %bitcast.26, ...), custom_call_target="tpu_custom_call" | custom-call | tf_op jit(solution)/shard_map/ffn/pallas_call | solution.py:1912
  117.6 20.4 %cross_back.1 = (f32[256,768]{1,0:T(8,128)}, f32[1,768]{1,0:T(1,128)}, bf16[8,3,64,128]{3,2,1,0:T(8,128)(2,1)}, bf16[1024,768]{1,0:T(8,128)(2,1)}, bf16[768,768]...) custom-call(f32[256,768]{1,0:T(8,128)} %get-tuple-element.94.refs_0_, ...), custom_call_target="tpu_custom_call" | custom-call | tf_op jit(solution)/shard_map/cross_back/pallas_call | solution.py:751
  138.0 160.3 %tail.1 = (bf16[384,2048]{1,0:T(8,128)(2,1)}, bf16[384,2048]{1,0:T(8,128)(2,1)}, bf16[1024,768]{1,0:T(8,128)(2,1)}, bf16[384,768]{1,0:T(8,128)(2,1)}, bf16[384,7...) custom-call(bf16[2,384,2048]{2,1,0:T(8,128)(2,1)} %bitcast.14, ...), custom_call_target="tpu_custom_call" | custom-call | tf_op jit(solution)/shard_map/tail/pallas_call | solution.py:1302
  298.3 0.0 slice-start
  298.3 0.0 copy-start
  298.3 0.0 copy-start.1
  298.4 9.3 %widen.1 = (f32[384,2048]{1,0:T(8,128)}, f32[384,2048]{1,0:T(8,128)}, f32[1024,768]{1,0:T(8,128)}, f32[384,768]{1,0:T(8,128)}, f32[384,768]{1,0:T(8,128)}, /*ind...) custom-call(bf16[384,2048]{1,0:T(8,128)(2,1)} %get-tuple-element.129, ...), custom_call_target="tpu_custom_call" | custom-call | tf_op jit(solution)/shard_map/widen/pallas_call | solution.py:1331
  307.7 0.0 slice-done
  307.7 1.0 fusion.1
  308.7 0.6 constant_dynamic-slice_fusion
  309.3 1.5 dynamic-slice_reduce_fusion
  310.8 0.0 copy-done
  310.8 0.7 copy.39
  311.5 0.0 copy-done.1
  311.6 0.6 copy.40
Async XLA Ops:
  298.3 9.4 %slice-start = ((s32[2048]{0:T(1024)}), s32[256]{0:T(256)S(1)}, s32[]{:S(2)}) async-start(s32[2048]{0:T(1024)} %refs_17_.2), calls=%async_computation | async-start | bytes 2048 | tf_op jit(solution)/shard_map/slice | solution.py:1785
  298.3 12.5 %copy-start = (bf16[2,128,768]{2,1,0:T(8,128)(2,1)S(1)}, bf16[2,128,768]{2,1,0:T(8,128)(2,1)}, u32[]{:S(2)}) copy-start(bf16[2,128,768]{2,1,0:T(8,128)(2,1)} %get-tuple-element.174) | copy-start | bytes 1179652
  298.3 13.2 %copy-start.1 = (bf16[2,32,768]{2,1,0:T(8,128)(2,1)S(1)}, bf16[2,32,768]{2,1,0:T(8,128)(2,1)}, u32[]{:S(2)}) copy-start(bf16[2,32,768]{2,1,0:T(8,128)(2,1)} %get-tuple-element.175) | copy-start | bytes 294916

commit v8 on v7

--- a/solution.py
+++ b/solution.py
@@ -1116,7 +1116,7 @@
 EARLY = [(ROW, 1, 2, 3), (2, ROW, 1, 3), (ROW, 1, 2, 3), (ROW, 1, 2, 3)]
 LATE = [(ROW, 1, 2, 3)] * 3
 SMALL_ROWS = 16
-FETCH_LAG = 3
+FETCH_LAG = 5
 FIRST_LAG = 3
 LAG = 2
 TICKS = (4, 1, 1, 2)
@@ -1556,7 +1556,7 @@
                 relayed += 1
 
     def slot():
-        begin()
+        begin(2)
         if started - relayed > FETCH_LAG or started == len(fetches):
             pass_on()
 

time: 313 us -> 311 us (level)
  no operation moved by 1% of the time
where the time goes in v8:
time: 311 us; the launch traced here: 310 us
  Pallas kernels  305 us (98%)
  local copies, waits for them, and re-layouts  3.5 us (1%)
    pallas_call x1, Pallas kernels, tail_call(): pl.pallas_call(functools.partial(tail_kernel, p, jobs, len(early), len(sh...  159 us
    pallas_call x1, Pallas kernels, head_call(): pl.pallas_call(functools.partial(head_kernel, p), out_shape=[jax.ShapeDty...  102 us
    pallas_call x1, Pallas kernels, cross_back_moves_call(): pl.pallas_call(functools.partial(cross_back_moves_kernel, kernel, len(arg...  20.4 us
    pallas_call x1, Pallas kernels, local(): pl.pallas_call(ffn_kernel, grid=(ff // chunk,), out_shape=[jax.ShapeDtype...  14.3 us
    pallas_call x1, Pallas kernels, widen(): pl.pallas_call(functools.partial(widen_kernel, len(mats)), grid=(parts,),...  9.33 us

profile of v8, /device:TPU:0, one launch (start us, length us, event | category | flops | bytes accessed | tf_op | source)
XLA Modules:
  0.0 310.2 jit_solution(8183016591914165942)
XLA Ops:
  0.7 102.0 %head.1 = (bf16[2,384,768]{2,1,0:T(8,128)(2,1)}, bf16[2,384,768]{2,1,0:T(8,128)(2,1)}, bf16[2,384,768]{2,1,0:T(8,128)(2,1)}, bf16[2,384,768]{2,1,0:T(8,128)(2,1)...) custom-call(f32[384,768]{1,0:T(8,128)} %refs_0_.1, ...), custom_call_target="tpu_custom_call" | custom-call | tf_op jit(solution)/shard_map/head/pallas_call | solution.py:1741
  102.6 14.3 %ffn.1 = (bf16[256,768]{1,0:T(8,128)(2,1)}, f32[256,768]{1,0:T(8,128)}, f32[1,768]{1,0:T(1,128)}, bf16[768,2048]{1,0:T(8,128)(2,1)}, bf16[768,2048]{1,0:T(8,128)(2,1)}, /*index=5*/bf16[2048,768]{1,0:T(8,128)(2,1)}) custom-call(f32[256,768]{1,0:T(8,128)} %get-tuple-element.85.x2_ref, bf16[256,768]{1,0:T(8,128)(2,1)} %bitcast.26, ...), custom_call_target="tpu_custom_call" | custom-call | tf_op jit(solution)/shard_map/ffn/pallas_call | solution.py:1912
  116.9 20.4 %cross_back.1 = (f32[256,768]{1,0:T(8,128)}, f32[1,768]{1,0:T(1,128)}, bf16[8,3,64,128]{3,2,1,0:T(8,128)(2,1)}, bf16[1024,768]{1,0:T(8,128)(2,1)}, bf16[768,768]...) custom-call(f32[256,768]{1,0:T(8,128)} %get-tuple-element.94.refs_0_, ...), custom_call_target="tpu_custom_call" | custom-call | tf_op jit(solution)/shard_map/cross_back/pallas_call | solution.py:751
  137.3 159.0 %tail.1 = (bf16[384,2048]{1,0:T(8,128)(2,1)}, bf16[384,2048]{1,0:T(8,128)(2,1)}, bf16[1024,768]{1,0:T(8,128)(2,1)}, bf16[384,768]{1,0:T(8,128)(2,1)}, bf16[384,7...) custom-call(bf16[2,384,2048]{2,1,0:T(8,128)(2,1)} %bitcast.14, ...), custom_call_target="tpu_custom_call" | custom-call | tf_op jit(solution)/shard_map/tail/pallas_call | solution.py:1302
  296.3 0.0 slice-start
  296.3 0.0 copy-start
  296.3 0.0 copy-start.1
  296.3 9.3 %widen.1 = (f32[384,2048]{1,0:T(8,128)}, f32[384,2048]{1,0:T(8,128)}, f32[1024,768]{1,0:T(8,128)}, f32[384,768]{1,0:T(8,128)}, f32[384,768]{1,0:T(8,128)}, /*ind...) custom-call(bf16[384,2048]{1,0:T(8,128)(2,1)} %get-tuple-element.129, ...), custom_call_target="tpu_custom_call" | custom-call | tf_op jit(solution)/shard_map/widen/pallas_call | solution.py:1331
  305.7 0.0 slice-done
  305.7 1.0 fusion.1
  306.7 0.6 constant_dynamic-slice_fusion
  307.3 1.5 dynamic-slice_reduce_fusion
  308.8 0.0 copy-done
  308.8 0.7 copy.39
  309.5 0.0 copy-done.1
  309.5 0.6 copy.40
Async XLA Ops:
  296.3 9.4 %slice-start = ((s32[2048]{0:T(1024)}), s32[256]{0:T(256)S(1)}, s32[]{:S(2)}) async-start(s32[2048]{0:T(1024)} %refs_17_.2), calls=%async_computation | async-start | bytes 2048 | tf_op jit(solution)/shard_map/slice | solution.py:1785
  296.3 12.5 %copy-start = (bf16[2,128,768]{2,1,0:T(8,128)(2,1)S(1)}, bf16[2,128,768]{2,1,0:T(8,128)(2,1)}, u32[]{:S(2)}) copy-start(bf16[2,128,768]{2,1,0:T(8,128)(2,1)} %get-tuple-element.174) | copy-start | bytes 1179652
  296.3 13.2 %copy-start.1 = (bf16[2,32,768]{2,1,0:T(8,128)(2,1)S(1)}, bf16[2,32,768]{2,1,0:T(8,128)(2,1)}, u32[]{:S(2)}) copy-start(bf16[2,32,768]{2,1,0:T(8,128)(2,1)} %get-tuple-element.175) | copy-start | bytes 294916
